TPU v7x, 32 devices: a whole 2x2x4 slice. The times are simulated.
32 devices in a mesh: groups: 2 (over y), rows: 4 (over z), mp: 2 (over x), sub: 2 (over core).
Axes of the slice: x: 2, y: 2, z: 4, core: 2. Of those that a mesh axis runs over, the one named last changes fastest.
Arguments:
- hidden: bfloat16 [4096, 4096], P(('groups', 'rows'), ('mp', 'sub')), parts along dimension 0, may hold values from -600 to 600
- neighbour_states: bfloat16 [128, 128, 4096], P(('groups', 'rows'), None, ('mp', 'sub')), parts along dimension 0, may hold values from -600 to 600
- query_weight: bfloat16 [4096, 4096], P(None, ('mp', 'sub')), may hold values from -0.1875 to 0.1875
- encoder_weight: bfloat16 [4096, 256], P(('mp', 'sub')), may hold values from -0.09375 to 0.09375
- output_weight: bfloat16 [4096, 4096], P(('mp', 'sub')), may hold values from -0.5 to 0.5
- neighbour_owner: int32 [64, 2], P(('groups', 'rows')), parts along dimension 0, may hold values from 0 to 3, all different within a row; in each aligned block of 8 rows (0 to 7, 8 to 15, ...) at most 4 rows name the same one
- neighbour_slot: int32 [64, 2], P(('groups', 'rows')), parts along dimension 0, may hold values from 0 to 15
- neighbour_length: int32 [128], P(('groups', 'rows')), parts along dimension 0, may hold values from 1 to 128, 6144 in all
Outputs:
- mixed: bfloat16 [4096, 4096], P(('groups', 'rows'), ('mp', 'sub')), parts along dimension 0
There are 2 independent parts, one for each index of `groups`. A program takes and returns all parts, laid end to end along the dimension named above; an argument that names none is the same for every part. Nothing has to cross between parts.
Inputs may be any that keep to these rules, and one draw needn't show every extreme that they name: `neighbour_owner`: A span's two owners differ; among the 8 spans of one index of rows no owner is named more than 4 times, a bound that some block reaches. `neighbour_length`: in each part (each index of groups) the lengths sum to 6144; some neighbour is live in all 128 slots.
All inputs are finite; a program needn't handle non-finite values.
Results may differ from a plain program's by a relative error of at most 0.033.
Values may be sent and summed in bfloat16 or wider, within the bound.
No kernel may reach another device: no remote copies, remote signals or barrier semaphores. Data moves between devices by JAX's collectives and lax.ppermute only.
A program may use at most 128 MiB of HBM per device.

v0:
```python
import math

import jax
import jax.numpy as jnp
from jax import lax
from jax.sharding import PartitionSpec as P

eps = 1e-05
softcap = 10.0


def request_ranks(owners):
    request_count = owners.shape[-1]
    same_owner = owners[..., :, None] == owners[..., None, :]
    earlier = jnp.arange(request_count)[None, :] < jnp.arange(request_count)[:, None]
    return jnp.sum((same_owner & earlier).astype(jnp.int32), axis=-1)


def shards(
    hidden,
    neighbour_states,
    query_weight,
    encoder_weight,
    output_weight,
    neighbour_owner,
    neighbour_slot,
    neighbour_length,
):
    row_count = lax.axis_size("rows")
    row_index = lax.axis_index("rows")
    group_size = lax.axis_size(("mp", "sub"))
    spans_here = neighbour_owner.shape[0]
    neighbours_here, slot_tokens, feature_shard = neighbour_states.shape
    feature_total = feature_shard * group_size
    pair_width = encoder_weight.shape[1]
    head_size = pair_width // 2
    token_count = hidden.shape[0]
    query_width = query_weight.shape[1]
    span_tokens = token_count // spans_here
    heads_here = query_width // head_size
    request_count = 2 * spans_here
    capacity = max(2, (request_count + row_count - 1) // row_count)
    all_owner, all_slot, all_length = (
        lax.all_gather(neighbour_owner, "rows", axis=0, tiled=True),
        lax.all_gather(neighbour_slot, "rows", axis=0, tiled=True),
        lax.all_gather(neighbour_length, "rows", axis=0, tiled=True),
    )
    owner_table = all_owner.reshape(row_count, request_count)
    slot_table = all_slot.reshape(row_count, request_count)
    rank_table = request_ranks(owner_table)
    slot_iota = jnp.arange(capacity)
    local_iota = jnp.arange(neighbours_here)
    send_match = (
        (owner_table == row_index)[:, :, None, None]
        & (rank_table[:, :, None, None] == slot_iota[None, None, :, None])
        & (slot_table[:, :, None, None] == local_iota[None, None, None, :])
    )
    selector = jnp.sum(send_match.astype(jnp.float32), axis=1).astype(jnp.bfloat16)
    own_owner = neighbour_owner.reshape(request_count)
    own_rank = request_ranks(own_owner[None, :])[0]
    target = own_owner * capacity + own_rank
    receive_pick = (target[:, None] == jnp.arange(row_count * capacity)[None, :]).astype(
        jnp.bfloat16
    )
    own_ids = (neighbour_owner * neighbours_here + neighbour_slot).reshape(request_count)
    id_match = own_ids[:, None] == jnp.arange(all_length.shape[0])[None, :]
    live_lengths = jnp.sum(jnp.where(id_match, all_length[None, :], 0), axis=1)
    flat_tokens = neighbour_states.reshape(neighbours_here * slot_tokens, feature_shard)
    encoder_terms = jnp.dot(flat_tokens, encoder_weight, preferred_element_type=jnp.float32)
    encoder_terms = encoder_terms.reshape(neighbours_here, slot_tokens, pair_width)
    square_terms = jnp.sum(jnp.square(neighbour_states.astype(jnp.float32)), axis=-1)
    summed, square_sums = (
        lax.psum(encoder_terms.astype(jnp.bfloat16), ("mp", "sub")).astype(jnp.float32),
        lax.psum(square_terms.astype(jnp.bfloat16), ("mp", "sub")).astype(jnp.float32),
    )
    encoded = (summed * lax.rsqrt(square_sums / feature_total + eps)[..., None]).astype(
        jnp.bfloat16
    )
    send_buffer = jnp.einsum(
        "rsn,ntc->rstc", selector, encoded, preferred_element_type=jnp.float32
    ).astype(jnp.bfloat16)
    received = lax.all_to_all(send_buffer, "rows", split_axis=0, concat_axis=0, tiled=True)
    received = received.reshape(row_count * capacity, slot_tokens, pair_width)
    gathered = jnp.einsum(
        "qm,mtc->qtc", receive_pick, received, preferred_element_type=jnp.float32
    ).astype(jnp.bfloat16)
    piece = lax.all_gather(hidden, ("mp", "sub"), axis=1, tiled=True)
    accumulated = jnp.dot(piece, query_weight, preferred_element_type=jnp.float32)
    squares = jnp.sum(jnp.square(piece.astype(jnp.float32)), axis=1)
    queries = (accumulated * lax.rsqrt(squares / feature_total + eps)[:, None]).astype(jnp.bfloat16)
    query_heads = queries.reshape(spans_here, span_tokens, heads_here, head_size)
    span_pairs = gathered.reshape(spans_here, 2 * slot_tokens, pair_width)
    keys = span_pairs[..., :head_size]
    values = span_pairs[..., head_size:]
    raw_scores = jnp.einsum("cthd,ckd->chtk", query_heads, keys, preferred_element_type=jnp.float32)
    scores = softcap * jnp.tanh(raw_scores / (softcap * math.sqrt(head_size)))
    valid = (jnp.arange(slot_tokens)[None, :] < live_lengths[:, None]).reshape(
        spans_here, 2 * slot_tokens
    )
    exp_scores = jnp.where(valid[:, None, None, :], jnp.exp(scores), 0.0)
    weights = (exp_scores / jnp.sum(exp_scores, axis=-1, keepdims=True)).astype(jnp.bfloat16)
    attended = jnp.einsum(
        "chtk,ckd->cthd", weights, values, preferred_element_type=jnp.float32
    ).astype(jnp.bfloat16)
    attended = attended.reshape(token_count, query_width)
    output_terms = jnp.dot(attended, output_weight, preferred_element_type=jnp.float32)
    mixed = lax.psum_scatter(
        output_terms.astype(jnp.bfloat16), ("mp", "sub"), scatter_dimension=1, tiled=True
    )
    return mixed


def solution(mesh):
    placed = (
        P(("groups", "rows"), ("mp", "sub")),
        P(("groups", "rows"), None, ("mp", "sub")),
        P(None, ("mp", "sub")),
        P(("mp", "sub"), None),
        P(("mp", "sub"), None),
        P(("groups", "rows"), None),
        P(("groups", "rows"), None),
        P(("groups", "rows")),
    )
    return jax.shard_map(
        shards,
        mesh=mesh,
        in_specs=placed,
        out_specs=P(("groups", "rows"), ("mp", "sub")),
        check_vma=False,
    )
```

profile of v0, /device:TPU:0, one launch (start us, length us, event | category | flops | bytes accessed | tf_op | source)
XLA Modules:
  0.0 162.0 jit_solution(14166260191659699522)
XLA Ops:
  6.5 1.0 copy-done
  7.6 5.7 %fusion.8 = bf16[16,128,256]{2,0,1:T(8,128)(2,1)} fusion(bf16[16,128,1024]{2,1,0:T(8,128)(2,1)} %param.9, bf16[1024,256]{1,0:T(8,128)(2,1)S(1)} %copy-done), kind=kOutput, calls=%fused_computation.13 | convolution fusion | flops 1074266112 | bytes 5767168 | tf_op jit(solution)/shard_map/dot_general | solution.py:69
  13.3 0.0 all-reduce.3.cloned.1.call-update
  13.3 0.0 all-gather.4.cloned.1.call-start
  13.4 0.7 all-gather.4.cloned.1.call-update
  14.1 12.6 %all-gather = s32[4,8,2]{1,2,0:T(2,128)S(1)} all-gather(s32[1,8,2]{1,2,0:T(2,128)S(1)} %bitcast.69), channel_id=1, replica_groups=mesh['groups'=2,'rows'=4,'mp'=2,'sub'=2] {'rows'}, dimensions={0}, use_global_device_ids=true | all-gather | bytes 320 | tf_op jit(solution)/shard_map/all_gather | solution.py:44
  26.7 0.1 copy.50
  26.8 0.1 copy.52
  26.9 0.1 copy.51
  27.0 7.6 %all-gather.1 = s32[4,8,2]{1,2,0:T(2,128)S(1)} all-gather(s32[1,8,2]{1,2,0:T(2,128)S(1)} %bitcast.70), channel_id=1, replica_groups=mesh['groups'=2,'rows'=4,'mp'=2,'sub'=2] {'rows'}, dimensions={0}, use_global_device_ids=true | all-gather | bytes 320 | tf_op jit(solution)/shard_map/all_gather | solution.py:45
  34.6 0.1 copy.54
  34.7 0.1 copy.55
  34.7 3.1 %multiply_reduce_fusion.1 = bf16[16,128]{1,0:T(8,128)(2,1)S(1)} fusion(bf16[16,128,1024]{2,1,0:T(8,128)(2,1)} %param.9), kind=kLoop, calls=%fused_computation.1 | loop fusion | flops 6289408 | bytes 4198400 | tf_op jit(solution)/shard_map/reduce_sum | solution.py:71
  37.8 5.7 %psum.15 = bf16[16,128]{1,0:T(8,128)(2,1)S(1)} all-reduce(bf16[16,128]{1,0:T(8,128)(2,1)S(1)} %multiply_reduce_fusion.1), channel_id=1, replica_groups=mesh['groups'=2,'rows'=4,'mp'=2,'sub'=2] {'mp','sub'}, use_global_device_ids=true, to_apply=%region_5.6 | all-reduce | flops 2048 | bytes 8192 | tf_op jit(solution)/shard_map/psum | solution.py:74
  43.5 0.1 copy.57
  43.7 0.2 convert_reduce_fusion.1
  43.9 0.1 iota_compare_fusion
  44.0 0.1 convert_reduce_fusion
  44.1 8.2 %all-reduce.3.cloned.1.call-done = bf16[16,128,256]{2,0,1:T(8,128)(2,1)} async-done(((bf16[16,128,256]{2,0,1:T(8,128)(2,1)}), bf16[16,128,256]{2,0,1:T(8,128)(2,1)}) %all-reduce.3.cloned.1.call-update) | async-done | bytes 1048592 | tf_op jit(solution)/shard_map/psum | solution.py:73
  52.3 2.7 %convolution_convert_fusion.2 = bf16[4,4,128,256]{3,1,2,0:T(4,128)(2,1)} fusion(bf16[16,128,256]{2,0,1:T(8,128)(2,1)} %all-reduce.3.cloned.1.call-done, f32[16,128]{0,1:T(8,128)S(1)} %copy.57, bf16[4,4,16]{2,1,0:T(4,128)(2,1)S(1)} %convert_reduce_fusion), kind=kOutput, calls=%fused_computation.15 | convolution fusion | flops 18874368 | bytes 2105856 | tf_op jit(solution)/shard_map/rsn,ntc->rstc/dot_general | solution.py:79
  55.1 4.6 %all-to-all-start = ((bf16[4,4,128,256]{3,1,2,0:T(4,128)(2,1)}), bf16[4,4,128,256]{3,1,2,0:T(4,128)(2,1)S(1)}, u32[]{:S(2)}, u32[]{:S(2)}) async-start(bf16[4,4,128,256]{3,1,2,0:T(4,128)(2,1)} %convolution_convert_fusion.2), calls=%async_computation | async-start | bytes 2097152 | tf_op jit(solution)/shard_map/all_to_all | solution.py:82
  59.7 0.1 copy.49
  59.8 0.1 copy.61
  59.9 0.1 eq.125
  59.9 0.6 dynamic-slice
  61.2 0.2 dynamic-update-slice
  61.4 23.7 %all-reduce = s32[64]{0:T(128)S(1)} all-reduce(s32[64]{0:T(128)S(1)} %dynamic-update-slice), channel_id=1, replica_groups=mesh['groups'=2,'rows'=4,'mp'=2,'sub'=2] {'rows'}, use_global_device_ids=true, to_apply=%add | all-reduce | flops 64 | bytes 512
  85.1 0.2 select_reduce_fusion
  85.3 0.1 lt.73
  85.4 0.1 copy.62
  85.5 0.1 reshape.181
  85.6 0.2 convert_reduce_fusion.2
  85.8 0.1 bitcast_compare_fusion
  85.8 0.2 copy.58
  86.0 0.7 convolution_convert_fusion.1
  86.7 0.4 copy.60
  87.1 1.8 %all-gather.4.cloned.1.call-done = bf16[512,4096]{1,0:T(8,128)(2,1)} async-done(((bf16[512,1024]{1,0:T(8,128)(2,1)}), bf16[512,4096]{1,0:T(8,128)(2,1)}) %all-gather.4.cloned.1.call-update) | async-done | bytes 4194320 | tf_op jit(solution)/shard_map/all_gather | solution.py:87
  88.9 3.2 %multiply_reduce_fusion = f32[512]{0:T(512)S(1)} fusion(bf16[512,4096]{1,0:T(8,128)(2,1)} %all-gather.4.cloned.1.call-done), kind=kLoop, calls=%fused_computation | loop fusion | flops 6290944 | bytes 4196352 | tf_op jit(solution)/shard_map/reduce_sum | solution.py:89
  92.1 0.2 copy-done.1
  92.3 7.9 %fusion.14 = bf16[64,8,8,128]{3,1,2,0:T(8,128)(2,1)S(1)} fusion(bf16[512,4096]{1,0:T(8,128)(2,1)S(1)} %copy-done.1, bf16[4096,1024]{1,0:T(8,128)(2,1)} %param.10, f32[512]{0:T(512)S(1)} %add_rsqrt_fusion.1), kind=kOutput, calls=%fused_computation.17 | convolution fusion | flops 4296015872 | bytes 13633536 | tf_op jit(solution)/shard_map/dot_general | solution.py:88
  100.2 0.3 copy.68
  100.5 1.7 %bitcast_reduce_fusion = (f32[8,8,64]{2,1,0:T(8,128)S(1)}, f32[8,256,64,8]{1,2,3,0:T(8,128)S(1)}) fusion(pred[8,256]{1,0:T(8,128)(4,1)S(1)} %bitcast_compare_fusion, bf16[8,64,8,128]{3,2,1,0:T(8,128)(2,1)S(1)} %bitcast.64, bf16[8,256,256]{2,1,0:T(8,128)(2,1)S(1)} %bitcast.62), kind=kOutput, calls=%fused_computation.4 | convolution fusion | flops 272625664 | bytes 5785600 | tf_op jit(solution)/shard_map/cthd,ckd->chtk/dot_general | solution.py:95
  102.2 0.0 slice-start.1
  102.2 1.7 %fusion.11 = bf16[8,64,8,128]{3,1,2,0:T(8,128)(2,1)S(1)} fusion(f32[8,256,64,8]{1,2,3,0:T(8,128)S(1)} %get-tuple-element.6, f32[8,8,64]{2,1,0:T(8,128)S(1)} %get-tuple-element.5, pred[8,256]{1,0:T(8,128)(4,1)S(1)} %bitcast_compare_fusion, bf16[8,256,256]{2,1,0:T(8,128)(2,1)S(1)} %bitcast.63), kind=kOutput, calls=%fused_computation.16 | convolution fusion | flops 274202624 | bytes 5801984 | tf_op jit(solution)/shard_map/chtk,ckd->cthd/dot_general | solution.py:102
  103.9 0.7 copy.64
  104.6 6.1 %convolution_convert_fusion = bf16[512,4096]{1,0:T(8,128)(2,1)} fusion(bf16[1024,4096]{1,0:T(8,128)(2,1)S(1)} %bitcast.72, bf16[64,8,8,128]{3,2,1,0:T(8,128)(2,1)S(1)} %bitcast.65), kind=kOutput, calls=%fused_computation.2 | convolution fusion | flops 4297064448 | bytes 13631488 | tf_op jit(solution)/shard_map/dot_general | solution.py:106
  110.8 0.0 reduce-scatter.2.cloned.1.call-update
  110.8 44.7 %reduce-scatter.2.cloned.1.call-done = bf16[512,1024]{1,0:T(8,128)(2,1)} async-done(((bf16[512,4096]{1,0:T(8,128)(2,1)}), bf16[512,1024]{1,0:T(8,128)(2,1)}) %reduce-scatter.2.cloned.1.call-update) | async-done | bytes 1048592 | tf_op jit(solution)/shard_map/reduce_scatter | solution.py:107
  (26 shorter events, 0.1 us)
Async XLA Ops:
  6.5 1.0 copy-start
  6.5 7.6 %copy-start.2 = (s32[8,2]{0,1:T(2,128)S(1)}, s32[8,2]{0,1:T(2,128)}, u32[]{:S(2)}) copy-start(s32[8,2]{0,1:T(2,128)} %param.13) | copy-start | bytes 196
  6.5 20.5 %copy-start.3 = (s32[8,2]{0,1:T(2,128)S(1)}, s32[8,2]{0,1:T(2,128)}, u32[]{:S(2)}) copy-start(s32[8,2]{0,1:T(2,128)} %param.14) | copy-start | bytes 196
  6.5 45.8 %all-reduce.3.cloned.1.call-start = ((), (), s32[]{:S(2)}) async-start(), calls=%async_computation.2 | async-start | bytes 2097152 | tf_op jit(solution)/shard_map/psum | solution.py:73
  13.3 75.5 %all-gather.4.cloned.1.call-start = ((), (), s32[]{:S(2)}) async-start(), calls=%async_computation.3 | async-start | bytes 5242880 | tf_op jit(solution)/shard_map/all_gather | solution.py:87
  34.7 25.2 %copy-start.5 = (u32[32]{0:T(128)S(1)}, u32[32]{0:T(128)}, u32[]{:S(2)}) copy-start(u32[32]{0:T(128)} %constant.28) | copy-start | bytes 388
  34.7 26.4 %copy-start.4 = (s32[16]{0:T(128)S(1)}, s32[16]{0:T(128)}, u32[]{:S(2)}) copy-start(s32[16]{0:T(128)} %param.15) | copy-start | bytes 196
  55.1 30.7 %all-to-all-start = ((bf16[4,4,128,256]{3,1,2,0:T(4,128)(2,1)}), bf16[4,4,128,256]{3,1,2,0:T(4,128)(2,1)S(1)}, u32[]{:S(2)}, u32[]{:S(2)}) async-start(bf16[4,4,128,256]{3,1,2,0:T(4,128)(2,1)} %convolution_convert_fusion.2), calls=%async_computation | async-start | bytes 2097152 | tf_op jit(solution)/shard_map/all_to_all | solution.py:82
  59.7 95.8 %reduce-scatter.2.cloned.1.call-start = ((), (), s32[]{:S(2)}) async-start(), calls=%async_computation.4 | async-start | bytes 5242880 | tf_op jit(solution)/shard_map/reduce_scatter | solution.py:107
  88.9 3.4 %copy-start.1 = (bf16[512,4096]{1,0:T(8,128)(2,1)S(1)}, bf16[512,4096]{1,0:T(8,128)(2,1)}, u32[]{:S(2)}) copy-start(bf16[512,4096]{1,0:T(8,128)(2,1)} %all-gather.4.cloned.1.call-done) | copy-start | bytes 12582916
  100.5 4.1 %slice-start = ((s8[8388608]{0:T(1024)(128)(4,1)}), s8[4194304]{0:T(1024)(128)(4,1)S(1)}, s32[]{:S(2)}) async-start(s8[8388608]{0:T(1024)(128)(4,1)} %bitcast.71), calls=%async_computation.5 | async-start | bytes 8388608
  102.2 2.5 %slice-start.1 = ((s8[8388608]{0:T(1024)(128)(4,1)}), s8[4194304]{0:T(1024)(128)(4,1)S(1)}, s32[]{:S(2)}) async-start(s8[8388608]{0:T(1024)(128)(4,1)} %bitcast.71), calls=%async_computation.6 | async-start | bytes 8388608
Sparse Core Ops, SparseCore 0:
  13.4 38.8 all-reduce.2
  54.0 34.8 all-gather.3
  110.9 44.5 reduce-scatter.1
where the time goes:
time: 162 us
  waiting for transfers between devices  55.4 us (34%)
  blocking collectives  49.6 us (31%)
  matrix products  26.6 us (16%)
  between operations  13.9 us (9%)
  other arithmetic  7.24 us (4%)
  local copies, waits for them, and re-layouts  4.65 us (3%)
  starting transfers between devices  4.65 us (3%)
    reduce_scatter x1, waiting for transfers between devices, shards(): lax.psum_scatter(output_terms.astype(jnp.bfloat16), ('mp', 'sub'), scatte...  44.7 us
    unnamed x1, blocking collectives  23.7 us
    all_gather x1, blocking collectives, shards(): lax.all_gather(neighbour_owner, 'rows', axis=0, tiled=True)  12.6 us
    psum x1, waiting for transfers between devices, shards(): lax.psum(encoder_terms.astype(jnp.bfloat16), ('mp', 'sub'))  8.24 us
    dot_general x1, matrix products, shards(): jnp.dot(piece, query_weight, preferred_element_type=jnp.float32)  7.87 us
    all_gather x1, blocking collectives, shards(): lax.all_gather(neighbour_slot, 'rows', axis=0, tiled=True)  7.56 us
    dot_general x1, matrix products, shards(): jnp.dot(attended, output_weight, preferred_element_type=jnp.float32)  6.11 us
    dot_general x1, matrix products, shards(): jnp.dot(flat_tokens, encoder_weight, preferred_element_type=jnp.float32)  5.73 us
  transfers between devices with their start and end apart: 4, of which 3 were waited for; matrix products, arithmetic and copies ran while one was open for 6% of the time, Pallas kernels for 0%

commit v1 on v0

v1 whole, which is shorter than its diff:
```python
import functools
import math

import jax
import jax.numpy as jnp
from jax import lax
from jax.experimental import pallas as pl
from jax.experimental.pallas import tpu as pltpu
from jax.sharding import PartitionSpec as P

eps = 1e-05
softcap = 10.0
f32 = jnp.float32
bf16 = jnp.bfloat16

VMEM_LIMIT = 48 * 1024 * 1024


def shift(value, axis, by):
    size = lax.axis_size(axis)
    return lax.ppermute(value, axis, [(i, (i + by) % size) for i in range(size)])


def cost(flops, nbytes, transcendentals=0):
    return pl.CostEstimate(flops=flops, bytes_accessed=nbytes, transcendentals=transcendentals)


def params():
    return pltpu.CompilerParams(vmem_limit_bytes=VMEM_LIMIT)


def encode_kernel(meta, x_ref, w_ref, out_ref, squares, *, pieces, piece, count):
    step = pl.program_id(0)
    mp, sub, size = meta[1], meta[2], pieces // 2
    block, tokens, width = x_ref.shape
    x = x_ref[...].reshape(block * tokens, width)
    product = jnp.dot(x, w_ref[...], preferred_element_type=f32).astype(bf16)
    xf = x.astype(f32)
    square = jnp.sum(xf * xf, axis=1, keepdims=True)
    diagonal = lax.broadcasted_iota(jnp.int32, (piece, 128), 0) == lax.broadcasted_iota(
        jnp.int32, (piece, 128), 1
    )
    for a in range(pieces):
        far_mp = lax.rem(a // 2 - mp + size, size)
        far_sub = lax.rem(a % 2 + sub, 2)
        for n in range(block):
            low = n * tokens + a * piece
            out_ref[far_sub, far_mp, pl.ds(pl.multiple_of((step * block + n) * piece, piece), piece), :] = (
                product[low : low + piece]
            )
            column = jnp.broadcast_to(square[low : low + piece], (piece, 128))
            squares[a, pl.ds(step * block + n, 1), :] = jnp.sum(
                jnp.where(diagonal, column, 0.0), axis=0, keepdims=True
            )

    @pl.when(step == pl.num_programs(0) - 1)
    def _():
        for a in range(pieces):
            far_mp = lax.rem(a // 2 - mp + size, size)
            far_sub = lax.rem(a % 2 + sub, 2)
            out_ref[far_sub, far_mp, pl.ds(count * piece, count), :] = jnp.concatenate(
                [squares[a], jnp.zeros_like(squares[a])], axis=1
            ).astype(bf16)


def encode(meta, states, weight, pieces):
    count, tokens, width = states.shape
    out_width = weight.shape[1]
    piece = tokens // pieces
    rows = count * piece + count
    block = 4
    return pl.pallas_call(
        functools.partial(encode_kernel, pieces=pieces, piece=piece, count=count),
        grid_spec=pltpu.PrefetchScalarGridSpec(
            num_scalar_prefetch=1,
            grid=(count // block,),
            in_specs=[
                pl.BlockSpec((block, tokens, width), lambda i, m: (i, 0, 0)),
                pl.BlockSpec((width, out_width), lambda i, m: (0, 0)),
            ],
            out_specs=pl.BlockSpec((2, pieces // 2, rows, out_width), lambda i, m: (0, 0, 0, 0)),
            scratch_shapes=[pltpu.VMEM((pieces, count, 128), f32)],
        ),
        out_shape=jax.ShapeDtypeStruct((2, pieces // 2, rows, out_width), bf16),
        compiler_params=params(),
        cost_estimate=cost(2 * count * tokens * width * out_width, 2 * count * tokens * width),
        name="encode",
    )(meta, states, weight)


def route_kernel(meta, table, *refs, row_count, cap, piece, count, requests, features, terms):
    ins, outs = refs[:terms], refs[terms : terms + row_count]
    encoded, picks = refs[terms + row_count :]
    me = meta[0]
    total = ins[0][...].astype(f32)
    for ref in ins[1:]:
        total = total + ref[...].astype(f32)
    total = total.reshape(total.shape[-2:])
    scale = lax.rsqrt(total[count * piece :, :128] * (1.0 / features) + eps)
    diagonal = lax.broadcasted_iota(jnp.int32, (piece, 128), 0) == lax.broadcasted_iota(
        jnp.int32, (piece, 128), 1
    )
    for n in range(count):
        row = jnp.broadcast_to(scale[n : n + 1], (piece, 128))
        column = jnp.sum(jnp.where(diagonal, row, 0.0), axis=1, keepdims=True)
        encoded[n] = (total[n * piece : (n + 1) * piece] * column).astype(bf16)
    for d in range(row_count):
        for r in range(cap):
            picks[d, r] = 0
        seen = jnp.int32(0)
        for q in range(requests):
            mine = table[d, q] == me

            @pl.when(mine)
            def _(seen=seen, q=q, d=d):
                picks[d, jnp.minimum(seen, cap - 1)] = table[d, requests + q]

            seen = seen + mine.astype(jnp.int32)
        for r in range(cap):
            outs[d][r] = encoded[picks[d, r]]


def route(meta, table, kept, received, crossed, cap, features, count, requests):
    row_count = table.shape[0]
    rows, width = kept.shape[-2:]
    piece = rows // count - 1
    terms = 2 + len(crossed)
    lead = pl.BlockSpec((None, 1, rows, width), lambda i, m, t: (0, 0, 0, 0))
    return pl.pallas_call(
        functools.partial(
            route_kernel, row_count=row_count, cap=cap, piece=piece, count=count,
            requests=requests, features=features, terms=terms,
        ),
        grid_spec=pltpu.PrefetchScalarGridSpec(
            num_scalar_prefetch=2,
            grid=(1,),
            in_specs=[lead, pl.BlockSpec((1, rows, width), lambda i, m, t: (0, 0, 0))]
            + [pl.BlockSpec((rows, width), lambda i, m, t: (0, 0))] * len(crossed),
            out_specs=[pl.BlockSpec((cap, piece, width), lambda i, m, t: (0, 0, 0))] * row_count,
            scratch_shapes=[
                pltpu.VMEM((count, piece, width), bf16),
                pltpu.SMEM((row_count, cap), jnp.int32),
            ],
        ),
        out_shape=[jax.ShapeDtypeStruct((cap, piece, width), bf16)] * row_count,
        compiler_params=params(),
        cost_estimate=cost(8 * rows * width, 2 * rows * width * terms),
        name="route",
    )(meta, table, kept, received, *crossed)


def query_kernel(blocks, *refs, pieces, features, gain):
    hs, w_ref, out_ref, total, squares = refs[:pieces], *refs[pieces:]
    step = pl.program_id(0)

    @pl.when(step == 0)
    def _():
        total[...] = jnp.zeros_like(total)
        squares[...] = jnp.zeros_like(squares)

    for k in range(pieces):

        @pl.when(step == k)
        def _(k=k):
            h = hs[k][...]
            total[...] += jnp.dot(h, w_ref[...], preferred_element_type=f32)
            hf = h.astype(f32)
            squares[...] += jnp.sum(hf * hf, axis=1, keepdims=True)

    @pl.when(step == pieces - 1)
    def _():
        scale = lax.rsqrt(squares[...] * (1.0 / features) + eps) * gain
        out_ref[...] = (total[...] * scale).astype(bf16)


def project_queries(blocks, parts, weight, gain):
    tokens, width = parts[0].shape
    pieces = len(parts)
    out_width = weight.shape[1]
    return pl.pallas_call(
        functools.partial(query_kernel, pieces=pieces, features=width * pieces, gain=gain),
        grid_spec=pltpu.PrefetchScalarGridSpec(
            num_scalar_prefetch=1,
            grid=(pieces,),
            in_specs=[pl.BlockSpec((tokens, width), lambda i, b: (0, 0))] * pieces
            + [pl.BlockSpec((width, out_width), lambda i, b: (b[i], 0))],
            out_specs=pl.BlockSpec((tokens, out_width), lambda i, b: (0, 0)),
            scratch_shapes=[pltpu.VMEM((tokens, out_width), f32), pltpu.VMEM((tokens, 1), f32)],
        ),
        out_shape=jax.ShapeDtypeStruct((tokens, out_width), bf16),
        compiler_params=params(),
        cost_estimate=cost(2 * tokens * width * pieces * out_width, 2 * width * pieces * out_width),
        name="queries",
    )(blocks, *parts, weight)


def attend_kernel(
    meta, table, live, blocks, *refs, chunk, spans, span, heads, size, pieces, cap, piece, requests
):
    q_ref = refs[0]
    kvs = refs[1 : 1 + pieces]
    w_ref, out_ref, att_ref, pair = refs[1 + pieces :]
    me, mp, sub = meta[0], meta[1], meta[2]
    row_count = table.shape[0]
    group = pieces // 2

    @pl.when(pl.program_id(0) == 0)
    def _():
        local = lax.broadcasted_iota(jnp.int32, (piece, size), 0)
        for c in range(spans):
            masks = []
            for j in range(2):
                q = 2 * (chunk * spans + c) + j
                owner = table[0, q]
                rank = jnp.int32(0)
                for e in range(q):
                    rank = rank + (table[0, e] == owner).astype(jnp.int32)
                slot = lax.rem(me - owner + row_count, row_count) * cap + rank
                length = live[lax.rem(owner - me + row_count, row_count), table[0, requests + q]]
                for p in range(pieces):
                    low = (j * pieces + p) * piece
                    pair[low : low + piece, :] = kvs[p][slot]
                    place = lax.rem(mp - p // 2 + group, group) * 2 + lax.rem(sub + p % 2, 2)
                    masks.append((local + place * piece < length).astype(f32))
            mask = jnp.concatenate(masks, axis=0)
            keys = pair[:, :size]
            values = jnp.concatenate(
                [(pair[:, size:].astype(f32) * mask).astype(bf16), mask.astype(bf16)], axis=1
            )
            rows = slice(c * span, (c + 1) * span)
            query = jnp.concatenate(
                [q_ref[rows, h * size : (h + 1) * size] for h in range(heads)], axis=0
            )
            scores = lax.dot_general(
                query, keys, (((1,), (1,)), ((), ())), preferred_element_type=f32
            )
            weights = jnp.exp(softcap * jnp.tanh(scores)).astype(bf16)
            summed = jnp.dot(weights, values, preferred_element_type=f32)
            attended = (summed[:, :size] / summed[:, size:]).astype(bf16)
            for h in range(heads):
                att_ref[rows, h * size : (h + 1) * size] = attended[h * span : (h + 1) * span]

    out_ref[...] = jnp.dot(att_ref[...], w_ref[...], preferred_element_type=f32).astype(bf16)


def attend(meta, table, live, blocks, queries, pairs, weight, chunk, spans, span, out_width, cap):
    tokens, width = queries.shape
    pieces = len(pairs)
    piece = pairs[0].shape[1]
    pair_width = pairs[0].shape[2]
    size = pair_width // 2
    steps = blocks.shape[0]
    requests = table.shape[1] // 2
    whole = lambda shape: pl.BlockSpec(shape, lambda i, *_: (0,) * len(shape))
    return pl.pallas_call(
        functools.partial(
            attend_kernel, chunk=chunk, spans=spans, span=span, heads=width // size, size=size,
            pieces=pieces, cap=cap, piece=piece, requests=requests,
        ),
        grid_spec=pltpu.PrefetchScalarGridSpec(
            num_scalar_prefetch=4,
            grid=(steps,),
            in_specs=[whole((tokens, width))]
            + [whole(pairs[0].shape)] * pieces
            + [pl.BlockSpec((width, out_width), lambda i, m, t, l, b: (0, b[i]))],
            out_specs=[
                pl.BlockSpec((None, tokens, out_width), lambda i, *_: (i, 0, 0)),
                whole((tokens, width)),
            ],
            scratch_shapes=[pltpu.VMEM((2 * pieces * piece, pair_width), bf16)],
        ),
        out_shape=[
            jax.ShapeDtypeStruct((steps, tokens, out_width), bf16),
            jax.ShapeDtypeStruct((tokens, width), bf16),
        ],
        compiler_params=params(),
        cost_estimate=cost(
            2 * tokens * width * out_width * steps, 2 * width * out_width * steps,
            2 * tokens * width * 2,
        ),
        name="attend",
    )(meta, table, live, blocks, queries, *pairs, weight)


def output_kernel(blocks, a_ref, w_ref, out_ref):
    out_ref[...] = jnp.dot(a_ref[...], w_ref[...], preferred_element_type=f32).astype(bf16)


def project_output(blocks, attended, weight, out_width):
    tokens, width = attended.shape
    steps = blocks.shape[0]
    return pl.pallas_call(
        output_kernel,
        grid_spec=pltpu.PrefetchScalarGridSpec(
            num_scalar_prefetch=1,
            grid=(steps,),
            in_specs=[
                pl.BlockSpec((tokens, width), lambda i, b: (0, 0)),
                pl.BlockSpec((width, out_width), lambda i, b: (0, b[i])),
            ],
            out_specs=pl.BlockSpec((None, tokens, out_width), lambda i, b: (i, 0, 0)),
        ),
        out_shape=jax.ShapeDtypeStruct((steps, tokens, out_width), bf16),
        compiler_params=params(),
        cost_estimate=cost(2 * tokens * width * out_width * steps, 2 * width * out_width * steps),
        name="output",
    )(blocks, attended, weight)


def shards(
    hidden,
    neighbour_states,
    query_weight,
    encoder_weight,
    output_weight,
    neighbour_owner,
    neighbour_slot,
    neighbour_length,
):
    row_count = lax.axis_size("rows")
    group = lax.axis_size("mp")
    pieces = group * lax.axis_size("sub")
    me, mp, sub = lax.axis_index("rows"), lax.axis_index("mp"), lax.axis_index("sub")
    spans_here = neighbour_owner.shape[0]
    count, slot_tokens, feature_shard = neighbour_states.shape
    features = feature_shard * pieces
    size = encoder_weight.shape[1] // 2
    token_count = hidden.shape[0]
    span_tokens = token_count // spans_here
    requests = 2 * spans_here
    cap = max(2, (requests + row_count - 1) // row_count)
    chunks = 4
    chunk_spans = spans_here // chunks
    chunk_tokens = token_count // chunks
    gain = 1.0 / (softcap * math.sqrt(size))
    add = lambda *terms: functools.reduce(
        lambda a, b: a + b, [t.astype(f32) for t in terms]
    ).astype(bf16)

    meta = jnp.stack([me, mp, sub]).astype(jnp.int32)
    gathered_blocks = jnp.stack(
        [((mp - dm + group) % group) * 2 + (sub + ds) % 2 for dm in range(group) for ds in range(2)]
    ).astype(jnp.int32)
    away_blocks = jnp.stack(
        [((mp + dm) % group) * 2 + (sub + ds) % 2 for ds in (1, 0) for dm in range(1, group)]
    ).astype(jnp.int32)
    here_blocks = jnp.stack([mp * 2 + (sub + 1) % 2, mp * 2 + sub]).astype(jnp.int32)

    own = jnp.concatenate(
        [neighbour_owner.reshape(1, -1), neighbour_slot.reshape(1, -1), neighbour_length.reshape(1, -1)],
        axis=1,
    )
    everyone = jnp.concatenate([own] + [shift(own, "rows", -d) for d in range(1, row_count)], axis=0)
    table, live = everyone[:, : 2 * requests], everyone[:, 2 * requests :]

    near = shift(hidden, "sub", 1)
    parts = []
    for c in range(chunks):
        low = c * chunk_tokens
        mine = hidden[low : low + chunk_tokens]
        chunk_parts = [mine, near[low : low + chunk_tokens]]
        for dm in range(1, group):
            far = shift(mine, "mp", dm)
            chunk_parts += [far, shift(far, "sub", 1)]
        parts.append(chunk_parts)

    partial = encode(meta, neighbour_states, encoder_weight, pieces)
    received = shift(partial[1], "sub", 1)
    crossed = []
    for dm in range(1, group):
        crossed.append(shift(add(partial[0, dm], received[dm]), "mp", dm))
    routed = route(meta, table, partial, received, crossed, cap, features, count, requests)
    encoded = jnp.concatenate(
        [routed[0]] + [shift(routed[d], "rows", d) for d in range(1, row_count)], axis=0
    )
    pairs = [encoded, shift(encoded, "sub", 1)]
    for dm in range(1, group):
        far = shift(encoded, "mp", dm)
        pairs += [far, shift(far, "sub", 1)]

    outs = []
    for c in range(chunks):
        queries = project_queries(gathered_blocks, parts[c], query_weight, gain)
        away, attended = attend(
            meta, table, live, away_blocks, queries, pairs, output_weight, c, chunk_spans,
            span_tokens, feature_shard, cap,
        )
        away_received = shift(away[: group - 1], "sub", 1)
        arrived = []
        for dm in range(1, group):
            arrived.append(shift(add(away[group - 1 + dm - 1], away_received[dm - 1]), "mp", dm))
        here = project_output(here_blocks, attended, output_weight, feature_shard)
        here_received = shift(here[0], "sub", 1)
        outs.append(add(here[1], here_received, *arrived))
    return jnp.concatenate(outs, axis=0)


def solution(mesh):
    placed = (
        P(("groups", "rows"), ("mp", "sub")),
        P(("groups", "rows"), None, ("mp", "sub")),
        P(None, ("mp", "sub")),
        P(("mp", "sub"), None),
        P(("mp", "sub"), None),
        P(("groups", "rows"), None),
        P(("groups", "rows"), None),
        P(("groups", "rows")),
    )
    return jax.shard_map(
        shards,
        mesh=mesh,
        in_specs=placed,
        out_specs=P(("groups", "rows"), ("mp", "sub")),
        check_vma=False,
    )
```

time: 162 us -> 131 us (0.81)
  Pallas kernels: 0 us -> 53.8 us
  blocking collectives: 49.6 us -> 0 us
  matrix products: 26.6 us -> 0 us
  starting transfers between devices: 4.65 us -> 21.9 us
  between operations: 13.9 us -> 0.44 us
  waiting for transfers between devices: 55.4 us -> 44.6 us
  other arithmetic: 7.24 us -> 2.32 us
  local copies, waits for them, and re-layouts: 4.65 us -> 7.16 us
    pallas_call x0 -> x14, Pallas kernels: none -> 53.8 us  [the longest x4 22.3 us: project_queries(): pl.pallas_call(functools.partial(query_kernel, pieces=pieces, features=wi...]
    reduce_scatter x1 -> x0, waiting for transfers between devices: 44.7 us -> none  [shards(): lax.psum_scatter(output_terms.astype(jnp.bfloat16), ('mp', 'sub'), scatte...]
    ppermute x0 -> x32, waiting for transfers between devices: none -> 44.6 us  [shift(): lax.ppermute(value, axis, [(i, (i + by) % size) for i in range(size)])]
    dot_general x7 -> x0, matrix products: 26.6 us -> none  [the longest x1 7.87 us: shards(): jnp.dot(piece, query_weight, preferred_element_type=jnp.float32)]
    unnamed x1 -> x0, blocking collectives: 23.7 us -> none
    ppermute x0 -> x32, starting transfers between devices: none -> 21.9 us  [shift(): lax.ppermute(value, axis, [(i, (i + by) % size) for i in range(size)])]
    all_gather x2 -> x0, blocking collectives: 20.2 us -> none  [the longest x1 12.6 us: shards(): lax.all_gather(neighbour_owner, 'rows', axis=0, tiled=True)]
    psum x1 -> x0, waiting for transfers between devices: 8.24 us -> none  [shards(): lax.psum(encoder_terms.astype(jnp.bfloat16), ('mp', 'sub'))]
  transfers between devices with their start and end apart: 4 -> 32, of which waited for: 3 -> 12; matrix products, arithmetic and copies ran while one was open for 6% -> 3% of each run, Pallas kernels for 0% -> 37%
where the time goes in v1:
time: 131 us; the launch traced here: 130 us
  Pallas kernels  53.8 us (41%)
  waiting for transfers between devices  44.6 us (34%)
  starting transfers between devices  21.9 us (17%)
  local copies, waits for them, and re-layouts  7.16 us (5%)
  other arithmetic  2.32 us (2%)
    ppermute x32, waiting for transfers between devices, shift(): lax.ppermute(value, axis, [(i, (i + by) % size) for i in range(size)])  44.6 us
    pallas_call x4, Pallas kernels, project_queries(): pl.pallas_call(functools.partial(query_kernel, pieces=pieces, features=wi...  22.3 us
    ppermute x32, starting transfers between devices, shift(): lax.ppermute(value, axis, [(i, (i + by) % size) for i in range(size)])  21.9 us
    pallas_call x4, Pallas kernels, attend(): pl.pallas_call(functools.partial(attend_kernel, chunk=chunk, spans=spans,...  15.2 us
    pallas_call x4, Pallas kernels, project_output(): pl.pallas_call(output_kernel, grid_spec=pltpu.PrefetchScalarGridSpec(num_...  13 us
    unnamed x15, local copies, waits for them, and re-layouts  3.42 us
  transfers between devices with their start and end apart: 32, of which 12 were waited for; matrix products, arithmetic and copies ran while one was open for 3% of the time, Pallas kernels for 37%

profile of v1, /device:TPU:0, one launch (start us, length us, event | category | flops | bytes accessed | tf_op | source)
XLA Modules:
  0.0 130.2 jit_solution(16572794628644387394)
XLA Ops:
  0.1 2.2 %copy-done = bf16[16,128,1024]{2,1,0:T(8,128)(2,1)S(1)} copy-done((bf16[16,128,1024]{2,1,0:T(8,128)(2,1)S(1)}, bf16[16,128,1024]{2,1,0:T(8,128)(2,1)}, u32[]{:S(2)}) %copy-start) | copy-done | bytes 4194328
  2.3 1.0 copy-done.1
  3.3 2.4 %encode.1.refs_0_ = bf16[2,2,528,256]{3,2,1,0:T(8,128)(2,1)S(1)} custom-call(s32[3]{0:T(128)S(1)} %pad_add_fusion.2.meta, bf16[16,128,1024]{2,1,0:T(8,128)(2,1)S(1)} %copy-done, bf16[1024,256]{1,0:T(8,128)(2,1)S(1)} %copy-done.1), custom_call_target="tpu_custom_call" | custom-call | flops 1073741824 | bytes 4194304 | tf_op jit(solution)/shard_map/encode/pallas_call | solution.py:72
  5.7 0.8 slice_bitcast_fusion
  7.4 2.6 %collective-permute-start.2 = (s32[1,48]{1,0:T(1,128)S(1)}, s32[1,48]{1,0:T(1,128)S(1)}, u32[]{:S(2)}, u32[]{:S(2)}) collective-permute-start(s32[1,48]{1,0:T(1,128)S(1)} %pad_add_fusion.3), channel_id=1, source_target_pairs={{0,4},{4,8},{8,12},{12,0},{1,5},{5,9},{9,13},{13,1},{2,6},{6,10},{... | collective-permute-start | bytes 584 | tf_op jit(solution)/shard_map/ppermute | solution.py:21
  10.0 2.6 %collective-permute-start.1 = (s32[1,48]{1,0:T(1,128)S(1)}, s32[1,48]{1,0:T(1,128)S(1)}, u32[]{:S(2)}, u32[]{:S(2)}) collective-permute-start(s32[1,48]{1,0:T(1,128)S(1)} %pad_add_fusion.3), channel_id=1, source_target_pairs={{0,8},{4,12},{8,0},{12,4},{1,9},{5,13},{9,1},{13,5},{2,10},{6,14},... | collective-permute-start | bytes 584 | tf_op jit(solution)/shard_map/ppermute | solution.py:21
  12.6 1.3 fusion.14
  13.9 1.6 %collective-permute-start.27 = (bf16[128,1024]{1,0:T(8,128)(2,1)S(1)}, bf16[128,1024]{1,0:T(8,128)(2,1)S(1)}, u32[]{:S(2)}, u32[]{:S(2)}) collective-permute-start(bf16[128,1024]{1,0:T(8,128)(2,1)S(1)} %get-tuple-element.35.refs_0_), channel_id=1, source_target_pairs={{0,2},{2,0},{1,3},{3,1},{4,6},{6,4},{5,7},{7,5},{8,10},{10,8},{9,1... | collective-permute-start | bytes 786440 | tf_op jit(solution)/shard_map/ppermute | solution.py:21
  15.6 0.6 collective-permute-start.7
  16.3 1.3 %collective-permute-start = (s32[1,48]{1,0:T(1,128)S(1)}, s32[1,48]{1,0:T(1,128)S(1)}, u32[]{:S(2)}, u32[]{:S(2)}) collective-permute-start(s32[1,48]{1,0:T(1,128)S(1)} %pad_add_fusion.3), channel_id=1, source_target_pairs={{0,12},{4,0},{8,4},{12,8},{1,13},{5,1},{9,5},{13,9},{2,14},{6,2},{... | collective-permute-start | bytes 584 | tf_op jit(solution)/shard_map/ppermute | solution.py:21
  17.7 1.5 %collective-permute-start.22 = (bf16[128,1024]{1,0:T(8,128)(2,1)S(1)}, bf16[128,1024]{1,0:T(8,128)(2,1)S(1)}, u32[]{:S(2)}, u32[]{:S(2)}) collective-permute-start(bf16[128,1024]{1,0:T(8,128)(2,1)S(1)} %get-tuple-element.36.refs_0_), channel_id=1, source_target_pairs={{0,2},{2,0},{1,3},{3,1},{4,6},{6,4},{5,7},{7,5},{8,10},{10,8},{9,1... | collective-permute-start | bytes 786440 | tf_op jit(solution)/shard_map/ppermute | solution.py:21
  19.2 0.7 collective-permute-done
  19.9 1.5 %collective-permute-start.17 = (bf16[128,1024]{1,0:T(8,128)(2,1)S(1)}, bf16[128,1024]{1,0:T(8,128)(2,1)S(1)}, u32[]{:S(2)}, u32[]{:S(2)}) collective-permute-start(bf16[128,1024]{1,0:T(8,128)(2,1)S(1)} %get-tuple-element.34.refs_0_), channel_id=1, source_target_pairs={{0,2},{2,0},{1,3},{3,1},{4,6},{6,4},{5,7},{7,5},{8,10},{10,8},{9,1... | collective-permute-start | bytes 786440 | tf_op jit(solution)/shard_map/ppermute | solution.py:21
  21.5 7.3 %collective-permute-done.7.refs_2_ = bf16[528,256]{1,0:T(8,128)(2,1)S(1)} collective-permute-done((bf16[528,256]{1,0:T(8,128)(2,1)S(1)}, bf16[528,256]{1,0:T(8,128)(2,1)S(1)}, u32[]{:S(2)}, u32[]{:S(2)}) %collective-permute-start.7) | collective-permute-done | bytes 270368 | tf_op jit(solution)/shard_map/ppermute | solution.py:21
  28.8 1.5 %collective-permute-start.4 = (bf16[128,1024]{1,0:T(8,128)(2,1)S(1)}, bf16[128,1024]{1,0:T(8,128)(2,1)S(1)}, u32[]{:S(2)}, u32[]{:S(2)}) collective-permute-start(bf16[128,1024]{1,0:T(8,128)(2,1)S(1)} %get-tuple-element.33.refs_0_), channel_id=1, source_target_pairs={{0,2},{2,0},{1,3},{3,1},{4,6},{6,4},{5,7},{7,5},{8,10},{10,8},{9,1... | collective-permute-start | bytes 786440 | tf_op jit(solution)/shard_map/ppermute | solution.py:21
  30.3 0.9 route.1
  31.6 6.1 %collective-permute-done.8 = bf16[4,32,256]{2,1,0:T(8,128)(2,1)S(1)} collective-permute-done((bf16[4,32,256]{2,1,0:T(8,128)(2,1)S(1)}, bf16[4,32,256]{2,1,0:T(8,128)(2,1)S(1)}, u32[]{:S(2)}, u32[]{:S(2)}) %collective-permute-start.8) | collective-permute-done | bytes 65568 | tf_op jit(solution)/shard_map/ppermute | solution.py:21
  37.8 5.3 %collective-permute-done.9 = bf16[4,32,256]{2,1,0:T(8,128)(2,1)S(1)} collective-permute-done((bf16[4,32,256]{2,1,0:T(8,128)(2,1)S(1)}, bf16[4,32,256]{2,1,0:T(8,128)(2,1)S(1)}, u32[]{:S(2)}, u32[]{:S(2)}) %collective-permute-start.9) | collective-permute-done | bytes 65568 | tf_op jit(solution)/shard_map/ppermute | solution.py:21
  43.6 1.7 %collective-permute-done.4.refs_2_ = bf16[128,1024]{1,0:T(8,128)(2,1)S(1)} collective-permute-done((bf16[128,1024]{1,0:T(8,128)(2,1)S(1)}, bf16[128,1024]{1,0:T(8,128)(2,1)S(1)}, u32[]{:S(2)}, u32[]{:S(2)}) %collective-permute-start.4) | collective-permute-done | bytes 262176 | tf_op jit(solution)/shard_map/ppermute | solution.py:21
  45.3 2.0 %collective-permute-done.10 = bf16[4,32,256]{2,1,0:T(8,128)(2,1)S(1)} collective-permute-done((bf16[4,32,256]{2,1,0:T(8,128)(2,1)S(1)}, bf16[4,32,256]{2,1,0:T(8,128)(2,1)S(1)}, u32[]{:S(2)}, u32[]{:S(2)}) %collective-permute-start.10) | collective-permute-done | bytes 65568 | tf_op jit(solution)/shard_map/ppermute | solution.py:21
  47.3 0.6 collective-permute-start.12
  47.9 1.3 fusion.13
  49.5 5.7 %queries.7.refs_0_ = bf16[128,1024]{1,0:T(8,128)(2,1)S(1)} custom-call(s32[4]{0:T(128)S(1)} %pad_add_fusion.5.blocks, bf16[128,1024]{1,0:T(8,128)(2,1)S(1)} %get-tuple-element.35.refs_0_, bf16[128,1024]{1,0:T(8,128)(2,1)S(1)} %get-tuple-element.30.refs_1_, bf16[128,1024]{1,0:T(8,128)(2,1)S(1)} %collective-permute-done.27.refs_2_, ...), custom_call_target="tpu_custom_call" | custom-call | flops 1073741824 | bytes 8388608 | tf_op jit(solution)/shard_map/queries/pallas_call | solution.py:180
  55.2 0.9 collective-permute-done.12.refs_3_
  56.1 5.5 %queries.6.refs_0_ = bf16[128,1024]{1,0:T(8,128)(2,1)S(1)} custom-call(s32[4]{0:T(128)S(1)} %pad_add_fusion.5.blocks, bf16[128,1024]{1,0:T(8,128)(2,1)S(1)} %get-tuple-element.36.refs_0_, bf16[128,1024]{1,0:T(8,128)(2,1)S(1)} %get-tuple-element.31.refs_1_, bf16[128,1024]{1,0:T(8,128)(2,1)S(1)} %collective-permute-done.22.refs_2_, ...), custom_call_target="tpu_custom_call" | custom-call | flops 1073741824 | bytes 8388608 | tf_op jit(solution)/shard_map/queries/pallas_call | solution.py:180
  61.7 5.5 %queries.5.refs_0_ = bf16[128,1024]{1,0:T(8,128)(2,1)S(1)} custom-call(s32[4]{0:T(128)S(1)} %pad_add_fusion.5.blocks, bf16[128,1024]{1,0:T(8,128)(2,1)S(1)} %get-tuple-element.34.refs_0_, bf16[128,1024]{1,0:T(8,128)(2,1)S(1)} %get-tuple-element.32.refs_1_, bf16[128,1024]{1,0:T(8,128)(2,1)S(1)} %collective-permute-done.17.refs_2_, ...), custom_call_target="tpu_custom_call" | custom-call | flops 1073741824 | bytes 8388608 | tf_op jit(solution)/shard_map/queries/pallas_call | solution.py:180
  67.2 5.5 %queries.4.refs_0_ = bf16[128,1024]{1,0:T(8,128)(2,1)S(1)} custom-call(s32[4]{0:T(128)S(1)} %pad_add_fusion.5.blocks, bf16[128,1024]{1,0:T(8,128)(2,1)S(1)} %get-tuple-element.33.refs_0_, bf16[128,1024]{1,0:T(8,128)(2,1)S(1)} %get-tuple-element.29.refs_1_, bf16[128,1024]{1,0:T(8,128)(2,1)S(1)} %collective-permute-done.4.refs_2_, ...), custom_call_target="tpu_custom_call" | custom-call | flops 1073741824 | bytes 8388608 | tf_op jit(solution)/shard_map/queries/pallas_call | solution.py:180
  72.8 3.8 %attend.7 = (bf16[2,128,1024]{2,1,0:T(8,128)(2,1)S(1)}, bf16[128,1024]{1,0:T(8,128)(2,1)S(1)}) custom-call(s32[3]{0:T(128)S(1)} %pad_add_fusion.2.meta, s32[4,32]{1,0:T(4,128)S(1)} %bitcast.60, s32[4,16]{1,0:T(4,128)S(1)} %slice.88.live, s32[2]{0:T(128)S(1)} %pad_add_fusion.4.blocks, bf16[128,1024]{1,0:T(8,128)(2,1)S(1)} %queries.7.refs_0_, ...), custom_call_target="tpu_custom_call" | custom-call | flops 536870912 | bytes 4194304 | tf_op jit(solution)/shard_map/attend/pallas_call | solution.py:255
  76.6 0.6 collective-permute-start.30
  77.2 3.3 %output.7 = bf16[2,128,1024]{2,1,0:T(8,128)(2,1)S(1)} custom-call(s32[2]{0:T(128)S(1)} %pad_add_fusion.1.blocks, bf16[128,1024]{1,0:T(8,128)(2,1)S(1)} %get-tuple-element.27.a_ref, bf16[1024,4096]{1,0:T(8,128)(2,1)} %w_ref.9), custom_call_target="tpu_custom_call" | custom-call | flops 536870912 | bytes 4194304 | tf_op jit(solution)/shard_map/output/pallas_call | solution.py:292
  80.6 3.8 %attend.6 = (bf16[2,128,1024]{2,1,0:T(8,128)(2,1)S(1)}, bf16[128,1024]{1,0:T(8,128)(2,1)S(1)}) custom-call(s32[3]{0:T(128)S(1)} %pad_add_fusion.2.meta, s32[4,32]{1,0:T(4,128)S(1)} %bitcast.61, s32[4,16]{1,0:T(4,128)S(1)} %slice.88.live, s32[2]{0:T(128)S(1)} %pad_add_fusion.4.blocks, bf16[128,1024]{1,0:T(8,128)(2,1)S(1)} %queries.6.refs_0_, ...), custom_call_target="tpu_custom_call" | custom-call | flops 536870912 | bytes 4194304 | tf_op jit(solution)/shard_map/attend/pallas_call | solution.py:255
  84.4 0.6 collective-permute-start.25
  84.9 3.3 %output.6 = bf16[2,128,1024]{2,1,0:T(8,128)(2,1)S(1)} custom-call(s32[2]{0:T(128)S(1)} %pad_add_fusion.1.blocks, bf16[128,1024]{1,0:T(8,128)(2,1)S(1)} %get-tuple-element.25.a_ref, bf16[1024,4096]{1,0:T(8,128)(2,1)} %w_ref.9), custom_call_target="tpu_custom_call" | custom-call | flops 536870912 | bytes 4194304 | tf_op jit(solution)/shard_map/output/pallas_call | solution.py:292
  88.3 3.8 %attend.5 = (bf16[2,128,1024]{2,1,0:T(8,128)(2,1)S(1)}, bf16[128,1024]{1,0:T(8,128)(2,1)S(1)}) custom-call(s32[3]{0:T(128)S(1)} %pad_add_fusion.2.meta, s32[4,32]{1,0:T(4,128)S(1)} %bitcast.62, s32[4,16]{1,0:T(4,128)S(1)} %slice.88.live, s32[2]{0:T(128)S(1)} %pad_add_fusion.4.blocks, bf16[128,1024]{1,0:T(8,128)(2,1)S(1)} %queries.5.refs_0_, ...), custom_call_target="tpu_custom_call" | custom-call | flops 536870912 | bytes 4194304 | tf_op jit(solution)/shard_map/attend/pallas_call | solution.py:255
  92.1 0.6 collective-permute-start.20
  92.7 3.3 %output.5 = bf16[2,128,1024]{2,1,0:T(8,128)(2,1)S(1)} custom-call(s32[2]{0:T(128)S(1)} %pad_add_fusion.1.blocks, bf16[128,1024]{1,0:T(8,128)(2,1)S(1)} %get-tuple-element.23.a_ref, bf16[1024,4096]{1,0:T(8,128)(2,1)} %w_ref.9), custom_call_target="tpu_custom_call" | custom-call | flops 536870912 | bytes 4194304 | tf_op jit(solution)/shard_map/output/pallas_call | solution.py:292
  96.0 3.8 %attend.4 = (bf16[2,128,1024]{2,1,0:T(8,128)(2,1)S(1)}, bf16[128,1024]{1,0:T(8,128)(2,1)S(1)}) custom-call(s32[3]{0:T(128)S(1)} %pad_add_fusion.2.meta, s32[4,32]{1,0:T(4,128)S(1)} %bitcast.63, s32[4,16]{1,0:T(4,128)S(1)} %slice.88.live, s32[2]{0:T(128)S(1)} %pad_add_fusion.4.blocks, bf16[128,1024]{1,0:T(8,128)(2,1)S(1)} %queries.4.refs_0_, ...), custom_call_target="tpu_custom_call" | custom-call | flops 536870912 | bytes 4194304 | tf_op jit(solution)/shard_map/attend/pallas_call | solution.py:255
  99.8 3.3 %output.4 = bf16[2,128,1024]{2,1,0:T(8,128)(2,1)S(1)} custom-call(s32[2]{0:T(128)S(1)} %pad_add_fusion.1.blocks, bf16[128,1024]{1,0:T(8,128)(2,1)S(1)} %get-tuple-element.21.a_ref, bf16[1024,4096]{1,0:T(8,128)(2,1)} %w_ref.9), custom_call_target="tpu_custom_call" | custom-call | flops 536870912 | bytes 4194304 | tf_op jit(solution)/shard_map/output/pallas_call | solution.py:292
  103.3 0.6 collective-permute-start.15
  103.9 0.7 collective-permute-start.31
  105.1 1.1 collective-permute-start.26
  106.3 6.8 %collective-permute-done.31 = bf16[128,1024]{1,0:T(8,128)(2,1)S(1)} collective-permute-done((bf16[128,1024]{1,0:T(8,128)(2,1)S(1)}, bf16[128,1024]{1,0:T(8,128)(2,1)S(1)}, u32[]{:S(2)}, u32[]{:S(2)}) %collective-permute-start.31) | collective-permute-done | bytes 262176 | tf_op jit(solution)/shard_map/ppermute | solution.py:21
  113.1 0.6 collective-permute-start.21
  113.9 1.5 %collective-permute-start.16 = (bf16[128,1024]{1,0:T(8,128)(2,1)S(1)}, bf16[128,1024]{1,0:T(8,128)(2,1)S(1)}, u32[]{:S(2)}, u32[]{:S(2)}) collective-permute-start(bf16[128,1024]{1,0:T(8,128)(2,1)S(1)} %fusion.9), channel_id=1, source_target_pairs={{0,2},{2,0},{1,3},{3,1},{4,6},{6,4},{5,7},{7,5},{8,10},{10,8},{9,1... | collective-permute-start | bytes 786440 | tf_op jit(solution)/shard_map/ppermute | solution.py:21
  115.4 3.4 %collective-permute-done.26 = bf16[128,1024]{1,0:T(8,128)(2,1)S(1)} collective-permute-done((bf16[128,1024]{1,0:T(8,128)(2,1)S(1)}, bf16[128,1024]{1,0:T(8,128)(2,1)S(1)}, u32[]{:S(2)}, u32[]{:S(2)}) %collective-permute-start.26) | collective-permute-done | bytes 262176 | tf_op jit(solution)/shard_map/ppermute | solution.py:21
  118.9 5.5 %collective-permute-done.21 = bf16[128,1024]{1,0:T(8,128)(2,1)S(1)} collective-permute-done((bf16[128,1024]{1,0:T(8,128)(2,1)S(1)}, bf16[128,1024]{1,0:T(8,128)(2,1)S(1)}, u32[]{:S(2)}, u32[]{:S(2)}) %collective-permute-start.21) | collective-permute-done | bytes 262176 | tf_op jit(solution)/shard_map/ppermute | solution.py:21
  124.5 4.5 %collective-permute-done.16 = bf16[128,1024]{1,0:T(8,128)(2,1)S(1)} collective-permute-done((bf16[128,1024]{1,0:T(8,128)(2,1)S(1)}, bf16[128,1024]{1,0:T(8,128)(2,1)S(1)}, u32[]{:S(2)}, u32[]{:S(2)}) %collective-permute-start.16) | collective-permute-done | bytes 262176 | tf_op jit(solution)/shard_map/ppermute | solution.py:21
  129.2 1.0 pad_maximum_fusion
  (76 shorter events, 4.2 us)
Async XLA Ops:
  0.1 2.2 %copy-start = (bf16[16,128,1024]{2,1,0:T(8,128)(2,1)S(1)}, bf16[16,128,1024]{2,1,0:T(8,128)(2,1)}, u32[]{:S(2)}) copy-start(bf16[16,128,1024]{2,1,0:T(8,128)(2,1)} %x_ref.1) | copy-start | bytes 12582916
  2.3 1.0 copy-start.1
  3.3 3.7 %copy-start.3 = (s32[8,2]{0,1:T(2,128)S(1)}, s32[8,2]{0,1:T(2,128)}, u32[]{:S(2)}) copy-start(s32[8,2]{0,1:T(2,128)} %param.14) | copy-start | bytes 196
  3.3 3.9 %copy-start.4 = (s32[8,2]{0,1:T(2,128)S(1)}, s32[8,2]{0,1:T(2,128)}, u32[]{:S(2)}) copy-start(s32[8,2]{0,1:T(2,128)} %param.13) | copy-start | bytes 196
  3.3 4.1 %copy-start.2 = (s32[16]{0:T(128)S(1)}, s32[16]{0:T(128)}, u32[]{:S(2)}) copy-start(s32[16]{0:T(128)} %param.15) | copy-start | bytes 196
  6.6 8.9 %collective-permute-start.6 = (bf16[2,528,256]{2,1,0:T(8,128)(2,1)}, bf16[2,528,256]{2,1,0:T(8,128)(2,1)S(1)}, u32[]{:S(2)}, u32[]{:S(2)}) collective-permute-start(bf16[2,528,256]{2,1,0:T(8,128)(2,1)} %slice_bitcast_fusion), channel_id=1, source_target_pairs={{0,1},{1,0},{2,3},{3,2},{4,5},{5,4},{6,7},{7,6},{8,9},{9,8},{10,11... | collective-permute-start | bytes 1622024 | tf_op jit(solution)/shard_map/ppermute | solution.py:21
  7.4 8.9 %collective-permute-start.2 = (s32[1,48]{1,0:T(1,128)S(1)}, s32[1,48]{1,0:T(1,128)S(1)}, u32[]{:S(2)}, u32[]{:S(2)}) collective-permute-start(s32[1,48]{1,0:T(1,128)S(1)} %pad_add_fusion.3), channel_id=1, source_target_pairs={{0,4},{4,8},{8,12},{12,0},{1,5},{5,9},{9,13},{13,1},{2,6},{6,10},{... | collective-permute-start | bytes 584 | tf_op jit(solution)/shard_map/ppermute | solution.py:21
  10.0 7.7 %collective-permute-start.1 = (s32[1,48]{1,0:T(1,128)S(1)}, s32[1,48]{1,0:T(1,128)S(1)}, u32[]{:S(2)}, u32[]{:S(2)}) collective-permute-start(s32[1,48]{1,0:T(1,128)S(1)} %pad_add_fusion.3), channel_id=1, source_target_pairs={{0,8},{4,12},{8,0},{12,4},{1,9},{5,13},{9,1},{13,5},{2,10},{6,14},... | collective-permute-start | bytes 584 | tf_op jit(solution)/shard_map/ppermute | solution.py:21
  12.6 34.7 %collective-permute-start.3 = (bf16[512,1024]{1,0:T(8,128)(2,1)}, bf16[512,1024]{1,0:T(8,128)(2,1)}, u32[]{:S(2)}, u32[]{:S(2)}) collective-permute-start(bf16[512,1024]{1,0:T(8,128)(2,1)} %param.8), channel_id=1, source_target_pairs={{0,1},{1,0},{2,3},{3,2},{4,5},{5,4},{6,7},{7,6},{8,9},{9,8},{10,11... | collective-permute-start | bytes 3145736 | tf_op jit(solution)/shard_map/ppermute | solution.py:21
  13.9 17.4 %collective-permute-start.27 = (bf16[128,1024]{1,0:T(8,128)(2,1)S(1)}, bf16[128,1024]{1,0:T(8,128)(2,1)S(1)}, u32[]{:S(2)}, u32[]{:S(2)}) collective-permute-start(bf16[128,1024]{1,0:T(8,128)(2,1)S(1)} %get-tuple-element.35.refs_0_), channel_id=1, source_target_pairs={{0,2},{2,0},{1,3},{3,1},{4,6},{6,4},{5,7},{7,5},{8,10},{10,8},{9,1... | collective-permute-start | bytes 786440 | tf_op jit(solution)/shard_map/ppermute | solution.py:21
  15.6 13.3 %collective-permute-start.7 = (bf16[528,256]{1,0:T(8,128)(2,1)S(1)}, bf16[528,256]{1,0:T(8,128)(2,1)S(1)}, u32[]{:S(2)}, u32[]{:S(2)}) collective-permute-start(bf16[528,256]{1,0:T(8,128)(2,1)S(1)} %fusion), channel_id=1, source_target_pairs={{0,2},{2,0},{1,3},{3,1},{4,6},{6,4},{5,7},{7,5},{8,10},{10,8},{9,1... | collective-permute-start | bytes 811016 | tf_op jit(solution)/shard_map/ppermute | solution.py:21
  16.3 3.5 %collective-permute-start = (s32[1,48]{1,0:T(1,128)S(1)}, s32[1,48]{1,0:T(1,128)S(1)}, u32[]{:S(2)}, u32[]{:S(2)}) collective-permute-start(s32[1,48]{1,0:T(1,128)S(1)} %pad_add_fusion.3), channel_id=1, source_target_pairs={{0,12},{4,0},{8,4},{12,8},{1,13},{5,1},{9,5},{13,9},{2,14},{6,2},{... | collective-permute-start | bytes 584 | tf_op jit(solution)/shard_map/ppermute | solution.py:21
  17.7 25.4 %collective-permute-start.22 = (bf16[128,1024]{1,0:T(8,128)(2,1)S(1)}, bf16[128,1024]{1,0:T(8,128)(2,1)S(1)}, u32[]{:S(2)}, u32[]{:S(2)}) collective-permute-start(bf16[128,1024]{1,0:T(8,128)(2,1)S(1)} %get-tuple-element.36.refs_0_), channel_id=1, source_target_pairs={{0,2},{2,0},{1,3},{3,1},{4,6},{6,4},{5,7},{7,5},{8,10},{10,8},{9,1... | collective-permute-start | bytes 786440 | tf_op jit(solution)/shard_map/ppermute | solution.py:21
  19.9 23.3 %collective-permute-start.17 = (bf16[128,1024]{1,0:T(8,128)(2,1)S(1)}, bf16[128,1024]{1,0:T(8,128)(2,1)S(1)}, u32[]{:S(2)}, u32[]{:S(2)}) collective-permute-start(bf16[128,1024]{1,0:T(8,128)(2,1)S(1)} %get-tuple-element.34.refs_0_), channel_id=1, source_target_pairs={{0,2},{2,0},{1,3},{3,1},{4,6},{6,4},{5,7},{7,5},{8,10},{10,8},{9,1... | collective-permute-start | bytes 786440 | tf_op jit(solution)/shard_map/ppermute | solution.py:21
  28.8 16.5 %collective-permute-start.4 = (bf16[128,1024]{1,0:T(8,128)(2,1)S(1)}, bf16[128,1024]{1,0:T(8,128)(2,1)S(1)}, u32[]{:S(2)}, u32[]{:S(2)}) collective-permute-start(bf16[128,1024]{1,0:T(8,128)(2,1)S(1)} %get-tuple-element.33.refs_0_), channel_id=1, source_target_pairs={{0,2},{2,0},{1,3},{3,1},{4,6},{6,4},{5,7},{7,5},{8,10},{10,8},{9,1... | collective-permute-start | bytes 786440 | tf_op jit(solution)/shard_map/ppermute | solution.py:21
  31.3 6.5 %collective-permute-start.8 = (bf16[4,32,256]{2,1,0:T(8,128)(2,1)S(1)}, bf16[4,32,256]{2,1,0:T(8,128)(2,1)S(1)}, u32[]{:S(2)}, u32[]{:S(2)}) collective-permute-start(bf16[4,32,256]{2,1,0:T(8,128)(2,1)S(1)} %get-tuple-element.18), channel_id=1, source_target_pairs={{0,4},{4,8},{8,12},{12,0},{1,5},{5,9},{9,13},{13,1},{2,6},{6,10},{... | collective-permute-start | bytes 196616 | tf_op jit(solution)/shard_map/ppermute | solution.py:21
  37.8 5.3 %collective-permute-start.9 = (bf16[4,32,256]{2,1,0:T(8,128)(2,1)S(1)}, bf16[4,32,256]{2,1,0:T(8,128)(2,1)S(1)}, u32[]{:S(2)}, u32[]{:S(2)}) collective-permute-start(bf16[4,32,256]{2,1,0:T(8,128)(2,1)S(1)} %get-tuple-element.19), channel_id=1, source_target_pairs={{0,8},{4,12},{8,0},{12,4},{1,9},{5,13},{9,1},{13,5},{2,10},{6,14},... | collective-permute-start | bytes 196616 | tf_op jit(solution)/shard_map/ppermute | solution.py:21
  43.0 4.3 %collective-permute-start.10 = (bf16[4,32,256]{2,1,0:T(8,128)(2,1)S(1)}, bf16[4,32,256]{2,1,0:T(8,128)(2,1)S(1)}, u32[]{:S(2)}, u32[]{:S(2)}) collective-permute-start(bf16[4,32,256]{2,1,0:T(8,128)(2,1)S(1)} %get-tuple-element.20), channel_id=1, source_target_pairs={{0,12},{4,0},{8,4},{12,8},{1,13},{5,1},{9,5},{13,9},{2,14},{6,2},{... | collective-permute-start | bytes 196616 | tf_op jit(solution)/shard_map/ppermute | solution.py:21
  43.1 6.1 %collective-permute-start.28 = (bf16[128,1024]{1,0:T(8,128)(2,1)S(1)}, bf16[128,1024]{1,0:T(8,128)(2,1)S(1)}, u32[]{:S(2)}, u32[]{:S(2)}) collective-permute-start(bf16[128,1024]{1,0:T(8,128)(2,1)S(1)} %collective-permute-done.27.refs_2_), channel_id=1, source_target_pairs={{0,1},{1,0},{2,3},{3,2},{4,5},{5,4},{6,7},{7,6},{8,9},{9,8},{10,11... | collective-permute-start | bytes 786440 | tf_op jit(solution)/shard_map/ppermute | solution.py:21
  43.1 13.0 %collective-permute-start.23 = (bf16[128,1024]{1,0:T(8,128)(2,1)S(1)}, bf16[128,1024]{1,0:T(8,128)(2,1)S(1)}, u32[]{:S(2)}, u32[]{:S(2)}) collective-permute-start(bf16[128,1024]{1,0:T(8,128)(2,1)S(1)} %collective-permute-done.22.refs_2_), channel_id=1, source_target_pairs={{0,1},{1,0},{2,3},{3,2},{4,5},{5,4},{6,7},{7,6},{8,9},{9,8},{10,11... | collective-permute-start | bytes 786440 | tf_op jit(solution)/shard_map/ppermute | solution.py:21
  45.3 16.3 %collective-permute-start.18 = (bf16[128,1024]{1,0:T(8,128)(2,1)S(1)}, bf16[128,1024]{1,0:T(8,128)(2,1)S(1)}, u32[]{:S(2)}, u32[]{:S(2)}) collective-permute-start(bf16[128,1024]{1,0:T(8,128)(2,1)S(1)} %collective-permute-done.17.refs_2_), channel_id=1, source_target_pairs={{0,1},{1,0},{2,3},{3,2},{4,5},{5,4},{6,7},{7,6},{8,9},{9,8},{10,11... | collective-permute-start | bytes 786440 | tf_op jit(solution)/shard_map/ppermute | solution.py:21
  47.3 19.9 %collective-permute-start.5 = (bf16[128,1024]{1,0:T(8,128)(2,1)S(1)}, bf16[128,1024]{1,0:T(8,128)(2,1)S(1)}, u32[]{:S(2)}, u32[]{:S(2)}) collective-permute-start(bf16[128,1024]{1,0:T(8,128)(2,1)S(1)} %collective-permute-done.4.refs_2_), channel_id=1, source_target_pairs={{0,1},{1,0},{2,3},{3,2},{4,5},{5,4},{6,7},{7,6},{8,9},{9,8},{10,11... | collective-permute-start | bytes 786440 | tf_op jit(solution)/shard_map/ppermute | solution.py:21
  47.3 8.8 %collective-permute-start.12 = (bf16[16,32,256]{2,1,0:T(8,128)(2,1)S(1)}, bf16[16,32,256]{2,1,0:T(8,128)(2,1)S(1)}, u32[]{:S(2)}, u32[]{:S(2)}) collective-permute-start(bf16[16,32,256]{2,1,0:T(8,128)(2,1)S(1)} %constant_dynamic-update-slice_fusion.refs_1_), channel_id=1, source_target_pairs={{0,2},{2,0},{1,3},{3,1},{4,6},{6,4},{5,7},{7,5},{8,10},{10,8},{9,1... | collective-permute-start | bytes 786440 | tf_op jit(solution)/shard_map/ppermute | solution.py:21
  49.2 23.6 %collective-permute-start.11 = (bf16[16,32,256]{2,1,0:T(8,128)(2,1)S(1)}, bf16[16,32,256]{2,1,0:T(8,128)(2,1)S(1)}, u32[]{:S(2)}, u32[]{:S(2)}) collective-permute-start(bf16[16,32,256]{2,1,0:T(8,128)(2,1)S(1)} %constant_dynamic-update-slice_fusion.refs_1_), channel_id=1, source_target_pairs={{0,1},{1,0},{2,3},{3,2},{4,5},{5,4},{6,7},{7,6},{8,9},{9,8},{10,11... | collective-permute-start | bytes 786440 | tf_op jit(solution)/shard_map/ppermute | solution.py:21
  56.1 16.7 %collective-permute-start.13 = (bf16[16,32,256]{2,1,0:T(8,128)(2,1)S(1)}, bf16[16,32,256]{2,1,0:T(8,128)(2,1)S(1)}, u32[]{:S(2)}, u32[]{:S(2)}) collective-permute-start(bf16[16,32,256]{2,1,0:T(8,128)(2,1)S(1)} %collective-permute-done.12.refs_3_), channel_id=1, source_target_pairs={{0,1},{1,0},{2,3},{3,2},{4,5},{5,4},{6,7},{7,6},{8,9},{9,8},{10,11... | collective-permute-start | bytes 786440 | tf_op jit(solution)/shard_map/ppermute | solution.py:21
  76.6 26.5 %collective-permute-start.30 = (bf16[1,128,1024]{2,1,0:T(8,128)(2,1)S(1)}, bf16[1,128,1024]{2,1,0:T(8,128)(2,1)S(1)}, u32[]{:S(2)}, u32[]{:S(2)}) collective-permute-start(bf16[1,128,1024]{2,1,0:T(8,128)(2,1)S(1)} %slice.115), channel_id=1, source_target_pairs={{0,1},{1,0},{2,3},{3,2},{4,5},{5,4},{6,7},{7,6},{8,9},{9,8},{10,11... | collective-permute-start | bytes 786440 | tf_op jit(solution)/shard_map/ppermute | solution.py:21
  80.5 25.8 %collective-permute-start.29 = (bf16[128,1024]{1,0:T(8,128)(2,1)S(1)}, bf16[128,1024]{1,0:T(8,128)(2,1)S(1)}, u32[]{:S(2)}, u32[]{:S(2)}) collective-permute-start(bf16[128,1024]{1,0:T(8,128)(2,1)S(1)} %slice_bitcast_fusion.3), channel_id=1, source_target_pairs={{0,1},{1,0},{2,3},{3,2},{4,5},{5,4},{6,7},{7,6},{8,9},{9,8},{10,11... | collective-permute-start | bytes 786440 | tf_op jit(solution)/shard_map/ppermute | solution.py:21
  84.4 18.9 %collective-permute-start.25 = (bf16[1,128,1024]{2,1,0:T(8,128)(2,1)S(1)}, bf16[1,128,1024]{2,1,0:T(8,128)(2,1)S(1)}, u32[]{:S(2)}, u32[]{:S(2)}) collective-permute-start(bf16[1,128,1024]{2,1,0:T(8,128)(2,1)S(1)} %slice.109), channel_id=1, source_target_pairs={{0,1},{1,0},{2,3},{3,2},{4,5},{5,4},{6,7},{7,6},{8,9},{9,8},{10,11... | collective-permute-start | bytes 786440 | tf_op jit(solution)/shard_map/ppermute | solution.py:21
  88.2 25.7 %collective-permute-start.24 = (bf16[128,1024]{1,0:T(8,128)(2,1)S(1)}, bf16[128,1024]{1,0:T(8,128)(2,1)S(1)}, u32[]{:S(2)}, u32[]{:S(2)}) collective-permute-start(bf16[128,1024]{1,0:T(8,128)(2,1)S(1)} %slice_bitcast_fusion.5), channel_id=1, source_target_pairs={{0,1},{1,0},{2,3},{3,2},{4,5},{5,4},{6,7},{7,6},{8,9},{9,8},{10,11... | collective-permute-start | bytes 786440 | tf_op jit(solution)/shard_map/ppermute | solution.py:21
  92.1 11.8 %collective-permute-start.20 = (bf16[1,128,1024]{2,1,0:T(8,128)(2,1)S(1)}, bf16[1,128,1024]{2,1,0:T(8,128)(2,1)S(1)}, u32[]{:S(2)}, u32[]{:S(2)}) collective-permute-start(bf16[1,128,1024]{2,1,0:T(8,128)(2,1)S(1)} %slice.103), channel_id=1, source_target_pairs={{0,1},{1,0},{2,3},{3,2},{4,5},{5,4},{6,7},{7,6},{8,9},{9,8},{10,11... | collective-permute-start | bytes 786440 | tf_op jit(solution)/shard_map/ppermute | solution.py:21
  103.1 15.8 %collective-permute-start.19 = (bf16[128,1024]{1,0:T(8,128)(2,1)S(1)}, bf16[128,1024]{1,0:T(8,128)(2,1)S(1)}, u32[]{:S(2)}, u32[]{:S(2)}) collective-permute-start(bf16[128,1024]{1,0:T(8,128)(2,1)S(1)} %slice_bitcast_fusion.7), channel_id=1, source_target_pairs={{0,1},{1,0},{2,3},{3,2},{4,5},{5,4},{6,7},{7,6},{8,9},{9,8},{10,11... | collective-permute-start | bytes 786440 | tf_op jit(solution)/shard_map/ppermute | solution.py:21
  103.3 1.8 %collective-permute-start.15 = (bf16[1,128,1024]{2,1,0:T(8,128)(2,1)S(1)}, bf16[1,128,1024]{2,1,0:T(8,128)(2,1)S(1)}, u32[]{:S(2)}, u32[]{:S(2)}) collective-permute-start(bf16[1,128,1024]{2,1,0:T(8,128)(2,1)S(1)} %slice.97), channel_id=1, source_target_pairs={{0,1},{1,0},{2,3},{3,2},{4,5},{5,4},{6,7},{7,6},{8,9},{9,8},{10,11... | collective-permute-start | bytes 786440 | tf_op jit(solution)/shard_map/ppermute | solution.py:21
  103.9 9.2 %collective-permute-start.31 = (bf16[128,1024]{1,0:T(8,128)(2,1)S(1)}, bf16[128,1024]{1,0:T(8,128)(2,1)S(1)}, u32[]{:S(2)}, u32[]{:S(2)}) collective-permute-start(bf16[128,1024]{1,0:T(8,128)(2,1)S(1)} %fusion.12), channel_id=1, source_target_pairs={{0,2},{2,0},{1,3},{3,1},{4,6},{6,4},{5,7},{7,5},{8,10},{10,8},{9,1... | collective-permute-start | bytes 786440 | tf_op jit(solution)/shard_map/ppermute | solution.py:21
  105.1 13.7 %collective-permute-start.26 = (bf16[128,1024]{1,0:T(8,128)(2,1)S(1)}, bf16[128,1024]{1,0:T(8,128)(2,1)S(1)}, u32[]{:S(2)}, u32[]{:S(2)}) collective-permute-start(bf16[128,1024]{1,0:T(8,128)(2,1)S(1)} %fusion.11), channel_id=1, source_target_pairs={{0,2},{2,0},{1,3},{3,1},{4,6},{6,4},{5,7},{7,5},{8,10},{10,8},{9,1... | collective-permute-start | bytes 786440 | tf_op jit(solution)/shard_map/ppermute | solution.py:21
  106.2 18.3 %collective-permute-start.14 = (bf16[128,1024]{1,0:T(8,128)(2,1)S(1)}, bf16[128,1024]{1,0:T(8,128)(2,1)S(1)}, u32[]{:S(2)}, u32[]{:S(2)}) collective-permute-start(bf16[128,1024]{1,0:T(8,128)(2,1)S(1)} %slice_bitcast_fusion.9), channel_id=1, source_target_pairs={{0,1},{1,0},{2,3},{3,2},{4,5},{5,4},{6,7},{7,6},{8,9},{9,8},{10,11... | collective-permute-start | bytes 786440 | tf_op jit(solution)/shard_map/ppermute | solution.py:21
  113.1 11.2 %collective-permute-start.21 = (bf16[128,1024]{1,0:T(8,128)(2,1)S(1)}, bf16[128,1024]{1,0:T(8,128)(2,1)S(1)}, u32[]{:S(2)}, u32[]{:S(2)}) collective-permute-start(bf16[128,1024]{1,0:T(8,128)(2,1)S(1)} %fusion.10), channel_id=1, source_target_pairs={{0,2},{2,0},{1,3},{3,1},{4,6},{6,4},{5,7},{7,5},{8,10},{10,8},{9,1... | collective-permute-start | bytes 786440 | tf_op jit(solution)/shard_map/ppermute | solution.py:21
  113.9 15.1 %collective-permute-start.16 = (bf16[128,1024]{1,0:T(8,128)(2,1)S(1)}, bf16[128,1024]{1,0:T(8,128)(2,1)S(1)}, u32[]{:S(2)}, u32[]{:S(2)}) collective-permute-start(bf16[128,1024]{1,0:T(8,128)(2,1)S(1)} %fusion.9), channel_id=1, source_target_pairs={{0,2},{2,0},{1,3},{3,1},{4,6},{6,4},{5,7},{7,5},{8,10},{10,8},{9,1... | collective-permute-start | bytes 786440 | tf_op jit(solution)/shard_map/ppermute | solution.py:21

commit v2 on v0

v2 whole, which is shorter than its diff:
```python
import functools
import math

import jax
import jax.numpy as jnp
from jax import lax
from jax.experimental import pallas as pl
from jax.experimental.pallas import tpu as pltpu
from jax.sharding import PartitionSpec as P

eps = 1e-05
softcap = 10.0
f32 = jnp.float32
bf16 = jnp.bfloat16

COST_SCALE = 64
VMEM = pl.BlockSpec(memory_space=pltpu.VMEM)
SMEM = pl.BlockSpec(memory_space=pltpu.SMEM)
HBM = pl.BlockSpec(memory_space=pltpu.HBM)


def shift(value, axis, by):
    size = lax.axis_size(axis)
    return lax.ppermute(value, axis, [(i, (i + by) % size) for i in range(size)])


def swap(value, axis, by):
    size = lax.axis_size(axis)
    return lax.ppermute(value, axis, [(i, i ^ by) for i in range(size)])


def after(value, *earlier):
    return lax.optimization_barrier((value, *earlier))[0]


def cost(flops, nbytes, transcendentals=0):
    return pl.CostEstimate(
        flops=flops // COST_SCALE, bytes_accessed=nbytes // COST_SCALE,
        transcendentals=transcendentals // COST_SCALE,
    )


def params(mib=16):
    return pltpu.CompilerParams(vmem_limit_bytes=mib * 1024 * 1024)


def diagonal_of(piece):
    down = lax.broadcasted_iota(jnp.int32, (piece, 128), 0)
    return down == lax.broadcasted_iota(jnp.int32, (piece, 128), 1)


def encode_kernel(meta, x_hbm, w_ref, kept_ref, sent_ref, held, squares, arrived, *, pieces, piece, block):
    mp, sub, size = meta[1], meta[2], pieces // 2
    count, tokens, width = held.shape
    steps = count // block
    copies = [
        pltpu.make_async_copy(
            x_hbm.at[pl.ds(i * block, block)], held.at[pl.ds(i * block, block)], arrived.at[i]
        )
        for i in range(steps)
    ]
    for copy in copies:
        copy.start()
    diagonal = diagonal_of(piece)

    def store(a, rows, values):
        far_mp = lax.rem(a // 2 - mp + size, size)

        @pl.when(sub == a % 2)
        def _():
            kept_ref[far_mp, rows, :] = values

        @pl.when(sub != a % 2)
        def _():
            sent_ref[far_mp, rows, :] = values

    for i, copy in enumerate(copies):
        copy.wait()
        x = held[i * block : (i + 1) * block].reshape(block * tokens, width)
        product = jnp.dot(x, w_ref[...], preferred_element_type=f32).astype(bf16)
        xf = x.astype(f32)
        square = jnp.sum(xf * xf, axis=1, keepdims=True)
        for a in range(pieces):
            own = []
            for n in range(block):
                low = n * tokens + a * piece
                own.append(product[low : low + piece])
                column = jnp.broadcast_to(square[low : low + piece], (piece, 128))
                squares[a, i * block + n : i * block + n + 1, :] = jnp.sum(
                    jnp.where(diagonal, column, 0.0), axis=0, keepdims=True
                )
            store(a, slice(i * block * piece, (i + 1) * block * piece), jnp.concatenate(own, axis=0))
    for a in range(pieces):
        tail = jnp.concatenate([squares[a], jnp.zeros_like(squares[a])], axis=1)
        store(a, slice(count * piece, count * piece + count), tail.astype(bf16))


def encode(meta, states, weight, pieces):
    count, tokens, width = states.shape
    out_width = weight.shape[1]
    piece = tokens // pieces
    rows = count * piece + count
    block = 4
    return pl.pallas_call(
        functools.partial(encode_kernel, pieces=pieces, piece=piece, block=block),
        in_specs=[SMEM, HBM, VMEM],
        out_specs=[VMEM] * 2,
        scratch_shapes=[
            pltpu.VMEM(states.shape, bf16),
            pltpu.VMEM((pieces, count, 128), f32),
            pltpu.SemaphoreType.DMA((count // block,)),
        ],
        out_shape=[jax.ShapeDtypeStruct((pieces // 2, rows, out_width), bf16)] * 2,
        compiler_params=params(57),
        cost_estimate=cost(2 * count * tokens * width * out_width, 2 * count * tokens * width),
        name="encode",
    )(meta, states, weight)


def join_kernel(a_ref, b_ref, *outs, first):
    for i, out in enumerate(outs):
        out[...] = (a_ref[first + i].astype(f32) + b_ref[first + i].astype(f32)).astype(bf16)


def join(a, b, first=0):
    return pl.pallas_call(
        functools.partial(join_kernel, first=first),
        in_specs=[VMEM, VMEM],
        out_specs=[VMEM] * (a.shape[0] - first),
        out_shape=[jax.ShapeDtypeStruct(a.shape[1:], bf16)] * (a.shape[0] - first),
        compiler_params=params(),
        cost_estimate=cost(a.size, 6 * a.size),
        name="join",
    )(a, b)


def route_kernel(meta, table, kept, received, *refs, row_count, cap, piece, count, requests, features):
    crossed, outs = refs[: -2 - row_count], refs[-2 - row_count : -2]
    encoded, picks = refs[-2:]
    me = meta[0]
    total = kept[0].astype(f32) + received[0].astype(f32)
    for ref in crossed:
        total = total + ref[...].astype(f32)
    scale = lax.rsqrt(total[count * piece :, :128] * (1.0 / features) + eps)
    diagonal = diagonal_of(piece)
    for n in range(count):
        row = jnp.broadcast_to(scale[n : n + 1], (piece, 128))
        column = jnp.sum(jnp.where(diagonal, row, 0.0), axis=1, keepdims=True)
        encoded[n] = (total[n * piece : (n + 1) * piece] * column).astype(bf16)
    for d in range(row_count):
        for r in range(cap):
            picks[d, r] = 0
        seen = jnp.int32(0)
        for q in range(requests):
            mine = table[d, q] == me

            @pl.when(mine)
            def _(seen=seen, q=q, d=d):
                picks[d, jnp.minimum(seen, cap - 1)] = table[d, requests + q]

            seen = seen + mine.astype(jnp.int32)
        for r in range(cap):
            outs[d][r] = encoded[picks[d, r]]


def route(meta, table, kept, received, crossed, cap, features, count, requests):
    row_count = table.shape[0]
    rows, width = kept.shape[-2:]
    piece = rows // count - 1
    return pl.pallas_call(
        functools.partial(
            route_kernel, row_count=row_count, cap=cap, piece=piece, count=count,
            requests=requests, features=features,
        ),
        in_specs=[SMEM] * 2 + [VMEM] * (2 + len(crossed)),
        out_specs=[VMEM] * row_count,
        scratch_shapes=[
            pltpu.VMEM((count, piece, width), bf16),
            pltpu.SMEM((row_count, cap), jnp.int32),
        ],
        out_shape=[jax.ShapeDtypeStruct((cap, piece, width), bf16)] * row_count,
        compiler_params=params(),
        cost_estimate=cost(8 * rows * width, 2 * rows * width * 3),
        name="route",
    )(meta, table, kept, received, *crossed)


def query_kernel(meta, *refs, low, features, gain):
    hs, w_ref, out_ref = refs[:-2], *refs[-2:]
    mp, sub = meta[1], meta[2]
    tokens, width = out_ref.shape[0], hs[0].shape[1]
    group = features // width // 2
    total, squares = None, None
    for k, part in enumerate(hs):
        block = lax.rem(mp - k // 2 + group, group) * 2 + lax.rem(sub + k % 2, 2)
        rows = pl.ds(pl.multiple_of(block * width, width), width)
        h = part[low : low + tokens] if part.shape[0] > tokens else part[...]
        hf = h.astype(f32)
        hf = hf * hf
        for i in range(0, width, 128):
            square = hf[:, i : i + 128]
            squares = square if squares is None else squares + square
        product = jnp.dot(h, w_ref[rows, :], preferred_element_type=f32)
        total = product if total is None else total + product
    squares = jnp.sum(squares, axis=1, keepdims=True)
    out_ref[...] = (total * (lax.rsqrt(squares * (1.0 / features) + eps) * gain)).astype(bf16)


def project_queries(meta, parts, weight, low, tokens, gain):
    depth, out_width = weight.shape
    return pl.pallas_call(
        functools.partial(query_kernel, low=low, features=depth, gain=gain),
        in_specs=[SMEM] + [VMEM] * (len(parts) + 1),
        out_specs=VMEM,
        out_shape=jax.ShapeDtypeStruct((tokens, out_width), bf16),
        compiler_params=params(),
        cost_estimate=cost(2 * tokens * depth * out_width, 2 * tokens * depth),
        name="queries",
    )(meta, *parts, weight)


def column_block(meta, dm, ds, w_ref, width):
    group = w_ref.shape[1] // width // 2
    block = lax.rem(meta[1] + dm, group) * 2 + lax.rem(meta[2] + ds, 2)
    return w_ref[:, pl.ds(pl.multiple_of(block * width, width), width)]


def attend_kernel(
    meta, table, live, *refs, first, low, span, heads, size, pieces, cap, piece, requests
):
    q_ref = refs[0]
    kvs = refs[1 : 1 + pieces]
    w_ref, kept_ref, sent_ref, att_ref, pair = refs[1 + pieces :]
    me, mp, sub = meta[0], meta[1], meta[2]
    group = pieces // 2
    local = lax.broadcasted_iota(jnp.int32, (piece, size), 0)
    for c in range(pair.shape[0]):
        masks = []
        for j in range(2):
            q = 2 * (first + c) + j
            owner = table[0, q]
            rank = jnp.int32(0)
            for e in range(q):
                rank = rank + (table[0, e] == owner).astype(jnp.int32)
            away = owner ^ me
            slot = away * cap + rank
            length = live[away, table[0, requests + q]]
            for p in range(pieces):
                at = (j * pieces + p) * piece
                pair[c, at : at + piece, :] = kvs[p][slot]
                place = lax.rem(mp - p // 2 + group, group) * 2 + lax.rem(sub + p % 2, 2)
                masks.append((local + place * piece < length).astype(f32))
        mask = jnp.concatenate(masks, axis=0)
        keys = pair[c, :, :size]
        values = jnp.concatenate(
            [(pair[c, :, size:].astype(f32) * mask).astype(bf16), mask.astype(bf16)], axis=1
        )
        rows = slice(c * span, (c + 1) * span)
        query = jnp.concatenate(
            [
                q_ref[low + c * span : low + (c + 1) * span, h * size : (h + 1) * size]
                for h in range(heads)
            ],
            axis=0,
        )
        scores = lax.dot_general(query, keys, (((1,), (1,)), ((), ())), preferred_element_type=f32)
        weights = jnp.exp(softcap * jnp.tanh(scores)).astype(bf16)
        summed = jnp.dot(weights, values, preferred_element_type=f32)
        attended = (summed[:, :size] / summed[:, size:]).astype(bf16)
        for h in range(heads):
            att_ref[rows, h * size : (h + 1) * size] = attended[h * span : (h + 1) * span]
    width = kept_ref.shape[2]
    for ds, out_ref in ((1, sent_ref), (0, kept_ref)):
        for dm in range(1, group):
            w = column_block(meta, dm, ds, w_ref, width)
            out_ref[dm - 1] = jnp.dot(att_ref[...], w, preferred_element_type=f32).astype(bf16)


def attend(meta, table, live, queries, pairs, weight, first, low, spans, span, out_width, cap):
    width = queries.shape[1]
    tokens = spans * span
    pieces = len(pairs)
    piece, pair_width = pairs[0].shape[1:]
    size = pair_width // 2
    steps = pieces // 2 - 1
    requests = table.shape[1] // 2
    return pl.pallas_call(
        functools.partial(
            attend_kernel, first=first, low=low, span=span, heads=width // size, size=size,
            pieces=pieces, cap=cap, piece=piece, requests=requests,
        ),
        in_specs=[SMEM] * 3 + [VMEM] * (2 + pieces),
        out_specs=[VMEM] * 3,
        scratch_shapes=[pltpu.VMEM((spans, 2 * pieces * piece, pair_width), bf16)],
        out_shape=[
            jax.ShapeDtypeStruct((steps, tokens, out_width), bf16),
            jax.ShapeDtypeStruct((steps, tokens, out_width), bf16),
            jax.ShapeDtypeStruct((tokens, width), bf16),
        ],
        compiler_params=params(),
        cost_estimate=cost(
            4 * tokens * width * out_width * steps + 4 * tokens * width * 2 * pieces * piece,
            2 * tokens * width, 2 * tokens * width * 2,
        ),
        name="attend",
    )(meta, table, live, queries, *pairs, weight)


def output_kernel(meta, a_ref, w_ref, kept_ref, sent_ref):
    for ds, out_ref in ((1, sent_ref), (0, kept_ref)):
        w = column_block(meta, 0, ds, w_ref, out_ref.shape[1])
        out_ref[...] = jnp.dot(a_ref[...], w, preferred_element_type=f32).astype(bf16)


def project_output(meta, attended, weight, out_width):
    tokens, width = attended.shape
    return pl.pallas_call(
        output_kernel,
        in_specs=[SMEM, VMEM, VMEM],
        out_specs=[VMEM] * 2,
        out_shape=[jax.ShapeDtypeStruct((tokens, out_width), bf16)] * 2,
        compiler_params=params(),
        cost_estimate=cost(4 * tokens * width * out_width, 2 * tokens * width),
        name="output",
    )(meta, attended, weight)


def shards(
    hidden,
    neighbour_states,
    query_weight,
    encoder_weight,
    output_weight,
    neighbour_owner,
    neighbour_slot,
    neighbour_length,
):
    row_count = lax.axis_size("rows")
    group = lax.axis_size("mp")
    pieces = group * lax.axis_size("sub")
    me, mp, sub = lax.axis_index("rows"), lax.axis_index("mp"), lax.axis_index("sub")
    spans_here = neighbour_owner.shape[0]
    count, slot_tokens, feature_shard = neighbour_states.shape
    features = feature_shard * pieces
    size = encoder_weight.shape[1] // 2
    token_count = hidden.shape[0]
    span_tokens = token_count // spans_here
    requests = 2 * spans_here
    cap = max(2, (requests + row_count - 1) // row_count)
    halves, chunks = 2, 4
    half_tokens, chunk_tokens = token_count // halves, token_count // chunks
    chunk_spans = spans_here // chunks
    gain = 1.0 / (softcap * math.sqrt(size))
    add = lambda *terms: functools.reduce(
        lambda a, b: a + b, [t.astype(f32) for t in terms]
    ).astype(bf16)

    meta = jnp.stack([me, mp, sub]).astype(jnp.int32)

    kept, sent = encode(meta, neighbour_states, encoder_weight, pieces)
    received = shift(sent, "sub", 1)
    leaving = join(kept, received, 1)
    crossed = [shift(leaving[dm - 1], "mp", dm) for dm in range(1, group)]

    def cross(c, *earlier):
        mine = after(hidden, *earlier)[c * half_tokens : (c + 1) * half_tokens]
        return [shift(mine, "mp", dm) for dm in range(1, group)]

    def queries_of(c, crossed, *earlier):
        parts = [hidden, near]
        for far in lax.optimization_barrier((crossed, *earlier))[0]:
            parts += [far, shift(far, "sub", 1)]
        return project_queries(meta, parts, query_weight, c * half_tokens, half_tokens, gain)

    fars = cross(0, *leaving)

    own = jnp.concatenate(
        [neighbour_owner.reshape(1, -1), neighbour_slot.reshape(1, -1), neighbour_length.reshape(1, -1)],
        axis=1,
    )
    own = after(own, *leaving)
    everyone = jnp.concatenate([own] + [swap(own, "rows", d) for d in range(1, row_count)], axis=0)
    table, live = everyone[:, : 2 * requests], everyone[:, 2 * requests :]
    near = shift(after(hidden, table), "sub", 1)

    routed = route(meta, table, kept, received, crossed, cap, features, count, requests)
    encoded = jnp.concatenate(
        [routed[0]]
        + list(lax.optimization_barrier([swap(routed[d], "rows", d) for d in range(1, row_count)])),
        axis=0,
    )
    pairs = [encoded, shift(encoded, "sub", 1)]
    for dm in range(1, group):
        far = shift(encoded, "mp", dm)
        pairs += [far, shift(far, "sub", 1)]
    queries = queries_of(0, fars, encoded)
    fars = cross(1, encoded)

    terms, outs = [], []
    earlier = []
    for c in range(chunks):
        half, low = divmod(c * chunk_tokens, half_tokens)
        if half and not low:
            queries = queries_of(half, fars, *earlier)
        kept, sent, attended = attend(
            meta, table, live, after(queries, *earlier, *outs[-1:]), pairs, output_weight,
            c * chunk_spans, low, chunk_spans, span_tokens, feature_shard, cap,
        )
        received = shift(sent, "sub", 1)
        here_kept, here_sent = project_output(meta, attended, output_weight, feature_shard)
        leaving = join(kept, after(received, here_kept))
        arrived = [shift(leaving[dm - 1], "mp", dm) for dm in range(1, group)]
        here = add(here_kept, shift(here_sent, "sub", 1))
        earlier = [*leaving, here]
        terms.append([here, *arrived])
        if c:
            outs.append(add(after(terms[c - 1][0], *earlier), *terms[c - 1][1:]))
    outs.append(add(*terms[-1]))
    return jnp.concatenate(outs, axis=0)


def solution(mesh):
    placed = (
        P(("groups", "rows"), ("mp", "sub")),
        P(("groups", "rows"), None, ("mp", "sub")),
        P(None, ("mp", "sub")),
        P(("mp", "sub"), None),
        P(("mp", "sub"), None),
        P(("groups", "rows"), None),
        P(("groups", "rows"), None),
        P(("groups", "rows")),
    )
    return jax.shard_map(
        shards,
        mesh=mesh,
        in_specs=placed,
        out_specs=P(("groups", "rows"), ("mp", "sub")),
        check_vma=False,
    )
```

time: 162 us -> 111 us (0.69)
  blocking collectives: 49.6 us -> 0 us
  matrix products: 26.6 us -> 0 us
  Pallas kernels: 0 us -> 26.3 us
  starting transfers between devices: 4.65 us -> 22.6 us
  between operations: 13.9 us -> 0.39 us
  other arithmetic: 7.24 us -> 2.3 us
  waiting for transfers between devices: 55.4 us -> 52.9 us
    ppermute x0 -> x28, waiting for transfers between devices: none -> 52.9 us  [the longest x22 43.8 us: shift(): lax.ppermute(value, axis, [(i, (i + by) % size) for i in range(size)])]
    reduce_scatter x1 -> x0, waiting for transfers between devices: 44.7 us -> none  [shards(): lax.psum_scatter(output_terms.astype(jnp.bfloat16), ('mp', 'sub'), scatte...]
    dot_general x7 -> x0, matrix products: 26.6 us -> none  [the longest x1 7.87 us: shards(): jnp.dot(piece, query_weight, preferred_element_type=jnp.float32)]
    pallas_call x0 -> x17, Pallas kernels: none -> 26.3 us  [the longest x4 7.28 us: attend(): pl.pallas_call(functools.partial(attend_kernel, first=first, low=low, spa...]
    unnamed x1 -> x0, blocking collectives: 23.7 us -> none
    ppermute x0 -> x28, starting transfers between devices: none -> 22.6 us  [the longest x22 13.8 us: shift(): lax.ppermute(value, axis, [(i, (i + by) % size) for i in range(size)])]
    all_gather x2 -> x0, blocking collectives: 20.2 us -> none  [the longest x1 12.6 us: shards(): lax.all_gather(neighbour_owner, 'rows', axis=0, tiled=True)]
    psum x1 -> x0, waiting for transfers between devices: 8.24 us -> none  [shards(): lax.psum(encoder_terms.astype(jnp.bfloat16), ('mp', 'sub'))]
  transfers between devices with their start and end apart: 4 -> 28, of which waited for: 3 -> 13; matrix products, arithmetic and copies ran while one was open for 6% -> 1% of each run, Pallas kernels for 0% -> 9%
where the time goes in v2:
time: 111 us
  waiting for transfers between devices  52.9 us (48%)
  Pallas kernels  26.3 us (24%)
  starting transfers between devices  22.6 us (20%)
  local copies, waits for them, and re-layouts  6.14 us (6%)
  other arithmetic  2.3 us (2%)
    ppermute x22, waiting for transfers between devices, shift(): lax.ppermute(value, axis, [(i, (i + by) % size) for i in range(size)])  43.8 us
    ppermute x22, starting transfers between devices, shift(): lax.ppermute(value, axis, [(i, (i + by) % size) for i in range(size)])  13.8 us
    ppermute x6, waiting for transfers between devices, swap(): return lax.ppermute(value, axis, [(i, i ^ by) for i in range(size)])  9.03 us
    ppermute x6, starting transfers between devices, swap(): return lax.ppermute(value, axis, [(i, i ^ by) for i in range(size)])  8.83 us
    pallas_call x4, Pallas kernels, attend(): pl.pallas_call(functools.partial(attend_kernel, first=first, low=low, spa...  7.28 us
    pallas_call x1, Pallas kernels, encode(): pl.pallas_call(functools.partial(encode_kernel, pieces=pieces, piece=piec...  6.68 us
    pallas_call x2, Pallas kernels, project_queries(): pl.pallas_call(functools.partial(query_kernel, low=low, features=depth, g...  5.99 us
    unnamed x29, local copies, waits for them, and re-layouts  5.83 us
  transfers between devices with their start and end apart: 28, of which 13 were waited for; matrix products, arithmetic and copies ran while one was open for 1% of the time, Pallas kernels for 9%

profile of v2, /device:TPU:0, one launch (start us, length us, event | category | flops | bytes accessed | tf_op | source)
XLA Modules:
  0.0 110.6 jit_solution(8775823007896815891)
XLA Ops:
  0.0 0.6 pad_add_fusion.1.meta
  0.7 6.7 %encode.1 = (bf16[2,528,256]{2,1,0:T(8,128)(2,1)}, bf16[2,528,256]{2,1,0:T(8,128)(2,1)}) custom-call(s32[3]{0:T(128)} %pad_add_fusion.1.meta, bf16[16,128,1024]{2,1,0:T(8,128)(2,1)} %x_hbm.1, bf16[1024,256]{1,0:T(8,128)(2,1)} %w_ref.5), custom_call_target="tpu_custom_call" | custom-call | flops 16777216 | bytes 65536 | tf_op jit(solution)/shard_map/encode/pallas_call | solution.py:104
  7.4 0.5 collective-permute-start
  8.2 1.4 %collective-permute-done.b_ref.received = bf16[2,528,256]{2,1,0:T(8,128)(2,1)S(1)} collective-permute-done((bf16[2,528,256]{2,1,0:T(8,128)(2,1)}, bf16[2,528,256]{2,1,0:T(8,128)(2,1)S(1)}, u32[]{:S(2)}, u32[]{:S(2)}) %collective-permute-start) | collective-permute-done | bytes 540704 | tf_op jit(solution)/shard_map/ppermute | solution.py:24
  9.6 1.0 copy-done.2
  10.8 2.9 %collective-permute-start.6 = (bf16[528,256]{1,0:T(8,128)(2,1)S(1)}, bf16[528,256]{1,0:T(8,128)(2,1)S(1)}, u32[]{:S(2)}, u32[]{:S(2)}) collective-permute-start(bf16[528,256]{1,0:T(8,128)(2,1)S(1)} %join.5), channel_id=1, source_target_pairs={{0,2},{2,0},{1,3},{3,1},{4,6},{6,4},{5,7},{7,5},{8,10},{10,8},{9,1... | collective-permute-start | bytes 811016 | tf_op jit(solution)/shard_map/ppermute | solution.py:24
  13.8 1.6 %collective-permute-start.1 = (s32[1,48]{1,0:T(1,128)S(1)}, s32[1,48]{1,0:T(1,128)S(1)}, u32[]{:S(2)}, u32[]{:S(2)}) collective-permute-start(s32[1,48]{1,0:T(1,128)S(1)} %pad_add_fusion.2), channel_id=1, source_target_pairs={{0,4},{4,0},{8,12},{12,8},{1,5},{5,1},{9,13},{13,9},{2,6},{6,2},{1... | collective-permute-start | bytes 584 | tf_op jit(solution)/shard_map/ppermute | solution.py:29
  15.4 2.6 %collective-permute-start.2 = (s32[1,48]{1,0:T(1,128)S(1)}, s32[1,48]{1,0:T(1,128)S(1)}, u32[]{:S(2)}, u32[]{:S(2)}) collective-permute-start(s32[1,48]{1,0:T(1,128)S(1)} %pad_add_fusion.2), channel_id=1, source_target_pairs={{0,8},{4,12},{8,0},{12,4},{1,9},{5,13},{9,1},{13,5},{2,10},{6,14},... | collective-permute-start | bytes 584 | tf_op jit(solution)/shard_map/ppermute | solution.py:29
  17.9 0.2 collective-permute-start.3
  18.2 0.4 collective-permute-start.5
  18.6 1.2 %collective-permute-done.2 = s32[1,48]{1,0:T(1,128)S(1)} collective-permute-done((s32[1,48]{1,0:T(1,128)S(1)}, s32[1,48]{1,0:T(1,128)S(1)}, u32[]{:S(2)}, u32[]{:S(2)}) %collective-permute-start.2) | collective-permute-done | bytes 224 | tf_op jit(solution)/shard_map/ppermute | solution.py:29
  19.8 3.5 %collective-permute-done.3 = s32[1,48]{1,0:T(1,128)S(1)} collective-permute-done((s32[1,48]{1,0:T(1,128)S(1)}, s32[1,48]{1,0:T(1,128)S(1)}, u32[]{:S(2)}, u32[]{:S(2)}) %collective-permute-start.3) | collective-permute-done | bytes 224 | tf_op jit(solution)/shard_map/ppermute | solution.py:29
  23.4 1.0 copy-done.3
  24.4 0.9 route.1
  25.5 2.3 %collective-permute-start.8 = (bf16[4,32,256]{2,1,0:T(8,128)(2,1)S(1)}, bf16[4,32,256]{2,1,0:T(8,128)(2,1)S(1)}, u32[]{:S(2)}, u32[]{:S(2)}) collective-permute-start(bf16[4,32,256]{2,1,0:T(8,128)(2,1)S(1)} %get-tuple-element.57), channel_id=1, source_target_pairs={{0,8},{4,12},{8,0},{12,4},{1,9},{5,13},{9,1},{13,5},{2,10},{6,14},... | collective-permute-start | bytes 196616 | tf_op jit(solution)/shard_map/ppermute | solution.py:29
  27.7 2.1 %collective-permute-start.9 = (bf16[4,32,256]{2,1,0:T(8,128)(2,1)S(1)}, bf16[4,32,256]{2,1,0:T(8,128)(2,1)S(1)}, u32[]{:S(2)}, u32[]{:S(2)}) collective-permute-start(bf16[4,32,256]{2,1,0:T(8,128)(2,1)S(1)} %get-tuple-element.58), channel_id=1, source_target_pairs={{0,12},{4,8},{8,4},{12,0},{1,13},{5,9},{9,5},{13,1},{2,14},{6,10},... | collective-permute-start | bytes 196616 | tf_op jit(solution)/shard_map/ppermute | solution.py:29
  29.8 1.2 %collective-permute-done.7 = bf16[4,32,256]{2,1,0:T(8,128)(2,1)S(1)} collective-permute-done((bf16[4,32,256]{2,1,0:T(8,128)(2,1)S(1)}, bf16[4,32,256]{2,1,0:T(8,128)(2,1)S(1)}, u32[]{:S(2)}, u32[]{:S(2)}) %collective-permute-start.7) | collective-permute-done | bytes 65568 | tf_op jit(solution)/shard_map/ppermute | solution.py:29
  31.0 3.2 %collective-permute-done.8 = bf16[4,32,256]{2,1,0:T(8,128)(2,1)S(1)} collective-permute-done((bf16[4,32,256]{2,1,0:T(8,128)(2,1)S(1)}, bf16[4,32,256]{2,1,0:T(8,128)(2,1)S(1)}, u32[]{:S(2)}, u32[]{:S(2)}) %collective-permute-start.8) | collective-permute-done | bytes 65568 | tf_op jit(solution)/shard_map/ppermute | solution.py:29
  34.3 1.3 %collective-permute-start.12 = (bf16[16,32,256]{2,1,0:T(8,128)(2,1)S(1)}, bf16[16,32,256]{2,1,0:T(8,128)(2,1)S(1)}, u32[]{:S(2)}, u32[]{:S(2)}) collective-permute-start(bf16[16,32,256]{2,1,0:T(8,128)(2,1)S(1)} %constant_dynamic-update-slice_fusion.refs_1_), channel_id=1, source_target_pairs={{0,2},{2,0},{1,3},{3,1},{4,6},{6,4},{5,7},{7,5},{8,10},{10,8},{9,1... | collective-permute-start | bytes 786440 | tf_op jit(solution)/shard_map/ppermute | solution.py:24
  35.8 7.3 %collective-permute-done.12.refs_3_ = bf16[16,32,256]{2,1,0:T(8,128)(2,1)S(1)} collective-permute-done((bf16[16,32,256]{2,1,0:T(8,128)(2,1)S(1)}, bf16[16,32,256]{2,1,0:T(8,128)(2,1)S(1)}, u32[]{:S(2)}, u32[]{:S(2)}) %collective-permute-start.12) | collective-permute-done | bytes 262176 | tf_op jit(solution)/shard_map/ppermute | solution.py:24
  43.1 3.5 %copy-done = bf16[4096,1024]{1,0:T(8,128)(2,1)S(1)} copy-done((bf16[4096,1024]{1,0:T(8,128)(2,1)S(1)}, bf16[4096,1024]{1,0:T(8,128)(2,1)}, u32[]{:S(2)}) %copy-start) | copy-done | bytes 8388632
  46.6 3.0 %queries.2.refs_0_ = bf16[256,1024]{1,0:T(8,128)(2,1)S(1)} custom-call(s32[3]{0:T(128)S(1)} %copy-done.4, bf16[512,1024]{1,0:T(8,128)(2,1)S(1)} %copy-done.1, bf16[512,1024]{1,0:T(8,128)(2,1)S(1)} %collective-permute-done.4.refs_1_, bf16[256,1024]{1,0:T(8,128)(2,1)S(1)} %collective-permute-done.5.refs_2_, ...), custom_call_target="tpu_custom_call" | custom-call | flops 33554432 | bytes 32768 | tf_op jit(solution)/shard_map/queries/pallas_call | solution.py:211
  49.7 1.8 %attend.4 = (bf16[1,128,1024]{2,1,0:T(8,128)(2,1)S(1)}, bf16[1,128,1024]{2,1,0:T(8,128)(2,1)S(1)}, bf16[128,1024]{1,0:T(8,128)(2,1)S(1)}) custom-call(s32[3]{0:T(128)S(1)} %copy-done.4, s32[4,32]{1,0:T(4,128)S(1)} %bitcast.10, s32[4,16]{1,0:T(4,128)S(1)} %slice.13.live, bf16[256,1024]{1,0:T(8,128)(2,1)S(1)} %queries.2.refs_0_, ...), custom_call_target="tpu_custom_call" | custom-call | flops 10485760 | bytes 4096 | tf_op jit(solution)/shard_map/attend/pallas_call | solution.py:287
  51.5 1.3 %output.4 = (bf16[128,1024]{1,0:T(8,128)(2,1)S(1)}, bf16[128,1024]{1,0:T(8,128)(2,1)S(1)}) custom-call(s32[3]{0:T(128)S(1)} %copy-done.4, bf16[128,1024]{1,0:T(8,128)(2,1)S(1)} %get-tuple-element.63.a_ref, bf16[1024,4096]{1,0:T(8,128)(2,1)S(1)} %bitcast.6), custom_call_target="tpu_custom_call" | custom-call | flops 8388608 | bytes 4096 | tf_op jit(solution)/shard_map/output/pallas_call | solution.py:317
  52.8 0.6 collective-permute-start.14
  53.5 1.3 %collective-permute-start.19 = (bf16[256,1024]{1,0:T(8,128)(2,1)S(1)}, bf16[256,1024]{1,0:T(8,128)(2,1)S(1)}, u32[]{:S(2)}, u32[]{:S(2)}) collective-permute-start(bf16[256,1024]{1,0:T(8,128)(2,1)S(1)} %slice.15), channel_id=1, source_target_pairs={{0,2},{2,0},{1,3},{3,1},{4,6},{6,4},{5,7},{7,5},{8,10},{10,8},{9,1... | collective-permute-start | bytes 1572872 | tf_op jit(solution)/shard_map/ppermute | solution.py:24
  55.0 1.8 %attend.5 = (bf16[1,128,1024]{2,1,0:T(8,128)(2,1)S(1)}, bf16[1,128,1024]{2,1,0:T(8,128)(2,1)S(1)}, bf16[128,1024]{1,0:T(8,128)(2,1)S(1)}) custom-call(s32[3]{0:T(128)S(1)} %copy-done.4, s32[4,32]{1,0:T(4,128)S(1)} %bitcast.11, s32[4,16]{1,0:T(4,128)S(1)} %slice.13.live, bf16[256,1024]{1,0:T(8,128)(2,1)S(1)} %queries.2.refs_0_, ...), custom_call_target="tpu_custom_call" | custom-call | flops 10485760 | bytes 4096 | tf_op jit(solution)/shard_map/attend/pallas_call | solution.py:287
  56.8 0.4 collective-permute-start.16
  57.2 1.3 %output.5 = (bf16[128,1024]{1,0:T(8,128)(2,1)S(1)}, bf16[128,1024]{1,0:T(8,128)(2,1)S(1)}) custom-call(s32[3]{0:T(128)S(1)} %copy-done.4, bf16[128,1024]{1,0:T(8,128)(2,1)S(1)} %get-tuple-element.72.a_ref, bf16[1024,4096]{1,0:T(8,128)(2,1)S(1)} %bitcast.6), custom_call_target="tpu_custom_call" | custom-call | flops 8388608 | bytes 4096 | tf_op jit(solution)/shard_map/output/pallas_call | solution.py:317
  58.5 0.2 collective-permute-start.17
  58.8 1.3 %collective-permute-done.17 = bf16[128,1024]{1,0:T(8,128)(2,1)S(1)} collective-permute-done((bf16[128,1024]{1,0:T(8,128)(2,1)S(1)}, bf16[128,1024]{1,0:T(8,128)(2,1)S(1)}, u32[]{:S(2)}, u32[]{:S(2)}) %collective-permute-start.17) | collective-permute-done | bytes 262176 | tf_op jit(solution)/shard_map/ppermute | solution.py:24
  60.2 7.6 %collective-permute-done.19.refs_2_ = bf16[256,1024]{1,0:T(8,128)(2,1)S(1)} collective-permute-done((bf16[256,1024]{1,0:T(8,128)(2,1)S(1)}, bf16[256,1024]{1,0:T(8,128)(2,1)S(1)}, u32[]{:S(2)}, u32[]{:S(2)}) %collective-permute-start.19) | collective-permute-done | bytes 524320 | tf_op jit(solution)/shard_map/ppermute | solution.py:24
  67.8 1.2 %collective-permute-start.18 = (bf16[128,1024]{1,0:T(8,128)(2,1)S(1)}, bf16[128,1024]{1,0:T(8,128)(2,1)S(1)}, u32[]{:S(2)}, u32[]{:S(2)}) collective-permute-start(bf16[128,1024]{1,0:T(8,128)(2,1)S(1)} %join.6), channel_id=1, source_target_pairs={{0,2},{2,0},{1,3},{3,1},{4,6},{6,4},{5,7},{7,5},{8,10},{10,8},{9,1... | collective-permute-start | bytes 786440 | tf_op jit(solution)/shard_map/ppermute | solution.py:24
  69.0 7.5 %collective-permute-done.18 = bf16[128,1024]{1,0:T(8,128)(2,1)S(1)} collective-permute-done((bf16[128,1024]{1,0:T(8,128)(2,1)S(1)}, bf16[128,1024]{1,0:T(8,128)(2,1)S(1)}, u32[]{:S(2)}, u32[]{:S(2)}) %collective-permute-start.18) | collective-permute-done | bytes 262176 | tf_op jit(solution)/shard_map/ppermute | solution.py:24
  76.6 3.0 %queries.3.refs_0_ = bf16[256,1024]{1,0:T(8,128)(2,1)S(1)} custom-call(s32[3]{0:T(128)S(1)} %copy-done.4, bf16[512,1024]{1,0:T(8,128)(2,1)S(1)} %copy-done.1, bf16[512,1024]{1,0:T(8,128)(2,1)S(1)} %collective-permute-done.4.refs_1_, bf16[256,1024]{1,0:T(8,128)(2,1)S(1)} %collective-permute-done.19.refs_2_, ...), custom_call_target="tpu_custom_call" | custom-call | flops 33554432 | bytes 32768 | tf_op jit(solution)/shard_map/queries/pallas_call | solution.py:211
  79.7 1.8 %attend.6 = (bf16[1,128,1024]{2,1,0:T(8,128)(2,1)S(1)}, bf16[1,128,1024]{2,1,0:T(8,128)(2,1)S(1)}, bf16[128,1024]{1,0:T(8,128)(2,1)S(1)}) custom-call(s32[3]{0:T(128)S(1)} %copy-done.4, s32[4,32]{1,0:T(4,128)S(1)} %bitcast.12, s32[4,16]{1,0:T(4,128)S(1)} %slice.13.live, bf16[256,1024]{1,0:T(8,128)(2,1)S(1)} %queries.3.refs_0_, ...), custom_call_target="tpu_custom_call" | custom-call | flops 10485760 | bytes 4096 | tf_op jit(solution)/shard_map/attend/pallas_call | solution.py:287
  81.6 1.3 %output.6 = (bf16[128,1024]{1,0:T(8,128)(2,1)S(1)}, bf16[128,1024]{1,0:T(8,128)(2,1)S(1)}) custom-call(s32[3]{0:T(128)S(1)} %copy-done.4, bf16[128,1024]{1,0:T(8,128)(2,1)S(1)} %get-tuple-element.82.a_ref, bf16[1024,4096]{1,0:T(8,128)(2,1)S(1)} %bitcast.6), custom_call_target="tpu_custom_call" | custom-call | flops 8388608 | bytes 4096 | tf_op jit(solution)/shard_map/output/pallas_call | solution.py:317
  82.9 0.6 collective-permute-start.22
  83.4 1.2 %collective-permute-start.23 = (bf16[128,1024]{1,0:T(8,128)(2,1)S(1)}, bf16[128,1024]{1,0:T(8,128)(2,1)S(1)}, u32[]{:S(2)}, u32[]{:S(2)}) collective-permute-start(bf16[128,1024]{1,0:T(8,128)(2,1)S(1)} %join.7), channel_id=1, source_target_pairs={{0,2},{2,0},{1,3},{3,1},{4,6},{6,4},{5,7},{7,5},{8,10},{10,8},{9,1... | collective-permute-start | bytes 786440 | tf_op jit(solution)/shard_map/ppermute | solution.py:24
  84.8 6.9 %collective-permute-done.23 = bf16[128,1024]{1,0:T(8,128)(2,1)S(1)} collective-permute-done((bf16[128,1024]{1,0:T(8,128)(2,1)S(1)}, bf16[128,1024]{1,0:T(8,128)(2,1)S(1)}, u32[]{:S(2)}, u32[]{:S(2)}) %collective-permute-start.23) | collective-permute-done | bytes 262176 | tf_op jit(solution)/shard_map/ppermute | solution.py:24
  91.8 1.8 %attend.7 = (bf16[1,128,1024]{2,1,0:T(8,128)(2,1)S(1)}, bf16[1,128,1024]{2,1,0:T(8,128)(2,1)S(1)}, bf16[128,1024]{1,0:T(8,128)(2,1)S(1)}) custom-call(s32[3]{0:T(128)S(1)} %copy-done.4, s32[4,32]{1,0:T(4,128)S(1)} %bitcast.13, s32[4,16]{1,0:T(4,128)S(1)} %slice.13.live, bf16[256,1024]{1,0:T(8,128)(2,1)S(1)} %queries.3.refs_0_, ...), custom_call_target="tpu_custom_call" | custom-call | flops 10485760 | bytes 4096 | tf_op jit(solution)/shard_map/attend/pallas_call | solution.py:287
  93.7 1.3 %output.7 = (bf16[128,1024]{1,0:T(8,128)(2,1)S(1)}, bf16[128,1024]{1,0:T(8,128)(2,1)S(1)}) custom-call(s32[3]{0:T(128)S(1)} %copy-done.4, bf16[128,1024]{1,0:T(8,128)(2,1)S(1)} %get-tuple-element.90.a_ref, bf16[1024,4096]{1,0:T(8,128)(2,1)S(1)} %bitcast.6), custom_call_target="tpu_custom_call" | custom-call | flops 8388608 | bytes 4096 | tf_op jit(solution)/shard_map/output/pallas_call | solution.py:317
  95.0 0.6 collective-permute-start.25
  95.6 1.3 %collective-permute-start.27 = (bf16[128,1024]{1,0:T(8,128)(2,1)S(1)}, bf16[128,1024]{1,0:T(8,128)(2,1)S(1)}, u32[]{:S(2)}, u32[]{:S(2)}) collective-permute-start(bf16[128,1024]{1,0:T(8,128)(2,1)S(1)} %join.9), channel_id=1, source_target_pairs={{0,2},{2,0},{1,3},{3,1},{4,6},{6,4},{5,7},{7,5},{8,10},{10,8},{9,1... | collective-permute-start | bytes 786440 | tf_op jit(solution)/shard_map/ppermute | solution.py:24
  96.9 0.8 collective-permute-start.26
  97.7 7.1 %collective-permute-done.27 = bf16[128,1024]{1,0:T(8,128)(2,1)S(1)} collective-permute-done((bf16[128,1024]{1,0:T(8,128)(2,1)S(1)}, bf16[128,1024]{1,0:T(8,128)(2,1)S(1)}, u32[]{:S(2)}, u32[]{:S(2)}) %collective-permute-start.27) | collective-permute-done | bytes 262176 | tf_op jit(solution)/shard_map/ppermute | solution.py:24
  105.0 4.6 %collective-permute-done.26 = bf16[128,1024]{1,0:T(8,128)(2,1)S(1)} collective-permute-done((bf16[128,1024]{1,0:T(8,128)(2,1)S(1)}, bf16[128,1024]{1,0:T(8,128)(2,1)S(1)}, u32[]{:S(2)}, u32[]{:S(2)}) %collective-permute-start.26) | collective-permute-done | bytes 262176 | tf_op jit(solution)/shard_map/ppermute | solution.py:24
  109.6 1.0 pad_maximum_fusion
  (73 shorter events, 2.2 us)
Async XLA Ops:
  0.7 7.2 %copy-start.5 = (s32[8,2]{0,1:T(2,128)S(1)}, s32[8,2]{0,1:T(2,128)}, u32[]{:S(2)}) copy-start(s32[8,2]{0,1:T(2,128)} %param.14) | copy-start | bytes 196
  0.7 7.4 %copy-start.6 = (s32[8,2]{0,1:T(2,128)S(1)}, s32[8,2]{0,1:T(2,128)}, u32[]{:S(2)}) copy-start(s32[8,2]{0,1:T(2,128)} %param.13) | copy-start | bytes 196
  0.7 13.0 %copy-start.7 = (s32[16]{0:T(128)S(1)}, s32[16]{0:T(128)}, u32[]{:S(2)}) copy-start(s32[16]{0:T(128)} %param.15) | copy-start | bytes 196
  0.7 17.5 %copy-start.1 = (bf16[512,1024]{1,0:T(8,128)(2,1)S(1)}, bf16[512,1024]{1,0:T(8,128)(2,1)}, u32[]{:S(2)}) copy-start(bf16[512,1024]{1,0:T(8,128)(2,1)} %refs_0_.3) | copy-start | bytes 3145732
  7.4 16.0 %copy-start.4 = (s32[3]{0:T(128)S(1)}, s32[3]{0:T(128)}, u32[]{:S(2)}) copy-start(s32[3]{0:T(128)} %pad_add_fusion.1.meta) | copy-start | bytes 40
  7.4 2.3 %collective-permute-start = (bf16[2,528,256]{2,1,0:T(8,128)(2,1)}, bf16[2,528,256]{2,1,0:T(8,128)(2,1)S(1)}, u32[]{:S(2)}, u32[]{:S(2)}) collective-permute-start(bf16[2,528,256]{2,1,0:T(8,128)(2,1)} %get-tuple-element.51), channel_id=1, source_target_pairs={{0,1},{1,0},{2,3},{3,2},{4,5},{5,4},{6,7},{7,6},{8,9},{9,8},{10,11... | collective-permute-start | bytes 1622024 | tf_op jit(solution)/shard_map/ppermute | solution.py:24
  9.6 1.0 copy-start.2
  10.7 39.0 %slice-start = ((s8[8388608]{0:T(1024)(128)(4,1)}), s8[4194304]{0:T(1024)(128)(4,1)S(1)}, s32[]{:S(2)}) async-start(s8[8388608]{0:T(1024)(128)(4,1)} %bitcast.5), calls=%async_computation | async-start | bytes 8388608
  10.8 12.6 %collective-permute-start.6 = (bf16[528,256]{1,0:T(8,128)(2,1)S(1)}, bf16[528,256]{1,0:T(8,128)(2,1)S(1)}, u32[]{:S(2)}, u32[]{:S(2)}) collective-permute-start(bf16[528,256]{1,0:T(8,128)(2,1)S(1)} %join.5), channel_id=1, source_target_pairs={{0,2},{2,0},{1,3},{3,1},{4,6},{6,4},{5,7},{7,5},{8,10},{10,8},{9,1... | collective-permute-start | bytes 811016 | tf_op jit(solution)/shard_map/ppermute | solution.py:24
  13.8 4.8 %collective-permute-start.1 = (s32[1,48]{1,0:T(1,128)S(1)}, s32[1,48]{1,0:T(1,128)S(1)}, u32[]{:S(2)}, u32[]{:S(2)}) collective-permute-start(s32[1,48]{1,0:T(1,128)S(1)} %pad_add_fusion.2), channel_id=1, source_target_pairs={{0,4},{4,0},{8,12},{12,8},{1,5},{5,1},{9,13},{13,9},{2,6},{6,2},{1... | collective-permute-start | bytes 584 | tf_op jit(solution)/shard_map/ppermute | solution.py:29
  15.4 4.4 %collective-permute-start.2 = (s32[1,48]{1,0:T(1,128)S(1)}, s32[1,48]{1,0:T(1,128)S(1)}, u32[]{:S(2)}, u32[]{:S(2)}) collective-permute-start(s32[1,48]{1,0:T(1,128)S(1)} %pad_add_fusion.2), channel_id=1, source_target_pairs={{0,8},{4,12},{8,0},{12,4},{1,9},{5,13},{9,1},{13,5},{2,10},{6,14},... | collective-permute-start | bytes 584 | tf_op jit(solution)/shard_map/ppermute | solution.py:29
  17.9 5.3 %collective-permute-start.3 = (s32[1,48]{1,0:T(1,128)S(1)}, s32[1,48]{1,0:T(1,128)S(1)}, u32[]{:S(2)}, u32[]{:S(2)}) collective-permute-start(s32[1,48]{1,0:T(1,128)S(1)} %pad_add_fusion.2), channel_id=1, source_target_pairs={{0,12},{4,8},{8,4},{12,0},{1,13},{5,9},{9,5},{13,1},{2,14},{6,10},... | collective-permute-start | bytes 584 | tf_op jit(solution)/shard_map/ppermute | solution.py:29
  18.2 16.0 %collective-permute-start.5 = (bf16[256,1024]{1,0:T(8,128)(2,1)S(1)}, bf16[256,1024]{1,0:T(8,128)(2,1)S(1)}, u32[]{:S(2)}, u32[]{:S(2)}) collective-permute-start(bf16[256,1024]{1,0:T(8,128)(2,1)S(1)} %slice.14), channel_id=1, source_target_pairs={{0,2},{2,0},{1,3},{3,1},{4,6},{6,4},{5,7},{7,5},{8,10},{10,8},{9,1... | collective-permute-start | bytes 1572872 | tf_op jit(solution)/shard_map/ppermute | solution.py:24
  23.3 19.8 %collective-permute-start.4 = (bf16[512,1024]{1,0:T(8,128)(2,1)S(1)}, bf16[512,1024]{1,0:T(8,128)(2,1)S(1)}, u32[]{:S(2)}, u32[]{:S(2)}) collective-permute-start(bf16[512,1024]{1,0:T(8,128)(2,1)S(1)} %copy-done.1), channel_id=1, source_target_pairs={{0,1},{1,0},{2,3},{3,2},{4,5},{5,4},{6,7},{7,6},{8,9},{9,8},{10,11... | collective-permute-start | bytes 3145736 | tf_op jit(solution)/shard_map/ppermute | solution.py:24
  23.4 1.1 copy-start.3
  25.4 5.6 %collective-permute-start.7 = (bf16[4,32,256]{2,1,0:T(8,128)(2,1)S(1)}, bf16[4,32,256]{2,1,0:T(8,128)(2,1)S(1)}, u32[]{:S(2)}, u32[]{:S(2)}) collective-permute-start(bf16[4,32,256]{2,1,0:T(8,128)(2,1)S(1)} %get-tuple-element.56), channel_id=1, source_target_pairs={{0,4},{4,0},{8,12},{12,8},{1,5},{5,1},{9,13},{13,9},{2,6},{6,2},{1... | collective-permute-start | bytes 196616 | tf_op jit(solution)/shard_map/ppermute | solution.py:29
  25.5 8.7 %collective-permute-start.8 = (bf16[4,32,256]{2,1,0:T(8,128)(2,1)S(1)}, bf16[4,32,256]{2,1,0:T(8,128)(2,1)S(1)}, u32[]{:S(2)}, u32[]{:S(2)}) collective-permute-start(bf16[4,32,256]{2,1,0:T(8,128)(2,1)S(1)} %get-tuple-element.57), channel_id=1, source_target_pairs={{0,8},{4,12},{8,0},{12,4},{1,9},{5,13},{9,1},{13,5},{2,10},{6,14},... | collective-permute-start | bytes 196616 | tf_op jit(solution)/shard_map/ppermute | solution.py:29
  27.7 6.4 %collective-permute-start.9 = (bf16[4,32,256]{2,1,0:T(8,128)(2,1)S(1)}, bf16[4,32,256]{2,1,0:T(8,128)(2,1)S(1)}, u32[]{:S(2)}, u32[]{:S(2)}) collective-permute-start(bf16[4,32,256]{2,1,0:T(8,128)(2,1)S(1)} %get-tuple-element.58), channel_id=1, source_target_pairs={{0,12},{4,8},{8,4},{12,0},{1,13},{5,9},{9,5},{13,1},{2,14},{6,10},... | collective-permute-start | bytes 196616 | tf_op jit(solution)/shard_map/ppermute | solution.py:29
  34.2 8.9 %collective-permute-start.10 = (bf16[256,1024]{1,0:T(8,128)(2,1)S(1)}, bf16[256,1024]{1,0:T(8,128)(2,1)S(1)}, u32[]{:S(2)}, u32[]{:S(2)}) collective-permute-start(bf16[256,1024]{1,0:T(8,128)(2,1)S(1)} %collective-permute-done.5.refs_2_), channel_id=1, source_target_pairs={{0,1},{1,0},{2,3},{3,2},{4,5},{5,4},{6,7},{7,6},{8,9},{9,8},{10,11... | collective-permute-start | bytes 1572872 | tf_op jit(solution)/shard_map/ppermute | solution.py:24
  34.3 8.7 %collective-permute-start.12 = (bf16[16,32,256]{2,1,0:T(8,128)(2,1)S(1)}, bf16[16,32,256]{2,1,0:T(8,128)(2,1)S(1)}, u32[]{:S(2)}, u32[]{:S(2)}) collective-permute-start(bf16[16,32,256]{2,1,0:T(8,128)(2,1)S(1)} %constant_dynamic-update-slice_fusion.refs_1_), channel_id=1, source_target_pairs={{0,2},{2,0},{1,3},{3,1},{4,6},{6,4},{5,7},{7,5},{8,10},{10,8},{9,1... | collective-permute-start | bytes 786440 | tf_op jit(solution)/shard_map/ppermute | solution.py:24
  35.6 14.0 %collective-permute-start.11 = (bf16[16,32,256]{2,1,0:T(8,128)(2,1)S(1)}, bf16[16,32,256]{2,1,0:T(8,128)(2,1)S(1)}, u32[]{:S(2)}, u32[]{:S(2)}) collective-permute-start(bf16[16,32,256]{2,1,0:T(8,128)(2,1)S(1)} %constant_dynamic-update-slice_fusion.refs_1_), channel_id=1, source_target_pairs={{0,1},{1,0},{2,3},{3,2},{4,5},{5,4},{6,7},{7,6},{8,9},{9,8},{10,11... | collective-permute-start | bytes 786440 | tf_op jit(solution)/shard_map/ppermute | solution.py:24
  43.0 6.6 %collective-permute-start.13 = (bf16[16,32,256]{2,1,0:T(8,128)(2,1)S(1)}, bf16[16,32,256]{2,1,0:T(8,128)(2,1)S(1)}, u32[]{:S(2)}, u32[]{:S(2)}) collective-permute-start(bf16[16,32,256]{2,1,0:T(8,128)(2,1)S(1)} %collective-permute-done.12.refs_3_), channel_id=1, source_target_pairs={{0,1},{1,0},{2,3},{3,2},{4,5},{5,4},{6,7},{7,6},{8,9},{9,8},{10,11... | collective-permute-start | bytes 786440 | tf_op jit(solution)/shard_map/ppermute | solution.py:24
  43.1 6.6 %slice-start.1 = ((s8[8388608]{0:T(1024)(128)(4,1)}), s8[4194304]{0:T(1024)(128)(4,1)S(1)}, s32[]{:S(2)}) async-start(s8[8388608]{0:T(1024)(128)(4,1)} %bitcast.5), calls=%async_computation.1 | async-start | bytes 8388608
  43.1 3.5 %copy-start = (bf16[4096,1024]{1,0:T(8,128)(2,1)S(1)}, bf16[4096,1024]{1,0:T(8,128)(2,1)}, u32[]{:S(2)}) copy-start(bf16[4096,1024]{1,0:T(8,128)(2,1)} %refs_4_.3) | copy-start | bytes 25165828
  52.8 2.0 %collective-permute-start.14 = (bf16[128,1024]{1,0:T(8,128)(2,1)S(1)}, bf16[128,1024]{1,0:T(8,128)(2,1)S(1)}, u32[]{:S(2)}, u32[]{:S(2)}) collective-permute-start(bf16[128,1024]{1,0:T(8,128)(2,1)S(1)} %get-tuple-element.65), channel_id=1, source_target_pairs={{0,1},{1,0},{2,3},{3,2},{4,5},{5,4},{6,7},{7,6},{8,9},{9,8},{10,11... | collective-permute-start | bytes 786440 | tf_op jit(solution)/shard_map/ppermute | solution.py:24
  53.4 1.5 %collective-permute-start.15 = (bf16[1,128,1024]{2,1,0:T(8,128)(2,1)S(1)}, bf16[1,128,1024]{2,1,0:T(8,128)(2,1)S(1)}, u32[]{:S(2)}, u32[]{:S(2)}) collective-permute-start(bf16[1,128,1024]{2,1,0:T(8,128)(2,1)S(1)} %get-tuple-element.67), channel_id=1, source_target_pairs={{0,1},{1,0},{2,3},{3,2},{4,5},{5,4},{6,7},{7,6},{8,9},{9,8},{10,11... | collective-permute-start | bytes 786440 | tf_op jit(solution)/shard_map/ppermute | solution.py:24
  53.5 14.3 %collective-permute-start.19 = (bf16[256,1024]{1,0:T(8,128)(2,1)S(1)}, bf16[256,1024]{1,0:T(8,128)(2,1)S(1)}, u32[]{:S(2)}, u32[]{:S(2)}) collective-permute-start(bf16[256,1024]{1,0:T(8,128)(2,1)S(1)} %slice.15), channel_id=1, source_target_pairs={{0,2},{2,0},{1,3},{3,1},{4,6},{6,4},{5,7},{7,5},{8,10},{10,8},{9,1... | collective-permute-start | bytes 1572872 | tf_op jit(solution)/shard_map/ppermute | solution.py:24
  55.0 21.7 %slice-start.2 = ((s8[8388608]{0:T(1024)(128)(4,1)}), s8[4194304]{0:T(1024)(128)(4,1)S(1)}, s32[]{:S(2)}) async-start(s8[8388608]{0:T(1024)(128)(4,1)} %bitcast.7), calls=%async_computation.2 | async-start | bytes 8388608
  56.8 1.9 %collective-permute-start.16 = (bf16[1,128,1024]{2,1,0:T(8,128)(2,1)S(1)}, bf16[1,128,1024]{2,1,0:T(8,128)(2,1)S(1)}, u32[]{:S(2)}, u32[]{:S(2)}) collective-permute-start(bf16[1,128,1024]{2,1,0:T(8,128)(2,1)S(1)} %get-tuple-element.71), channel_id=1, source_target_pairs={{0,1},{1,0},{2,3},{3,2},{4,5},{5,4},{6,7},{7,6},{8,9},{9,8},{10,11... | collective-permute-start | bytes 786440 | tf_op jit(solution)/shard_map/ppermute | solution.py:24
  57.2 19.4 %slice-start.3 = ((s8[8388608]{0:T(1024)(128)(4,1)}), s8[4194304]{0:T(1024)(128)(4,1)S(1)}, s32[]{:S(2)}) async-start(s8[8388608]{0:T(1024)(128)(4,1)} %bitcast.7), calls=%async_computation.3 | async-start | bytes 8388608
  58.5 1.6 %collective-permute-start.17 = (bf16[128,1024]{1,0:T(8,128)(2,1)S(1)}, bf16[128,1024]{1,0:T(8,128)(2,1)S(1)}, u32[]{:S(2)}, u32[]{:S(2)}) collective-permute-start(bf16[128,1024]{1,0:T(8,128)(2,1)S(1)} %get-tuple-element.75), channel_id=1, source_target_pairs={{0,1},{1,0},{2,3},{3,2},{4,5},{5,4},{6,7},{7,6},{8,9},{9,8},{10,11... | collective-permute-start | bytes 786440 | tf_op jit(solution)/shard_map/ppermute | solution.py:24
  67.8 8.8 %collective-permute-start.20 = (bf16[256,1024]{1,0:T(8,128)(2,1)S(1)}, bf16[256,1024]{1,0:T(8,128)(2,1)S(1)}, u32[]{:S(2)}, u32[]{:S(2)}) collective-permute-start(bf16[256,1024]{1,0:T(8,128)(2,1)S(1)} %collective-permute-done.19.refs_2_), channel_id=1, source_target_pairs={{0,1},{1,0},{2,3},{3,2},{4,5},{5,4},{6,7},{7,6},{8,9},{9,8},{10,11... | collective-permute-start | bytes 1572872 | tf_op jit(solution)/shard_map/ppermute | solution.py:24
  67.8 8.7 %collective-permute-start.18 = (bf16[128,1024]{1,0:T(8,128)(2,1)S(1)}, bf16[128,1024]{1,0:T(8,128)(2,1)S(1)}, u32[]{:S(2)}, u32[]{:S(2)}) collective-permute-start(bf16[128,1024]{1,0:T(8,128)(2,1)S(1)} %join.6), channel_id=1, source_target_pairs={{0,2},{2,0},{1,3},{3,1},{4,6},{6,4},{5,7},{7,5},{8,10},{10,8},{9,1... | collective-permute-start | bytes 786440 | tf_op jit(solution)/shard_map/ppermute | solution.py:24
  81.5 3.1 %collective-permute-start.21 = (bf16[1,128,1024]{2,1,0:T(8,128)(2,1)S(1)}, bf16[1,128,1024]{2,1,0:T(8,128)(2,1)S(1)}, u32[]{:S(2)}, u32[]{:S(2)}) collective-permute-start(bf16[1,128,1024]{2,1,0:T(8,128)(2,1)S(1)} %get-tuple-element.81), channel_id=1, source_target_pairs={{0,1},{1,0},{2,3},{3,2},{4,5},{5,4},{6,7},{7,6},{8,9},{9,8},{10,11... | collective-permute-start | bytes 786440 | tf_op jit(solution)/shard_map/ppermute | solution.py:24
  82.9 1.9 %collective-permute-start.22 = (bf16[128,1024]{1,0:T(8,128)(2,1)S(1)}, bf16[128,1024]{1,0:T(8,128)(2,1)S(1)}, u32[]{:S(2)}, u32[]{:S(2)}) collective-permute-start(bf16[128,1024]{1,0:T(8,128)(2,1)S(1)} %get-tuple-element.85), channel_id=1, source_target_pairs={{0,1},{1,0},{2,3},{3,2},{4,5},{5,4},{6,7},{7,6},{8,9},{9,8},{10,11... | collective-permute-start | bytes 786440 | tf_op jit(solution)/shard_map/ppermute | solution.py:24
  83.4 8.3 %collective-permute-start.23 = (bf16[128,1024]{1,0:T(8,128)(2,1)S(1)}, bf16[128,1024]{1,0:T(8,128)(2,1)S(1)}, u32[]{:S(2)}, u32[]{:S(2)}) collective-permute-start(bf16[128,1024]{1,0:T(8,128)(2,1)S(1)} %join.7), channel_id=1, source_target_pairs={{0,2},{2,0},{1,3},{3,1},{4,6},{6,4},{5,7},{7,5},{8,10},{10,8},{9,1... | collective-permute-start | bytes 786440 | tf_op jit(solution)/shard_map/ppermute | solution.py:24
  93.6 1.9 %collective-permute-start.24 = (bf16[1,128,1024]{2,1,0:T(8,128)(2,1)S(1)}, bf16[1,128,1024]{2,1,0:T(8,128)(2,1)S(1)}, u32[]{:S(2)}, u32[]{:S(2)}) collective-permute-start(bf16[1,128,1024]{2,1,0:T(8,128)(2,1)S(1)} %get-tuple-element.89), channel_id=1, source_target_pairs={{0,1},{1,0},{2,3},{3,2},{4,5},{5,4},{6,7},{7,6},{8,9},{9,8},{10,11... | collective-permute-start | bytes 786440 | tf_op jit(solution)/shard_map/ppermute | solution.py:24
  95.0 2.7 %collective-permute-start.25 = (bf16[128,1024]{1,0:T(8,128)(2,1)S(1)}, bf16[128,1024]{1,0:T(8,128)(2,1)S(1)}, u32[]{:S(2)}, u32[]{:S(2)}) collective-permute-start(bf16[128,1024]{1,0:T(8,128)(2,1)S(1)} %get-tuple-element.93), channel_id=1, source_target_pairs={{0,1},{1,0},{2,3},{3,2},{4,5},{5,4},{6,7},{7,6},{8,9},{9,8},{10,11... | collective-permute-start | bytes 786440 | tf_op jit(solution)/shard_map/ppermute | solution.py:24
  95.6 9.2 %collective-permute-start.27 = (bf16[128,1024]{1,0:T(8,128)(2,1)S(1)}, bf16[128,1024]{1,0:T(8,128)(2,1)S(1)}, u32[]{:S(2)}, u32[]{:S(2)}) collective-permute-start(bf16[128,1024]{1,0:T(8,128)(2,1)S(1)} %join.9), channel_id=1, source_target_pairs={{0,2},{2,0},{1,3},{3,1},{4,6},{6,4},{5,7},{7,5},{8,10},{10,8},{9,1... | collective-permute-start | bytes 786440 | tf_op jit(solution)/shard_map/ppermute | solution.py:24
  96.9 12.6 %collective-permute-start.26 = (bf16[128,1024]{1,0:T(8,128)(2,1)S(1)}, bf16[128,1024]{1,0:T(8,128)(2,1)S(1)}, u32[]{:S(2)}, u32[]{:S(2)}) collective-permute-start(bf16[128,1024]{1,0:T(8,128)(2,1)S(1)} %join.8), channel_id=1, source_target_pairs={{0,2},{2,0},{1,3},{3,1},{4,6},{6,4},{5,7},{7,5},{8,10},{10,8},{9,1... | collective-permute-start | bytes 786440 | tf_op jit(solution)/shard_map/ppermute | solution.py:24

commit v3 on v2

v3 whole, which is shorter than its diff:
```python
import functools
import math

import jax
import jax.numpy as jnp
from jax import lax
from jax.experimental import pallas as pl
from jax.experimental.pallas import tpu as pltpu
from jax.sharding import PartitionSpec as P

eps = 1e-05
softcap = 10.0
FIRST = 48
f32 = jnp.float32
bf16 = jnp.bfloat16

VMEM = pl.BlockSpec(memory_space=pltpu.VMEM)
SMEM = pl.BlockSpec(memory_space=pltpu.SMEM)


def shift(value, axis, by):
    size = lax.axis_size(axis)
    return lax.ppermute(value, axis, [(i, (i + by) % size) for i in range(size)])


def swap(value, axis, by):
    size = lax.axis_size(axis)
    return lax.ppermute(value, axis, [(i, i ^ by) for i in range(size)])


def after(value, *earlier):
    return lax.optimization_barrier((value, *earlier))[0]


def cost(flops, nbytes, transcendentals=0):
    return pl.CostEstimate(flops=flops, bytes_accessed=nbytes, transcendentals=transcendentals)


def params():
    return pltpu.CompilerParams(vmem_limit_bytes=16 * 1024 * 1024)


def diagonal_of(piece):
    down = lax.broadcasted_iota(jnp.int32, (piece, 128), 0)
    return down == lax.broadcasted_iota(jnp.int32, (piece, 128), 1)


def encode_kernel(meta, x_ref, w_ref, kept_ref, sent_ref, squares, *, pieces, piece, block):
    mp, sub, size = meta[1], meta[2], pieces // 2
    count, tokens, width = x_ref.shape
    diagonal = diagonal_of(piece)

    def store(a, rows, values):
        far_mp = lax.rem(a // 2 - mp + size, size)

        @pl.when(sub == a % 2)
        def _():
            kept_ref[far_mp, rows, :] = values

        @pl.when(sub != a % 2)
        def _():
            sent_ref[far_mp, rows, :] = values

    for i in range(count // block):
        x = x_ref[i * block : (i + 1) * block].reshape(block * tokens, width)
        product = jnp.dot(x, w_ref[...], preferred_element_type=f32).astype(bf16)
        lanes = None
        for j in range(0, width, 128):
            part = x[:, j : j + 128].astype(f32)
            lanes = part * part if lanes is None else lanes + part * part
        square = jnp.sum(lanes, axis=1, keepdims=True)
        for a in range(pieces):
            own = []
            for n in range(block):
                low = n * tokens + a * piece
                own.append(product[low : low + piece])
                column = jnp.broadcast_to(square[low : low + piece], (piece, 128))
                squares[a, i * block + n : i * block + n + 1, :] = jnp.sum(
                    jnp.where(diagonal, column, 0.0), axis=0, keepdims=True
                )
            store(a, slice(i * block * piece, (i + 1) * block * piece), jnp.concatenate(own, axis=0))
    for a in range(pieces):
        tail = jnp.concatenate([squares[a], jnp.zeros_like(squares[a])], axis=1)
        store(a, slice(count * piece, count * piece + count), tail.astype(bf16))


def encode(meta, states, weight, pieces):
    count, tokens, width = states.shape
    out_width = weight.shape[1]
    piece = tokens // pieces
    rows = count * piece + count
    return pl.pallas_call(
        functools.partial(encode_kernel, pieces=pieces, piece=piece, block=2),
        in_specs=[SMEM, VMEM, VMEM],
        out_specs=[VMEM] * 2,
        scratch_shapes=[pltpu.VMEM((pieces, count, 128), f32)],
        out_shape=[jax.ShapeDtypeStruct((pieces // 2, rows, out_width), bf16)] * 2,
        compiler_params=params(),
        cost_estimate=cost(2 * count * tokens * width * out_width, 2 * count * tokens * width),
        name="encode",
    )(meta, states, weight)


def route_kernel(meta, table, kept, received, *refs, row_count, cap, piece, count, requests, features):
    crossed, outs = refs[: -2 - row_count], refs[-2 - row_count : -2]
    encoded, picks = refs[-2:]
    me = meta[0]
    total = kept[0].astype(f32) + received[0].astype(f32)
    for ref in crossed:
        total = total + ref[...].astype(f32)
    scale = lax.rsqrt(total[count * piece :, :128] * (1.0 / features) + eps)
    diagonal = diagonal_of(piece)
    for n in range(count):
        row = jnp.broadcast_to(scale[n : n + 1], (piece, 128))
        column = jnp.sum(jnp.where(diagonal, row, 0.0), axis=1, keepdims=True)
        encoded[n] = (total[n * piece : (n + 1) * piece] * column).astype(bf16)
    for d in range(row_count):
        for r in range(cap):
            picks[d, r] = 0
        seen = jnp.int32(0)
        for q in range(requests):
            mine = table[d, q] == me

            @pl.when(mine)
            def _(seen=seen, q=q, d=d):
                picks[d, jnp.minimum(seen, cap - 1)] = table[d, requests + q]

            seen = seen + mine.astype(jnp.int32)
        for r in range(cap):
            outs[d][r] = encoded[picks[d, r]]


def route(meta, table, kept, received, crossed, cap, features, count, requests):
    row_count = table.shape[0]
    rows, width = kept.shape[-2:]
    piece = rows // count - 1
    return pl.pallas_call(
        functools.partial(
            route_kernel, row_count=row_count, cap=cap, piece=piece, count=count,
            requests=requests, features=features,
        ),
        in_specs=[SMEM] * 2 + [VMEM] * (2 + len(crossed)),
        out_specs=[VMEM] * row_count,
        scratch_shapes=[
            pltpu.VMEM((count, piece, width), bf16),
            pltpu.SMEM((row_count, cap), jnp.int32),
        ],
        out_shape=[jax.ShapeDtypeStruct((cap, piece, width), bf16)] * row_count,
        compiler_params=params(),
        cost_estimate=cost(8 * rows * width, 2 * rows * width * 3),
        name="route",
    )(meta, table, kept, received, *crossed)


def queries_from(meta, hs, w_ref, low, gain):
    mp, sub = meta[1], meta[2]
    tokens, width = hs[-1].shape
    features = w_ref.shape[0]
    group = features // width // 2
    total, squares = None, None
    for k, part in enumerate(hs):
        block = lax.rem(mp - k // 2 + group, group) * 2 + lax.rem(sub + k % 2, 2)
        rows = pl.ds(pl.multiple_of(block * width, width), width)
        h = part[low : low + tokens] if k < 2 else part[...]
        for i in range(0, width, 128):
            square = h[:, i : i + 128].astype(f32)
            square = square * square
            squares = square if squares is None else squares + square
        product = jnp.dot(h, w_ref[rows, :], preferred_element_type=f32)
        total = product if total is None else total + product
    squares = jnp.sum(squares, axis=1, keepdims=True)
    return (total * (lax.rsqrt(squares * (1.0 / features) + eps) * gain)).astype(bf16)


def query_kernel(meta, own_ref, near_ref, *refs, lows, gain):
    fars, w_ref, out_ref = refs[:-2], *refs[-2:]
    each = len(fars) // len(lows)
    for i, low in enumerate(lows):
        far = fars[i * each : (i + 1) * each]
        out_ref[low : low + far[0].shape[0], :] = queries_from(
            meta, (own_ref, near_ref, *far), w_ref, low, gain
        )


def project_queries(meta, own, near, segments, weight, gain):
    lows, tokens = [], 0
    for far in segments:
        lows.append(tokens)
        tokens += far[0].shape[0]
    parts = [own, near] + [part for far in segments for part in far]
    depth, out_width = weight.shape
    return pl.pallas_call(
        functools.partial(query_kernel, lows=tuple(lows), gain=gain),
        in_specs=[SMEM] + [VMEM] * (len(parts) + 1),
        out_specs=VMEM,
        out_shape=jax.ShapeDtypeStruct((tokens, out_width), bf16),
        compiler_params=params(),
        cost_estimate=cost(2 * tokens * depth * out_width, 2 * tokens * depth),
        name="queries",
    )(meta, *parts, weight)


def chunk_kernel(
    meta, table, live, *refs, first, low, span, heads, size, pieces, cap, requests, gain
):
    sources, kvs = refs[: -5 - pieces], refs[-5 - pieces : -5]
    w_ref, kept_ref, sent_ref, att, pair = refs[-5:]
    me, mp, sub = meta[0], meta[1], meta[2]
    group = pieces // 2
    piece = kvs[0].shape[1]
    tokens = att.shape[0]
    if len(sources) == 1:
        queries = sources[0][low : low + tokens]
    else:
        queries = queries_from(meta, sources[:-1], sources[-1], low, gain)
    local = lax.broadcasted_iota(jnp.int32, (piece, size), 0)
    for c in range(pair.shape[0]):
        masks = []
        for j in range(2):
            q = 2 * (first + c) + j
            owner = table[0, q]
            rank = jnp.int32(0)
            for e in range(q):
                rank = rank + (table[0, e] == owner).astype(jnp.int32)
            away = owner ^ me
            slot = away * cap + rank
            length = live[away, table[0, requests + q]]
            for p in range(pieces):
                at = (j * pieces + p) * piece
                pair[c, at : at + piece, :] = kvs[p][slot]
                place = lax.rem(mp - p // 2 + group, group) * 2 + lax.rem(sub + p % 2, 2)
                masks.append((local + place * piece < length).astype(f32))
        mask = jnp.concatenate(masks, axis=0)
        keys = pair[c, :, :size]
        values = jnp.concatenate(
            [(pair[c, :, size:].astype(f32) * mask).astype(bf16), mask.astype(bf16)], axis=1
        )
        rows = slice(c * span, (c + 1) * span)
        query = jnp.concatenate(
            [queries[rows, h * size : (h + 1) * size] for h in range(heads)], axis=0
        )
        scores = lax.dot_general(query, keys, (((1,), (1,)), ((), ())), preferred_element_type=f32)
        weights = jnp.exp(softcap * jnp.tanh(scores)).astype(bf16)
        summed = jnp.dot(weights, values, preferred_element_type=f32)
        attended = (summed[:, :size] / summed[:, size:]).astype(bf16)
        for h in range(heads):
            att[rows, h * size : (h + 1) * size] = attended[h * span : (h + 1) * span]
    width = kept_ref.shape[2]
    for ds, out_ref in ((1, sent_ref), (0, kept_ref)):
        for dm in range(group):
            block = lax.rem(mp + dm, group) * 2 + lax.rem(sub + ds, 2)
            w = w_ref[:, pl.ds(pl.multiple_of(block * width, width), width)]
            out_ref[dm] = jnp.dot(att[...], w, preferred_element_type=f32).astype(bf16)


def run_chunk(meta, table, live, sources, pairs, weight, first, low, spans, span, out_width, cap, gain):
    width = weight.shape[0]
    tokens = spans * span
    pieces = len(pairs)
    piece, pair_width = pairs[0].shape[1:]
    size = pair_width // 2
    group = pieces // 2
    requests = table.shape[1] // 2
    return pl.pallas_call(
        functools.partial(
            chunk_kernel, first=first, low=low, span=span, heads=width // size, size=size,
            pieces=pieces, cap=cap, requests=requests, gain=gain,
        ),
        in_specs=[SMEM] * 3 + [VMEM] * (1 + pieces + len(sources)),
        out_specs=[VMEM] * 2,
        scratch_shapes=[
            pltpu.VMEM((tokens, width), bf16),
            pltpu.VMEM((spans, 2 * pieces * piece, pair_width), bf16),
        ],
        out_shape=[jax.ShapeDtypeStruct((group, tokens, out_width), bf16)] * 2,
        compiler_params=params(),
        cost_estimate=cost(
            4 * tokens * width * out_width * group + 4 * tokens * width * 2 * pieces * piece,
            2 * tokens * width, 2 * tokens * width * 2,
        ),
        name="chunk",
    )(meta, table, live, *sources, *pairs, weight)


def shards(
    hidden,
    neighbour_states,
    query_weight,
    encoder_weight,
    output_weight,
    neighbour_owner,
    neighbour_slot,
    neighbour_length,
):
    row_count = lax.axis_size("rows")
    group = lax.axis_size("mp")
    pieces = group * lax.axis_size("sub")
    me, mp, sub = lax.axis_index("rows"), lax.axis_index("mp"), lax.axis_index("sub")
    spans_here = neighbour_owner.shape[0]
    count, slot_tokens, feature_shard = neighbour_states.shape
    features = feature_shard * pieces
    size = encoder_weight.shape[1] // 2
    token_count = hidden.shape[0]
    span_tokens = token_count // spans_here
    requests = 2 * spans_here
    cap = max(2, (requests + row_count - 1) // row_count)
    chunks = 4
    chunk_spans = spans_here // chunks
    chunk_tokens = token_count // chunks
    gain = 1.0 / (softcap * math.sqrt(size))
    add = lambda *terms: functools.reduce(
        lambda a, b: a + b, [t.astype(f32) for t in terms]
    ).astype(bf16)

    meta = jnp.stack([me, mp, sub]).astype(jnp.int32)

    def cross(mine):
        return [shift(mine, "mp", dm) for dm in range(1, group)]

    def with_near(fars, *earlier):
        out = []
        for far in lax.optimization_barrier((fars, *earlier))[0]:
            out += [far, shift(far, "sub", 1)]
        return out

    fars_first = cross(hidden[:FIRST])

    table = jnp.concatenate(
        [neighbour_owner.reshape(1, -1), neighbour_slot.reshape(1, -1), neighbour_length.reshape(1, -1)],
        axis=1,
    )
    table = jnp.concatenate([table, swap(table, "rows", 1)], axis=0)

    kept, sent = encode(meta, neighbour_states, encoder_weight, pieces)
    received = after(shift(after(sent, *fars_first), "sub", 1), table)
    leaving = [add(kept[dm], received[dm]) for dm in range(1, group)]
    crossed = [shift(leaving[dm - 1], "mp", dm) for dm in range(1, group)]
    near = shift(after(hidden, *leaving), "sub", 1)
    table = after(table, *leaving)
    while table.shape[0] < row_count:
        table = jnp.concatenate([table, swap(table, "rows", table.shape[0])], axis=0)
    table, live = table[:, : 2 * requests], table[:, 2 * requests :]

    fars_rest = cross(after(hidden, table, *crossed)[FIRST:])

    routed = route(meta, table, kept, received, crossed, cap, features, count, requests)
    encoded = jnp.concatenate(
        [routed[0]]
        + list(lax.optimization_barrier([swap(routed[d], "rows", d) for d in range(1, row_count)])),
        axis=0,
    )
    pairs = [encoded, shift(encoded, "sub", 1)]
    fars = [shift(encoded, "mp", dm) for dm in range(1, group)]
    queries = project_queries(
        after(meta, encoded), hidden, near,
        [with_near(fars_first, encoded), with_near(fars_rest, encoded)], query_weight, gain,
    )
    pairs += with_near(fars, queries)

    kept, sent, received, leaving, arrived, outs = [], [], [], [], [], []

    def send(c, *earlier):
        got = after(received[c], *earlier)
        leaving.append([add(kept[c][dm], got[dm]) for dm in range(1, group)])
        arrived.append([shift(leaving[c][dm - 1], "mp", dm) for dm in range(1, group)])

    def total(c, *earlier):
        outs.append(add(after(kept[c], *earlier)[0], received[c][0], *arrived[c]))

    for c in range(chunks):
        gate = (leaving[c - 2] if c > 1 else []) + ([outs[c - 3]] if c > 2 else [])
        one, other = run_chunk(
            after(meta, *gate), table, live, [queries], pairs, output_weight, c * chunk_spans,
            c * chunk_tokens, chunk_spans, span_tokens, feature_shard, cap, gain,
        )
        kept.append(one)
        if c:
            send(c - 1, one)
            other = after(other, *leaving[c - 1])
        if c > 1:
            total(c - 2, *leaving[c - 1])
        if c > 1 and c == chunks - 1:
            other = after(other, outs[-1])
        received.append(shift(other, "sub", 1))
    send(chunks - 1)
    total(chunks - 2, *leaving[-1])
    total(chunks - 1)
    return jnp.concatenate(outs, axis=0)


def solution(mesh):
    placed = (
        P(("groups", "rows"), ("mp", "sub")),
        P(("groups", "rows"), None, ("mp", "sub")),
        P(None, ("mp", "sub")),
        P(("mp", "sub"), None),
        P(("mp", "sub"), None),
        P(("groups", "rows"), None),
        P(("groups", "rows"), None),
        P(("groups", "rows")),
    )
    return jax.shard_map(
        shards,
        mesh=mesh,
        in_specs=placed,
        out_specs=P(("groups", "rows"), ("mp", "sub")),
        check_vma=False,
    )
```

time: 111 us -> 94.6 us (0.85)
  waiting for transfers between devices: 52.9 us -> 44.3 us
  Pallas kernels: 26.3 us -> 21.4 us
  starting transfers between devices: 22.6 us -> 18.4 us
  local copies, waits for them, and re-layouts: 6.14 us -> 8.02 us
    ppermute x22 -> x18, waiting for transfers between devices: 43.8 us -> 34.7 us  [shift(): lax.ppermute(value, axis, [(i, (i + by) % size) for i in range(size)])]
    ppermute x22 -> x18, starting transfers between devices: 13.8 us -> 9.31 us  [shift(): lax.ppermute(value, axis, [(i, (i + by) % size) for i in range(size)])]
    pallas_call x15 -> x5, Pallas kernels: 18.7 us -> 15.9 us  [the longest x4 9.63 us: run_chunk(): pl.pallas_call(functools.partial(chunk_kernel, first=first, low=low, span...]
    pallas_call x1, Pallas kernels: 6.68 us -> 4.54 us  [encode(): pl.pallas_call(functools.partial(encode_kernel, pieces=pieces, piece=piec...]
    unnamed x29 -> x23, local copies, waits for them, and re-layouts: 5.83 us -> 6.82 us
    ppermute x6 -> x5, waiting for transfers between devices: 9.03 us -> 9.56 us  [swap(): return lax.ppermute(value, axis, [(i, i ^ by) for i in range(size)])]
    ppermute x6 -> x5, starting transfers between devices: 8.83 us -> 9.07 us  [swap(): return lax.ppermute(value, axis, [(i, i ^ by) for i in range(size)])]
  transfers between devices with their start and end apart: 28 -> 23, of which waited for: 13 -> 14; matrix products, arithmetic and copies ran while one was open for 1% -> 1% of each run, Pallas kernels for 9% -> 20%
where the time goes in v3:
time: 94.6 us; the launch traced here: 94.4 us
  waiting for transfers between devices  44.3 us (47%)
  Pallas kernels  21.4 us (23%)
  starting transfers between devices  18.4 us (19%)
  local copies, waits for them, and re-layouts  8.02 us (8%)
  other arithmetic  2.1 us (2%)
    ppermute x18, waiting for transfers between devices, shift(): lax.ppermute(value, axis, [(i, (i + by) % size) for i in range(size)])  34.7 us
    pallas_call x4, Pallas kernels, run_chunk(): pl.pallas_call(functools.partial(chunk_kernel, first=first, low=low, span...  9.63 us
    ppermute x5, waiting for transfers between devices, swap(): return lax.ppermute(value, axis, [(i, i ^ by) for i in range(size)])  9.56 us
    ppermute x18, starting transfers between devices, shift(): lax.ppermute(value, axis, [(i, (i + by) % size) for i in range(size)])  9.31 us
    ppermute x5, starting transfers between devices, swap(): return lax.ppermute(value, axis, [(i, i ^ by) for i in range(size)])  9.07 us
    unnamed x23, local copies, waits for them, and re-layouts  6.82 us
    pallas_call x1, Pallas kernels, project_queries(): pl.pallas_call(functools.partial(query_kernel, lows=tuple(lows), gain=gai...  6.27 us
    pallas_call x1, Pallas kernels, encode(): pl.pallas_call(functools.partial(encode_kernel, pieces=pieces, piece=piec...  4.54 us
  transfers between devices with their start and end apart: 23, of which 14 were waited for; matrix products, arithmetic and copies ran while one was open for 1% of the time, Pallas kernels for 20%

profile of v3, /device:TPU:0, one launch (start us, length us, event | category | flops | bytes accessed | tf_op | source)
XLA Modules:
  0.0 94.4 jit_solution(12706849181438341953)
XLA Ops:
  0.0 0.9 slice.67
  0.9 2.9 %collective-permute-start.1 = (bf16[48,1024]{1,0:T(8,128)(2,1)S(1)}, bf16[48,1024]{1,0:T(8,128)(2,1)S(1)}, u32[]{:S(2)}, u32[]{:S(2)}) collective-permute-start(bf16[48,1024]{1,0:T(8,128)(2,1)S(1)} %slice.67), channel_id=1, source_target_pairs={{0,2},{2,0},{1,3},{3,1},{4,6},{6,4},{5,7},{7,5},{8,10},{10,8},{9,1... | collective-permute-start | bytes 294920 | tf_op jit(solution)/shard_map/ppermute | solution.py:23
  3.9 2.2 %copy-done = bf16[16,128,1024]{2,1,0:T(8,128)(2,1)S(1)} copy-done((bf16[16,128,1024]{2,1,0:T(8,128)(2,1)S(1)}, bf16[16,128,1024]{2,1,0:T(8,128)(2,1)}, u32[]{:S(2)}) %copy-start) | copy-done | bytes 4194328
  6.1 1.0 %copy-done.2 = bf16[1024,256]{1,0:T(8,128)(2,1)S(1)} copy-done((bf16[1024,256]{1,0:T(8,128)(2,1)S(1)}, bf16[1024,256]{1,0:T(8,128)(2,1)}, u32[]{:S(2)}) %copy-start.2) | copy-done | bytes 524312
  7.2 4.5 %encode.1 = (bf16[2,528,256]{2,1,0:T(8,128)(2,1)S(1)}, bf16[2,528,256]{2,1,0:T(8,128)(2,1)S(1)}) custom-call(s32[3]{0:T(128)S(1)} %pad_add_fusion.2.meta, bf16[16,128,1024]{2,1,0:T(8,128)(2,1)S(1)} %copy-done, bf16[1024,256]{1,0:T(8,128)(2,1)S(1)} %copy-done.2), custom_call_target="tpu_custom_call" | custom-call | flops 1073741824 | bytes 4194304 | tf_op jit(solution)/shard_map/encode/pallas_call | solution.py:92
  11.8 0.1 copy.11
  11.9 0.1 reshape.41
  12.2 1.6 %collective-permute-start = (s32[1,48]{1,0:T(1,128)S(1)}, s32[1,48]{1,0:T(1,128)S(1)}, u32[]{:S(2)}, u32[]{:S(2)}) collective-permute-start(s32[1,48]{1,0:T(1,128)S(1)} %pad_add_fusion.3), channel_id=1, source_target_pairs={{0,4},{4,0},{8,12},{12,8},{1,5},{5,1},{9,13},{13,9},{2,6},{6,2},{1... | collective-permute-start | bytes 584 | tf_op jit(solution)/shard_map/ppermute | solution.py:28
  13.8 2.0 %collective-permute-done = s32[1,48]{1,0:T(1,128)S(1)} collective-permute-done((s32[1,48]{1,0:T(1,128)S(1)}, s32[1,48]{1,0:T(1,128)S(1)}, u32[]{:S(2)}, u32[]{:S(2)}) %collective-permute-start) | collective-permute-done | bytes 224 | tf_op jit(solution)/shard_map/ppermute | solution.py:28
  15.9 0.2 collective-permute-start.4
  16.1 3.0 %collective-permute-start.3 = (s32[2,48]{1,0:T(2,128)S(1)}, s32[2,48]{1,0:T(2,128)S(1)}, u32[]{:S(2)}, u32[]{:S(2)}) collective-permute-start(s32[2,48]{1,0:T(2,128)S(1)} %pad_add_fusion.1), channel_id=1, source_target_pairs={{0,8},{4,12},{8,0},{12,4},{1,9},{5,13},{9,1},{13,5},{2,10},{6,14},... | collective-permute-start | bytes 1160 | tf_op jit(solution)/shard_map/ppermute | solution.py:28
  19.1 1.5 %collective-permute-done.3 = s32[2,48]{1,0:T(2,128)S(1)} collective-permute-done((s32[2,48]{1,0:T(2,128)S(1)}, s32[2,48]{1,0:T(2,128)S(1)}, u32[]{:S(2)}, u32[]{:S(2)}) %collective-permute-start.3) | collective-permute-done | bytes 416 | tf_op jit(solution)/shard_map/ppermute | solution.py:28
  20.7 3.0 %collective-permute-done.4.refs_0_ = bf16[528,256]{1,0:T(8,128)(2,1)S(1)} collective-permute-done((bf16[528,256]{1,0:T(8,128)(2,1)S(1)}, bf16[528,256]{1,0:T(8,128)(2,1)S(1)}, u32[]{:S(2)}, u32[]{:S(2)}) %collective-permute-start.4) | collective-permute-done | bytes 270368 | tf_op jit(solution)/shard_map/ppermute | solution.py:23
  23.8 0.4 collective-permute-start.10
  24.2 0.9 route.1
  25.1 1.8 %collective-permute-start.5 = (bf16[4,32,256]{2,1,0:T(8,128)(2,1)S(1)}, bf16[4,32,256]{2,1,0:T(8,128)(2,1)S(1)}, u32[]{:S(2)}, u32[]{:S(2)}) collective-permute-start(bf16[4,32,256]{2,1,0:T(8,128)(2,1)S(1)} %get-tuple-element.49), channel_id=1, source_target_pairs={{0,4},{4,0},{8,12},{12,8},{1,5},{5,1},{9,13},{13,9},{2,6},{6,2},{1... | collective-permute-start | bytes 196616 | tf_op jit(solution)/shard_map/ppermute | solution.py:28
  26.9 2.6 %collective-permute-start.6 = (bf16[4,32,256]{2,1,0:T(8,128)(2,1)S(1)}, bf16[4,32,256]{2,1,0:T(8,128)(2,1)S(1)}, u32[]{:S(2)}, u32[]{:S(2)}) collective-permute-start(bf16[4,32,256]{2,1,0:T(8,128)(2,1)S(1)} %get-tuple-element.50), channel_id=1, source_target_pairs={{0,8},{4,12},{8,0},{12,4},{1,9},{5,13},{9,1},{13,5},{2,10},{6,14},... | collective-permute-start | bytes 196616 | tf_op jit(solution)/shard_map/ppermute | solution.py:28
  29.6 0.1 collective-permute-done.5
  29.7 4.2 %collective-permute-done.6 = bf16[4,32,256]{2,1,0:T(8,128)(2,1)S(1)} collective-permute-done((bf16[4,32,256]{2,1,0:T(8,128)(2,1)S(1)}, bf16[4,32,256]{2,1,0:T(8,128)(2,1)S(1)}, u32[]{:S(2)}, u32[]{:S(2)}) %collective-permute-start.6) | collective-permute-done | bytes 65568 | tf_op jit(solution)/shard_map/ppermute | solution.py:28
  33.9 1.8 %collective-permute-done.7 = bf16[4,32,256]{2,1,0:T(8,128)(2,1)S(1)} collective-permute-done((bf16[4,32,256]{2,1,0:T(8,128)(2,1)S(1)}, bf16[4,32,256]{2,1,0:T(8,128)(2,1)S(1)}, u32[]{:S(2)}, u32[]{:S(2)}) %collective-permute-start.7) | collective-permute-done | bytes 65568 | tf_op jit(solution)/shard_map/ppermute | solution.py:28
  35.7 9.5 %collective-permute-done.10.refs_2_ = bf16[464,1024]{1,0:T(8,128)(2,1)S(1)} collective-permute-done((bf16[464,1024]{1,0:T(8,128)(2,1)S(1)}, bf16[464,1024]{1,0:T(8,128)(2,1)S(1)}, u32[]{:S(2)}, u32[]{:S(2)}) %collective-permute-start.10) | collective-permute-done | bytes 950304 | tf_op jit(solution)/shard_map/ppermute | solution.py:23
  45.2 0.5 collective-permute-start.9
  45.7 0.7 collective-permute-start.13
  46.4 1.5 %collective-permute-done.9.refs_1_ = bf16[48,1024]{1,0:T(8,128)(2,1)S(1)} collective-permute-done((bf16[48,1024]{1,0:T(8,128)(2,1)S(1)}, bf16[48,1024]{1,0:T(8,128)(2,1)S(1)}, u32[]{:S(2)}, u32[]{:S(2)}) %collective-permute-start.9) | collective-permute-done | bytes 98336 | tf_op jit(solution)/shard_map/ppermute | solution.py:23
  47.9 3.4 %copy-done.3 = bf16[4096,1024]{1,0:T(8,128)(2,1)S(1)} copy-done((bf16[4096,1024]{1,0:T(8,128)(2,1)S(1)}, bf16[4096,1024]{1,0:T(8,128)(2,1)}, u32[]{:S(2)}) %copy-start.3) | copy-done | bytes 8388632
  51.3 6.3 %queries.1.refs_0_ = bf16[512,1024]{1,0:T(8,128)(2,1)S(1)} custom-call(s32[3]{0:T(128)S(1)} %pad_add_fusion.2.meta, bf16[512,1024]{1,0:T(8,128)(2,1)S(1)} %copy-done.1, bf16[512,1024]{1,0:T(8,128)(2,1)S(1)} %collective-permute-done.8.near_ref, bf16[48,1024]{1,0:T(8,128)(2,1)S(1)} %collective-permute-done.1.refs_0_, ...), custom_call_target="tpu_custom_call" | custom-call | flops 4294967296 | bytes 4194304 | tf_op jit(solution)/shard_map/queries/pallas_call | solution.py:192
  57.5 0.2 collective-permute-start.14
  57.8 1.3 %collective-permute-done.14.refs_4_ = bf16[16,32,256]{2,1,0:T(8,128)(2,1)S(1)} collective-permute-done((bf16[16,32,256]{2,1,0:T(8,128)(2,1)S(1)}, bf16[16,32,256]{2,1,0:T(8,128)(2,1)S(1)}, u32[]{:S(2)}, u32[]{:S(2)}) %collective-permute-start.14) | collective-permute-done | bytes 262176 | tf_op jit(solution)/shard_map/ppermute | solution.py:23
  59.2 2.4 %chunk.4 = (bf16[2,128,1024]{2,1,0:T(8,128)(2,1)S(1)}, bf16[2,128,1024]{2,1,0:T(8,128)(2,1)S(1)}) custom-call(s32[3]{0:T(128)S(1)} %pad_add_fusion.2.meta, s32[4,32]{1,0:T(4,128)S(1)} %bitcast.34, s32[4,16]{1,0:T(4,128)S(1)} %slice.70.live, bf16[512,1024]{1,0:T(8,128)(2,1)S(1)} %queries.1.refs_0_, ...), custom_call_target="tpu_custom_call" | custom-call | flops 1207959552 | bytes 262144 | tf_op jit(solution)/shard_map/chunk/pallas_call | solution.py:264
  61.6 0.2 collective-permute-start.15
  61.8 2.4 %chunk.5 = (bf16[2,128,1024]{2,1,0:T(8,128)(2,1)S(1)}, bf16[2,128,1024]{2,1,0:T(8,128)(2,1)S(1)}) custom-call(s32[3]{0:T(128)S(1)} %pad_add_fusion.2.meta, s32[4,32]{1,0:T(4,128)S(1)} %bitcast.35, s32[4,16]{1,0:T(4,128)S(1)} %slice.70.live, bf16[512,1024]{1,0:T(8,128)(2,1)S(1)} %queries.1.refs_0_, ...), custom_call_target="tpu_custom_call" | custom-call | flops 1207959552 | bytes 262144 | tf_op jit(solution)/shard_map/chunk/pallas_call | solution.py:264
  64.3 0.4 collective-permute-start.16
  64.7 0.7 collective-permute-start.17
  65.4 2.4 %chunk.6 = (bf16[2,128,1024]{2,1,0:T(8,128)(2,1)S(1)}, bf16[2,128,1024]{2,1,0:T(8,128)(2,1)S(1)}) custom-call(s32[3]{0:T(128)S(1)} %pad_add_fusion.2.meta, s32[4,32]{1,0:T(4,128)S(1)} %bitcast.36, s32[4,16]{1,0:T(4,128)S(1)} %slice.70.live, bf16[512,1024]{1,0:T(8,128)(2,1)S(1)} %queries.1.refs_0_, ...), custom_call_target="tpu_custom_call" | custom-call | flops 1207959552 | bytes 262144 | tf_op jit(solution)/shard_map/chunk/pallas_call | solution.py:264
  67.9 1.4 %collective-permute-start.19 = (bf16[128,1024]{1,0:T(8,128)(2,1)S(1)}, bf16[128,1024]{1,0:T(8,128)(2,1)S(1)}, u32[]{:S(2)}, u32[]{:S(2)}) collective-permute-start(bf16[128,1024]{1,0:T(8,128)(2,1)S(1)} %fusion.6), channel_id=1, source_target_pairs={{0,2},{2,0},{1,3},{3,1},{4,6},{6,4},{5,7},{7,5},{8,10},{10,8},{9,1... | collective-permute-start | bytes 786440 | tf_op jit(solution)/shard_map/ppermute | solution.py:23
  69.4 4.5 %collective-permute-done.17 = bf16[128,1024]{1,0:T(8,128)(2,1)S(1)} collective-permute-done((bf16[128,1024]{1,0:T(8,128)(2,1)S(1)}, bf16[128,1024]{1,0:T(8,128)(2,1)S(1)}, u32[]{:S(2)}, u32[]{:S(2)}) %collective-permute-start.17) | collective-permute-done | bytes 262176 | tf_op jit(solution)/shard_map/ppermute | solution.py:23
  73.8 0.1 fusion.3
  74.0 2.4 %chunk.7 = (bf16[2,128,1024]{2,1,0:T(8,128)(2,1)S(1)}, bf16[2,128,1024]{2,1,0:T(8,128)(2,1)S(1)}) custom-call(s32[3]{0:T(128)S(1)} %pad_add_fusion.2.meta, s32[4,32]{1,0:T(4,128)S(1)} %bitcast.37, s32[4,16]{1,0:T(4,128)S(1)} %slice.70.live, bf16[512,1024]{1,0:T(8,128)(2,1)S(1)} %queries.1.refs_0_, ...), custom_call_target="tpu_custom_call" | custom-call | flops 1207959552 | bytes 262144 | tf_op jit(solution)/shard_map/chunk/pallas_call | solution.py:264
  76.5 2.2 %collective-permute-done.19 = bf16[128,1024]{1,0:T(8,128)(2,1)S(1)} collective-permute-done((bf16[128,1024]{1,0:T(8,128)(2,1)S(1)}, bf16[128,1024]{1,0:T(8,128)(2,1)S(1)}, u32[]{:S(2)}, u32[]{:S(2)}) %collective-permute-start.19) | collective-permute-done | bytes 262176 | tf_op jit(solution)/shard_map/ppermute | solution.py:23
  78.7 0.1 fusion.2
  78.9 0.7 collective-permute-start.21
  79.6 1.2 %collective-permute-done.20 = bf16[2,128,1024]{2,1,0:T(8,128)(2,1)S(1)} collective-permute-done((bf16[2,128,1024]{2,1,0:T(8,128)(2,1)S(1)}, bf16[2,128,1024]{2,1,0:T(8,128)(2,1)S(1)}, u32[]{:S(2)}, u32[]{:S(2)}) %collective-permute-start.20) | collective-permute-done | bytes 524320 | tf_op jit(solution)/shard_map/ppermute | solution.py:23
  80.8 0.7 collective-permute-start.22
  81.6 6.5 %collective-permute-done.21 = bf16[128,1024]{1,0:T(8,128)(2,1)S(1)} collective-permute-done((bf16[128,1024]{1,0:T(8,128)(2,1)S(1)}, bf16[128,1024]{1,0:T(8,128)(2,1)S(1)}, u32[]{:S(2)}, u32[]{:S(2)}) %collective-permute-start.21) | collective-permute-done | bytes 262176 | tf_op jit(solution)/shard_map/ppermute | solution.py:23
  88.1 0.1 fusion.1
  88.2 5.0 %collective-permute-done.22 = bf16[128,1024]{1,0:T(8,128)(2,1)S(1)} collective-permute-done((bf16[128,1024]{1,0:T(8,128)(2,1)S(1)}, bf16[128,1024]{1,0:T(8,128)(2,1)S(1)}, u32[]{:S(2)}, u32[]{:S(2)}) %collective-permute-start.22) | collective-permute-done | bytes 262176 | tf_op jit(solution)/shard_map/ppermute | solution.py:23
  93.2 0.1 fusion
  93.3 1.0 %pad_maximum_fusion = bf16[512,1024]{1,0:T(8,128)(2,1)} fusion(bf16[128,1024]{1,0:T(8,128)(2,1)S(1)} %fusion, bf16[128,1024]{1,0:T(8,128)(2,1)S(1)} %fusion.1, bf16[128,1024]{1,0:T(8,128)(2,1)S(1)} %fusion.2, bf16[128,1024]{1,0:T(8,128)(2,1)S(1)} %fusion.3), kind=kLoop, calls=%fused_computation | loop fusion | flops 4194304 | bytes 2097152 | tf_op jit(solution)/shard_map/concatenate | solution.py:388
  (49 shorter events, 1.2 us)
Async XLA Ops:
  0.9 10.8 %collective-permute-start.1 = (bf16[48,1024]{1,0:T(8,128)(2,1)S(1)}, bf16[48,1024]{1,0:T(8,128)(2,1)S(1)}, u32[]{:S(2)}, u32[]{:S(2)}) collective-permute-start(bf16[48,1024]{1,0:T(8,128)(2,1)S(1)} %slice.67), channel_id=1, source_target_pairs={{0,2},{2,0},{1,3},{3,1},{4,6},{6,4},{5,7},{7,5},{8,10},{10,8},{9,1... | collective-permute-start | bytes 294920 | tf_op jit(solution)/shard_map/ppermute | solution.py:23
  3.9 2.2 %copy-start = (bf16[16,128,1024]{2,1,0:T(8,128)(2,1)S(1)}, bf16[16,128,1024]{2,1,0:T(8,128)(2,1)}, u32[]{:S(2)}) copy-start(bf16[16,128,1024]{2,1,0:T(8,128)(2,1)} %x_ref.1) | copy-start | bytes 12582916
  6.1 1.0 %copy-start.2 = (bf16[1024,256]{1,0:T(8,128)(2,1)S(1)}, bf16[1024,256]{1,0:T(8,128)(2,1)}, u32[]{:S(2)}) copy-start(bf16[1024,256]{1,0:T(8,128)(2,1)} %w_ref.1) | copy-start | bytes 1572868
  7.1 4.6 %copy-start.5 = (s32[8,2]{0,1:T(2,128)S(1)}, s32[8,2]{0,1:T(2,128)}, u32[]{:S(2)}) copy-start(s32[8,2]{0,1:T(2,128)} %param.13) | copy-start | bytes 196
  7.1 4.8 %copy-start.6 = (s32[8,2]{0,1:T(2,128)S(1)}, s32[8,2]{0,1:T(2,128)}, u32[]{:S(2)}) copy-start(s32[8,2]{0,1:T(2,128)} %param.14) | copy-start | bytes 196
  7.2 5.0 %copy-start.4 = (s32[16]{0:T(128)S(1)}, s32[16]{0:T(128)}, u32[]{:S(2)}) copy-start(s32[16]{0:T(128)} %param.15) | copy-start | bytes 196
  7.2 16.6 %copy-start.1 = (bf16[512,1024]{1,0:T(8,128)(2,1)S(1)}, bf16[512,1024]{1,0:T(8,128)(2,1)}, u32[]{:S(2)}) copy-start(bf16[512,1024]{1,0:T(8,128)(2,1)} %own_ref.1) | copy-start | bytes 3145732
  11.7 4.1 %collective-permute-start.2 = (bf16[2,528,256]{2,1,0:T(8,128)(2,1)S(1)}, bf16[2,528,256]{2,1,0:T(8,128)(2,1)S(1)}, u32[]{:S(2)}, u32[]{:S(2)}) collective-permute-start(bf16[2,528,256]{2,1,0:T(8,128)(2,1)S(1)} %get-tuple-element.45), channel_id=1, source_target_pairs={{0,1},{1,0},{2,3},{3,2},{4,5},{5,4},{6,7},{7,6},{8,9},{9,8},{10,11... | collective-permute-start | bytes 1622024 | tf_op jit(solution)/shard_map/ppermute | solution.py:23
  12.2 3.5 %collective-permute-start = (s32[1,48]{1,0:T(1,128)S(1)}, s32[1,48]{1,0:T(1,128)S(1)}, u32[]{:S(2)}, u32[]{:S(2)}) collective-permute-start(s32[1,48]{1,0:T(1,128)S(1)} %pad_add_fusion.3), channel_id=1, source_target_pairs={{0,4},{4,0},{8,12},{12,8},{1,5},{5,1},{9,13},{13,9},{2,6},{6,2},{1... | collective-permute-start | bytes 584 | tf_op jit(solution)/shard_map/ppermute | solution.py:28
  15.9 7.8 %collective-permute-start.4 = (bf16[528,256]{1,0:T(8,128)(2,1)S(1)}, bf16[528,256]{1,0:T(8,128)(2,1)S(1)}, u32[]{:S(2)}, u32[]{:S(2)}) collective-permute-start(bf16[528,256]{1,0:T(8,128)(2,1)S(1)} %fusion.4), channel_id=1, source_target_pairs={{0,2},{2,0},{1,3},{3,1},{4,6},{6,4},{5,7},{7,5},{8,10},{10,8},{9,1... | collective-permute-start | bytes 811016 | tf_op jit(solution)/shard_map/ppermute | solution.py:23
  16.1 4.6 %collective-permute-start.3 = (s32[2,48]{1,0:T(2,128)S(1)}, s32[2,48]{1,0:T(2,128)S(1)}, u32[]{:S(2)}, u32[]{:S(2)}) collective-permute-start(s32[2,48]{1,0:T(2,128)S(1)} %pad_add_fusion.1), channel_id=1, source_target_pairs={{0,8},{4,12},{8,0},{12,4},{1,9},{5,13},{9,1},{13,5},{2,10},{6,14},... | collective-permute-start | bytes 1160 | tf_op jit(solution)/shard_map/ppermute | solution.py:28
  23.8 21.4 %collective-permute-start.10 = (bf16[464,1024]{1,0:T(8,128)(2,1)S(1)}, bf16[464,1024]{1,0:T(8,128)(2,1)S(1)}, u32[]{:S(2)}, u32[]{:S(2)}) collective-permute-start(bf16[464,1024]{1,0:T(8,128)(2,1)S(1)} %slice.71), channel_id=1, source_target_pairs={{0,2},{2,0},{1,3},{3,1},{4,6},{6,4},{5,7},{7,5},{8,10},{10,8},{9,1... | collective-permute-start | bytes 2850824 | tf_op jit(solution)/shard_map/ppermute | solution.py:23
  24.2 23.7 %collective-permute-start.8 = (bf16[512,1024]{1,0:T(8,128)(2,1)S(1)}, bf16[512,1024]{1,0:T(8,128)(2,1)S(1)}, u32[]{:S(2)}, u32[]{:S(2)}) collective-permute-start(bf16[512,1024]{1,0:T(8,128)(2,1)S(1)} %copy-done.1), channel_id=1, source_target_pairs={{0,1},{1,0},{2,3},{3,2},{4,5},{5,4},{6,7},{7,6},{8,9},{9,8},{10,11... | collective-permute-start | bytes 3145736 | tf_op jit(solution)/shard_map/ppermute | solution.py:23
  25.1 4.6 %collective-permute-start.5 = (bf16[4,32,256]{2,1,0:T(8,128)(2,1)S(1)}, bf16[4,32,256]{2,1,0:T(8,128)(2,1)S(1)}, u32[]{:S(2)}, u32[]{:S(2)}) collective-permute-start(bf16[4,32,256]{2,1,0:T(8,128)(2,1)S(1)} %get-tuple-element.49), channel_id=1, source_target_pairs={{0,4},{4,0},{8,12},{12,8},{1,5},{5,1},{9,13},{13,9},{2,6},{6,2},{1... | collective-permute-start | bytes 196616 | tf_op jit(solution)/shard_map/ppermute | solution.py:28
  26.9 7.0 %collective-permute-start.6 = (bf16[4,32,256]{2,1,0:T(8,128)(2,1)S(1)}, bf16[4,32,256]{2,1,0:T(8,128)(2,1)S(1)}, u32[]{:S(2)}, u32[]{:S(2)}) collective-permute-start(bf16[4,32,256]{2,1,0:T(8,128)(2,1)S(1)} %get-tuple-element.50), channel_id=1, source_target_pairs={{0,8},{4,12},{8,0},{12,4},{1,9},{5,13},{9,1},{13,5},{2,10},{6,14},... | collective-permute-start | bytes 196616 | tf_op jit(solution)/shard_map/ppermute | solution.py:28
  29.5 6.1 %collective-permute-start.7 = (bf16[4,32,256]{2,1,0:T(8,128)(2,1)S(1)}, bf16[4,32,256]{2,1,0:T(8,128)(2,1)S(1)}, u32[]{:S(2)}, u32[]{:S(2)}) collective-permute-start(bf16[4,32,256]{2,1,0:T(8,128)(2,1)S(1)} %get-tuple-element.51), channel_id=1, source_target_pairs={{0,12},{4,8},{8,4},{12,0},{1,13},{5,9},{9,5},{13,1},{2,14},{6,10},... | collective-permute-start | bytes 196616 | tf_op jit(solution)/shard_map/ppermute | solution.py:28
  35.7 23.5 %slice-start = ((s8[8388608]{0:T(1024)(128)(4,1)}), s8[4194304]{0:T(1024)(128)(4,1)S(1)}, s32[]{:S(2)}) async-start(s8[8388608]{0:T(1024)(128)(4,1)} %bitcast.31), calls=%async_computation | async-start | bytes 8388608
  35.7 23.5 %slice-start.1 = ((s8[8388608]{0:T(1024)(128)(4,1)}), s8[4194304]{0:T(1024)(128)(4,1)S(1)}, s32[]{:S(2)}) async-start(s8[8388608]{0:T(1024)(128)(4,1)} %bitcast.31), calls=%async_computation.1 | async-start | bytes 8388608
  45.2 2.7 %collective-permute-start.11 = (bf16[464,1024]{1,0:T(8,128)(2,1)S(1)}, bf16[464,1024]{1,0:T(8,128)(2,1)S(1)}, u32[]{:S(2)}, u32[]{:S(2)}) collective-permute-start(bf16[464,1024]{1,0:T(8,128)(2,1)S(1)} %collective-permute-done.10.refs_2_), channel_id=1, source_target_pairs={{0,1},{1,0},{2,3},{3,2},{4,5},{5,4},{6,7},{7,6},{8,9},{9,8},{10,11... | collective-permute-start | bytes 2850824 | tf_op jit(solution)/shard_map/ppermute | solution.py:23
  45.2 2.7 %collective-permute-start.9 = (bf16[48,1024]{1,0:T(8,128)(2,1)S(1)}, bf16[48,1024]{1,0:T(8,128)(2,1)S(1)}, u32[]{:S(2)}, u32[]{:S(2)}) collective-permute-start(bf16[48,1024]{1,0:T(8,128)(2,1)S(1)} %collective-permute-done.1.refs_0_), channel_id=1, source_target_pairs={{0,1},{1,0},{2,3},{3,2},{4,5},{5,4},{6,7},{7,6},{8,9},{9,8},{10,11... | collective-permute-start | bytes 294920 | tf_op jit(solution)/shard_map/ppermute | solution.py:23
  45.7 11.8 %collective-permute-start.13 = (bf16[16,32,256]{2,1,0:T(8,128)(2,1)S(1)}, bf16[16,32,256]{2,1,0:T(8,128)(2,1)S(1)}, u32[]{:S(2)}, u32[]{:S(2)}) collective-permute-start(bf16[16,32,256]{2,1,0:T(8,128)(2,1)S(1)} %constant_dynamic-update-slice_fusion.refs_1_), channel_id=1, source_target_pairs={{0,2},{2,0},{1,3},{3,1},{4,6},{6,4},{5,7},{7,5},{8,10},{10,8},{9,1... | collective-permute-start | bytes 786440 | tf_op jit(solution)/shard_map/ppermute | solution.py:23
  46.4 11.4 %collective-permute-start.12 = (bf16[16,32,256]{2,1,0:T(8,128)(2,1)S(1)}, bf16[16,32,256]{2,1,0:T(8,128)(2,1)S(1)}, u32[]{:S(2)}, u32[]{:S(2)}) collective-permute-start(bf16[16,32,256]{2,1,0:T(8,128)(2,1)S(1)} %constant_dynamic-update-slice_fusion.refs_1_), channel_id=1, source_target_pairs={{0,1},{1,0},{2,3},{3,2},{4,5},{5,4},{6,7},{7,6},{8,9},{9,8},{10,11... | collective-permute-start | bytes 786440 | tf_op jit(solution)/shard_map/ppermute | solution.py:23
  47.9 3.4 %copy-start.3 = (bf16[4096,1024]{1,0:T(8,128)(2,1)S(1)}, bf16[4096,1024]{1,0:T(8,128)(2,1)}, u32[]{:S(2)}) copy-start(bf16[4096,1024]{1,0:T(8,128)(2,1)} %refs_4_.1) | copy-start | bytes 25165828
  57.5 1.6 %collective-permute-start.14 = (bf16[16,32,256]{2,1,0:T(8,128)(2,1)S(1)}, bf16[16,32,256]{2,1,0:T(8,128)(2,1)S(1)}, u32[]{:S(2)}, u32[]{:S(2)}) collective-permute-start(bf16[16,32,256]{2,1,0:T(8,128)(2,1)S(1)} %collective-permute-done.13.refs_3_), channel_id=1, source_target_pairs={{0,1},{1,0},{2,3},{3,2},{4,5},{5,4},{6,7},{7,6},{8,9},{9,8},{10,11... | collective-permute-start | bytes 786440 | tf_op jit(solution)/shard_map/ppermute | solution.py:23
  61.6 2.6 %collective-permute-start.15 = (bf16[2,128,1024]{2,1,0:T(8,128)(2,1)S(1)}, bf16[2,128,1024]{2,1,0:T(8,128)(2,1)S(1)}, u32[]{:S(2)}, u32[]{:S(2)}) collective-permute-start(bf16[2,128,1024]{2,1,0:T(8,128)(2,1)S(1)} %get-tuple-element.64), channel_id=1, source_target_pairs={{0,1},{1,0},{2,3},{3,2},{4,5},{5,4},{6,7},{7,6},{8,9},{9,8},{10,11... | collective-permute-start | bytes 1572872 | tf_op jit(solution)/shard_map/ppermute | solution.py:23
  64.3 3.5 %collective-permute-start.16 = (bf16[2,128,1024]{2,1,0:T(8,128)(2,1)S(1)}, bf16[2,128,1024]{2,1,0:T(8,128)(2,1)S(1)}, u32[]{:S(2)}, u32[]{:S(2)}) collective-permute-start(bf16[2,128,1024]{2,1,0:T(8,128)(2,1)S(1)} %get-tuple-element.66), channel_id=1, source_target_pairs={{0,1},{1,0},{2,3},{3,2},{4,5},{5,4},{6,7},{7,6},{8,9},{9,8},{10,11... | collective-permute-start | bytes 1572872 | tf_op jit(solution)/shard_map/ppermute | solution.py:23
  64.7 9.2 %collective-permute-start.17 = (bf16[128,1024]{1,0:T(8,128)(2,1)S(1)}, bf16[128,1024]{1,0:T(8,128)(2,1)S(1)}, u32[]{:S(2)}, u32[]{:S(2)}) collective-permute-start(bf16[128,1024]{1,0:T(8,128)(2,1)S(1)} %fusion.5), channel_id=1, source_target_pairs={{0,2},{2,0},{1,3},{3,1},{4,6},{6,4},{5,7},{7,5},{8,10},{10,8},{9,1... | collective-permute-start | bytes 786440 | tf_op jit(solution)/shard_map/ppermute | solution.py:23
  67.9 8.6 %collective-permute-start.18 = (bf16[2,128,1024]{2,1,0:T(8,128)(2,1)S(1)}, bf16[2,128,1024]{2,1,0:T(8,128)(2,1)S(1)}, u32[]{:S(2)}, u32[]{:S(2)}) collective-permute-start(bf16[2,128,1024]{2,1,0:T(8,128)(2,1)S(1)} %get-tuple-element.72), channel_id=1, source_target_pairs={{0,1},{1,0},{2,3},{3,2},{4,5},{5,4},{6,7},{7,6},{8,9},{9,8},{10,11... | collective-permute-start | bytes 1572872 | tf_op jit(solution)/shard_map/ppermute | solution.py:23
  67.9 10.7 %collective-permute-start.19 = (bf16[128,1024]{1,0:T(8,128)(2,1)S(1)}, bf16[128,1024]{1,0:T(8,128)(2,1)S(1)}, u32[]{:S(2)}, u32[]{:S(2)}) collective-permute-start(bf16[128,1024]{1,0:T(8,128)(2,1)S(1)} %fusion.6), channel_id=1, source_target_pairs={{0,2},{2,0},{1,3},{3,1},{4,6},{6,4},{5,7},{7,5},{8,10},{10,8},{9,1... | collective-permute-start | bytes 786440 | tf_op jit(solution)/shard_map/ppermute | solution.py:23
  78.8 2.0 %collective-permute-start.20 = (bf16[2,128,1024]{2,1,0:T(8,128)(2,1)S(1)}, bf16[2,128,1024]{2,1,0:T(8,128)(2,1)S(1)}, u32[]{:S(2)}, u32[]{:S(2)}) collective-permute-start(bf16[2,128,1024]{2,1,0:T(8,128)(2,1)S(1)} %get-tuple-element.79), channel_id=1, source_target_pairs={{0,1},{1,0},{2,3},{3,2},{4,5},{5,4},{6,7},{7,6},{8,9},{9,8},{10,11... | collective-permute-start | bytes 1572872 | tf_op jit(solution)/shard_map/ppermute | solution.py:23
  78.9 9.2 %collective-permute-start.21 = (bf16[128,1024]{1,0:T(8,128)(2,1)S(1)}, bf16[128,1024]{1,0:T(8,128)(2,1)S(1)}, u32[]{:S(2)}, u32[]{:S(2)}) collective-permute-start(bf16[128,1024]{1,0:T(8,128)(2,1)S(1)} %fusion.7), channel_id=1, source_target_pairs={{0,2},{2,0},{1,3},{3,1},{4,6},{6,4},{5,7},{7,5},{8,10},{10,8},{9,1... | collective-permute-start | bytes 786440 | tf_op jit(solution)/shard_map/ppermute | solution.py:23
  80.8 12.4 %collective-permute-start.22 = (bf16[128,1024]{1,0:T(8,128)(2,1)S(1)}, bf16[128,1024]{1,0:T(8,128)(2,1)S(1)}, u32[]{:S(2)}, u32[]{:S(2)}) collective-permute-start(bf16[128,1024]{1,0:T(8,128)(2,1)S(1)} %fusion.8), channel_id=1, source_target_pairs={{0,2},{2,0},{1,3},{3,1},{4,6},{6,4},{5,7},{7,5},{8,10},{10,8},{9,1... | collective-permute-start | bytes 786440 | tf_op jit(solution)/shard_map/ppermute | solution.py:23

commit v4 on v3

--- a/solution.py
+++ b/solution.py
@@ -10,7 +10,6 @@
 
 eps = 1e-05
 softcap = 10.0
-FIRST = 48
 f32 = jnp.float32
 bf16 = jnp.bfloat16
 
@@ -45,43 +44,36 @@
     return down == lax.broadcasted_iota(jnp.int32, (piece, 128), 1)
 
 
-def encode_kernel(meta, x_ref, w_ref, kept_ref, sent_ref, squares, *, pieces, piece, block):
+def encode_kernel(meta, x_ref, w_ref, kept_ref, sent_ref, product, squares, *, pieces, piece, count):
+    step = pl.program_id(0)
     mp, sub, size = meta[1], meta[2], pieces // 2
-    count, tokens, width = x_ref.shape
+    block, tokens, width = x_ref.shape
+    x = x_ref[...].reshape(block * tokens, width)
+    product[...] = jnp.dot(x, w_ref[...], preferred_element_type=f32).astype(bf16).reshape(product.shape)
+    xf = x.astype(f32)
+    square = jnp.sum(xf * xf, axis=1, keepdims=True)
     diagonal = diagonal_of(piece)
-
-    def store(a, rows, values):
-        far_mp = lax.rem(a // 2 - mp + size, size)
-
-        @pl.when(sub == a % 2)
-        def _():
-            kept_ref[far_mp, rows, :] = values
-
-        @pl.when(sub != a % 2)
-        def _():
-            sent_ref[far_mp, rows, :] = values
-
-    for i in range(count // block):
-        x = x_ref[i * block : (i + 1) * block].reshape(block * tokens, width)
-        product = jnp.dot(x, w_ref[...], preferred_element_type=f32).astype(bf16)
-        lanes = None
-        for j in range(0, width, 128):
-            part = x[:, j : j + 128].astype(f32)
-            lanes = part * part if lanes is None else lanes + part * part
-        square = jnp.sum(lanes, axis=1, keepdims=True)
-        for a in range(pieces):
-            own = []
-            for n in range(block):
-                low = n * tokens + a * piece
-                own.append(product[low : low + piece])
-                column = jnp.broadcast_to(square[low : low + piece], (piece, 128))
-                squares[a, i * block + n : i * block + n + 1, :] = jnp.sum(
-                    jnp.where(diagonal, column, 0.0), axis=0, keepdims=True
-                )
-            store(a, slice(i * block * piece, (i + 1) * block * piece), jnp.concatenate(own, axis=0))
     for a in range(pieces):
-        tail = jnp.concatenate([squares[a], jnp.zeros_like(squares[a])], axis=1)
-        store(a, slice(count * piece, count * piece + count), tail.astype(bf16))
+        for n in range(block):
+            low = n * tokens + a * piece
+            column = jnp.broadcast_to(square[low : low + piece], (piece, 128))
+            squares[a, pl.ds(step * block + n, 1), :] = jnp.sum(
+                jnp.where(diagonal, column, 0.0), axis=0, keepdims=True
+            )
+    rows = pl.ds(pl.multiple_of(step * block * piece, block * piece), block * piece)
+    for ds, out_ref in ((0, kept_ref), (1, sent_ref)):
+        for dm in range(size):
+            a = lax.rem(mp + dm, size) * 2 + lax.rem(sub + ds, 2)
+            taken = product[:, pl.ds(pl.multiple_of(a * piece, piece), piece), :]
+            out_ref[dm, rows, :] = taken.reshape(block * piece, taken.shape[2])
+
+    @pl.when(step == pl.num_programs(0) - 1)
+    def _():
+        for ds, out_ref in ((0, kept_ref), (1, sent_ref)):
+            for dm in range(size):
+                a = lax.rem(mp + dm, size) * 2 + lax.rem(sub + ds, 2)
+                tail = jnp.concatenate([squares[a], jnp.zeros_like(squares[a])], axis=1)
+                out_ref[dm, pl.ds(count * piece, count), :] = tail.astype(bf16)
 
 
 def encode(meta, states, weight, pieces):
@@ -89,11 +81,22 @@
     out_width = weight.shape[1]
     piece = tokens // pieces
     rows = count * piece + count
+    block = 4
     return pl.pallas_call(
-        functools.partial(encode_kernel, pieces=pieces, piece=piece, block=2),
-        in_specs=[SMEM, VMEM, VMEM],
-        out_specs=[VMEM] * 2,
-        scratch_shapes=[pltpu.VMEM((pieces, count, 128), f32)],
+        functools.partial(encode_kernel, pieces=pieces, piece=piece, count=count),
+        grid_spec=pltpu.PrefetchScalarGridSpec(
+            num_scalar_prefetch=1,
+            grid=(count // block,),
+            in_specs=[
+                pl.BlockSpec((block, tokens, width), lambda i, m: (i, 0, 0)),
+                pl.BlockSpec((width, out_width), lambda i, m: (0, 0)),
+            ],
+            out_specs=[pl.BlockSpec((pieces // 2, rows, out_width), lambda i, m: (0, 0, 0))] * 2,
+            scratch_shapes=[
+                pltpu.VMEM((block, tokens, out_width), bf16),
+                pltpu.VMEM((pieces, count, 128), f32),
+            ],
+        ),
         out_shape=[jax.ShapeDtypeStruct((pieces // 2, rows, out_width), bf16)] * 2,
         compiler_params=params(),
         cost_estimate=cost(2 * count * tokens * width * out_width, 2 * count * tokens * width),
@@ -323,16 +326,15 @@
             out += [far, shift(far, "sub", 1)]
         return out
 
-    fars_first = cross(hidden[:FIRST])
+    fars_first = cross(hidden[:chunk_tokens])
 
     table = jnp.concatenate(
         [neighbour_owner.reshape(1, -1), neighbour_slot.reshape(1, -1), neighbour_length.reshape(1, -1)],
         axis=1,
     )
-    table = jnp.concatenate([table, swap(table, "rows", 1)], axis=0)
 
     kept, sent = encode(meta, neighbour_states, encoder_weight, pieces)
-    received = after(shift(after(sent, *fars_first), "sub", 1), table)
+    received = shift(after(sent, *fars_first), "sub", 1)
     leaving = [add(kept[dm], received[dm]) for dm in range(1, group)]
     crossed = [shift(leaving[dm - 1], "mp", dm) for dm in range(1, group)]
     near = shift(after(hidden, *leaving), "sub", 1)
@@ -341,7 +343,8 @@
         table = jnp.concatenate([table, swap(table, "rows", table.shape[0])], axis=0)
     table, live = table[:, : 2 * requests], table[:, 2 * requests :]
 
-    fars_rest = cross(after(hidden, table, *crossed)[FIRST:])
+    last_low = token_count - chunk_tokens
+    fars_second = cross(after(hidden, table, *crossed)[chunk_tokens:last_low])
 
     routed = route(meta, table, kept, received, crossed, cap, features, count, requests)
     encoded = jnp.concatenate(
@@ -353,8 +356,9 @@
     fars = [shift(encoded, "mp", dm) for dm in range(1, group)]
     queries = project_queries(
         after(meta, encoded), hidden, near,
-        [with_near(fars_first, encoded), with_near(fars_rest, encoded)], query_weight, gain,
+        [with_near(fars_first, encoded), with_near(fars_second, encoded)], query_weight, gain,
     )
+    fars_last = cross(after(hidden, encoded)[last_low:])
     pairs += with_near(fars, queries)
 
     kept, sent, received, leaving, arrived, outs = [], [], [], [], [], []
@@ -368,9 +372,12 @@
         outs.append(add(after(kept[c], *earlier)[0], received[c][0], *arrived[c]))
 
     for c in range(chunks):
-        gate = (leaving[c - 2] if c > 1 else []) + ([outs[c - 3]] if c > 2 else [])
+        sources = [queries]
+        if c == chunks - 1:
+            sources = [hidden, near, *with_near(fars_last, *leaving[0]), query_weight]
+        gate = (fars_last if c == 2 else []) + (leaving[c - 2] if c > 1 else []) + ([outs[c - 3]] if c > 2 else [])
         one, other = run_chunk(
-            after(meta, *gate), table, live, [queries], pairs, output_weight, c * chunk_spans,
+            after(meta, *gate), table, live, sources, pairs, output_weight, c * chunk_spans,
             c * chunk_tokens, chunk_spans, span_tokens, feature_shard, cap, gain,
         )
         kept.append(one)

time: 94.6 us -> 87.9 us (0.929)
  waiting for transfers between devices: 44.3 us -> 34.6 us
  starting transfers between devices: 18.4 us -> 24.4 us
  Pallas kernels: 21.4 us -> 18.3 us
    ppermute x18 -> x20, waiting for transfers between devices: 34.7 us -> 24.6 us  [shift(): lax.ppermute(value, axis, [(i, (i + by) % size) for i in range(size)])]
    ppermute x18 -> x20, starting transfers between devices: 9.31 us -> 15.7 us  [shift(): lax.ppermute(value, axis, [(i, (i + by) % size) for i in range(size)])]
    pallas_call x1, Pallas kernels: 6.27 us -> 4.19 us  [project_queries(): pl.pallas_call(functools.partial(query_kernel, lows=tuple(lows), gain=gai...]
    pallas_call x1, Pallas kernels: 4.54 us -> 2.46 us  [encode(): pl.pallas_call(functools.partial(encode_kernel, pieces=pieces, piece=piec...]
    pallas_call x4, Pallas kernels: 9.63 us -> 10.7 us  [run_chunk(): pl.pallas_call(functools.partial(chunk_kernel, first=first, low=low, span...]
    unnamed x23 -> x27, local copies, waits for them, and re-layouts: 6.82 us -> 6.83 us
  transfers between devices with their start and end apart: 23 -> 25, of which waited for: 14 -> 15; matrix products, arithmetic and copies ran while one was open for 1% -> 1% of each run, Pallas kernels for 20% -> 18%
where the time goes in v4:
time: 87.9 us; the launch traced here: 87.6 us
  waiting for transfers between devices  34.6 us (39%)
  starting transfers between devices  24.4 us (28%)
  Pallas kernels  18.3 us (21%)
  local copies, waits for them, and re-layouts  8.09 us (9%)
  other arithmetic  2.03 us (2%)
    ppermute x20, waiting for transfers between devices, shift(): lax.ppermute(value, axis, [(i, (i + by) % size) for i in range(size)])  24.6 us
    ppermute x20, starting transfers between devices, shift(): lax.ppermute(value, axis, [(i, (i + by) % size) for i in range(size)])  15.7 us
    pallas_call x4, Pallas kernels, run_chunk(): pl.pallas_call(functools.partial(chunk_kernel, first=first, low=low, span...  10.7 us
    ppermute x5, waiting for transfers between devices, swap(): return lax.ppermute(value, axis, [(i, i ^ by) for i in range(size)])  9.95 us
    ppermute x5, starting transfers between devices, swap(): return lax.ppermute(value, axis, [(i, i ^ by) for i in range(size)])  8.68 us
    unnamed x27, local copies, waits for them, and re-layouts  6.83 us
    pallas_call x1, Pallas kernels, project_queries(): pl.pallas_call(functools.partial(query_kernel, lows=tuple(lows), gain=gai...  4.19 us
    pallas_call x1, Pallas kernels, encode(): pl.pallas_call(functools.partial(encode_kernel, pieces=pieces, piece=piec...  2.46 us
  transfers between devices with their start and end apart: 25, of which 15 were waited for; matrix products, arithmetic and copies ran while one was open for 1% of the time, Pallas kernels for 18%

profile of v4, /device:TPU:0, one launch (start us, length us, event | category | flops | bytes accessed | tf_op | source)
XLA Modules:
  0.0 87.6 jit_solution(3237673615354711387)
XLA Ops:
  0.0 1.0 %slice.70 = bf16[128,1024]{1,0:T(8,128)(2,1)S(1)} slice(bf16[512,1024]{1,0:T(8,128)(2,1)} %refs_0_.1), slice={[0:128], [0:1024]} | slice | bytes 524288 | tf_op jit(solution)/shard_map/slice | solution.py:329
  1.0 3.0 %collective-permute-start = (bf16[128,1024]{1,0:T(8,128)(2,1)S(1)}, bf16[128,1024]{1,0:T(8,128)(2,1)S(1)}, u32[]{:S(2)}, u32[]{:S(2)}) collective-permute-start(bf16[128,1024]{1,0:T(8,128)(2,1)S(1)} %slice.70), channel_id=1, source_target_pairs={{0,2},{2,0},{1,3},{3,1},{4,6},{6,4},{5,7},{7,5},{8,10},{10,8},{9,1... | collective-permute-start | bytes 786440 | tf_op jit(solution)/shard_map/ppermute | solution.py:22
  4.1 2.2 %copy-done.2 = bf16[16,128,1024]{2,1,0:T(8,128)(2,1)S(1)} copy-done((bf16[16,128,1024]{2,1,0:T(8,128)(2,1)S(1)}, bf16[16,128,1024]{2,1,0:T(8,128)(2,1)}, u32[]{:S(2)}) %copy-start.2) | copy-done | bytes 4194328
  6.2 1.0 %copy-done.3 = bf16[1024,256]{1,0:T(8,128)(2,1)S(1)} copy-done((bf16[1024,256]{1,0:T(8,128)(2,1)S(1)}, bf16[1024,256]{1,0:T(8,128)(2,1)}, u32[]{:S(2)}) %copy-start.3) | copy-done | bytes 524312
  7.3 2.5 %encode.1 = (bf16[2,528,256]{2,1,0:T(8,128)(2,1)S(1)}, bf16[2,528,256]{2,1,0:T(8,128)(2,1)S(1)}) custom-call(s32[3]{0:T(128)S(1)} %pad_add_fusion.2.meta, bf16[16,128,1024]{2,1,0:T(8,128)(2,1)S(1)} %copy-done.2, bf16[1024,256]{1,0:T(8,128)(2,1)S(1)} %copy-done.3), custom_call_target="tpu_custom_call" | custom-call | flops 1073741824 | bytes 4194304 | tf_op jit(solution)/shard_map/encode/pallas_call | solution.py:85
  9.8 0.5 collective-permute-done.refs_0_
  10.6 1.6 %collective-permute-done.1.received = bf16[2,528,256]{2,1,0:T(8,128)(2,1)S(1)} collective-permute-done((bf16[2,528,256]{2,1,0:T(8,128)(2,1)S(1)}, bf16[2,528,256]{2,1,0:T(8,128)(2,1)S(1)}, u32[]{:S(2)}, u32[]{:S(2)}) %collective-permute-start.1) | collective-permute-done | bytes 540704 | tf_op jit(solution)/shard_map/ppermute | solution.py:22
  12.3 1.8 %collective-permute-start.4 = (bf16[528,256]{1,0:T(8,128)(2,1)S(1)}, bf16[528,256]{1,0:T(8,128)(2,1)S(1)}, u32[]{:S(2)}, u32[]{:S(2)}) collective-permute-start(bf16[528,256]{1,0:T(8,128)(2,1)S(1)} %fusion.4), channel_id=1, source_target_pairs={{0,2},{2,0},{1,3},{3,1},{4,6},{6,4},{5,7},{7,5},{8,10},{10,8},{9,1... | collective-permute-start | bytes 811016 | tf_op jit(solution)/shard_map/ppermute | solution.py:22
  14.2 1.6 %collective-permute-start.2 = (s32[1,48]{1,0:T(1,128)S(1)}, s32[1,48]{1,0:T(1,128)S(1)}, u32[]{:S(2)}, u32[]{:S(2)}) collective-permute-start(s32[1,48]{1,0:T(1,128)S(1)} %pad_add_fusion.3), channel_id=1, source_target_pairs={{0,4},{4,0},{8,12},{12,8},{1,5},{5,1},{9,13},{13,9},{2,6},{6,2},{1... | collective-permute-start | bytes 584 | tf_op jit(solution)/shard_map/ppermute | solution.py:27
  15.7 2.0 %collective-permute-done.2 = s32[1,48]{1,0:T(1,128)S(1)} collective-permute-done((s32[1,48]{1,0:T(1,128)S(1)}, s32[1,48]{1,0:T(1,128)S(1)}, u32[]{:S(2)}, u32[]{:S(2)}) %collective-permute-start.2) | collective-permute-done | bytes 224 | tf_op jit(solution)/shard_map/ppermute | solution.py:27
  17.7 2.6 %collective-permute-start.3 = (s32[2,48]{1,0:T(2,128)S(1)}, s32[2,48]{1,0:T(2,128)S(1)}, u32[]{:S(2)}, u32[]{:S(2)}) collective-permute-start(s32[2,48]{1,0:T(2,128)S(1)} %pad_add_fusion.1), channel_id=1, source_target_pairs={{0,8},{4,12},{8,0},{12,4},{1,9},{5,13},{9,1},{13,5},{2,10},{6,14},... | collective-permute-start | bytes 1160 | tf_op jit(solution)/shard_map/ppermute | solution.py:27
  20.4 1.9 %collective-permute-done.3 = s32[2,48]{1,0:T(2,128)S(1)} collective-permute-done((s32[2,48]{1,0:T(2,128)S(1)}, s32[2,48]{1,0:T(2,128)S(1)}, u32[]{:S(2)}, u32[]{:S(2)}) %collective-permute-start.3) | collective-permute-done | bytes 416 | tf_op jit(solution)/shard_map/ppermute | solution.py:27
  22.3 0.4 collective-permute-start.10
  22.7 0.9 %route.1 = (bf16[4,32,256]{2,1,0:T(8,128)(2,1)S(1)}, bf16[4,32,256]{2,1,0:T(8,128)(2,1)S(1)}, bf16[4,32,256]{2,1,0:T(8,128)(2,1)S(1)}, bf16[4,32,256]{2,1,0:T(8,128)(2,1)S(1)}) custom-call(s32[3]{0:T(128)S(1)} %pad_add_fusion.2.meta, s32[4,32]{1,0:T(4,128)S(1)} %bitcast.35, bf16[2,528,256]{2,1,0:T(8,128)(2,1)S(1)} %get-tuple-element.44.kept, ...), custom_call_target="tpu_custom_call" | custom-call | flops 1081344 | bytes 811008 | tf_op jit(solution)/shard_map/route/pallas_call | solution.py:140
  23.7 1.9 %collective-permute-start.5 = (bf16[4,32,256]{2,1,0:T(8,128)(2,1)S(1)}, bf16[4,32,256]{2,1,0:T(8,128)(2,1)S(1)}, u32[]{:S(2)}, u32[]{:S(2)}) collective-permute-start(bf16[4,32,256]{2,1,0:T(8,128)(2,1)S(1)} %get-tuple-element.49), channel_id=1, source_target_pairs={{0,4},{4,0},{8,12},{12,8},{1,5},{5,1},{9,13},{13,9},{2,6},{6,2},{1... | collective-permute-start | bytes 196616 | tf_op jit(solution)/shard_map/ppermute | solution.py:27
  25.5 2.6 %collective-permute-start.6 = (bf16[4,32,256]{2,1,0:T(8,128)(2,1)S(1)}, bf16[4,32,256]{2,1,0:T(8,128)(2,1)S(1)}, u32[]{:S(2)}, u32[]{:S(2)}) collective-permute-start(bf16[4,32,256]{2,1,0:T(8,128)(2,1)S(1)} %get-tuple-element.50), channel_id=1, source_target_pairs={{0,8},{4,12},{8,0},{12,4},{1,9},{5,13},{9,1},{13,5},{2,10},{6,14},... | collective-permute-start | bytes 196616 | tf_op jit(solution)/shard_map/ppermute | solution.py:27
  28.1 0.2 collective-permute-done.5
  28.3 4.2 %collective-permute-done.6 = bf16[4,32,256]{2,1,0:T(8,128)(2,1)S(1)} collective-permute-done((bf16[4,32,256]{2,1,0:T(8,128)(2,1)S(1)}, bf16[4,32,256]{2,1,0:T(8,128)(2,1)S(1)}, u32[]{:S(2)}, u32[]{:S(2)}) %collective-permute-start.6) | collective-permute-done | bytes 65568 | tf_op jit(solution)/shard_map/ppermute | solution.py:27
  32.5 1.8 %collective-permute-done.7 = bf16[4,32,256]{2,1,0:T(8,128)(2,1)S(1)} collective-permute-done((bf16[4,32,256]{2,1,0:T(8,128)(2,1)S(1)}, bf16[4,32,256]{2,1,0:T(8,128)(2,1)S(1)}, u32[]{:S(2)}, u32[]{:S(2)}) %collective-permute-start.7) | collective-permute-done | bytes 65568 | tf_op jit(solution)/shard_map/ppermute | solution.py:27
  34.4 0.5 collective-permute-start.9
  34.9 1.5 %collective-permute-start.13 = (bf16[16,32,256]{2,1,0:T(8,128)(2,1)S(1)}, bf16[16,32,256]{2,1,0:T(8,128)(2,1)S(1)}, u32[]{:S(2)}, u32[]{:S(2)}) collective-permute-start(bf16[16,32,256]{2,1,0:T(8,128)(2,1)S(1)} %constant_dynamic-update-slice_fusion.refs_1_.refs_5_), channel_id=1, source_target_pairs={{0,2},{2,0},{1,3},{3,1},{4,6},{6,4},{5,7},{7,5},{8,10},{10,8},{9,1... | collective-permute-start | bytes 786440 | tf_op jit(solution)/shard_map/ppermute | solution.py:22
  36.4 0.2 collective-permute-done.9.refs_1_
  36.6 3.4 %copy-done = bf16[4096,1024]{1,0:T(8,128)(2,1)S(1)} copy-done((bf16[4096,1024]{1,0:T(8,128)(2,1)S(1)}, bf16[4096,1024]{1,0:T(8,128)(2,1)}, u32[]{:S(2)}) %copy-start) | copy-done | bytes 8388632
  40.0 4.2 %queries.1.refs_0_ = bf16[384,1024]{1,0:T(8,128)(2,1)S(1)} custom-call(s32[3]{0:T(128)S(1)} %pad_add_fusion.2.meta, bf16[512,1024]{1,0:T(8,128)(2,1)S(1)} %copy-done.1, bf16[512,1024]{1,0:T(8,128)(2,1)S(1)} %collective-permute-done.8.near_ref.refs_1_, bf16[128,1024]{1,0:T(8,128)(2,1)S(1)} %collective-permute-done.refs_0_, ...), custom_call_target="tpu_custom_call" | custom-call | flops 3221225472 | bytes 3145728 | tf_op jit(solution)/shard_map/queries/pallas_call | solution.py:195
  44.2 0.2 collective-permute-start.14
  44.5 1.3 %collective-permute-done.14.refs_4_.refs_8_ = bf16[16,32,256]{2,1,0:T(8,128)(2,1)S(1)} collective-permute-done((bf16[16,32,256]{2,1,0:T(8,128)(2,1)S(1)}, bf16[16,32,256]{2,1,0:T(8,128)(2,1)S(1)}, u32[]{:S(2)}, u32[]{:S(2)}) %collective-permute-start.14) | collective-permute-done | bytes 262176 | tf_op jit(solution)/shard_map/ppermute | solution.py:22
  45.8 2.4 %chunk.4 = (bf16[2,128,1024]{2,1,0:T(8,128)(2,1)S(1)}, bf16[2,128,1024]{2,1,0:T(8,128)(2,1)S(1)}) custom-call(s32[3]{0:T(128)S(1)} %pad_add_fusion.2.meta, s32[4,32]{1,0:T(4,128)S(1)} %bitcast.36, s32[4,16]{1,0:T(4,128)S(1)} %slice.73.live, bf16[384,1024]{1,0:T(8,128)(2,1)S(1)} %queries.1.refs_0_, ...), custom_call_target="tpu_custom_call" | custom-call | flops 1207959552 | bytes 262144 | tf_op jit(solution)/shard_map/chunk/pallas_call | solution.py:267
  48.2 0.2 collective-permute-start.15
  48.4 2.4 %chunk.5 = (bf16[2,128,1024]{2,1,0:T(8,128)(2,1)S(1)}, bf16[2,128,1024]{2,1,0:T(8,128)(2,1)S(1)}) custom-call(s32[3]{0:T(128)S(1)} %pad_add_fusion.2.meta, s32[4,32]{1,0:T(4,128)S(1)} %bitcast.37, s32[4,16]{1,0:T(4,128)S(1)} %slice.73.live, bf16[384,1024]{1,0:T(8,128)(2,1)S(1)} %queries.1.refs_0_, ...), custom_call_target="tpu_custom_call" | custom-call | flops 1207959552 | bytes 262144 | tf_op jit(solution)/shard_map/chunk/pallas_call | solution.py:267
  50.9 0.4 collective-permute-start.16
  51.3 1.6 %collective-permute-start.17 = (bf16[128,1024]{1,0:T(8,128)(2,1)S(1)}, bf16[128,1024]{1,0:T(8,128)(2,1)S(1)}, u32[]{:S(2)}, u32[]{:S(2)}) collective-permute-start(bf16[128,1024]{1,0:T(8,128)(2,1)S(1)} %slice.78), channel_id=1, source_target_pairs={{0,2},{2,0},{1,3},{3,1},{4,6},{6,4},{5,7},{7,5},{8,10},{10,8},{9,1... | collective-permute-start | bytes 786440 | tf_op jit(solution)/shard_map/ppermute | solution.py:22
  53.0 0.5 collective-permute-start.18
  53.4 7.1 %collective-permute-done.17.refs_2_ = bf16[128,1024]{1,0:T(8,128)(2,1)S(1)} collective-permute-done((bf16[128,1024]{1,0:T(8,128)(2,1)S(1)}, bf16[128,1024]{1,0:T(8,128)(2,1)S(1)}, u32[]{:S(2)}, u32[]{:S(2)}) %collective-permute-start.17) | collective-permute-done | bytes 262176 | tf_op jit(solution)/shard_map/ppermute | solution.py:22
  60.6 2.4 %chunk.6 = (bf16[2,128,1024]{2,1,0:T(8,128)(2,1)S(1)}, bf16[2,128,1024]{2,1,0:T(8,128)(2,1)S(1)}) custom-call(s32[3]{0:T(128)S(1)} %pad_add_fusion.2.meta, s32[4,32]{1,0:T(4,128)S(1)} %bitcast.38, s32[4,16]{1,0:T(4,128)S(1)} %slice.73.live, bf16[384,1024]{1,0:T(8,128)(2,1)S(1)} %queries.1.refs_0_, ...), custom_call_target="tpu_custom_call" | custom-call | flops 1207959552 | bytes 262144 | tf_op jit(solution)/shard_map/chunk/pallas_call | solution.py:267
  63.1 0.5 collective-permute-start.20
  63.6 1.5 %collective-permute-start.21 = (bf16[128,1024]{1,0:T(8,128)(2,1)S(1)}, bf16[128,1024]{1,0:T(8,128)(2,1)S(1)}, u32[]{:S(2)}, u32[]{:S(2)}) collective-permute-start(bf16[128,1024]{1,0:T(8,128)(2,1)S(1)} %fusion.6), channel_id=1, source_target_pairs={{0,2},{2,0},{1,3},{3,1},{4,6},{6,4},{5,7},{7,5},{8,10},{10,8},{9,1... | collective-permute-start | bytes 786440 | tf_op jit(solution)/shard_map/ppermute | solution.py:22
  65.2 0.2 collective-permute-done.18
  65.4 0.1 fusion.3
  65.5 3.6 %chunk.7 = (bf16[2,128,1024]{2,1,0:T(8,128)(2,1)S(1)}, bf16[2,128,1024]{2,1,0:T(8,128)(2,1)S(1)}) custom-call(s32[3]{0:T(128)S(1)} %pad_add_fusion.2.meta, s32[4,32]{1,0:T(4,128)S(1)} %bitcast.39, s32[4,16]{1,0:T(4,128)S(1)} %slice.73.live, bf16[512,1024]{1,0:T(8,128)(2,1)S(1)} %copy-done.1, bf16[512,1024]{1,0:T(8,128)(2,1)S(1)} %collective-permute-done.8.near_ref.refs_1_, ...), custom_call_target="tpu_custom_call" | custom-call | flops 1207959552 | bytes 262144 | tf_op jit(solution)/shard_map/chunk/pallas_call | solution.py:267
  69.2 2.7 %collective-permute-done.21 = bf16[128,1024]{1,0:T(8,128)(2,1)S(1)} collective-permute-done((bf16[128,1024]{1,0:T(8,128)(2,1)S(1)}, bf16[128,1024]{1,0:T(8,128)(2,1)S(1)}, u32[]{:S(2)}, u32[]{:S(2)}) %collective-permute-start.21) | collective-permute-done | bytes 262176 | tf_op jit(solution)/shard_map/ppermute | solution.py:22
  72.1 1.6 %collective-permute-start.23 = (bf16[128,1024]{1,0:T(8,128)(2,1)S(1)}, bf16[128,1024]{1,0:T(8,128)(2,1)S(1)}, u32[]{:S(2)}, u32[]{:S(2)}) collective-permute-start(bf16[128,1024]{1,0:T(8,128)(2,1)S(1)} %fusion.7), channel_id=1, source_target_pairs={{0,2},{2,0},{1,3},{3,1},{4,6},{6,4},{5,7},{7,5},{8,10},{10,8},{9,1... | collective-permute-start | bytes 786440 | tf_op jit(solution)/shard_map/ppermute | solution.py:22
  73.7 0.3 collective-permute-done.22
  74.1 1.6 %collective-permute-start.24 = (bf16[128,1024]{1,0:T(8,128)(2,1)S(1)}, bf16[128,1024]{1,0:T(8,128)(2,1)S(1)}, u32[]{:S(2)}, u32[]{:S(2)}) collective-permute-start(bf16[128,1024]{1,0:T(8,128)(2,1)S(1)} %fusion.8), channel_id=1, source_target_pairs={{0,2},{2,0},{1,3},{3,1},{4,6},{6,4},{5,7},{7,5},{8,10},{10,8},{9,1... | collective-permute-start | bytes 786440 | tf_op jit(solution)/shard_map/ppermute | solution.py:22
  75.7 5.6 %collective-permute-done.23 = bf16[128,1024]{1,0:T(8,128)(2,1)S(1)} collective-permute-done((bf16[128,1024]{1,0:T(8,128)(2,1)S(1)}, bf16[128,1024]{1,0:T(8,128)(2,1)S(1)}, u32[]{:S(2)}, u32[]{:S(2)}) %collective-permute-start.23) | collective-permute-done | bytes 262176 | tf_op jit(solution)/shard_map/ppermute | solution.py:22
  81.3 0.1 fusion.1
  81.4 5.0 %collective-permute-done.24 = bf16[128,1024]{1,0:T(8,128)(2,1)S(1)} collective-permute-done((bf16[128,1024]{1,0:T(8,128)(2,1)S(1)}, bf16[128,1024]{1,0:T(8,128)(2,1)S(1)}, u32[]{:S(2)}, u32[]{:S(2)}) %collective-permute-start.24) | collective-permute-done | bytes 262176 | tf_op jit(solution)/shard_map/ppermute | solution.py:22
  86.4 0.1 fusion
  86.6 1.0 %pad_maximum_fusion = bf16[512,1024]{1,0:T(8,128)(2,1)} fusion(bf16[128,1024]{1,0:T(8,128)(2,1)S(1)} %fusion, bf16[128,1024]{1,0:T(8,128)(2,1)S(1)} %fusion.1, bf16[128,1024]{1,0:T(8,128)(2,1)S(1)} %fusion.2, bf16[128,1024]{1,0:T(8,128)(2,1)S(1)} %fusion.3), kind=kLoop, calls=%fused_computation | loop fusion | flops 4194304 | bytes 2097152 | tf_op jit(solution)/shard_map/concatenate | solution.py:395
  (59 shorter events, 1.5 us)
Async XLA Ops:
  1.0 9.3 %collective-permute-start = (bf16[128,1024]{1,0:T(8,128)(2,1)S(1)}, bf16[128,1024]{1,0:T(8,128)(2,1)S(1)}, u32[]{:S(2)}, u32[]{:S(2)}) collective-permute-start(bf16[128,1024]{1,0:T(8,128)(2,1)S(1)} %slice.70), channel_id=1, source_target_pairs={{0,2},{2,0},{1,3},{3,1},{4,6},{6,4},{5,7},{7,5},{8,10},{10,8},{9,1... | collective-permute-start | bytes 786440 | tf_op jit(solution)/shard_map/ppermute | solution.py:22
  4.1 2.2 %copy-start.2 = (bf16[16,128,1024]{2,1,0:T(8,128)(2,1)S(1)}, bf16[16,128,1024]{2,1,0:T(8,128)(2,1)}, u32[]{:S(2)}) copy-start(bf16[16,128,1024]{2,1,0:T(8,128)(2,1)} %x_ref.1) | copy-start | bytes 12582916
  6.2 1.0 %copy-start.3 = (bf16[1024,256]{1,0:T(8,128)(2,1)S(1)}, bf16[1024,256]{1,0:T(8,128)(2,1)}, u32[]{:S(2)}) copy-start(bf16[1024,256]{1,0:T(8,128)(2,1)} %w_ref.1) | copy-start | bytes 1572868
  7.3 3.0 %copy-start.4 = (s32[8,2]{0,1:T(2,128)S(1)}, s32[8,2]{0,1:T(2,128)}, u32[]{:S(2)}) copy-start(s32[8,2]{0,1:T(2,128)} %param.14) | copy-start | bytes 196
  7.3 3.2 %copy-start.5 = (s32[8,2]{0,1:T(2,128)S(1)}, s32[8,2]{0,1:T(2,128)}, u32[]{:S(2)}) copy-start(s32[8,2]{0,1:T(2,128)} %param.13) | copy-start | bytes 196
  7.3 6.8 %copy-start.6 = (s32[16]{0:T(128)S(1)}, s32[16]{0:T(128)}, u32[]{:S(2)}) copy-start(s32[16]{0:T(128)} %param.15) | copy-start | bytes 196
  7.3 15.0 %copy-start.1 = (bf16[512,1024]{1,0:T(8,128)(2,1)S(1)}, bf16[512,1024]{1,0:T(8,128)(2,1)}, u32[]{:S(2)}) copy-start(bf16[512,1024]{1,0:T(8,128)(2,1)} %refs_0_.1) | copy-start | bytes 3145732
  10.3 1.9 %collective-permute-start.1 = (bf16[2,528,256]{2,1,0:T(8,128)(2,1)S(1)}, bf16[2,528,256]{2,1,0:T(8,128)(2,1)S(1)}, u32[]{:S(2)}, u32[]{:S(2)}) collective-permute-start(bf16[2,528,256]{2,1,0:T(8,128)(2,1)S(1)} %get-tuple-element.46), channel_id=1, source_target_pairs={{0,1},{1,0},{2,3},{3,2},{4,5},{5,4},{6,7},{7,6},{8,9},{9,8},{10,11... | collective-permute-start | bytes 1622024 | tf_op jit(solution)/shard_map/ppermute | solution.py:22
  12.3 10.0 %collective-permute-start.4 = (bf16[528,256]{1,0:T(8,128)(2,1)S(1)}, bf16[528,256]{1,0:T(8,128)(2,1)S(1)}, u32[]{:S(2)}, u32[]{:S(2)}) collective-permute-start(bf16[528,256]{1,0:T(8,128)(2,1)S(1)} %fusion.4), channel_id=1, source_target_pairs={{0,2},{2,0},{1,3},{3,1},{4,6},{6,4},{5,7},{7,5},{8,10},{10,8},{9,1... | collective-permute-start | bytes 811016 | tf_op jit(solution)/shard_map/ppermute | solution.py:22
  14.2 3.5 %collective-permute-start.2 = (s32[1,48]{1,0:T(1,128)S(1)}, s32[1,48]{1,0:T(1,128)S(1)}, u32[]{:S(2)}, u32[]{:S(2)}) collective-permute-start(s32[1,48]{1,0:T(1,128)S(1)} %pad_add_fusion.3), channel_id=1, source_target_pairs={{0,4},{4,0},{8,12},{12,8},{1,5},{5,1},{9,13},{13,9},{2,6},{6,2},{1... | collective-permute-start | bytes 584 | tf_op jit(solution)/shard_map/ppermute | solution.py:27
  17.7 4.5 %collective-permute-start.3 = (s32[2,48]{1,0:T(2,128)S(1)}, s32[2,48]{1,0:T(2,128)S(1)}, u32[]{:S(2)}, u32[]{:S(2)}) collective-permute-start(s32[2,48]{1,0:T(2,128)S(1)} %pad_add_fusion.1), channel_id=1, source_target_pairs={{0,8},{4,12},{8,0},{12,4},{1,9},{5,13},{9,1},{13,5},{2,10},{6,14},... | collective-permute-start | bytes 1160 | tf_op jit(solution)/shard_map/ppermute | solution.py:27
  22.3 23.5 %slice-start = ((s8[8388608]{0:T(1024)(128)(4,1)}), s8[4194304]{0:T(1024)(128)(4,1)S(1)}, s32[]{:S(2)}) async-start(s8[8388608]{0:T(1024)(128)(4,1)} %bitcast.31), calls=%async_computation | async-start | bytes 8388608
  22.3 11.9 %collective-permute-start.10 = (bf16[256,1024]{1,0:T(8,128)(2,1)S(1)}, bf16[256,1024]{1,0:T(8,128)(2,1)S(1)}, u32[]{:S(2)}, u32[]{:S(2)}) collective-permute-start(bf16[256,1024]{1,0:T(8,128)(2,1)S(1)} %slice.74), channel_id=1, source_target_pairs={{0,2},{2,0},{1,3},{3,1},{4,6},{6,4},{5,7},{7,5},{8,10},{10,8},{9,1... | collective-permute-start | bytes 1572872 | tf_op jit(solution)/shard_map/ppermute | solution.py:22
  22.7 13.9 %collective-permute-start.8 = (bf16[512,1024]{1,0:T(8,128)(2,1)S(1)}, bf16[512,1024]{1,0:T(8,128)(2,1)S(1)}, u32[]{:S(2)}, u32[]{:S(2)}) collective-permute-start(bf16[512,1024]{1,0:T(8,128)(2,1)S(1)} %copy-done.1), channel_id=1, source_target_pairs={{0,1},{1,0},{2,3},{3,2},{4,5},{5,4},{6,7},{7,6},{8,9},{9,8},{10,11... | collective-permute-start | bytes 3145736 | tf_op jit(solution)/shard_map/ppermute | solution.py:22
  23.7 4.6 %collective-permute-start.5 = (bf16[4,32,256]{2,1,0:T(8,128)(2,1)S(1)}, bf16[4,32,256]{2,1,0:T(8,128)(2,1)S(1)}, u32[]{:S(2)}, u32[]{:S(2)}) collective-permute-start(bf16[4,32,256]{2,1,0:T(8,128)(2,1)S(1)} %get-tuple-element.49), channel_id=1, source_target_pairs={{0,4},{4,0},{8,12},{12,8},{1,5},{5,1},{9,13},{13,9},{2,6},{6,2},{1... | collective-permute-start | bytes 196616 | tf_op jit(solution)/shard_map/ppermute | solution.py:27
  25.5 7.0 %collective-permute-start.6 = (bf16[4,32,256]{2,1,0:T(8,128)(2,1)S(1)}, bf16[4,32,256]{2,1,0:T(8,128)(2,1)S(1)}, u32[]{:S(2)}, u32[]{:S(2)}) collective-permute-start(bf16[4,32,256]{2,1,0:T(8,128)(2,1)S(1)} %get-tuple-element.50), channel_id=1, source_target_pairs={{0,8},{4,12},{8,0},{12,4},{1,9},{5,13},{9,1},{13,5},{2,10},{6,14},... | collective-permute-start | bytes 196616 | tf_op jit(solution)/shard_map/ppermute | solution.py:27
  28.1 6.1 %collective-permute-start.7 = (bf16[4,32,256]{2,1,0:T(8,128)(2,1)S(1)}, bf16[4,32,256]{2,1,0:T(8,128)(2,1)S(1)}, u32[]{:S(2)}, u32[]{:S(2)}) collective-permute-start(bf16[4,32,256]{2,1,0:T(8,128)(2,1)S(1)} %get-tuple-element.51), channel_id=1, source_target_pairs={{0,12},{4,8},{8,4},{12,0},{1,13},{5,9},{9,5},{13,1},{2,14},{6,10},... | collective-permute-start | bytes 196616 | tf_op jit(solution)/shard_map/ppermute | solution.py:27
  34.3 11.6 %slice-start.1 = ((s8[8388608]{0:T(1024)(128)(4,1)}), s8[4194304]{0:T(1024)(128)(4,1)S(1)}, s32[]{:S(2)}) async-start(s8[8388608]{0:T(1024)(128)(4,1)} %bitcast.31), calls=%async_computation.1 | async-start | bytes 8388608
  34.3 2.4 %collective-permute-start.11 = (bf16[256,1024]{1,0:T(8,128)(2,1)S(1)}, bf16[256,1024]{1,0:T(8,128)(2,1)S(1)}, u32[]{:S(2)}, u32[]{:S(2)}) collective-permute-start(bf16[256,1024]{1,0:T(8,128)(2,1)S(1)} %collective-permute-done.10.refs_2_), channel_id=1, source_target_pairs={{0,1},{1,0},{2,3},{3,2},{4,5},{5,4},{6,7},{7,6},{8,9},{9,8},{10,11... | collective-permute-start | bytes 1572872 | tf_op jit(solution)/shard_map/ppermute | solution.py:22
  34.4 2.3 %collective-permute-start.9 = (bf16[128,1024]{1,0:T(8,128)(2,1)S(1)}, bf16[128,1024]{1,0:T(8,128)(2,1)S(1)}, u32[]{:S(2)}, u32[]{:S(2)}) collective-permute-start(bf16[128,1024]{1,0:T(8,128)(2,1)S(1)} %collective-permute-done.refs_0_), channel_id=1, source_target_pairs={{0,1},{1,0},{2,3},{3,2},{4,5},{5,4},{6,7},{7,6},{8,9},{9,8},{10,11... | collective-permute-start | bytes 786440 | tf_op jit(solution)/shard_map/ppermute | solution.py:22
  34.9 9.7 %collective-permute-start.12 = (bf16[16,32,256]{2,1,0:T(8,128)(2,1)S(1)}, bf16[16,32,256]{2,1,0:T(8,128)(2,1)S(1)}, u32[]{:S(2)}, u32[]{:S(2)}) collective-permute-start(bf16[16,32,256]{2,1,0:T(8,128)(2,1)S(1)} %constant_dynamic-update-slice_fusion.refs_1_.refs_5_), channel_id=1, source_target_pairs={{0,1},{1,0},{2,3},{3,2},{4,5},{5,4},{6,7},{7,6},{8,9},{9,8},{10,11... | collective-permute-start | bytes 786440 | tf_op jit(solution)/shard_map/ppermute | solution.py:22
  34.9 9.3 %collective-permute-start.13 = (bf16[16,32,256]{2,1,0:T(8,128)(2,1)S(1)}, bf16[16,32,256]{2,1,0:T(8,128)(2,1)S(1)}, u32[]{:S(2)}, u32[]{:S(2)}) collective-permute-start(bf16[16,32,256]{2,1,0:T(8,128)(2,1)S(1)} %constant_dynamic-update-slice_fusion.refs_1_.refs_5_), channel_id=1, source_target_pairs={{0,2},{2,0},{1,3},{3,1},{4,6},{6,4},{5,7},{7,5},{8,10},{10,8},{9,1... | collective-permute-start | bytes 786440 | tf_op jit(solution)/shard_map/ppermute | solution.py:22
  36.6 3.4 %copy-start = (bf16[4096,1024]{1,0:T(8,128)(2,1)S(1)}, bf16[4096,1024]{1,0:T(8,128)(2,1)}, u32[]{:S(2)}) copy-start(bf16[4096,1024]{1,0:T(8,128)(2,1)} %refs_4_.3) | copy-start | bytes 25165828
  44.2 1.6 %collective-permute-start.14 = (bf16[16,32,256]{2,1,0:T(8,128)(2,1)S(1)}, bf16[16,32,256]{2,1,0:T(8,128)(2,1)S(1)}, u32[]{:S(2)}, u32[]{:S(2)}) collective-permute-start(bf16[16,32,256]{2,1,0:T(8,128)(2,1)S(1)} %collective-permute-done.13.refs_3_.refs_7_), channel_id=1, source_target_pairs={{0,1},{1,0},{2,3},{3,2},{4,5},{5,4},{6,7},{7,6},{8,9},{9,8},{10,11... | collective-permute-start | bytes 786440 | tf_op jit(solution)/shard_map/ppermute | solution.py:22
  48.2 2.6 %collective-permute-start.15 = (bf16[2,128,1024]{2,1,0:T(8,128)(2,1)S(1)}, bf16[2,128,1024]{2,1,0:T(8,128)(2,1)S(1)}, u32[]{:S(2)}, u32[]{:S(2)}) collective-permute-start(bf16[2,128,1024]{2,1,0:T(8,128)(2,1)S(1)} %get-tuple-element.64), channel_id=1, source_target_pairs={{0,1},{1,0},{2,3},{3,2},{4,5},{5,4},{6,7},{7,6},{8,9},{9,8},{10,11... | collective-permute-start | bytes 1572872 | tf_op jit(solution)/shard_map/ppermute | solution.py:22
  48.4 17.1 %slice-start.2 = ((s8[8388608]{0:T(1024)(128)(4,1)}), s8[4194304]{0:T(1024)(128)(4,1)S(1)}, s32[]{:S(2)}) async-start(s8[8388608]{0:T(1024)(128)(4,1)} %bitcast.33), calls=%async_computation.2 | async-start | bytes 8388608
  50.9 12.1 %collective-permute-start.16 = (bf16[2,128,1024]{2,1,0:T(8,128)(2,1)S(1)}, bf16[2,128,1024]{2,1,0:T(8,128)(2,1)S(1)}, u32[]{:S(2)}, u32[]{:S(2)}) collective-permute-start(bf16[2,128,1024]{2,1,0:T(8,128)(2,1)S(1)} %get-tuple-element.66), channel_id=1, source_target_pairs={{0,1},{1,0},{2,3},{3,2},{4,5},{5,4},{6,7},{7,6},{8,9},{9,8},{10,11... | collective-permute-start | bytes 1572872 | tf_op jit(solution)/shard_map/ppermute | solution.py:22
  51.3 14.2 %slice-start.3 = ((s8[8388608]{0:T(1024)(128)(4,1)}), s8[4194304]{0:T(1024)(128)(4,1)S(1)}, s32[]{:S(2)}) async-start(s8[8388608]{0:T(1024)(128)(4,1)} %bitcast.33), calls=%async_computation.3 | async-start | bytes 8388608
  51.3 9.2 %collective-permute-start.17 = (bf16[128,1024]{1,0:T(8,128)(2,1)S(1)}, bf16[128,1024]{1,0:T(8,128)(2,1)S(1)}, u32[]{:S(2)}, u32[]{:S(2)}) collective-permute-start(bf16[128,1024]{1,0:T(8,128)(2,1)S(1)} %slice.78), channel_id=1, source_target_pairs={{0,2},{2,0},{1,3},{3,1},{4,6},{6,4},{5,7},{7,5},{8,10},{10,8},{9,1... | collective-permute-start | bytes 786440 | tf_op jit(solution)/shard_map/ppermute | solution.py:22
  53.0 12.4 %collective-permute-start.18 = (bf16[128,1024]{1,0:T(8,128)(2,1)S(1)}, bf16[128,1024]{1,0:T(8,128)(2,1)S(1)}, u32[]{:S(2)}, u32[]{:S(2)}) collective-permute-start(bf16[128,1024]{1,0:T(8,128)(2,1)S(1)} %fusion.5), channel_id=1, source_target_pairs={{0,2},{2,0},{1,3},{3,1},{4,6},{6,4},{5,7},{7,5},{8,10},{10,8},{9,1... | collective-permute-start | bytes 786440 | tf_op jit(solution)/shard_map/ppermute | solution.py:22
  63.0 6.1 %collective-permute-start.19 = (bf16[2,128,1024]{2,1,0:T(8,128)(2,1)S(1)}, bf16[2,128,1024]{2,1,0:T(8,128)(2,1)S(1)}, u32[]{:S(2)}, u32[]{:S(2)}) collective-permute-start(bf16[2,128,1024]{2,1,0:T(8,128)(2,1)S(1)} %get-tuple-element.73), channel_id=1, source_target_pairs={{0,1},{1,0},{2,3},{3,2},{4,5},{5,4},{6,7},{7,6},{8,9},{9,8},{10,11... | collective-permute-start | bytes 1572872 | tf_op jit(solution)/shard_map/ppermute | solution.py:22
  63.1 2.4 %collective-permute-start.20 = (bf16[128,1024]{1,0:T(8,128)(2,1)S(1)}, bf16[128,1024]{1,0:T(8,128)(2,1)S(1)}, u32[]{:S(2)}, u32[]{:S(2)}) collective-permute-start(bf16[128,1024]{1,0:T(8,128)(2,1)S(1)} %collective-permute-done.17.refs_2_), channel_id=1, source_target_pairs={{0,1},{1,0},{2,3},{3,2},{4,5},{5,4},{6,7},{7,6},{8,9},{9,8},{10,11... | collective-permute-start | bytes 786440 | tf_op jit(solution)/shard_map/ppermute | solution.py:22
  63.6 8.3 %collective-permute-start.21 = (bf16[128,1024]{1,0:T(8,128)(2,1)S(1)}, bf16[128,1024]{1,0:T(8,128)(2,1)S(1)}, u32[]{:S(2)}, u32[]{:S(2)}) collective-permute-start(bf16[128,1024]{1,0:T(8,128)(2,1)S(1)} %fusion.6), channel_id=1, source_target_pairs={{0,2},{2,0},{1,3},{3,1},{4,6},{6,4},{5,7},{7,5},{8,10},{10,8},{9,1... | collective-permute-start | bytes 786440 | tf_op jit(solution)/shard_map/ppermute | solution.py:22
  72.0 2.0 %collective-permute-start.22 = (bf16[2,128,1024]{2,1,0:T(8,128)(2,1)S(1)}, bf16[2,128,1024]{2,1,0:T(8,128)(2,1)S(1)}, u32[]{:S(2)}, u32[]{:S(2)}) collective-permute-start(bf16[2,128,1024]{2,1,0:T(8,128)(2,1)S(1)} %get-tuple-element.81), channel_id=1, source_target_pairs={{0,1},{1,0},{2,3},{3,2},{4,5},{5,4},{6,7},{7,6},{8,9},{9,8},{10,11... | collective-permute-start | bytes 1572872 | tf_op jit(solution)/shard_map/ppermute | solution.py:22
  72.1 9.2 %collective-permute-start.23 = (bf16[128,1024]{1,0:T(8,128)(2,1)S(1)}, bf16[128,1024]{1,0:T(8,128)(2,1)S(1)}, u32[]{:S(2)}, u32[]{:S(2)}) collective-permute-start(bf16[128,1024]{1,0:T(8,128)(2,1)S(1)} %fusion.7), channel_id=1, source_target_pairs={{0,2},{2,0},{1,3},{3,1},{4,6},{6,4},{5,7},{7,5},{8,10},{10,8},{9,1... | collective-permute-start | bytes 786440 | tf_op jit(solution)/shard_map/ppermute | solution.py:22
  74.1 12.4 %collective-permute-start.24 = (bf16[128,1024]{1,0:T(8,128)(2,1)S(1)}, bf16[128,1024]{1,0:T(8,128)(2,1)S(1)}, u32[]{:S(2)}, u32[]{:S(2)}) collective-permute-start(bf16[128,1024]{1,0:T(8,128)(2,1)S(1)} %fusion.8), channel_id=1, source_target_pairs={{0,2},{2,0},{1,3},{3,1},{4,6},{6,4},{5,7},{7,5},{8,10},{10,8},{9,1... | collective-permute-start | bytes 786440 | tf_op jit(solution)/shard_map/ppermute | solution.py:22

commit v5 on v4

--- a/solution.py
+++ b/solution.py
@@ -206,8 +206,8 @@
 def chunk_kernel(
     meta, table, live, *refs, first, low, span, heads, size, pieces, cap, requests, gain
 ):
-    sources, kvs = refs[: -5 - pieces], refs[-5 - pieces : -5]
-    w_ref, kept_ref, sent_ref, att, pair = refs[-5:]
+    sources, kvs = refs[: -6 - pieces], refs[-6 - pieces : -6]
+    w_ref, kept_ref, upper_ref, lower_ref, att, pair = refs[-6:]
     me, mp, sub = meta[0], meta[1], meta[2]
     group = pieces // 2
     piece = kvs[0].shape[1]
@@ -249,11 +249,17 @@
         for h in range(heads):
             att[rows, h * size : (h + 1) * size] = attended[h * span : (h + 1) * span]
     width = kept_ref.shape[2]
-    for ds, out_ref in ((1, sent_ref), (0, kept_ref)):
+    half = tokens // 2
+    for ds in (1, 0):
         for dm in range(group):
             block = lax.rem(mp + dm, group) * 2 + lax.rem(sub + ds, 2)
             w = w_ref[:, pl.ds(pl.multiple_of(block * width, width), width)]
-            out_ref[dm] = jnp.dot(att[...], w, preferred_element_type=f32).astype(bf16)
+            result = jnp.dot(att[...], w, preferred_element_type=f32).astype(bf16)
+            if ds:
+                upper_ref[dm] = result[:half]
+                lower_ref[dm] = result[half:]
+            else:
+                kept_ref[dm] = result
 
 
 def run_chunk(meta, table, live, sources, pairs, weight, first, low, spans, span, out_width, cap, gain):
@@ -270,12 +276,16 @@
             pieces=pieces, cap=cap, requests=requests, gain=gain,
         ),
         in_specs=[SMEM] * 3 + [VMEM] * (1 + pieces + len(sources)),
-        out_specs=[VMEM] * 2,
+        out_specs=[VMEM] * 3,
         scratch_shapes=[
             pltpu.VMEM((tokens, width), bf16),
             pltpu.VMEM((spans, 2 * pieces * piece, pair_width), bf16),
         ],
-        out_shape=[jax.ShapeDtypeStruct((group, tokens, out_width), bf16)] * 2,
+        out_shape=[
+            jax.ShapeDtypeStruct((group, tokens, out_width), bf16),
+            jax.ShapeDtypeStruct((group, tokens // 2, out_width), bf16),
+            jax.ShapeDtypeStruct((group, tokens // 2, out_width), bf16),
+        ],
         compiler_params=params(),
         cost_estimate=cost(
             4 * tokens * width * out_width * group + 4 * tokens * width * 2 * pieces * piece,
@@ -332,9 +342,10 @@
         [neighbour_owner.reshape(1, -1), neighbour_slot.reshape(1, -1), neighbour_length.reshape(1, -1)],
         axis=1,
     )
+    table = jnp.concatenate([table, swap(table, "rows", 1)], axis=0)
 
     kept, sent = encode(meta, neighbour_states, encoder_weight, pieces)
-    received = shift(after(sent, *fars_first), "sub", 1)
+    received = shift(after(sent, table, *fars_first), "sub", 1)
     leaving = [add(kept[dm], received[dm]) for dm in range(1, group)]
     crossed = [shift(leaving[dm - 1], "mp", dm) for dm in range(1, group)]
     near = shift(after(hidden, *leaving), "sub", 1)
@@ -361,38 +372,41 @@
     fars_last = cross(after(hidden, encoded)[last_low:])
     pairs += with_near(fars, queries)
 
-    kept, sent, received, leaving, arrived, outs = [], [], [], [], [], []
-
-    def send(c, *earlier):
+    def join(c, *earlier):
         got = after(received[c], *earlier)
-        leaving.append([add(kept[c][dm], got[dm]) for dm in range(1, group)])
-        arrived.append([shift(leaving[c][dm - 1], "mp", dm) for dm in range(1, group)])
+        step = chunk_tokens // 2
+        parts = [
+            [add(kept[c][dm, i * step : (i + 1) * step], g[dm]) for i, g in enumerate(got)]
+            for dm in range(1, group)
+        ]
+        return [jnp.concatenate(p, axis=0) for p in parts]
+
+    kept, received, leaving, arrived, outs = [], [], [], [], []
 
     def total(c, *earlier):
-        outs.append(add(after(kept[c], *earlier)[0], received[c][0], *arrived[c]))
+        got = jnp.concatenate([g[0] for g in received[c]], axis=0)
+        outs.append(add(after(kept[c], *earlier)[0], got, *arrived[c]))
 
     for c in range(chunks):
-        sources = [queries]
+        sources, low = [queries], c * chunk_tokens
         if c == chunks - 1:
             sources = [hidden, near, *with_near(fars_last, *leaving[0]), query_weight]
-        gate = (fars_last if c == 2 else []) + (leaving[c - 2] if c > 1 else []) + ([outs[c - 3]] if c > 2 else [])
-        one, other = run_chunk(
+        gate = (leaving[c - 1] if c else []) + ([outs[c - 2]] if c > 1 else [])
+        one, *others = run_chunk(
             after(meta, *gate), table, live, sources, pairs, output_weight, c * chunk_spans,
-            c * chunk_tokens, chunk_spans, span_tokens, feature_shard, cap, gain,
+            low, chunk_spans, span_tokens, feature_shard, cap, gain,
         )
         kept.append(one)
+        received.append([shift(other, "sub", 1) for other in others])
+        leaving.append(join(c, *([] if c else fars_last)))
+        arrived.append([shift(leaving[c][dm - 1], "mp", dm) for dm in range(1, group)])
         if c:
-            send(c - 1, one)
-            other = after(other, *leaving[c - 1])
-        if c > 1:
-            total(c - 2, *leaving[c - 1])
-        if c > 1 and c == chunks - 1:
-            other = after(other, outs[-1])
-        received.append(shift(other, "sub", 1))
-    send(chunks - 1)
-    total(chunks - 2, *leaving[-1])
+            total(c - 1, *leaving[c])
     total(chunks - 1)
-    return jnp.concatenate(outs, axis=0)
+    mixed = jnp.zeros((token_count, feature_shard), bf16)
+    for c, out in enumerate(outs):
+        mixed = lax.dynamic_update_slice(after(mixed, meta), out, (c * chunk_tokens, 0))
+    return mixed
 
 
 def solution(mesh):

time: 87.9 us -> 87.2 us (level)
  starting transfers between devices: 24.4 us -> 22.3 us
  other arithmetic: 2.03 us -> 3.17 us
  waiting for transfers between devices: 34.6 us -> 33.7 us
    ppermute x20 -> x24, starting transfers between devices: 15.7 us -> 12.3 us  [shift(): lax.ppermute(value, axis, [(i, (i + by) % size) for i in range(size)])]
    ppermute x5, waiting for transfers between devices: 9.95 us -> 6.93 us  [swap(): return lax.ppermute(value, axis, [(i, i ^ by) for i in range(size)])]
    ppermute x20 -> x24, waiting for transfers between devices: 24.6 us -> 26.7 us  [shift(): lax.ppermute(value, axis, [(i, (i + by) % size) for i in range(size)])]
    ppermute x5, starting transfers between devices: 8.68 us -> 10.1 us  [swap(): return lax.ppermute(value, axis, [(i, i ^ by) for i in range(size)])]
    dynamic_update_slice x0 -> x4, other arithmetic: none -> 1.2 us  [shards(): lax.dynamic_update_slice(after(mixed, meta), out, (c * chunk_tokens, 0))]
    slice x1, local copies, waits for them, and re-layouts: 0.04 us -> 1.08 us  [shards(): fars_second = cross(after(hidden, table, *crossed)[chunk_tokens:last_low])]
    unnamed x27 -> x21, local copies, waits for them, and re-layouts: 6.83 us -> 6.42 us
  transfers between devices with their start and end apart: 25 -> 29, of which waited for: 15 -> 19; matrix products, arithmetic and copies ran while one was open for 1% -> 3% of each run, Pallas kernels for 18% -> 21%
where the time goes in v5:
time: 87.2 us; the launch traced here: 86.9 us
  waiting for transfers between devices  33.7 us (39%)
  starting transfers between devices  22.3 us (26%)
  Pallas kernels  18.5 us (21%)
  local copies, waits for them, and re-layouts  8.91 us (10%)
  other arithmetic  3.17 us (4%)
    ppermute x24, waiting for transfers between devices, shift(): lax.ppermute(value, axis, [(i, (i + by) % size) for i in range(size)])  26.7 us
    ppermute x24, starting transfers between devices, shift(): lax.ppermute(value, axis, [(i, (i + by) % size) for i in range(size)])  12.3 us
    pallas_call x4, Pallas kernels, run_chunk(): pl.pallas_call(functools.partial(chunk_kernel, first=first, low=low, span...  10.9 us
    ppermute x5, starting transfers between devices, swap(): return lax.ppermute(value, axis, [(i, i ^ by) for i in range(size)])  10.1 us
    ppermute x5, waiting for transfers between devices, swap(): return lax.ppermute(value, axis, [(i, i ^ by) for i in range(size)])  6.93 us
    unnamed x21, local copies, waits for them, and re-layouts  6.42 us
    pallas_call x1, Pallas kernels, project_queries(): pl.pallas_call(functools.partial(query_kernel, lows=tuple(lows), gain=gai...  4.19 us
    pallas_call x1, Pallas kernels, encode(): pl.pallas_call(functools.partial(encode_kernel, pieces=pieces, piece=piec...  2.46 us
  transfers between devices with their start and end apart: 29, of which 19 were waited for; matrix products, arithmetic and copies ran while one was open for 3% of the time, Pallas kernels for 21%

profile of v5, /device:TPU:0, one launch (start us, length us, event | category | flops | bytes accessed | tf_op | source)
XLA Modules:
  0.0 86.9 jit_solution(17924849393480195567)
XLA Ops:
  0.0 0.8 copy.11
  0.8 0.8 copy.12
  1.7 0.7 pad_add_fusion.3
  2.4 3.0 %collective-permute-start = (s32[1,48]{1,0:T(1,128)S(1)}, s32[1,48]{1,0:T(1,128)S(1)}, u32[]{:S(2)}, u32[]{:S(2)}) collective-permute-start(s32[1,48]{1,0:T(1,128)S(1)} %pad_add_fusion.3), channel_id=1, source_target_pairs={{0,4},{4,0},{8,12},{12,8},{1,5},{5,1},{9,13},{13,9},{2,6},{6,2},{1... | collective-permute-start | bytes 584 | tf_op jit(solution)/shard_map/ppermute | solution.py:27
  5.4 1.0 %slice.106 = bf16[128,1024]{1,0:T(8,128)(2,1)S(1)} slice(bf16[512,1024]{1,0:T(8,128)(2,1)} %refs_0_.1), slice={[0:128], [0:1024]} | slice | bytes 524288 | tf_op jit(solution)/shard_map/slice | solution.py:339
  6.4 1.6 %collective-permute-start.1 = (bf16[128,1024]{1,0:T(8,128)(2,1)S(1)}, bf16[128,1024]{1,0:T(8,128)(2,1)S(1)}, u32[]{:S(2)}, u32[]{:S(2)}) collective-permute-start(bf16[128,1024]{1,0:T(8,128)(2,1)S(1)} %slice.106), channel_id=1, source_target_pairs={{0,2},{2,0},{1,3},{3,1},{4,6},{6,4},{5,7},{7,5},{8,10},{10,8},{9,1... | collective-permute-start | bytes 786440 | tf_op jit(solution)/shard_map/ppermute | solution.py:22
  8.0 2.3 %copy-done.3 = bf16[16,128,1024]{2,1,0:T(8,128)(2,1)S(1)} copy-done((bf16[16,128,1024]{2,1,0:T(8,128)(2,1)S(1)}, bf16[16,128,1024]{2,1,0:T(8,128)(2,1)}, u32[]{:S(2)}) %copy-start.3) | copy-done | bytes 4194328
  10.4 1.3 %copy-done.4 = bf16[1024,256]{1,0:T(8,128)(2,1)S(1)} copy-done((bf16[1024,256]{1,0:T(8,128)(2,1)S(1)}, bf16[1024,256]{1,0:T(8,128)(2,1)}, u32[]{:S(2)}) %copy-start.4) | copy-done | bytes 524312
  11.7 2.5 %encode.1 = (bf16[2,528,256]{2,1,0:T(8,128)(2,1)S(1)}, bf16[2,528,256]{2,1,0:T(8,128)(2,1)S(1)}) custom-call(s32[3]{0:T(128)S(1)} %pad_add_fusion.2.meta, bf16[16,128,1024]{2,1,0:T(8,128)(2,1)S(1)} %copy-done.3, bf16[1024,256]{1,0:T(8,128)(2,1)S(1)} %copy-done.4), custom_call_target="tpu_custom_call" | custom-call | flops 1073741824 | bytes 4194304 | tf_op jit(solution)/shard_map/encode/pallas_call | solution.py:85
  14.2 0.7 pad_add_fusion.1
  14.9 1.9 %collective-permute-done.2.received = bf16[2,528,256]{2,1,0:T(8,128)(2,1)S(1)} collective-permute-done((bf16[2,528,256]{2,1,0:T(8,128)(2,1)S(1)}, bf16[2,528,256]{2,1,0:T(8,128)(2,1)S(1)}, u32[]{:S(2)}, u32[]{:S(2)}) %collective-permute-start.2) | collective-permute-done | bytes 540704 | tf_op jit(solution)/shard_map/ppermute | solution.py:22
  16.9 0.9 %collective-permute-start.4 = (bf16[528,256]{1,0:T(8,128)(2,1)S(1)}, bf16[528,256]{1,0:T(8,128)(2,1)S(1)}, u32[]{:S(2)}, u32[]{:S(2)}) collective-permute-start(bf16[528,256]{1,0:T(8,128)(2,1)S(1)} %fusion.8), channel_id=1, source_target_pairs={{0,2},{2,0},{1,3},{3,1},{4,6},{6,4},{5,7},{7,5},{8,10},{10,8},{9,1... | collective-permute-start | bytes 811016 | tf_op jit(solution)/shard_map/ppermute | solution.py:22
  17.8 2.6 %collective-permute-start.3 = (s32[2,48]{1,0:T(2,128)S(1)}, s32[2,48]{1,0:T(2,128)S(1)}, u32[]{:S(2)}, u32[]{:S(2)}) collective-permute-start(s32[2,48]{1,0:T(2,128)S(1)} %pad_add_fusion.1), channel_id=1, source_target_pairs={{0,8},{4,12},{8,0},{12,4},{1,9},{5,13},{9,1},{13,5},{2,10},{6,14},... | collective-permute-start | bytes 1160 | tf_op jit(solution)/shard_map/ppermute | solution.py:27
  20.4 1.9 %collective-permute-done.3 = s32[2,48]{1,0:T(2,128)S(1)} collective-permute-done((s32[2,48]{1,0:T(2,128)S(1)}, s32[2,48]{1,0:T(2,128)S(1)}, u32[]{:S(2)}, u32[]{:S(2)}) %collective-permute-start.3) | collective-permute-done | bytes 416 | tf_op jit(solution)/shard_map/ppermute | solution.py:27
  22.3 3.2 %collective-permute-done.4.refs_0_ = bf16[528,256]{1,0:T(8,128)(2,1)S(1)} collective-permute-done((bf16[528,256]{1,0:T(8,128)(2,1)S(1)}, bf16[528,256]{1,0:T(8,128)(2,1)S(1)}, u32[]{:S(2)}, u32[]{:S(2)}) %collective-permute-start.4) | collective-permute-done | bytes 270368 | tf_op jit(solution)/shard_map/ppermute | solution.py:22
  25.5 1.1 %slice.110 = bf16[256,1024]{1,0:T(8,128)(2,1)S(1)} slice(bf16[512,1024]{1,0:T(8,128)(2,1)} %refs_0_.1), slice={[128:384], [0:1024]} | slice | bytes 1048576 | tf_op jit(solution)/shard_map/slice | solution.py:358
  26.6 0.9 %collective-permute-start.10 = (bf16[256,1024]{1,0:T(8,128)(2,1)S(1)}, bf16[256,1024]{1,0:T(8,128)(2,1)S(1)}, u32[]{:S(2)}, u32[]{:S(2)}) collective-permute-start(bf16[256,1024]{1,0:T(8,128)(2,1)S(1)} %slice.110), channel_id=1, source_target_pairs={{0,2},{2,0},{1,3},{3,1},{4,6},{6,4},{5,7},{7,5},{8,10},{10,8},{9,1... | collective-permute-start | bytes 1572872 | tf_op jit(solution)/shard_map/ppermute | solution.py:22
  27.5 0.9 %route.1 = (bf16[4,32,256]{2,1,0:T(8,128)(2,1)S(1)}, bf16[4,32,256]{2,1,0:T(8,128)(2,1)S(1)}, bf16[4,32,256]{2,1,0:T(8,128)(2,1)S(1)}, bf16[4,32,256]{2,1,0:T(8,128)(2,1)S(1)}) custom-call(s32[3]{0:T(128)S(1)} %pad_add_fusion.2.meta, s32[4,32]{1,0:T(4,128)S(1)} %bitcast.57, bf16[2,528,256]{2,1,0:T(8,128)(2,1)S(1)} %get-tuple-element.55.kept, ...), custom_call_target="tpu_custom_call" | custom-call | flops 1081344 | bytes 811008 | tf_op jit(solution)/shard_map/route/pallas_call | solution.py:140
  28.4 0.5 collective-permute-start.5
  28.9 2.6 %collective-permute-start.6 = (bf16[4,32,256]{2,1,0:T(8,128)(2,1)S(1)}, bf16[4,32,256]{2,1,0:T(8,128)(2,1)S(1)}, u32[]{:S(2)}, u32[]{:S(2)}) collective-permute-start(bf16[4,32,256]{2,1,0:T(8,128)(2,1)S(1)} %get-tuple-element.61), channel_id=1, source_target_pairs={{0,8},{4,12},{8,0},{12,4},{1,9},{5,13},{9,1},{13,5},{2,10},{6,14},... | collective-permute-start | bytes 196616 | tf_op jit(solution)/shard_map/ppermute | solution.py:27
  31.5 1.3 %collective-permute-start.7 = (bf16[4,32,256]{2,1,0:T(8,128)(2,1)S(1)}, bf16[4,32,256]{2,1,0:T(8,128)(2,1)S(1)}, u32[]{:S(2)}, u32[]{:S(2)}) collective-permute-start(bf16[4,32,256]{2,1,0:T(8,128)(2,1)S(1)} %get-tuple-element.62), channel_id=1, source_target_pairs={{0,12},{4,8},{8,4},{12,0},{1,13},{5,9},{9,5},{13,1},{2,14},{6,10},... | collective-permute-start | bytes 196616 | tf_op jit(solution)/shard_map/ppermute | solution.py:27
  32.9 1.5 %collective-permute-done.5 = bf16[4,32,256]{2,1,0:T(8,128)(2,1)S(1)} collective-permute-done((bf16[4,32,256]{2,1,0:T(8,128)(2,1)S(1)}, bf16[4,32,256]{2,1,0:T(8,128)(2,1)S(1)}, u32[]{:S(2)}, u32[]{:S(2)}) %collective-permute-start.5) | collective-permute-done | bytes 65568 | tf_op jit(solution)/shard_map/ppermute | solution.py:27
  34.4 3.5 %collective-permute-done.7 = bf16[4,32,256]{2,1,0:T(8,128)(2,1)S(1)} collective-permute-done((bf16[4,32,256]{2,1,0:T(8,128)(2,1)S(1)}, bf16[4,32,256]{2,1,0:T(8,128)(2,1)S(1)}, u32[]{:S(2)}, u32[]{:S(2)}) %collective-permute-start.7) | collective-permute-done | bytes 65568 | tf_op jit(solution)/shard_map/ppermute | solution.py:27
  38.0 1.8 %collective-permute-done.10.refs_2_ = bf16[256,1024]{1,0:T(8,128)(2,1)S(1)} collective-permute-done((bf16[256,1024]{1,0:T(8,128)(2,1)S(1)}, bf16[256,1024]{1,0:T(8,128)(2,1)S(1)}, u32[]{:S(2)}, u32[]{:S(2)}) %collective-permute-start.10) | collective-permute-done | bytes 524320 | tf_op jit(solution)/shard_map/ppermute | solution.py:22
  40.3 0.8 collective-permute-start.13
  41.1 1.0 %collective-permute-done.9.refs_1_ = bf16[128,1024]{1,0:T(8,128)(2,1)S(1)} collective-permute-done((bf16[128,1024]{1,0:T(8,128)(2,1)S(1)}, bf16[128,1024]{1,0:T(8,128)(2,1)S(1)}, u32[]{:S(2)}, u32[]{:S(2)}) %collective-permute-start.9) | collective-permute-done | bytes 262176 | tf_op jit(solution)/shard_map/ppermute | solution.py:22
  42.1 1.2 %copy-done.1 = bf16[512,1024]{1,0:T(8,128)(2,1)S(1)} copy-done((bf16[512,1024]{1,0:T(8,128)(2,1)S(1)}, bf16[512,1024]{1,0:T(8,128)(2,1)}, u32[]{:S(2)}) %copy-start.1) | copy-done | bytes 1048600
  43.3 4.2 %queries.1.refs_0_ = bf16[384,1024]{1,0:T(8,128)(2,1)S(1)} custom-call(s32[3]{0:T(128)S(1)} %pad_add_fusion.2.meta, bf16[512,1024]{1,0:T(8,128)(2,1)S(1)} %copy-done.1, bf16[512,1024]{1,0:T(8,128)(2,1)S(1)} %collective-permute-done.8.near_ref.refs_1_, bf16[128,1024]{1,0:T(8,128)(2,1)S(1)} %collective-permute-done.1.refs_0_, ...), custom_call_target="tpu_custom_call" | custom-call | flops 3221225472 | bytes 3145728 | tf_op jit(solution)/shard_map/queries/pallas_call | solution.py:195
  47.5 1.0 %collective-permute-done.13.refs_3_.refs_7_ = bf16[16,32,256]{2,1,0:T(8,128)(2,1)S(1)} collective-permute-done((bf16[16,32,256]{2,1,0:T(8,128)(2,1)S(1)}, bf16[16,32,256]{2,1,0:T(8,128)(2,1)S(1)}, u32[]{:S(2)}, u32[]{:S(2)}) %collective-permute-start.13) | collective-permute-done | bytes 262176 | tf_op jit(solution)/shard_map/ppermute | solution.py:22
  48.6 0.9 %collective-permute-start.17 = (bf16[128,1024]{1,0:T(8,128)(2,1)S(1)}, bf16[128,1024]{1,0:T(8,128)(2,1)S(1)}, u32[]{:S(2)}, u32[]{:S(2)}) collective-permute-start(bf16[128,1024]{1,0:T(8,128)(2,1)S(1)} %slice.112), channel_id=1, source_target_pairs={{0,2},{2,0},{1,3},{3,1},{4,6},{6,4},{5,7},{7,5},{8,10},{10,8},{9,1... | collective-permute-start | bytes 786440 | tf_op jit(solution)/shard_map/ppermute | solution.py:22
  49.5 0.5 collective-permute-done.14.refs_4_.refs_8_
  50.1 2.4 %chunk.4 = (bf16[2,128,1024]{2,1,0:T(8,128)(2,1)S(1)}, bf16[2,64,1024]{2,1,0:T(8,128)(2,1)S(1)}, bf16[2,64,1024]{2,1,0:T(8,128)(2,1)S(1)}) custom-call(s32[3]{0:T(128)S(1)} %pad_add_fusion.2.meta, s32[4,32]{1,0:T(4,128)S(1)} %bitcast.58, s32[4,16]{1,0:T(4,128)S(1)} %slice.109.live, bf16[384,1024]{1,0:T(8,128)(2,1)S(1)} %queries.1.refs_0_, ...), custom_call_target="tpu_custom_call" | custom-call | flops 1207959552 | bytes 262144 | tf_op jit(solution)/shard_map/chunk/pallas_call | solution.py:273
  53.0 4.4 %collective-permute-done.17.refs_2_ = bf16[128,1024]{1,0:T(8,128)(2,1)S(1)} collective-permute-done((bf16[128,1024]{1,0:T(8,128)(2,1)S(1)}, bf16[128,1024]{1,0:T(8,128)(2,1)S(1)}, u32[]{:S(2)}, u32[]{:S(2)}) %collective-permute-start.17) | collective-permute-done | bytes 262176 | tf_op jit(solution)/shard_map/ppermute | solution.py:22
  57.5 0.9 %collective-permute-start.20 = (bf16[128,1024]{1,0:T(8,128)(2,1)S(1)}, bf16[128,1024]{1,0:T(8,128)(2,1)S(1)}, u32[]{:S(2)}, u32[]{:S(2)}) collective-permute-start(bf16[128,1024]{1,0:T(8,128)(2,1)S(1)} %pad_maximum_fusion), channel_id=1, source_target_pairs={{0,2},{2,0},{1,3},{3,1},{4,6},{6,4},{5,7},{7,5},{8,10},{10,8},{9,1... | collective-permute-start | bytes 786440 | tf_op jit(solution)/shard_map/ppermute | solution.py:22
  58.4 2.4 %chunk.5 = (bf16[2,128,1024]{2,1,0:T(8,128)(2,1)S(1)}, bf16[2,64,1024]{2,1,0:T(8,128)(2,1)S(1)}, bf16[2,64,1024]{2,1,0:T(8,128)(2,1)S(1)}) custom-call(s32[3]{0:T(128)S(1)} %pad_add_fusion.2.meta, s32[4,32]{1,0:T(4,128)S(1)} %bitcast.59, s32[4,16]{1,0:T(4,128)S(1)} %slice.109.live, bf16[384,1024]{1,0:T(8,128)(2,1)S(1)} %queries.1.refs_0_, ...), custom_call_target="tpu_custom_call" | custom-call | flops 1207959552 | bytes 262144 | tf_op jit(solution)/shard_map/chunk/pallas_call | solution.py:273
  60.8 0.6 collective-permute-start.18
  61.5 1.0 %collective-permute-done.18 = bf16[2,64,1024]{2,1,0:T(8,128)(2,1)S(1)} collective-permute-done((bf16[2,64,1024]{2,1,0:T(8,128)(2,1)S(1)}, bf16[2,64,1024]{2,1,0:T(8,128)(2,1)S(1)}, u32[]{:S(2)}, u32[]{:S(2)}) %collective-permute-start.18) | collective-permute-done | bytes 262176 | tf_op jit(solution)/shard_map/ppermute | solution.py:22
  63.0 1.3 %collective-permute-start.23 = (bf16[128,1024]{1,0:T(8,128)(2,1)S(1)}, bf16[128,1024]{1,0:T(8,128)(2,1)S(1)}, u32[]{:S(2)}, u32[]{:S(2)}) collective-permute-start(bf16[128,1024]{1,0:T(8,128)(2,1)S(1)} %pad_maximum_fusion.1), channel_id=1, source_target_pairs={{0,2},{2,0},{1,3},{3,1},{4,6},{6,4},{5,7},{7,5},{8,10},{10,8},{9,1... | collective-permute-start | bytes 786440 | tf_op jit(solution)/shard_map/ppermute | solution.py:22
  64.3 1.2 %collective-permute-done.20 = bf16[128,1024]{1,0:T(8,128)(2,1)S(1)} collective-permute-done((bf16[128,1024]{1,0:T(8,128)(2,1)S(1)}, bf16[128,1024]{1,0:T(8,128)(2,1)S(1)}, u32[]{:S(2)}, u32[]{:S(2)}) %collective-permute-start.20) | collective-permute-done | bytes 262176 | tf_op jit(solution)/shard_map/ppermute | solution.py:22
  65.8 2.4 %chunk.6 = (bf16[2,128,1024]{2,1,0:T(8,128)(2,1)S(1)}, bf16[2,64,1024]{2,1,0:T(8,128)(2,1)S(1)}, bf16[2,64,1024]{2,1,0:T(8,128)(2,1)S(1)}) custom-call(s32[3]{0:T(128)S(1)} %pad_add_fusion.2.meta, s32[4,32]{1,0:T(4,128)S(1)} %bitcast.60, s32[4,16]{1,0:T(4,128)S(1)} %slice.109.live, bf16[384,1024]{1,0:T(8,128)(2,1)S(1)} %queries.1.refs_0_, ...), custom_call_target="tpu_custom_call" | custom-call | flops 1207959552 | bytes 262144 | tf_op jit(solution)/shard_map/chunk/pallas_call | solution.py:273
  68.8 1.0 %collective-permute-done.21 = bf16[2,64,1024]{2,1,0:T(8,128)(2,1)S(1)} collective-permute-done((bf16[2,64,1024]{2,1,0:T(8,128)(2,1)S(1)}, bf16[2,64,1024]{2,1,0:T(8,128)(2,1)S(1)}, u32[]{:S(2)}, u32[]{:S(2)}) %collective-permute-start.21) | collective-permute-done | bytes 262176 | tf_op jit(solution)/shard_map/ppermute | solution.py:22
  70.2 0.9 %collective-permute-start.27 = (bf16[128,1024]{1,0:T(8,128)(2,1)S(1)}, bf16[128,1024]{1,0:T(8,128)(2,1)S(1)}, u32[]{:S(2)}, u32[]{:S(2)}) collective-permute-start(bf16[128,1024]{1,0:T(8,128)(2,1)S(1)} %pad_maximum_fusion.2), channel_id=1, source_target_pairs={{0,2},{2,0},{1,3},{3,1},{4,6},{6,4},{5,7},{7,5},{8,10},{10,8},{9,1... | collective-permute-start | bytes 786440 | tf_op jit(solution)/shard_map/ppermute | solution.py:22
  71.1 0.5 collective-permute-done.23
  71.8 3.8 %chunk.7 = (bf16[2,128,1024]{2,1,0:T(8,128)(2,1)S(1)}, bf16[2,64,1024]{2,1,0:T(8,128)(2,1)S(1)}, bf16[2,64,1024]{2,1,0:T(8,128)(2,1)S(1)}) custom-call(s32[3]{0:T(128)S(1)} %pad_add_fusion.2.meta, s32[4,32]{1,0:T(4,128)S(1)} %bitcast.61, s32[4,16]{1,0:T(4,128)S(1)} %slice.109.live, bf16[512,1024]{1,0:T(8,128)(2,1)S(1)} %copy-done.2, ...), custom_call_target="tpu_custom_call" | custom-call | flops 1207959552 | bytes 262144 | tf_op jit(solution)/shard_map/chunk/pallas_call | solution.py:273
  76.2 1.0 %collective-permute-done.25 = bf16[2,64,1024]{2,1,0:T(8,128)(2,1)S(1)} collective-permute-done((bf16[2,64,1024]{2,1,0:T(8,128)(2,1)S(1)}, bf16[2,64,1024]{2,1,0:T(8,128)(2,1)S(1)}, u32[]{:S(2)}, u32[]{:S(2)}) %collective-permute-start.25) | collective-permute-done | bytes 262176 | tf_op jit(solution)/shard_map/ppermute | solution.py:22
  77.7 1.3 %collective-permute-start.28 = (bf16[128,1024]{1,0:T(8,128)(2,1)S(1)}, bf16[128,1024]{1,0:T(8,128)(2,1)S(1)}, u32[]{:S(2)}, u32[]{:S(2)}) collective-permute-start(bf16[128,1024]{1,0:T(8,128)(2,1)S(1)} %pad_maximum_fusion.3), channel_id=1, source_target_pairs={{0,2},{2,0},{1,3},{3,1},{4,6},{6,4},{5,7},{7,5},{8,10},{10,8},{9,1... | collective-permute-start | bytes 786440 | tf_op jit(solution)/shard_map/ppermute | solution.py:22
  79.1 7.0 %collective-permute-done.28 = bf16[128,1024]{1,0:T(8,128)(2,1)S(1)} collective-permute-done((bf16[128,1024]{1,0:T(8,128)(2,1)S(1)}, bf16[128,1024]{1,0:T(8,128)(2,1)S(1)}, u32[]{:S(2)}, u32[]{:S(2)}) %collective-permute-start.28) | collective-permute-done | bytes 262176 | tf_op jit(solution)/shard_map/ppermute | solution.py:22
  86.1 0.8 fusion.10
  (72 shorter events, 4.9 us)
Async XLA Ops:
  2.4 11.7 %collective-permute-start = (s32[1,48]{1,0:T(1,128)S(1)}, s32[1,48]{1,0:T(1,128)S(1)}, u32[]{:S(2)}, u32[]{:S(2)}) collective-permute-start(s32[1,48]{1,0:T(1,128)S(1)} %pad_add_fusion.3), channel_id=1, source_target_pairs={{0,4},{4,0},{8,12},{12,8},{1,5},{5,1},{9,13},{13,9},{2,6},{6,2},{1... | collective-permute-start | bytes 584 | tf_op jit(solution)/shard_map/ppermute | solution.py:27
  6.4 8.5 %collective-permute-start.1 = (bf16[128,1024]{1,0:T(8,128)(2,1)S(1)}, bf16[128,1024]{1,0:T(8,128)(2,1)S(1)}, u32[]{:S(2)}, u32[]{:S(2)}) collective-permute-start(bf16[128,1024]{1,0:T(8,128)(2,1)S(1)} %slice.106), channel_id=1, source_target_pairs={{0,2},{2,0},{1,3},{3,1},{4,6},{6,4},{5,7},{7,5},{8,10},{10,8},{9,1... | collective-permute-start | bytes 786440 | tf_op jit(solution)/shard_map/ppermute | solution.py:22
  8.0 34.1 %copy-start = (bf16[4096,1024]{1,0:T(8,128)(2,1)S(1)}, bf16[4096,1024]{1,0:T(8,128)(2,1)}, u32[]{:S(2)}) copy-start(bf16[4096,1024]{1,0:T(8,128)(2,1)} %refs_4_.3) | copy-start | bytes 25165828
  8.0 2.3 %copy-start.3 = (bf16[16,128,1024]{2,1,0:T(8,128)(2,1)S(1)}, bf16[16,128,1024]{2,1,0:T(8,128)(2,1)}, u32[]{:S(2)}) copy-start(bf16[16,128,1024]{2,1,0:T(8,128)(2,1)} %x_ref.1) | copy-start | bytes 12582916
  10.4 1.3 %copy-start.4 = (bf16[1024,256]{1,0:T(8,128)(2,1)S(1)}, bf16[1024,256]{1,0:T(8,128)(2,1)}, u32[]{:S(2)}) copy-start(bf16[1024,256]{1,0:T(8,128)(2,1)} %w_ref.1) | copy-start | bytes 1572868
  14.9 1.9 %collective-permute-start.2 = (bf16[2,528,256]{2,1,0:T(8,128)(2,1)S(1)}, bf16[2,528,256]{2,1,0:T(8,128)(2,1)S(1)}, u32[]{:S(2)}, u32[]{:S(2)}) collective-permute-start(bf16[2,528,256]{2,1,0:T(8,128)(2,1)S(1)} %get-tuple-element.57), channel_id=1, source_target_pairs={{0,1},{1,0},{2,3},{3,2},{4,5},{5,4},{6,7},{7,6},{8,9},{9,8},{10,11... | collective-permute-start | bytes 1622024 | tf_op jit(solution)/shard_map/ppermute | solution.py:22
  16.8 33.2 %slice-start = ((s8[8388608]{0:T(1024)(128)(4,1)}), s8[4194304]{0:T(1024)(128)(4,1)S(1)}, s32[]{:S(2)}) async-start(s8[8388608]{0:T(1024)(128)(4,1)} %bitcast.55), calls=%async_computation | async-start | bytes 8388608
  16.9 8.6 %collective-permute-start.4 = (bf16[528,256]{1,0:T(8,128)(2,1)S(1)}, bf16[528,256]{1,0:T(8,128)(2,1)S(1)}, u32[]{:S(2)}, u32[]{:S(2)}) collective-permute-start(bf16[528,256]{1,0:T(8,128)(2,1)S(1)} %fusion.8), channel_id=1, source_target_pairs={{0,2},{2,0},{1,3},{3,1},{4,6},{6,4},{5,7},{7,5},{8,10},{10,8},{9,1... | collective-permute-start | bytes 811016 | tf_op jit(solution)/shard_map/ppermute | solution.py:22
  17.8 4.5 %collective-permute-start.3 = (s32[2,48]{1,0:T(2,128)S(1)}, s32[2,48]{1,0:T(2,128)S(1)}, u32[]{:S(2)}, u32[]{:S(2)}) collective-permute-start(s32[2,48]{1,0:T(2,128)S(1)} %pad_add_fusion.1), channel_id=1, source_target_pairs={{0,8},{4,12},{8,0},{12,4},{1,9},{5,13},{9,1},{13,5},{2,10},{6,14},... | collective-permute-start | bytes 1160 | tf_op jit(solution)/shard_map/ppermute | solution.py:27
  26.6 13.2 %collective-permute-start.10 = (bf16[256,1024]{1,0:T(8,128)(2,1)S(1)}, bf16[256,1024]{1,0:T(8,128)(2,1)S(1)}, u32[]{:S(2)}, u32[]{:S(2)}) collective-permute-start(bf16[256,1024]{1,0:T(8,128)(2,1)S(1)} %slice.110), channel_id=1, source_target_pairs={{0,2},{2,0},{1,3},{3,1},{4,6},{6,4},{5,7},{7,5},{8,10},{10,8},{9,1... | collective-permute-start | bytes 1572872 | tf_op jit(solution)/shard_map/ppermute | solution.py:22
  27.5 14.6 %collective-permute-start.8 = (bf16[512,1024]{1,0:T(8,128)(2,1)}, bf16[512,1024]{1,0:T(8,128)(2,1)S(1)}, u32[]{:S(2)}, u32[]{:S(2)}) collective-permute-start(bf16[512,1024]{1,0:T(8,128)(2,1)} %refs_0_.1), channel_id=1, source_target_pairs={{0,1},{1,0},{2,3},{3,2},{4,5},{5,4},{6,7},{7,6},{8,9},{9,8},{10,11... | collective-permute-start | bytes 3145736 | tf_op jit(solution)/shard_map/ppermute | solution.py:22
  28.4 6.0 %collective-permute-start.5 = (bf16[4,32,256]{2,1,0:T(8,128)(2,1)S(1)}, bf16[4,32,256]{2,1,0:T(8,128)(2,1)S(1)}, u32[]{:S(2)}, u32[]{:S(2)}) collective-permute-start(bf16[4,32,256]{2,1,0:T(8,128)(2,1)S(1)} %get-tuple-element.60), channel_id=1, source_target_pairs={{0,4},{4,0},{8,12},{12,8},{1,5},{5,1},{9,13},{13,9},{2,6},{6,2},{1... | collective-permute-start | bytes 196616 | tf_op jit(solution)/shard_map/ppermute | solution.py:27
  28.9 5.5 %collective-permute-start.6 = (bf16[4,32,256]{2,1,0:T(8,128)(2,1)S(1)}, bf16[4,32,256]{2,1,0:T(8,128)(2,1)S(1)}, u32[]{:S(2)}, u32[]{:S(2)}) collective-permute-start(bf16[4,32,256]{2,1,0:T(8,128)(2,1)S(1)} %get-tuple-element.61), channel_id=1, source_target_pairs={{0,8},{4,12},{8,0},{12,4},{1,9},{5,13},{9,1},{13,5},{2,10},{6,14},... | collective-permute-start | bytes 196616 | tf_op jit(solution)/shard_map/ppermute | solution.py:27
  31.5 6.4 %collective-permute-start.7 = (bf16[4,32,256]{2,1,0:T(8,128)(2,1)S(1)}, bf16[4,32,256]{2,1,0:T(8,128)(2,1)S(1)}, u32[]{:S(2)}, u32[]{:S(2)}) collective-permute-start(bf16[4,32,256]{2,1,0:T(8,128)(2,1)S(1)} %get-tuple-element.62), channel_id=1, source_target_pairs={{0,12},{4,8},{8,4},{12,0},{1,13},{5,9},{9,5},{13,1},{2,14},{6,10},... | collective-permute-start | bytes 196616 | tf_op jit(solution)/shard_map/ppermute | solution.py:27
  37.9 12.1 %slice-start.1 = ((s8[8388608]{0:T(1024)(128)(4,1)}), s8[4194304]{0:T(1024)(128)(4,1)S(1)}, s32[]{:S(2)}) async-start(s8[8388608]{0:T(1024)(128)(4,1)} %bitcast.55), calls=%async_computation.1 | async-start | bytes 8388608
  39.8 2.3 %collective-permute-start.11 = (bf16[256,1024]{1,0:T(8,128)(2,1)S(1)}, bf16[256,1024]{1,0:T(8,128)(2,1)S(1)}, u32[]{:S(2)}, u32[]{:S(2)}) collective-permute-start(bf16[256,1024]{1,0:T(8,128)(2,1)S(1)} %collective-permute-done.10.refs_2_), channel_id=1, source_target_pairs={{0,1},{1,0},{2,3},{3,2},{4,5},{5,4},{6,7},{7,6},{8,9},{9,8},{10,11... | collective-permute-start | bytes 1572872 | tf_op jit(solution)/shard_map/ppermute | solution.py:22
  39.8 2.3 %collective-permute-start.9 = (bf16[128,1024]{1,0:T(8,128)(2,1)S(1)}, bf16[128,1024]{1,0:T(8,128)(2,1)S(1)}, u32[]{:S(2)}, u32[]{:S(2)}) collective-permute-start(bf16[128,1024]{1,0:T(8,128)(2,1)S(1)} %collective-permute-done.1.refs_0_), channel_id=1, source_target_pairs={{0,1},{1,0},{2,3},{3,2},{4,5},{5,4},{6,7},{7,6},{8,9},{9,8},{10,11... | collective-permute-start | bytes 786440 | tf_op jit(solution)/shard_map/ppermute | solution.py:22
  40.3 8.2 %collective-permute-start.13 = (bf16[16,32,256]{2,1,0:T(8,128)(2,1)S(1)}, bf16[16,32,256]{2,1,0:T(8,128)(2,1)S(1)}, u32[]{:S(2)}, u32[]{:S(2)}) collective-permute-start(bf16[16,32,256]{2,1,0:T(8,128)(2,1)S(1)} %constant_dynamic-update-slice_fusion.refs_1_.refs_5_), channel_id=1, source_target_pairs={{0,2},{2,0},{1,3},{3,1},{4,6},{6,4},{5,7},{7,5},{8,10},{10,8},{9,1... | collective-permute-start | bytes 786440 | tf_op jit(solution)/shard_map/ppermute | solution.py:22
  41.1 8.4 %collective-permute-start.12 = (bf16[16,32,256]{2,1,0:T(8,128)(2,1)S(1)}, bf16[16,32,256]{2,1,0:T(8,128)(2,1)S(1)}, u32[]{:S(2)}, u32[]{:S(2)}) collective-permute-start(bf16[16,32,256]{2,1,0:T(8,128)(2,1)S(1)} %constant_dynamic-update-slice_fusion.refs_1_.refs_5_), channel_id=1, source_target_pairs={{0,1},{1,0},{2,3},{3,2},{4,5},{5,4},{6,7},{7,6},{8,9},{9,8},{10,11... | collective-permute-start | bytes 786440 | tf_op jit(solution)/shard_map/ppermute | solution.py:22
  42.1 1.2 %copy-start.1 = (bf16[512,1024]{1,0:T(8,128)(2,1)S(1)}, bf16[512,1024]{1,0:T(8,128)(2,1)}, u32[]{:S(2)}) copy-start(bf16[512,1024]{1,0:T(8,128)(2,1)} %refs_0_.1) | copy-start | bytes 3145732
  48.5 1.5 %collective-permute-start.14 = (bf16[16,32,256]{2,1,0:T(8,128)(2,1)S(1)}, bf16[16,32,256]{2,1,0:T(8,128)(2,1)S(1)}, u32[]{:S(2)}, u32[]{:S(2)}) collective-permute-start(bf16[16,32,256]{2,1,0:T(8,128)(2,1)S(1)} %collective-permute-done.13.refs_3_.refs_7_), channel_id=1, source_target_pairs={{0,1},{1,0},{2,3},{3,2},{4,5},{5,4},{6,7},{7,6},{8,9},{9,8},{10,11... | collective-permute-start | bytes 786440 | tf_op jit(solution)/shard_map/ppermute | solution.py:22
  48.6 8.8 %collective-permute-start.17 = (bf16[128,1024]{1,0:T(8,128)(2,1)S(1)}, bf16[128,1024]{1,0:T(8,128)(2,1)S(1)}, u32[]{:S(2)}, u32[]{:S(2)}) collective-permute-start(bf16[128,1024]{1,0:T(8,128)(2,1)S(1)} %slice.112), channel_id=1, source_target_pairs={{0,2},{2,0},{1,3},{3,1},{4,6},{6,4},{5,7},{7,5},{8,10},{10,8},{9,1... | collective-permute-start | bytes 786440 | tf_op jit(solution)/shard_map/ppermute | solution.py:22
  52.4 5.0 %collective-permute-start.15 = (bf16[2,64,1024]{2,1,0:T(8,128)(2,1)S(1)}, bf16[2,64,1024]{2,1,0:T(8,128)(2,1)S(1)}, u32[]{:S(2)}, u32[]{:S(2)}) collective-permute-start(bf16[2,64,1024]{2,1,0:T(8,128)(2,1)S(1)} %get-tuple-element.73), channel_id=1, source_target_pairs={{0,1},{1,0},{2,3},{3,2},{4,5},{5,4},{6,7},{7,6},{8,9},{9,8},{10,11... | collective-permute-start | bytes 786440 | tf_op jit(solution)/shard_map/ppermute | solution.py:22
  52.6 4.8 %collective-permute-start.16 = (bf16[2,64,1024]{2,1,0:T(8,128)(2,1)S(1)}, bf16[2,64,1024]{2,1,0:T(8,128)(2,1)S(1)}, u32[]{:S(2)}, u32[]{:S(2)}) collective-permute-start(bf16[2,64,1024]{2,1,0:T(8,128)(2,1)S(1)} %get-tuple-element.74), channel_id=1, source_target_pairs={{0,1},{1,0},{2,3},{3,2},{4,5},{5,4},{6,7},{7,6},{8,9},{9,8},{10,11... | collective-permute-start | bytes 786440 | tf_op jit(solution)/shard_map/ppermute | solution.py:22
  57.5 8.0 %collective-permute-start.20 = (bf16[128,1024]{1,0:T(8,128)(2,1)S(1)}, bf16[128,1024]{1,0:T(8,128)(2,1)S(1)}, u32[]{:S(2)}, u32[]{:S(2)}) collective-permute-start(bf16[128,1024]{1,0:T(8,128)(2,1)S(1)} %pad_maximum_fusion), channel_id=1, source_target_pairs={{0,2},{2,0},{1,3},{3,1},{4,6},{6,4},{5,7},{7,5},{8,10},{10,8},{9,1... | collective-permute-start | bytes 786440 | tf_op jit(solution)/shard_map/ppermute | solution.py:22
  58.4 13.4 %collective-permute-start.24 = (bf16[128,1024]{1,0:T(8,128)(2,1)S(1)}, bf16[128,1024]{1,0:T(8,128)(2,1)S(1)}, u32[]{:S(2)}, u32[]{:S(2)}) collective-permute-start(bf16[128,1024]{1,0:T(8,128)(2,1)S(1)} %collective-permute-done.17.refs_2_), channel_id=1, source_target_pairs={{0,1},{1,0},{2,3},{3,2},{4,5},{5,4},{6,7},{7,6},{8,9},{9,8},{10,11... | collective-permute-start | bytes 786440 | tf_op jit(solution)/shard_map/ppermute | solution.py:22
  60.8 1.7 %collective-permute-start.18 = (bf16[2,64,1024]{2,1,0:T(8,128)(2,1)S(1)}, bf16[2,64,1024]{2,1,0:T(8,128)(2,1)S(1)}, u32[]{:S(2)}, u32[]{:S(2)}) collective-permute-start(bf16[2,64,1024]{2,1,0:T(8,128)(2,1)S(1)} %get-tuple-element.80), channel_id=1, source_target_pairs={{0,1},{1,0},{2,3},{3,2},{4,5},{5,4},{6,7},{7,6},{8,9},{9,8},{10,11... | collective-permute-start | bytes 786440 | tf_op jit(solution)/shard_map/ppermute | solution.py:22
  61.3 1.5 %collective-permute-start.19 = (bf16[2,64,1024]{2,1,0:T(8,128)(2,1)S(1)}, bf16[2,64,1024]{2,1,0:T(8,128)(2,1)S(1)}, u32[]{:S(2)}, u32[]{:S(2)}) collective-permute-start(bf16[2,64,1024]{2,1,0:T(8,128)(2,1)S(1)} %get-tuple-element.81), channel_id=1, source_target_pairs={{0,1},{1,0},{2,3},{3,2},{4,5},{5,4},{6,7},{7,6},{8,9},{9,8},{10,11... | collective-permute-start | bytes 786440 | tf_op jit(solution)/shard_map/ppermute | solution.py:22
  61.4 10.3 %copy-start.2 = (bf16[512,1024]{1,0:T(8,128)(2,1)S(1)}, bf16[512,1024]{1,0:T(8,128)(2,1)}, u32[]{:S(2)}) copy-start(bf16[512,1024]{1,0:T(8,128)(2,1)} %refs_0_.1) | copy-start | bytes 3145732
  63.0 8.7 %collective-permute-start.23 = (bf16[128,1024]{1,0:T(8,128)(2,1)S(1)}, bf16[128,1024]{1,0:T(8,128)(2,1)S(1)}, u32[]{:S(2)}, u32[]{:S(2)}) collective-permute-start(bf16[128,1024]{1,0:T(8,128)(2,1)S(1)} %pad_maximum_fusion.1), channel_id=1, source_target_pairs={{0,2},{2,0},{1,3},{3,1},{4,6},{6,4},{5,7},{7,5},{8,10},{10,8},{9,1... | collective-permute-start | bytes 786440 | tf_op jit(solution)/shard_map/ppermute | solution.py:22
  68.2 1.6 %collective-permute-start.21 = (bf16[2,64,1024]{2,1,0:T(8,128)(2,1)S(1)}, bf16[2,64,1024]{2,1,0:T(8,128)(2,1)S(1)}, u32[]{:S(2)}, u32[]{:S(2)}) collective-permute-start(bf16[2,64,1024]{2,1,0:T(8,128)(2,1)S(1)} %get-tuple-element.88), channel_id=1, source_target_pairs={{0,1},{1,0},{2,3},{3,2},{4,5},{5,4},{6,7},{7,6},{8,9},{9,8},{10,11... | collective-permute-start | bytes 786440 | tf_op jit(solution)/shard_map/ppermute | solution.py:22
  68.2 1.9 %collective-permute-start.22 = (bf16[2,64,1024]{2,1,0:T(8,128)(2,1)S(1)}, bf16[2,64,1024]{2,1,0:T(8,128)(2,1)S(1)}, u32[]{:S(2)}, u32[]{:S(2)}) collective-permute-start(bf16[2,64,1024]{2,1,0:T(8,128)(2,1)S(1)} %get-tuple-element.89), channel_id=1, source_target_pairs={{0,1},{1,0},{2,3},{3,2},{4,5},{5,4},{6,7},{7,6},{8,9},{9,8},{10,11... | collective-permute-start | bytes 786440 | tf_op jit(solution)/shard_map/ppermute | solution.py:22
  70.2 8.7 %collective-permute-start.27 = (bf16[128,1024]{1,0:T(8,128)(2,1)S(1)}, bf16[128,1024]{1,0:T(8,128)(2,1)S(1)}, u32[]{:S(2)}, u32[]{:S(2)}) collective-permute-start(bf16[128,1024]{1,0:T(8,128)(2,1)S(1)} %pad_maximum_fusion.2), channel_id=1, source_target_pairs={{0,2},{2,0},{1,3},{3,1},{4,6},{6,4},{5,7},{7,5},{8,10},{10,8},{9,1... | collective-permute-start | bytes 786440 | tf_op jit(solution)/shard_map/ppermute | solution.py:22
  75.6 1.6 %collective-permute-start.25 = (bf16[2,64,1024]{2,1,0:T(8,128)(2,1)S(1)}, bf16[2,64,1024]{2,1,0:T(8,128)(2,1)S(1)}, u32[]{:S(2)}, u32[]{:S(2)}) collective-permute-start(bf16[2,64,1024]{2,1,0:T(8,128)(2,1)S(1)} %get-tuple-element.97), channel_id=1, source_target_pairs={{0,1},{1,0},{2,3},{3,2},{4,5},{5,4},{6,7},{7,6},{8,9},{9,8},{10,11... | collective-permute-start | bytes 786440 | tf_op jit(solution)/shard_map/ppermute | solution.py:22
  75.7 1.9 %collective-permute-start.26 = (bf16[2,64,1024]{2,1,0:T(8,128)(2,1)S(1)}, bf16[2,64,1024]{2,1,0:T(8,128)(2,1)S(1)}, u32[]{:S(2)}, u32[]{:S(2)}) collective-permute-start(bf16[2,64,1024]{2,1,0:T(8,128)(2,1)S(1)} %get-tuple-element.98), channel_id=1, source_target_pairs={{0,1},{1,0},{2,3},{3,2},{4,5},{5,4},{6,7},{7,6},{8,9},{9,8},{10,11... | collective-permute-start | bytes 786440 | tf_op jit(solution)/shard_map/ppermute | solution.py:22
  77.7 8.4 %collective-permute-start.28 = (bf16[128,1024]{1,0:T(8,128)(2,1)S(1)}, bf16[128,1024]{1,0:T(8,128)(2,1)S(1)}, u32[]{:S(2)}, u32[]{:S(2)}) collective-permute-start(bf16[128,1024]{1,0:T(8,128)(2,1)S(1)} %pad_maximum_fusion.3), channel_id=1, source_target_pairs={{0,2},{2,0},{1,3},{3,1},{4,6},{6,4},{5,7},{7,5},{8,10},{10,8},{9,1... | collective-permute-start | bytes 786440 | tf_op jit(solution)/shard_map/ppermute | solution.py:22
  79.1 7.0 %copy-start.5 = (bf16[512,1024]{1,0:T(8,128)(2,1)}, bf16[512,1024]{1,0:T(8,128)(2,1)S(1)}, u32[]{:S(2)}) copy-start(bf16[512,1024]{1,0:T(8,128)(2,1)S(1)} %fusion.9) | copy-start | bytes 3145732

commit v6 on v5

--- a/solution.py
+++ b/solution.py
@@ -317,9 +317,12 @@
     span_tokens = token_count // spans_here
     requests = 2 * spans_here
     cap = max(2, (requests + row_count - 1) // row_count)
-    chunks = 4
-    chunk_spans = spans_here // chunks
-    chunk_tokens = token_count // chunks
+    last_spans = spans_here // 4
+    chunk_spans = [last_spans] * 4
+    firsts = [c * last_spans for c in range(4)]
+    chunks = len(chunk_spans)
+    first_tokens = token_count // 4
+    last_low = token_count - last_spans * span_tokens
     gain = 1.0 / (softcap * math.sqrt(size))
     add = lambda *terms: functools.reduce(
         lambda a, b: a + b, [t.astype(f32) for t in terms]
@@ -336,16 +339,15 @@
             out += [far, shift(far, "sub", 1)]
         return out
 
-    fars_first = cross(hidden[:chunk_tokens])
+    fars_first = cross(hidden[:first_tokens])
 
     table = jnp.concatenate(
         [neighbour_owner.reshape(1, -1), neighbour_slot.reshape(1, -1), neighbour_length.reshape(1, -1)],
         axis=1,
     )
-    table = jnp.concatenate([table, swap(table, "rows", 1)], axis=0)
 
     kept, sent = encode(meta, neighbour_states, encoder_weight, pieces)
-    received = shift(after(sent, table, *fars_first), "sub", 1)
+    received = shift(after(sent, *fars_first), "sub", 1)
     leaving = [add(kept[dm], received[dm]) for dm in range(1, group)]
     crossed = [shift(leaving[dm - 1], "mp", dm) for dm in range(1, group)]
     near = shift(after(hidden, *leaving), "sub", 1)
@@ -354,8 +356,7 @@
         table = jnp.concatenate([table, swap(table, "rows", table.shape[0])], axis=0)
     table, live = table[:, : 2 * requests], table[:, 2 * requests :]
 
-    last_low = token_count - chunk_tokens
-    fars_second = cross(after(hidden, table, *crossed)[chunk_tokens:last_low])
+    fars_second = cross(after(hidden, table, *crossed)[first_tokens:last_low])
 
     routed = route(meta, table, kept, received, crossed, cap, features, count, requests)
     encoded = jnp.concatenate(
@@ -374,7 +375,7 @@
 
     def join(c, *earlier):
         got = after(received[c], *earlier)
-        step = chunk_tokens // 2
+        step = chunk_spans[c] * span_tokens // 2
         parts = [
             [add(kept[c][dm, i * step : (i + 1) * step], g[dm]) for i, g in enumerate(got)]
             for dm in range(1, group)
@@ -388,13 +389,13 @@
         outs.append(add(after(kept[c], *earlier)[0], got, *arrived[c]))
 
     for c in range(chunks):
-        sources, low = [queries], c * chunk_tokens
+        sources, low = [queries], firsts[c] * span_tokens
         if c == chunks - 1:
             sources = [hidden, near, *with_near(fars_last, *leaving[0]), query_weight]
         gate = (leaving[c - 1] if c else []) + ([outs[c - 2]] if c > 1 else [])
         one, *others = run_chunk(
-            after(meta, *gate), table, live, sources, pairs, output_weight, c * chunk_spans,
-            low, chunk_spans, span_tokens, feature_shard, cap, gain,
+            after(meta, *gate), table, live, sources, pairs, output_weight, firsts[c],
+            low, chunk_spans[c], span_tokens, feature_shard, cap, gain,
         )
         kept.append(one)
         received.append([shift(other, "sub", 1) for other in others])
@@ -405,7 +406,7 @@
     total(chunks - 1)
     mixed = jnp.zeros((token_count, feature_shard), bf16)
     for c, out in enumerate(outs):
-        mixed = lax.dynamic_update_slice(after(mixed, meta), out, (c * chunk_tokens, 0))
+        mixed = lax.dynamic_update_slice(after(mixed, meta), out, (firsts[c] * span_tokens, 0))
     return mixed
 
 

time: 87.2 us -> 85.5 us (0.981)
  waiting for transfers between devices: 33.7 us -> 29 us
  local copies, waits for them, and re-layouts: 8.91 us -> 10.8 us
  starting transfers between devices: 22.3 us -> 24.1 us
    ppermute x24, waiting for transfers between devices: 26.7 us -> 19.1 us  [shift(): lax.ppermute(value, axis, [(i, (i + by) % size) for i in range(size)])]
    ppermute x5, waiting for transfers between devices: 6.93 us -> 9.95 us  [swap(): return lax.ppermute(value, axis, [(i, i ^ by) for i in range(size)])]
    ppermute x24, starting transfers between devices: 12.3 us -> 15.3 us  [shift(): lax.ppermute(value, axis, [(i, (i + by) % size) for i in range(size)])]
    unnamed x21 -> x23, local copies, waits for them, and re-layouts: 6.42 us -> 8.17 us
    ppermute x5, starting transfers between devices: 10.1 us -> 8.79 us  [swap(): return lax.ppermute(value, axis, [(i, i ^ by) for i in range(size)])]
  transfers between devices with their start and end apart: 29 -> 29, of which waited for: 19 -> 19; matrix products, arithmetic and copies ran while one was open for 3% -> 4% of each run, Pallas kernels for 21% -> 22%
where the time goes in v6:
time: 85.5 us; the launch traced here: 85.1 us
  waiting for transfers between devices  29 us (34%)
  starting transfers between devices  24.1 us (28%)
  Pallas kernels  18.5 us (22%)
  local copies, waits for them, and re-layouts  10.8 us (13%)
  other arithmetic  2.43 us (3%)
    ppermute x24, waiting for transfers between devices, shift(): lax.ppermute(value, axis, [(i, (i + by) % size) for i in range(size)])  19.1 us
    ppermute x24, starting transfers between devices, shift(): lax.ppermute(value, axis, [(i, (i + by) % size) for i in range(size)])  15.3 us
    pallas_call x4, Pallas kernels, run_chunk(): pl.pallas_call(functools.partial(chunk_kernel, first=first, low=low, span...  10.9 us
    ppermute x5, waiting for transfers between devices, swap(): return lax.ppermute(value, axis, [(i, i ^ by) for i in range(size)])  9.95 us
    ppermute x5, starting transfers between devices, swap(): return lax.ppermute(value, axis, [(i, i ^ by) for i in range(size)])  8.79 us
    unnamed x23, local copies, waits for them, and re-layouts  8.17 us
    pallas_call x1, Pallas kernels, project_queries(): pl.pallas_call(functools.partial(query_kernel, lows=tuple(lows), gain=gai...  4.21 us
    pallas_call x1, Pallas kernels, encode(): pl.pallas_call(functools.partial(encode_kernel, pieces=pieces, piece=piec...  2.46 us
  transfers between devices with their start and end apart: 29, of which 19 were waited for; matrix products, arithmetic and copies ran while one was open for 4% of the time, Pallas kernels for 22%

profile of v6, /device:TPU:0, one launch (start us, length us, event | category | flops | bytes accessed | tf_op | source)
XLA Modules:
  0.0 85.1 jit_solution(5233167970080113626)
XLA Ops:
  0.0 1.1 %slice.106 = bf16[128,1024]{1,0:T(8,128)(2,1)S(1)} slice(bf16[512,1024]{1,0:T(8,128)(2,1)} %refs_0_.1), slice={[0:128], [0:1024]} | slice | bytes 524288 | tf_op jit(solution)/shard_map/slice | solution.py:342
  1.1 3.0 %collective-permute-start = (bf16[128,1024]{1,0:T(8,128)(2,1)S(1)}, bf16[128,1024]{1,0:T(8,128)(2,1)S(1)}, u32[]{:S(2)}, u32[]{:S(2)}) collective-permute-start(bf16[128,1024]{1,0:T(8,128)(2,1)S(1)} %slice.106), channel_id=1, source_target_pairs={{0,2},{2,0},{1,3},{3,1},{4,6},{6,4},{5,7},{7,5},{8,10},{10,8},{9,1... | collective-permute-start | bytes 786440 | tf_op jit(solution)/shard_map/ppermute | solution.py:22
  4.1 2.2 %copy-done.2 = bf16[16,128,1024]{2,1,0:T(8,128)(2,1)S(1)} copy-done((bf16[16,128,1024]{2,1,0:T(8,128)(2,1)S(1)}, bf16[16,128,1024]{2,1,0:T(8,128)(2,1)}, u32[]{:S(2)}) %copy-start.2) | copy-done | bytes 4194328
  6.3 1.0 %copy-done.3 = bf16[1024,256]{1,0:T(8,128)(2,1)S(1)} copy-done((bf16[1024,256]{1,0:T(8,128)(2,1)S(1)}, bf16[1024,256]{1,0:T(8,128)(2,1)}, u32[]{:S(2)}) %copy-start.3) | copy-done | bytes 524312
  7.4 2.5 %encode.1 = (bf16[2,528,256]{2,1,0:T(8,128)(2,1)S(1)}, bf16[2,528,256]{2,1,0:T(8,128)(2,1)S(1)}) custom-call(s32[3]{0:T(128)S(1)} %pad_add_fusion.2.meta, bf16[16,128,1024]{2,1,0:T(8,128)(2,1)S(1)} %copy-done.2, bf16[1024,256]{1,0:T(8,128)(2,1)S(1)} %copy-done.3), custom_call_target="tpu_custom_call" | custom-call | flops 1073741824 | bytes 4194304 | tf_op jit(solution)/shard_map/encode/pallas_call | solution.py:85
  9.8 0.5 collective-permute-done.refs_0_
  10.4 0.8 copy.11
  11.2 0.8 copy.12
  12.4 1.8 %collective-permute-start.4 = (bf16[528,256]{1,0:T(8,128)(2,1)S(1)}, bf16[528,256]{1,0:T(8,128)(2,1)S(1)}, u32[]{:S(2)}, u32[]{:S(2)}) collective-permute-start(bf16[528,256]{1,0:T(8,128)(2,1)S(1)} %fusion.8), channel_id=1, source_target_pairs={{0,2},{2,0},{1,3},{3,1},{4,6},{6,4},{5,7},{7,5},{8,10},{10,8},{9,1... | collective-permute-start | bytes 811016 | tf_op jit(solution)/shard_map/ppermute | solution.py:22
  14.2 0.7 pad_add_fusion.3
  14.9 1.6 %collective-permute-start.2 = (s32[1,48]{1,0:T(1,128)S(1)}, s32[1,48]{1,0:T(1,128)S(1)}, u32[]{:S(2)}, u32[]{:S(2)}) collective-permute-start(s32[1,48]{1,0:T(1,128)S(1)} %pad_add_fusion.3), channel_id=1, source_target_pairs={{0,4},{4,0},{8,12},{12,8},{1,5},{5,1},{9,13},{13,9},{2,6},{6,2},{1... | collective-permute-start | bytes 584 | tf_op jit(solution)/shard_map/ppermute | solution.py:27
  16.5 2.0 %collective-permute-done.2 = s32[1,48]{1,0:T(1,128)S(1)} collective-permute-done((s32[1,48]{1,0:T(1,128)S(1)}, s32[1,48]{1,0:T(1,128)S(1)}, u32[]{:S(2)}, u32[]{:S(2)}) %collective-permute-start.2) | collective-permute-done | bytes 224 | tf_op jit(solution)/shard_map/ppermute | solution.py:27
  18.5 2.6 %collective-permute-start.3 = (s32[2,48]{1,0:T(2,128)S(1)}, s32[2,48]{1,0:T(2,128)S(1)}, u32[]{:S(2)}, u32[]{:S(2)}) collective-permute-start(s32[2,48]{1,0:T(2,128)S(1)} %pad_add_fusion.1), channel_id=1, source_target_pairs={{0,8},{4,12},{8,0},{12,4},{1,9},{5,13},{9,1},{13,5},{2,10},{6,14},... | collective-permute-start | bytes 1160 | tf_op jit(solution)/shard_map/ppermute | solution.py:27
  21.1 1.9 %collective-permute-done.3 = s32[2,48]{1,0:T(2,128)S(1)} collective-permute-done((s32[2,48]{1,0:T(2,128)S(1)}, s32[2,48]{1,0:T(2,128)S(1)}, u32[]{:S(2)}, u32[]{:S(2)}) %collective-permute-start.3) | collective-permute-done | bytes 416 | tf_op jit(solution)/shard_map/ppermute | solution.py:27
  23.0 1.1 %slice.110 = bf16[256,1024]{1,0:T(8,128)(2,1)S(1)} slice(bf16[512,1024]{1,0:T(8,128)(2,1)} %refs_0_.1), slice={[128:384], [0:1024]} | slice | bytes 1048576 | tf_op jit(solution)/shard_map/slice | solution.py:359
  24.1 0.6 collective-permute-start.10
  24.7 0.9 %route.1 = (bf16[4,32,256]{2,1,0:T(8,128)(2,1)S(1)}, bf16[4,32,256]{2,1,0:T(8,128)(2,1)S(1)}, bf16[4,32,256]{2,1,0:T(8,128)(2,1)S(1)}, bf16[4,32,256]{2,1,0:T(8,128)(2,1)S(1)}) custom-call(s32[3]{0:T(128)S(1)} %pad_add_fusion.2.meta, s32[4,32]{1,0:T(4,128)S(1)} %bitcast.59, bf16[2,528,256]{2,1,0:T(8,128)(2,1)S(1)} %get-tuple-element.55.kept, ...), custom_call_target="tpu_custom_call" | custom-call | flops 1081344 | bytes 811008 | tf_op jit(solution)/shard_map/route/pallas_call | solution.py:140
  25.6 2.0 %collective-permute-start.5 = (bf16[4,32,256]{2,1,0:T(8,128)(2,1)S(1)}, bf16[4,32,256]{2,1,0:T(8,128)(2,1)S(1)}, u32[]{:S(2)}, u32[]{:S(2)}) collective-permute-start(bf16[4,32,256]{2,1,0:T(8,128)(2,1)S(1)} %get-tuple-element.60), channel_id=1, source_target_pairs={{0,4},{4,0},{8,12},{12,8},{1,5},{5,1},{9,13},{13,9},{2,6},{6,2},{1... | collective-permute-start | bytes 196616 | tf_op jit(solution)/shard_map/ppermute | solution.py:27
  27.6 2.6 %collective-permute-start.6 = (bf16[4,32,256]{2,1,0:T(8,128)(2,1)S(1)}, bf16[4,32,256]{2,1,0:T(8,128)(2,1)S(1)}, u32[]{:S(2)}, u32[]{:S(2)}) collective-permute-start(bf16[4,32,256]{2,1,0:T(8,128)(2,1)S(1)} %get-tuple-element.61), channel_id=1, source_target_pairs={{0,8},{4,12},{8,0},{12,4},{1,9},{5,13},{9,1},{13,5},{2,10},{6,14},... | collective-permute-start | bytes 196616 | tf_op jit(solution)/shard_map/ppermute | solution.py:27
  30.4 4.2 %collective-permute-done.6 = bf16[4,32,256]{2,1,0:T(8,128)(2,1)S(1)} collective-permute-done((bf16[4,32,256]{2,1,0:T(8,128)(2,1)S(1)}, bf16[4,32,256]{2,1,0:T(8,128)(2,1)S(1)}, u32[]{:S(2)}, u32[]{:S(2)}) %collective-permute-start.6) | collective-permute-done | bytes 65568 | tf_op jit(solution)/shard_map/ppermute | solution.py:27
  34.6 1.8 %collective-permute-done.7 = bf16[4,32,256]{2,1,0:T(8,128)(2,1)S(1)} collective-permute-done((bf16[4,32,256]{2,1,0:T(8,128)(2,1)S(1)}, bf16[4,32,256]{2,1,0:T(8,128)(2,1)S(1)}, u32[]{:S(2)}, u32[]{:S(2)}) %collective-permute-start.7) | collective-permute-done | bytes 65568 | tf_op jit(solution)/shard_map/ppermute | solution.py:27
  36.4 0.5 collective-permute-start.9
  36.9 1.2 %collective-permute-start.13 = (bf16[16,32,256]{2,1,0:T(8,128)(2,1)S(1)}, bf16[16,32,256]{2,1,0:T(8,128)(2,1)S(1)}, u32[]{:S(2)}, u32[]{:S(2)}) collective-permute-start(bf16[16,32,256]{2,1,0:T(8,128)(2,1)S(1)} %constant_dynamic-update-slice_fusion.refs_1_.refs_5_), channel_id=1, source_target_pairs={{0,2},{2,0},{1,3},{3,1},{4,6},{6,4},{5,7},{7,5},{8,10},{10,8},{9,1... | collective-permute-start | bytes 786440 | tf_op jit(solution)/shard_map/ppermute | solution.py:22
  38.1 0.6 collective-permute-done.9.refs_1_
  38.7 3.4 %copy-done = bf16[4096,1024]{1,0:T(8,128)(2,1)S(1)} copy-done((bf16[4096,1024]{1,0:T(8,128)(2,1)S(1)}, bf16[4096,1024]{1,0:T(8,128)(2,1)}, u32[]{:S(2)}) %copy-start) | copy-done | bytes 8388632
  42.1 4.2 %queries.1.refs_0_ = bf16[384,1024]{1,0:T(8,128)(2,1)S(1)} custom-call(s32[3]{0:T(128)S(1)} %pad_add_fusion.2.meta, bf16[512,1024]{1,0:T(8,128)(2,1)S(1)} %copy-done.1, bf16[512,1024]{1,0:T(8,128)(2,1)S(1)} %collective-permute-done.8.near_ref.refs_1_, bf16[128,1024]{1,0:T(8,128)(2,1)S(1)} %collective-permute-done.refs_0_, ...), custom_call_target="tpu_custom_call" | custom-call | flops 3221225472 | bytes 3145728 | tf_op jit(solution)/shard_map/queries/pallas_call | solution.py:195
  46.6 1.2 %collective-permute-start.17 = (bf16[128,1024]{1,0:T(8,128)(2,1)S(1)}, bf16[128,1024]{1,0:T(8,128)(2,1)S(1)}, u32[]{:S(2)}, u32[]{:S(2)}) collective-permute-start(bf16[128,1024]{1,0:T(8,128)(2,1)S(1)} %slice.112), channel_id=1, source_target_pairs={{0,2},{2,0},{1,3},{3,1},{4,6},{6,4},{5,7},{7,5},{8,10},{10,8},{9,1... | collective-permute-start | bytes 786440 | tf_op jit(solution)/shard_map/ppermute | solution.py:22
  48.0 2.4 %chunk.4 = (bf16[2,128,1024]{2,1,0:T(8,128)(2,1)S(1)}, bf16[2,64,1024]{2,1,0:T(8,128)(2,1)S(1)}, bf16[2,64,1024]{2,1,0:T(8,128)(2,1)S(1)}) custom-call(s32[3]{0:T(128)S(1)} %pad_add_fusion.2.meta, s32[4,32]{1,0:T(4,128)S(1)} %bitcast.60, s32[4,16]{1,0:T(4,128)S(1)} %slice.109.live, bf16[384,1024]{1,0:T(8,128)(2,1)S(1)} %queries.1.refs_0_, ...), custom_call_target="tpu_custom_call" | custom-call | flops 1207959552 | bytes 262144 | tf_op jit(solution)/shard_map/chunk/pallas_call | solution.py:273
  50.9 4.4 %collective-permute-done.17.refs_2_ = bf16[128,1024]{1,0:T(8,128)(2,1)S(1)} collective-permute-done((bf16[128,1024]{1,0:T(8,128)(2,1)S(1)}, bf16[128,1024]{1,0:T(8,128)(2,1)S(1)}, u32[]{:S(2)}, u32[]{:S(2)}) %collective-permute-start.17) | collective-permute-done | bytes 262176 | tf_op jit(solution)/shard_map/ppermute | solution.py:22
  55.4 1.2 %collective-permute-start.20 = (bf16[128,1024]{1,0:T(8,128)(2,1)S(1)}, bf16[128,1024]{1,0:T(8,128)(2,1)S(1)}, u32[]{:S(2)}, u32[]{:S(2)}) collective-permute-start(bf16[128,1024]{1,0:T(8,128)(2,1)S(1)} %pad_maximum_fusion), channel_id=1, source_target_pairs={{0,2},{2,0},{1,3},{3,1},{4,6},{6,4},{5,7},{7,5},{8,10},{10,8},{9,1... | collective-permute-start | bytes 786440 | tf_op jit(solution)/shard_map/ppermute | solution.py:22
  56.6 2.4 %chunk.5 = (bf16[2,128,1024]{2,1,0:T(8,128)(2,1)S(1)}, bf16[2,64,1024]{2,1,0:T(8,128)(2,1)S(1)}, bf16[2,64,1024]{2,1,0:T(8,128)(2,1)S(1)}) custom-call(s32[3]{0:T(128)S(1)} %pad_add_fusion.2.meta, s32[4,32]{1,0:T(4,128)S(1)} %bitcast.61, s32[4,16]{1,0:T(4,128)S(1)} %slice.109.live, bf16[384,1024]{1,0:T(8,128)(2,1)S(1)} %queries.1.refs_0_, ...), custom_call_target="tpu_custom_call" | custom-call | flops 1207959552 | bytes 262144 | tf_op jit(solution)/shard_map/chunk/pallas_call | solution.py:273
  59.0 0.6 collective-permute-start.18
  59.7 1.0 %collective-permute-done.18 = bf16[2,64,1024]{2,1,0:T(8,128)(2,1)S(1)} collective-permute-done((bf16[2,64,1024]{2,1,0:T(8,128)(2,1)S(1)}, bf16[2,64,1024]{2,1,0:T(8,128)(2,1)S(1)}, u32[]{:S(2)}, u32[]{:S(2)}) %collective-permute-start.18) | collective-permute-done | bytes 262176 | tf_op jit(solution)/shard_map/ppermute | solution.py:22
  60.7 0.4 collective-permute-done.19
  61.2 1.0 %collective-permute-start.23 = (bf16[128,1024]{1,0:T(8,128)(2,1)S(1)}, bf16[128,1024]{1,0:T(8,128)(2,1)S(1)}, u32[]{:S(2)}, u32[]{:S(2)}) collective-permute-start(bf16[128,1024]{1,0:T(8,128)(2,1)S(1)} %pad_maximum_fusion.1), channel_id=1, source_target_pairs={{0,2},{2,0},{1,3},{3,1},{4,6},{6,4},{5,7},{7,5},{8,10},{10,8},{9,1... | collective-permute-start | bytes 786440 | tf_op jit(solution)/shard_map/ppermute | solution.py:22
  62.2 1.1 %collective-permute-done.20 = bf16[128,1024]{1,0:T(8,128)(2,1)S(1)} collective-permute-done((bf16[128,1024]{1,0:T(8,128)(2,1)S(1)}, bf16[128,1024]{1,0:T(8,128)(2,1)S(1)}, u32[]{:S(2)}, u32[]{:S(2)}) %collective-permute-start.20) | collective-permute-done | bytes 262176 | tf_op jit(solution)/shard_map/ppermute | solution.py:22
  63.5 2.4 %chunk.6 = (bf16[2,128,1024]{2,1,0:T(8,128)(2,1)S(1)}, bf16[2,64,1024]{2,1,0:T(8,128)(2,1)S(1)}, bf16[2,64,1024]{2,1,0:T(8,128)(2,1)S(1)}) custom-call(s32[3]{0:T(128)S(1)} %pad_add_fusion.2.meta, s32[4,32]{1,0:T(4,128)S(1)} %bitcast.62, s32[4,16]{1,0:T(4,128)S(1)} %slice.109.live, bf16[384,1024]{1,0:T(8,128)(2,1)S(1)} %queries.1.refs_0_, ...), custom_call_target="tpu_custom_call" | custom-call | flops 1207959552 | bytes 262144 | tf_op jit(solution)/shard_map/chunk/pallas_call | solution.py:273
  66.0 0.5 collective-permute-start.22
  66.5 1.0 %collective-permute-done.21 = bf16[2,64,1024]{2,1,0:T(8,128)(2,1)S(1)} collective-permute-done((bf16[2,64,1024]{2,1,0:T(8,128)(2,1)S(1)}, bf16[2,64,1024]{2,1,0:T(8,128)(2,1)S(1)}, u32[]{:S(2)}, u32[]{:S(2)}) %collective-permute-start.21) | collective-permute-done | bytes 262176 | tf_op jit(solution)/shard_map/ppermute | solution.py:22
  68.0 1.2 %collective-permute-start.27 = (bf16[128,1024]{1,0:T(8,128)(2,1)S(1)}, bf16[128,1024]{1,0:T(8,128)(2,1)S(1)}, u32[]{:S(2)}, u32[]{:S(2)}) collective-permute-start(bf16[128,1024]{1,0:T(8,128)(2,1)S(1)} %pad_maximum_fusion.2), channel_id=1, source_target_pairs={{0,2},{2,0},{1,3},{3,1},{4,6},{6,4},{5,7},{7,5},{8,10},{10,8},{9,1... | collective-permute-start | bytes 786440 | tf_op jit(solution)/shard_map/ppermute | solution.py:22
  69.2 0.7 collective-permute-done.23
  70.0 3.8 %chunk.7 = (bf16[2,128,1024]{2,1,0:T(8,128)(2,1)S(1)}, bf16[2,64,1024]{2,1,0:T(8,128)(2,1)S(1)}, bf16[2,64,1024]{2,1,0:T(8,128)(2,1)S(1)}) custom-call(s32[3]{0:T(128)S(1)} %pad_add_fusion.2.meta, s32[4,32]{1,0:T(4,128)S(1)} %bitcast.63, s32[4,16]{1,0:T(4,128)S(1)} %slice.109.live, bf16[512,1024]{1,0:T(8,128)(2,1)S(1)} %copy-done.1, ...), custom_call_target="tpu_custom_call" | custom-call | flops 1207959552 | bytes 262144 | tf_op jit(solution)/shard_map/chunk/pallas_call | solution.py:273
  73.9 0.5 collective-permute-start.26
  74.4 1.0 %collective-permute-done.25 = bf16[2,64,1024]{2,1,0:T(8,128)(2,1)S(1)} collective-permute-done((bf16[2,64,1024]{2,1,0:T(8,128)(2,1)S(1)}, bf16[2,64,1024]{2,1,0:T(8,128)(2,1)S(1)}, u32[]{:S(2)}, u32[]{:S(2)}) %collective-permute-start.25) | collective-permute-done | bytes 262176 | tf_op jit(solution)/shard_map/ppermute | solution.py:22
  75.4 0.4 collective-permute-done.26
  75.9 0.9 %collective-permute-start.28 = (bf16[128,1024]{1,0:T(8,128)(2,1)S(1)}, bf16[128,1024]{1,0:T(8,128)(2,1)S(1)}, u32[]{:S(2)}, u32[]{:S(2)}) collective-permute-start(bf16[128,1024]{1,0:T(8,128)(2,1)S(1)} %pad_maximum_fusion.3), channel_id=1, source_target_pairs={{0,2},{2,0},{1,3},{3,1},{4,6},{6,4},{5,7},{7,5},{8,10},{10,8},{9,1... | collective-permute-start | bytes 786440 | tf_op jit(solution)/shard_map/ppermute | solution.py:22
  77.0 7.3 %collective-permute-done.28 = bf16[128,1024]{1,0:T(8,128)(2,1)S(1)} collective-permute-done((bf16[128,1024]{1,0:T(8,128)(2,1)S(1)}, bf16[128,1024]{1,0:T(8,128)(2,1)S(1)}, u32[]{:S(2)}, u32[]{:S(2)}) %collective-permute-start.28) | collective-permute-done | bytes 262176 | tf_op jit(solution)/shard_map/ppermute | solution.py:22
  84.3 0.8 fusion.10
  (75 shorter events, 3.4 us)
Async XLA Ops:
  0.0 38.7 %copy-start.1 = (bf16[512,1024]{1,0:T(8,128)(2,1)S(1)}, bf16[512,1024]{1,0:T(8,128)(2,1)}, u32[]{:S(2)}) copy-start(bf16[512,1024]{1,0:T(8,128)(2,1)} %refs_0_.1) | copy-start | bytes 3145732
  1.1 9.3 %collective-permute-start = (bf16[128,1024]{1,0:T(8,128)(2,1)S(1)}, bf16[128,1024]{1,0:T(8,128)(2,1)S(1)}, u32[]{:S(2)}, u32[]{:S(2)}) collective-permute-start(bf16[128,1024]{1,0:T(8,128)(2,1)S(1)} %slice.106), channel_id=1, source_target_pairs={{0,2},{2,0},{1,3},{3,1},{4,6},{6,4},{5,7},{7,5},{8,10},{10,8},{9,1... | collective-permute-start | bytes 786440 | tf_op jit(solution)/shard_map/ppermute | solution.py:22
  4.1 2.2 %copy-start.2 = (bf16[16,128,1024]{2,1,0:T(8,128)(2,1)S(1)}, bf16[16,128,1024]{2,1,0:T(8,128)(2,1)}, u32[]{:S(2)}) copy-start(bf16[16,128,1024]{2,1,0:T(8,128)(2,1)} %x_ref.1) | copy-start | bytes 12582916
  6.3 1.0 %copy-start.3 = (bf16[1024,256]{1,0:T(8,128)(2,1)S(1)}, bf16[1024,256]{1,0:T(8,128)(2,1)}, u32[]{:S(2)}) copy-start(bf16[1024,256]{1,0:T(8,128)(2,1)} %w_ref.1) | copy-start | bytes 1572868
  10.4 1.9 %collective-permute-start.1 = (bf16[2,528,256]{2,1,0:T(8,128)(2,1)S(1)}, bf16[2,528,256]{2,1,0:T(8,128)(2,1)S(1)}, u32[]{:S(2)}, u32[]{:S(2)}) collective-permute-start(bf16[2,528,256]{2,1,0:T(8,128)(2,1)S(1)} %get-tuple-element.57), channel_id=1, source_target_pairs={{0,1},{1,0},{2,3},{3,2},{4,5},{5,4},{6,7},{7,6},{8,9},{9,8},{10,11... | collective-permute-start | bytes 1622024 | tf_op jit(solution)/shard_map/ppermute | solution.py:22
  12.3 35.6 %slice-start = ((s8[8388608]{0:T(1024)(128)(4,1)}), s8[4194304]{0:T(1024)(128)(4,1)S(1)}, s32[]{:S(2)}) async-start(s8[8388608]{0:T(1024)(128)(4,1)} %bitcast.55), calls=%async_computation | async-start | bytes 8388608
  12.4 10.6 %collective-permute-start.4 = (bf16[528,256]{1,0:T(8,128)(2,1)S(1)}, bf16[528,256]{1,0:T(8,128)(2,1)S(1)}, u32[]{:S(2)}, u32[]{:S(2)}) collective-permute-start(bf16[528,256]{1,0:T(8,128)(2,1)S(1)} %fusion.8), channel_id=1, source_target_pairs={{0,2},{2,0},{1,3},{3,1},{4,6},{6,4},{5,7},{7,5},{8,10},{10,8},{9,1... | collective-permute-start | bytes 811016 | tf_op jit(solution)/shard_map/ppermute | solution.py:22
  14.9 3.5 %collective-permute-start.2 = (s32[1,48]{1,0:T(1,128)S(1)}, s32[1,48]{1,0:T(1,128)S(1)}, u32[]{:S(2)}, u32[]{:S(2)}) collective-permute-start(s32[1,48]{1,0:T(1,128)S(1)} %pad_add_fusion.3), channel_id=1, source_target_pairs={{0,4},{4,0},{8,12},{12,8},{1,5},{5,1},{9,13},{13,9},{2,6},{6,2},{1... | collective-permute-start | bytes 584 | tf_op jit(solution)/shard_map/ppermute | solution.py:27
  18.5 4.5 %collective-permute-start.3 = (s32[2,48]{1,0:T(2,128)S(1)}, s32[2,48]{1,0:T(2,128)S(1)}, u32[]{:S(2)}, u32[]{:S(2)}) collective-permute-start(s32[2,48]{1,0:T(2,128)S(1)} %pad_add_fusion.1), channel_id=1, source_target_pairs={{0,8},{4,12},{8,0},{12,4},{1,9},{5,13},{9,1},{13,5},{2,10},{6,14},... | collective-permute-start | bytes 1160 | tf_op jit(solution)/shard_map/ppermute | solution.py:27
  24.1 12.3 %collective-permute-start.10 = (bf16[256,1024]{1,0:T(8,128)(2,1)S(1)}, bf16[256,1024]{1,0:T(8,128)(2,1)S(1)}, u32[]{:S(2)}, u32[]{:S(2)}) collective-permute-start(bf16[256,1024]{1,0:T(8,128)(2,1)S(1)} %slice.110), channel_id=1, source_target_pairs={{0,2},{2,0},{1,3},{3,1},{4,6},{6,4},{5,7},{7,5},{8,10},{10,8},{9,1... | collective-permute-start | bytes 1572872 | tf_op jit(solution)/shard_map/ppermute | solution.py:22
  24.7 14.0 %collective-permute-start.8 = (bf16[512,1024]{1,0:T(8,128)(2,1)}, bf16[512,1024]{1,0:T(8,128)(2,1)S(1)}, u32[]{:S(2)}, u32[]{:S(2)}) collective-permute-start(bf16[512,1024]{1,0:T(8,128)(2,1)} %refs_0_.1), channel_id=1, source_target_pairs={{0,1},{1,0},{2,3},{3,2},{4,5},{5,4},{6,7},{7,6},{8,9},{9,8},{10,11... | collective-permute-start | bytes 3145736 | tf_op jit(solution)/shard_map/ppermute | solution.py:22
  25.6 4.7 %collective-permute-start.5 = (bf16[4,32,256]{2,1,0:T(8,128)(2,1)S(1)}, bf16[4,32,256]{2,1,0:T(8,128)(2,1)S(1)}, u32[]{:S(2)}, u32[]{:S(2)}) collective-permute-start(bf16[4,32,256]{2,1,0:T(8,128)(2,1)S(1)} %get-tuple-element.60), channel_id=1, source_target_pairs={{0,4},{4,0},{8,12},{12,8},{1,5},{5,1},{9,13},{13,9},{2,6},{6,2},{1... | collective-permute-start | bytes 196616 | tf_op jit(solution)/shard_map/ppermute | solution.py:27
  27.6 7.0 %collective-permute-start.6 = (bf16[4,32,256]{2,1,0:T(8,128)(2,1)S(1)}, bf16[4,32,256]{2,1,0:T(8,128)(2,1)S(1)}, u32[]{:S(2)}, u32[]{:S(2)}) collective-permute-start(bf16[4,32,256]{2,1,0:T(8,128)(2,1)S(1)} %get-tuple-element.61), channel_id=1, source_target_pairs={{0,8},{4,12},{8,0},{12,4},{1,9},{5,13},{9,1},{13,5},{2,10},{6,14},... | collective-permute-start | bytes 196616 | tf_op jit(solution)/shard_map/ppermute | solution.py:27
  30.2 6.1 %collective-permute-start.7 = (bf16[4,32,256]{2,1,0:T(8,128)(2,1)S(1)}, bf16[4,32,256]{2,1,0:T(8,128)(2,1)S(1)}, u32[]{:S(2)}, u32[]{:S(2)}) collective-permute-start(bf16[4,32,256]{2,1,0:T(8,128)(2,1)S(1)} %get-tuple-element.62), channel_id=1, source_target_pairs={{0,12},{4,8},{8,4},{12,0},{1,13},{5,9},{9,5},{13,1},{2,14},{6,10},... | collective-permute-start | bytes 196616 | tf_op jit(solution)/shard_map/ppermute | solution.py:27
  36.3 11.6 %slice-start.1 = ((s8[8388608]{0:T(1024)(128)(4,1)}), s8[4194304]{0:T(1024)(128)(4,1)S(1)}, s32[]{:S(2)}) async-start(s8[8388608]{0:T(1024)(128)(4,1)} %bitcast.55), calls=%async_computation.1 | async-start | bytes 8388608
  36.4 2.4 %collective-permute-start.11 = (bf16[256,1024]{1,0:T(8,128)(2,1)S(1)}, bf16[256,1024]{1,0:T(8,128)(2,1)S(1)}, u32[]{:S(2)}, u32[]{:S(2)}) collective-permute-start(bf16[256,1024]{1,0:T(8,128)(2,1)S(1)} %collective-permute-done.10.refs_2_), channel_id=1, source_target_pairs={{0,1},{1,0},{2,3},{3,2},{4,5},{5,4},{6,7},{7,6},{8,9},{9,8},{10,11... | collective-permute-start | bytes 1572872 | tf_op jit(solution)/shard_map/ppermute | solution.py:22
  36.4 2.3 %collective-permute-start.9 = (bf16[128,1024]{1,0:T(8,128)(2,1)S(1)}, bf16[128,1024]{1,0:T(8,128)(2,1)S(1)}, u32[]{:S(2)}, u32[]{:S(2)}) collective-permute-start(bf16[128,1024]{1,0:T(8,128)(2,1)S(1)} %collective-permute-done.refs_0_), channel_id=1, source_target_pairs={{0,1},{1,0},{2,3},{3,2},{4,5},{5,4},{6,7},{7,6},{8,9},{9,8},{10,11... | collective-permute-start | bytes 786440 | tf_op jit(solution)/shard_map/ppermute | solution.py:22
  36.9 9.4 %collective-permute-start.13 = (bf16[16,32,256]{2,1,0:T(8,128)(2,1)S(1)}, bf16[16,32,256]{2,1,0:T(8,128)(2,1)S(1)}, u32[]{:S(2)}, u32[]{:S(2)}) collective-permute-start(bf16[16,32,256]{2,1,0:T(8,128)(2,1)S(1)} %constant_dynamic-update-slice_fusion.refs_1_.refs_5_), channel_id=1, source_target_pairs={{0,2},{2,0},{1,3},{3,1},{4,6},{6,4},{5,7},{7,5},{8,10},{10,8},{9,1... | collective-permute-start | bytes 786440 | tf_op jit(solution)/shard_map/ppermute | solution.py:22
  38.1 9.8 %collective-permute-start.12 = (bf16[16,32,256]{2,1,0:T(8,128)(2,1)S(1)}, bf16[16,32,256]{2,1,0:T(8,128)(2,1)S(1)}, u32[]{:S(2)}, u32[]{:S(2)}) collective-permute-start(bf16[16,32,256]{2,1,0:T(8,128)(2,1)S(1)} %constant_dynamic-update-slice_fusion.refs_1_.refs_5_), channel_id=1, source_target_pairs={{0,1},{1,0},{2,3},{3,2},{4,5},{5,4},{6,7},{7,6},{8,9},{9,8},{10,11... | collective-permute-start | bytes 786440 | tf_op jit(solution)/shard_map/ppermute | solution.py:22
  38.7 3.4 %copy-start = (bf16[4096,1024]{1,0:T(8,128)(2,1)S(1)}, bf16[4096,1024]{1,0:T(8,128)(2,1)}, u32[]{:S(2)}) copy-start(bf16[4096,1024]{1,0:T(8,128)(2,1)} %refs_4_.3) | copy-start | bytes 25165828
  46.3 1.6 %collective-permute-start.14 = (bf16[16,32,256]{2,1,0:T(8,128)(2,1)S(1)}, bf16[16,32,256]{2,1,0:T(8,128)(2,1)S(1)}, u32[]{:S(2)}, u32[]{:S(2)}) collective-permute-start(bf16[16,32,256]{2,1,0:T(8,128)(2,1)S(1)} %collective-permute-done.13.refs_3_.refs_7_), channel_id=1, source_target_pairs={{0,1},{1,0},{2,3},{3,2},{4,5},{5,4},{6,7},{7,6},{8,9},{9,8},{10,11... | collective-permute-start | bytes 786440 | tf_op jit(solution)/shard_map/ppermute | solution.py:22
  46.6 8.7 %collective-permute-start.17 = (bf16[128,1024]{1,0:T(8,128)(2,1)S(1)}, bf16[128,1024]{1,0:T(8,128)(2,1)S(1)}, u32[]{:S(2)}, u32[]{:S(2)}) collective-permute-start(bf16[128,1024]{1,0:T(8,128)(2,1)S(1)} %slice.112), channel_id=1, source_target_pairs={{0,2},{2,0},{1,3},{3,1},{4,6},{6,4},{5,7},{7,5},{8,10},{10,8},{9,1... | collective-permute-start | bytes 786440 | tf_op jit(solution)/shard_map/ppermute | solution.py:22
  50.3 5.0 %collective-permute-start.15 = (bf16[2,64,1024]{2,1,0:T(8,128)(2,1)S(1)}, bf16[2,64,1024]{2,1,0:T(8,128)(2,1)S(1)}, u32[]{:S(2)}, u32[]{:S(2)}) collective-permute-start(bf16[2,64,1024]{2,1,0:T(8,128)(2,1)S(1)} %get-tuple-element.73), channel_id=1, source_target_pairs={{0,1},{1,0},{2,3},{3,2},{4,5},{5,4},{6,7},{7,6},{8,9},{9,8},{10,11... | collective-permute-start | bytes 786440 | tf_op jit(solution)/shard_map/ppermute | solution.py:22
  50.5 4.8 %collective-permute-start.16 = (bf16[2,64,1024]{2,1,0:T(8,128)(2,1)S(1)}, bf16[2,64,1024]{2,1,0:T(8,128)(2,1)S(1)}, u32[]{:S(2)}, u32[]{:S(2)}) collective-permute-start(bf16[2,64,1024]{2,1,0:T(8,128)(2,1)S(1)} %get-tuple-element.74), channel_id=1, source_target_pairs={{0,1},{1,0},{2,3},{3,2},{4,5},{5,4},{6,7},{7,6},{8,9},{9,8},{10,11... | collective-permute-start | bytes 786440 | tf_op jit(solution)/shard_map/ppermute | solution.py:22
  55.4 7.8 %collective-permute-start.20 = (bf16[128,1024]{1,0:T(8,128)(2,1)S(1)}, bf16[128,1024]{1,0:T(8,128)(2,1)S(1)}, u32[]{:S(2)}, u32[]{:S(2)}) collective-permute-start(bf16[128,1024]{1,0:T(8,128)(2,1)S(1)} %pad_maximum_fusion), channel_id=1, source_target_pairs={{0,2},{2,0},{1,3},{3,1},{4,6},{6,4},{5,7},{7,5},{8,10},{10,8},{9,1... | collective-permute-start | bytes 786440 | tf_op jit(solution)/shard_map/ppermute | solution.py:22
  56.6 13.4 %collective-permute-start.24 = (bf16[128,1024]{1,0:T(8,128)(2,1)S(1)}, bf16[128,1024]{1,0:T(8,128)(2,1)S(1)}, u32[]{:S(2)}, u32[]{:S(2)}) collective-permute-start(bf16[128,1024]{1,0:T(8,128)(2,1)S(1)} %collective-permute-done.17.refs_2_), channel_id=1, source_target_pairs={{0,1},{1,0},{2,3},{3,2},{4,5},{5,4},{6,7},{7,6},{8,9},{9,8},{10,11... | collective-permute-start | bytes 786440 | tf_op jit(solution)/shard_map/ppermute | solution.py:22
  59.0 1.7 %collective-permute-start.18 = (bf16[2,64,1024]{2,1,0:T(8,128)(2,1)S(1)}, bf16[2,64,1024]{2,1,0:T(8,128)(2,1)S(1)}, u32[]{:S(2)}, u32[]{:S(2)}) collective-permute-start(bf16[2,64,1024]{2,1,0:T(8,128)(2,1)S(1)} %get-tuple-element.80), channel_id=1, source_target_pairs={{0,1},{1,0},{2,3},{3,2},{4,5},{5,4},{6,7},{7,6},{8,9},{9,8},{10,11... | collective-permute-start | bytes 786440 | tf_op jit(solution)/shard_map/ppermute | solution.py:22
  59.6 1.5 %collective-permute-start.19 = (bf16[2,64,1024]{2,1,0:T(8,128)(2,1)S(1)}, bf16[2,64,1024]{2,1,0:T(8,128)(2,1)S(1)}, u32[]{:S(2)}, u32[]{:S(2)}) collective-permute-start(bf16[2,64,1024]{2,1,0:T(8,128)(2,1)S(1)} %get-tuple-element.81), channel_id=1, source_target_pairs={{0,1},{1,0},{2,3},{3,2},{4,5},{5,4},{6,7},{7,6},{8,9},{9,8},{10,11... | collective-permute-start | bytes 786440 | tf_op jit(solution)/shard_map/ppermute | solution.py:22
  59.7 10.3 %slice-start.2 = ((s8[8388608]{0:T(1024)(128)(4,1)}), s8[4194304]{0:T(1024)(128)(4,1)S(1)}, s32[]{:S(2)}) async-start(s8[8388608]{0:T(1024)(128)(4,1)} %bitcast.57), calls=%async_computation.2 | async-start | bytes 8388608
  61.2 8.7 %collective-permute-start.23 = (bf16[128,1024]{1,0:T(8,128)(2,1)S(1)}, bf16[128,1024]{1,0:T(8,128)(2,1)S(1)}, u32[]{:S(2)}, u32[]{:S(2)}) collective-permute-start(bf16[128,1024]{1,0:T(8,128)(2,1)S(1)} %pad_maximum_fusion.1), channel_id=1, source_target_pairs={{0,2},{2,0},{1,3},{3,1},{4,6},{6,4},{5,7},{7,5},{8,10},{10,8},{9,1... | collective-permute-start | bytes 786440 | tf_op jit(solution)/shard_map/ppermute | solution.py:22
  63.5 6.5 %slice-start.3 = ((s8[8388608]{0:T(1024)(128)(4,1)}), s8[4194304]{0:T(1024)(128)(4,1)S(1)}, s32[]{:S(2)}) async-start(s8[8388608]{0:T(1024)(128)(4,1)} %bitcast.57), calls=%async_computation.3 | async-start | bytes 8388608
  65.9 1.6 %collective-permute-start.21 = (bf16[2,64,1024]{2,1,0:T(8,128)(2,1)S(1)}, bf16[2,64,1024]{2,1,0:T(8,128)(2,1)S(1)}, u32[]{:S(2)}, u32[]{:S(2)}) collective-permute-start(bf16[2,64,1024]{2,1,0:T(8,128)(2,1)S(1)} %get-tuple-element.88), channel_id=1, source_target_pairs={{0,1},{1,0},{2,3},{3,2},{4,5},{5,4},{6,7},{7,6},{8,9},{9,8},{10,11... | collective-permute-start | bytes 786440 | tf_op jit(solution)/shard_map/ppermute | solution.py:22
  66.0 1.9 %collective-permute-start.22 = (bf16[2,64,1024]{2,1,0:T(8,128)(2,1)S(1)}, bf16[2,64,1024]{2,1,0:T(8,128)(2,1)S(1)}, u32[]{:S(2)}, u32[]{:S(2)}) collective-permute-start(bf16[2,64,1024]{2,1,0:T(8,128)(2,1)S(1)} %get-tuple-element.89), channel_id=1, source_target_pairs={{0,1},{1,0},{2,3},{3,2},{4,5},{5,4},{6,7},{7,6},{8,9},{9,8},{10,11... | collective-permute-start | bytes 786440 | tf_op jit(solution)/shard_map/ppermute | solution.py:22
  68.0 8.9 %collective-permute-start.27 = (bf16[128,1024]{1,0:T(8,128)(2,1)S(1)}, bf16[128,1024]{1,0:T(8,128)(2,1)S(1)}, u32[]{:S(2)}, u32[]{:S(2)}) collective-permute-start(bf16[128,1024]{1,0:T(8,128)(2,1)S(1)} %pad_maximum_fusion.2), channel_id=1, source_target_pairs={{0,2},{2,0},{1,3},{3,1},{4,6},{6,4},{5,7},{7,5},{8,10},{10,8},{9,1... | collective-permute-start | bytes 786440 | tf_op jit(solution)/shard_map/ppermute | solution.py:22
  73.8 1.6 %collective-permute-start.25 = (bf16[2,64,1024]{2,1,0:T(8,128)(2,1)S(1)}, bf16[2,64,1024]{2,1,0:T(8,128)(2,1)S(1)}, u32[]{:S(2)}, u32[]{:S(2)}) collective-permute-start(bf16[2,64,1024]{2,1,0:T(8,128)(2,1)S(1)} %get-tuple-element.97), channel_id=1, source_target_pairs={{0,1},{1,0},{2,3},{3,2},{4,5},{5,4},{6,7},{7,6},{8,9},{9,8},{10,11... | collective-permute-start | bytes 786440 | tf_op jit(solution)/shard_map/ppermute | solution.py:22
  73.9 1.9 %collective-permute-start.26 = (bf16[2,64,1024]{2,1,0:T(8,128)(2,1)S(1)}, bf16[2,64,1024]{2,1,0:T(8,128)(2,1)S(1)}, u32[]{:S(2)}, u32[]{:S(2)}) collective-permute-start(bf16[2,64,1024]{2,1,0:T(8,128)(2,1)S(1)} %get-tuple-element.98), channel_id=1, source_target_pairs={{0,1},{1,0},{2,3},{3,2},{4,5},{5,4},{6,7},{7,6},{8,9},{9,8},{10,11... | collective-permute-start | bytes 786440 | tf_op jit(solution)/shard_map/ppermute | solution.py:22
  75.9 8.4 %collective-permute-start.28 = (bf16[128,1024]{1,0:T(8,128)(2,1)S(1)}, bf16[128,1024]{1,0:T(8,128)(2,1)S(1)}, u32[]{:S(2)}, u32[]{:S(2)}) collective-permute-start(bf16[128,1024]{1,0:T(8,128)(2,1)S(1)} %pad_maximum_fusion.3), channel_id=1, source_target_pairs={{0,2},{2,0},{1,3},{3,1},{4,6},{6,4},{5,7},{7,5},{8,10},{10,8},{9,1... | collective-permute-start | bytes 786440 | tf_op jit(solution)/shard_map/ppermute | solution.py:22
  77.0 7.3 %copy-start.4 = (bf16[512,1024]{1,0:T(8,128)(2,1)}, bf16[512,1024]{1,0:T(8,128)(2,1)S(1)}, u32[]{:S(2)}) copy-start(bf16[512,1024]{1,0:T(8,128)(2,1)S(1)} %fusion.9) | copy-start | bytes 3145732

commit v7 on v6

--- a/solution.py
+++ b/solution.py
@@ -122,11 +122,11 @@
             picks[d, r] = 0
         seen = jnp.int32(0)
         for q in range(requests):
-            mine = table[d, q] == me
+            mine = table[d, q % 2, q // 2] == me
 
             @pl.when(mine)
             def _(seen=seen, q=q, d=d):
-                picks[d, jnp.minimum(seen, cap - 1)] = table[d, requests + q]
+                picks[d, jnp.minimum(seen, cap - 1)] = table[d, 2 + q % 2, q // 2]
 
             seen = seen + mine.astype(jnp.int32)
         for r in range(cap):
@@ -204,10 +204,11 @@
 
 
 def chunk_kernel(
-    meta, table, live, *refs, first, low, span, heads, size, pieces, cap, requests, gain
+    meta, table, *refs, first, low, spans, span, heads, size, pieces, cap, gain
 ):
-    sources, kvs = refs[: -6 - pieces], refs[-6 - pieces : -6]
-    w_ref, kept_ref, upper_ref, lower_ref, att, pair = refs[-6:]
+    own_end = -4 - spans
+    sources, kvs = refs[: own_end - pieces], refs[own_end - pieces : own_end]
+    w_ref, kept_ref, *sent_refs, att, pair = refs[-4 - spans :]
     me, mp, sub = meta[0], meta[1], meta[2]
     group = pieces // 2
     piece = kvs[0].shape[1]
@@ -221,13 +222,13 @@
         masks = []
         for j in range(2):
             q = 2 * (first + c) + j
-            owner = table[0, q]
+            owner = table[0, j, first + c]
             rank = jnp.int32(0)
             for e in range(q):
-                rank = rank + (table[0, e] == owner).astype(jnp.int32)
+                rank = rank + (table[0, e % 2, e // 2] == owner).astype(jnp.int32)
             away = owner ^ me
             slot = away * cap + rank
-            length = live[away, table[0, requests + q]]
+            length = table[away, 4, table[0, 2 + j, first + c]]
             for p in range(pieces):
                 at = (j * pieces + p) * piece
                 pair[c, at : at + piece, :] = kvs[p][slot]
@@ -249,50 +250,45 @@
         for h in range(heads):
             att[rows, h * size : (h + 1) * size] = attended[h * span : (h + 1) * span]
     width = kept_ref.shape[2]
-    half = tokens // 2
     for ds in (1, 0):
         for dm in range(group):
             block = lax.rem(mp + dm, group) * 2 + lax.rem(sub + ds, 2)
             w = w_ref[:, pl.ds(pl.multiple_of(block * width, width), width)]
             result = jnp.dot(att[...], w, preferred_element_type=f32).astype(bf16)
             if ds:
-                upper_ref[dm] = result[:half]
-                lower_ref[dm] = result[half:]
+                for c, sent_ref in enumerate(sent_refs):
+                    sent_ref[dm] = result[c * span : (c + 1) * span]
             else:
                 kept_ref[dm] = result
 
 
-def run_chunk(meta, table, live, sources, pairs, weight, first, low, spans, span, out_width, cap, gain):
+def run_chunk(meta, table, sources, pairs, weight, first, low, spans, span, out_width, cap, gain):
     width = weight.shape[0]
     tokens = spans * span
     pieces = len(pairs)
     piece, pair_width = pairs[0].shape[1:]
     size = pair_width // 2
     group = pieces // 2
-    requests = table.shape[1] // 2
     return pl.pallas_call(
         functools.partial(
-            chunk_kernel, first=first, low=low, span=span, heads=width // size, size=size,
-            pieces=pieces, cap=cap, requests=requests, gain=gain,
+            chunk_kernel, first=first, low=low, spans=spans, span=span, heads=width // size, size=size,
+            pieces=pieces, cap=cap, gain=gain,
         ),
-        in_specs=[SMEM] * 3 + [VMEM] * (1 + pieces + len(sources)),
-        out_specs=[VMEM] * 3,
+        in_specs=[SMEM] * 2 + [VMEM] * (1 + pieces + len(sources)),
+        out_specs=[VMEM] * (1 + spans),
         scratch_shapes=[
             pltpu.VMEM((tokens, width), bf16),
             pltpu.VMEM((spans, 2 * pieces * piece, pair_width), bf16),
         ],
-        out_shape=[
-            jax.ShapeDtypeStruct((group, tokens, out_width), bf16),
-            jax.ShapeDtypeStruct((group, tokens // 2, out_width), bf16),
-            jax.ShapeDtypeStruct((group, tokens // 2, out_width), bf16),
-        ],
+        out_shape=[jax.ShapeDtypeStruct((group, tokens, out_width), bf16)]
+        + [jax.ShapeDtypeStruct((group, span, out_width), bf16)] * spans,
         compiler_params=params(),
         cost_estimate=cost(
             4 * tokens * width * out_width * group + 4 * tokens * width * 2 * pieces * piece,
             2 * tokens * width, 2 * tokens * width * 2,
         ),
         name="chunk",
-    )(meta, table, live, *sources, *pairs, weight)
+    )(meta, table, *sources, *pairs, weight)
 
 
 def shards(
@@ -318,8 +314,9 @@
     requests = 2 * spans_here
     cap = max(2, (requests + row_count - 1) // row_count)
     last_spans = spans_here // 4
-    chunk_spans = [last_spans] * 4
-    firsts = [c * last_spans for c in range(4)]
+    middle_spans = (spans_here - last_spans) // 2
+    chunk_spans = [spans_here - last_spans - middle_spans, middle_spans, last_spans]
+    firsts = [0, chunk_spans[0], spans_here - last_spans]
     chunks = len(chunk_spans)
     first_tokens = token_count // 4
     last_low = token_count - last_spans * span_tokens
@@ -341,10 +338,11 @@
 
     fars_first = cross(hidden[:first_tokens])
 
+    lanes = max(spans_here, count)
+    widen = lambda t: jnp.pad(t, ((0, 0), (0, lanes - t.shape[1])))
     table = jnp.concatenate(
-        [neighbour_owner.reshape(1, -1), neighbour_slot.reshape(1, -1), neighbour_length.reshape(1, -1)],
-        axis=1,
-    )
+        [widen(neighbour_owner.T), widen(neighbour_slot.T), widen(neighbour_length[None])], axis=0
+    )[None]
 
     kept, sent = encode(meta, neighbour_states, encoder_weight, pieces)
     received = shift(after(sent, *fars_first), "sub", 1)
@@ -354,9 +352,8 @@
     table = after(table, *leaving)
     while table.shape[0] < row_count:
         table = jnp.concatenate([table, swap(table, "rows", table.shape[0])], axis=0)
-    table, live = table[:, : 2 * requests], table[:, 2 * requests :]
-
-    fars_second = cross(after(hidden, table, *crossed)[first_tokens:last_low])
+
+    fars_second = cross(after(hidden[first_tokens:last_low], table, *crossed))
 
     routed = route(meta, table, kept, received, crossed, cap, features, count, requests)
     encoded = jnp.concatenate(
@@ -370,12 +367,12 @@
         after(meta, encoded), hidden, near,
         [with_near(fars_first, encoded), with_near(fars_second, encoded)], query_weight, gain,
     )
-    fars_last = cross(after(hidden, encoded)[last_low:])
+    fars_last = cross(after(hidden[last_low:], encoded))
     pairs += with_near(fars, queries)
 
     def join(c, *earlier):
         got = after(received[c], *earlier)
-        step = chunk_spans[c] * span_tokens // 2
+        step = span_tokens
         parts = [
             [add(kept[c][dm, i * step : (i + 1) * step], g[dm]) for i, g in enumerate(got)]
             for dm in range(1, group)
@@ -394,7 +391,7 @@
             sources = [hidden, near, *with_near(fars_last, *leaving[0]), query_weight]
         gate = (leaving[c - 1] if c else []) + ([outs[c - 2]] if c > 1 else [])
         one, *others = run_chunk(
-            after(meta, *gate), table, live, sources, pairs, output_weight, firsts[c],
+            after(meta, *gate), table, sources, pairs, output_weight, firsts[c],
             low, chunk_spans[c], span_tokens, feature_shard, cap, gain,
         )
         kept.append(one)

time: 85.5 us -> 81.1 us (0.949)
  local copies, waits for them, and re-layouts: 10.8 us -> 6.27 us
  starting transfers between devices: 24.1 us -> 25.8 us
  waiting for transfers between devices: 29 us -> 27.6 us
    unnamed x23 -> x19, local copies, waits for them, and re-layouts: 8.17 us -> 3.69 us
    ppermute x5, waiting for transfers between devices: 9.95 us -> 7.15 us  [swap(): return lax.ppermute(value, axis, [(i, i ^ by) for i in range(size)])]
    ppermute x24 -> x23, starting transfers between devices: 15.3 us -> 16.7 us  [shift(): lax.ppermute(value, axis, [(i, (i + by) % size) for i in range(size)])]
    ppermute x24 -> x23, waiting for transfers between devices: 19.1 us -> 20.4 us  [shift(): lax.ppermute(value, axis, [(i, (i + by) % size) for i in range(size)])]
    pallas_call x4 -> x3, Pallas kernels: 10.9 us -> 10.6 us  [run_chunk(): pl.pallas_call(functools.partial(chunk_kernel, first=first, low=low, span...]
    slice x4 -> x2, local copies, waits for them, and re-layouts: 2.22 us -> 2.38 us  [the longest x1 1.23 us: shards(): fars_second = cross(after(hidden[first_tokens:last_low], table, *crossed))]
  transfers between devices with their start and end apart: 29 -> 28, of which waited for: 19 -> 17; matrix products, arithmetic and copies ran while one was open for 4% -> 4% of each run, Pallas kernels for 22% -> 23%
where the time goes in v7:
time: 81.1 us; the launch traced here: 80.9 us
  waiting for transfers between devices  27.6 us (34%)
  starting transfers between devices  25.8 us (32%)
  Pallas kernels  18.4 us (23%)
  local copies, waits for them, and re-layouts  6.27 us (8%)
  other arithmetic  2.55 us (3%)
    ppermute x23, waiting for transfers between devices, shift(): lax.ppermute(value, axis, [(i, (i + by) % size) for i in range(size)])  20.4 us
    ppermute x23, starting transfers between devices, shift(): lax.ppermute(value, axis, [(i, (i + by) % size) for i in range(size)])  16.7 us
    pallas_call x3, Pallas kernels, run_chunk(): pl.pallas_call(functools.partial(chunk_kernel, first=first, low=low, span...  10.6 us
    ppermute x5, starting transfers between devices, swap(): return lax.ppermute(value, axis, [(i, i ^ by) for i in range(size)])  9.11 us
    ppermute x5, waiting for transfers between devices, swap(): return lax.ppermute(value, axis, [(i, i ^ by) for i in range(size)])  7.15 us
    pallas_call x1, Pallas kernels, project_queries(): pl.pallas_call(functools.partial(query_kernel, lows=tuple(lows), gain=gai...  4.18 us
    unnamed x19, local copies, waits for them, and re-layouts  3.69 us
    pallas_call x1, Pallas kernels, encode(): pl.pallas_call(functools.partial(encode_kernel, pieces=pieces, piece=piec...  2.46 us
  transfers between devices with their start and end apart: 28, of which 17 were waited for; matrix products, arithmetic and copies ran while one was open for 4% of the time, Pallas kernels for 23%

profile of v7, /device:TPU:0, one launch (start us, length us, event | category | flops | bytes accessed | tf_op | source)
XLA Modules:
  0.0 80.9 jit_solution(15470838298225517927)
XLA Ops:
  0.0 1.2 %fusion.20 = (bf16[128,1024]{1,0:T(8,128)(2,1)S(1)}, bf16[128,1024]{1,0:T(8,128)(2,1)S(1)}) fusion(bf16[512,1024]{1,0:T(8,128)(2,1)} %refs_0_.1), kind=kLoop, calls=%fused_computation.54 | loop fusion | bytes 1048576 | tf_op jit(solution)/shard_map/slice | solution.py:370
  1.2 3.0 %collective-permute-start = (bf16[128,1024]{1,0:T(8,128)(2,1)S(1)}, bf16[128,1024]{1,0:T(8,128)(2,1)S(1)}, u32[]{:S(2)}, u32[]{:S(2)}) collective-permute-start(bf16[128,1024]{1,0:T(8,128)(2,1)S(1)} %get-tuple-element.98), channel_id=1, source_target_pairs={{0,2},{2,0},{1,3},{3,1},{4,6},{6,4},{5,7},{7,5},{8,10},{10,8},{9,1... | collective-permute-start | bytes 786440 | tf_op jit(solution)/shard_map/ppermute | solution.py:22
  4.2 2.3 %copy-done.2 = bf16[16,128,1024]{2,1,0:T(8,128)(2,1)S(1)} copy-done((bf16[16,128,1024]{2,1,0:T(8,128)(2,1)S(1)}, bf16[16,128,1024]{2,1,0:T(8,128)(2,1)}, u32[]{:S(2)}) %copy-start.2) | copy-done | bytes 4194328
  6.6 1.3 %copy-done.3 = bf16[1024,256]{1,0:T(8,128)(2,1)S(1)} copy-done((bf16[1024,256]{1,0:T(8,128)(2,1)S(1)}, bf16[1024,256]{1,0:T(8,128)(2,1)}, u32[]{:S(2)}) %copy-start.3) | copy-done | bytes 524312
  7.9 2.5 %encode.1 = (bf16[2,528,256]{2,1,0:T(8,128)(2,1)S(1)}, bf16[2,528,256]{2,1,0:T(8,128)(2,1)S(1)}) custom-call(s32[3]{0:T(128)S(1)} %pad_add_fusion.2.meta, bf16[16,128,1024]{2,1,0:T(8,128)(2,1)S(1)} %copy-done.2, bf16[1024,256]{1,0:T(8,128)(2,1)S(1)} %copy-done.3), custom_call_target="tpu_custom_call" | custom-call | flops 1073741824 | bytes 4194304 | tf_op jit(solution)/shard_map/encode/pallas_call | solution.py:85
  10.5 1.2 %slice.99 = bf16[256,1024]{1,0:T(8,128)(2,1)S(1)} slice(bf16[512,1024]{1,0:T(8,128)(2,1)} %refs_0_.1), slice={[128:384], [0:1024]} | slice | bytes 1048576 | tf_op jit(solution)/shard_map/slice | solution.py:356
  11.7 0.8 fusion.18
  12.6 1.9 %collective-permute-start.2 = (s32[1,5,16]{2,1,0:T(8,128)S(1)}, s32[1,5,16]{2,1,0:T(8,128)S(1)}, u32[]{:S(2)}, u32[]{:S(2)}) collective-permute-start(s32[1,5,16]{2,1,0:T(8,128)S(1)} %fusion.18), channel_id=1, source_target_pairs={{0,4},{4,0},{8,12},{12,8},{1,5},{5,1},{9,13},{13,9},{2,6},{6,2},{1... | collective-permute-start | bytes 968 | tf_op jit(solution)/shard_map/ppermute | solution.py:27
  14.4 1.5 %collective-permute-start.4 = (bf16[528,256]{1,0:T(8,128)(2,1)S(1)}, bf16[528,256]{1,0:T(8,128)(2,1)S(1)}, u32[]{:S(2)}, u32[]{:S(2)}) collective-permute-start(bf16[528,256]{1,0:T(8,128)(2,1)S(1)} %fusion.7), channel_id=1, source_target_pairs={{0,2},{2,0},{1,3},{3,1},{4,6},{6,4},{5,7},{7,5},{8,10},{10,8},{9,1... | collective-permute-start | bytes 811016 | tf_op jit(solution)/shard_map/ppermute | solution.py:22
  15.9 0.4 collective-permute-done.2
  16.2 2.8 %collective-permute-start.3 = (s32[2,5,16]{2,1,0:T(8,128)S(1)}, s32[2,5,16]{2,1,0:T(8,128)S(1)}, u32[]{:S(2)}, u32[]{:S(2)}) collective-permute-start(s32[2,5,16]{2,1,0:T(8,128)S(1)} %pad_add_fusion), channel_id=1, source_target_pairs={{0,8},{4,12},{8,0},{12,4},{1,9},{5,13},{9,1},{13,5},{2,10},{6,14},... | collective-permute-start | bytes 1928 | tf_op jit(solution)/shard_map/ppermute | solution.py:27
  19.0 1.7 %collective-permute-done.3 = s32[2,5,16]{2,1,0:T(8,128)S(1)} collective-permute-done((s32[2,5,16]{2,1,0:T(8,128)S(1)}, s32[2,5,16]{2,1,0:T(8,128)S(1)}, u32[]{:S(2)}, u32[]{:S(2)}) %collective-permute-start.3) | collective-permute-done | bytes 672 | tf_op jit(solution)/shard_map/ppermute | solution.py:27
  20.8 2.1 %collective-permute-done.4.refs_0_ = bf16[528,256]{1,0:T(8,128)(2,1)S(1)} collective-permute-done((bf16[528,256]{1,0:T(8,128)(2,1)S(1)}, bf16[528,256]{1,0:T(8,128)(2,1)S(1)}, u32[]{:S(2)}, u32[]{:S(2)}) %collective-permute-start.4) | collective-permute-done | bytes 270368 | tf_op jit(solution)/shard_map/ppermute | solution.py:22
  22.8 1.5 %collective-permute-start.10 = (bf16[256,1024]{1,0:T(8,128)(2,1)S(1)}, bf16[256,1024]{1,0:T(8,128)(2,1)S(1)}, u32[]{:S(2)}, u32[]{:S(2)}) collective-permute-start(bf16[256,1024]{1,0:T(8,128)(2,1)S(1)} %slice.99), channel_id=1, source_target_pairs={{0,2},{2,0},{1,3},{3,1},{4,6},{6,4},{5,7},{7,5},{8,10},{10,8},{9,1... | collective-permute-start | bytes 1572872 | tf_op jit(solution)/shard_map/ppermute | solution.py:22
  24.3 1.2 %route.1 = (bf16[4,32,256]{2,1,0:T(8,128)(2,1)S(1)}, bf16[4,32,256]{2,1,0:T(8,128)(2,1)S(1)}, bf16[4,32,256]{2,1,0:T(8,128)(2,1)S(1)}, bf16[4,32,256]{2,1,0:T(8,128)(2,1)S(1)}) custom-call(s32[3]{0:T(128)S(1)} %pad_add_fusion.2.meta, s32[4,5,16]{2,1,0:T(8,128)S(1)} %constant_dynamic-update-slice_fusion.table, ...), custom_call_target="tpu_custom_call" | custom-call | flops 1081344 | bytes 811008 | tf_op jit(solution)/shard_map/route/pallas_call | solution.py:140
  25.5 0.5 collective-permute-start.5
  26.0 2.6 %collective-permute-start.6 = (bf16[4,32,256]{2,1,0:T(8,128)(2,1)S(1)}, bf16[4,32,256]{2,1,0:T(8,128)(2,1)S(1)}, u32[]{:S(2)}, u32[]{:S(2)}) collective-permute-start(bf16[4,32,256]{2,1,0:T(8,128)(2,1)S(1)} %get-tuple-element.57), channel_id=1, source_target_pairs={{0,8},{4,12},{8,0},{12,4},{1,9},{5,13},{9,1},{13,5},{2,10},{6,14},... | collective-permute-start | bytes 196616 | tf_op jit(solution)/shard_map/ppermute | solution.py:27
  28.6 1.3 %collective-permute-start.7 = (bf16[4,32,256]{2,1,0:T(8,128)(2,1)S(1)}, bf16[4,32,256]{2,1,0:T(8,128)(2,1)S(1)}, u32[]{:S(2)}, u32[]{:S(2)}) collective-permute-start(bf16[4,32,256]{2,1,0:T(8,128)(2,1)S(1)} %get-tuple-element.58), channel_id=1, source_target_pairs={{0,12},{4,8},{8,4},{12,0},{1,13},{5,9},{9,5},{13,1},{2,14},{6,10},... | collective-permute-start | bytes 196616 | tf_op jit(solution)/shard_map/ppermute | solution.py:27
  30.0 1.5 %collective-permute-done.5 = bf16[4,32,256]{2,1,0:T(8,128)(2,1)S(1)} collective-permute-done((bf16[4,32,256]{2,1,0:T(8,128)(2,1)S(1)}, bf16[4,32,256]{2,1,0:T(8,128)(2,1)S(1)}, u32[]{:S(2)}, u32[]{:S(2)}) %collective-permute-start.5) | collective-permute-done | bytes 65568 | tf_op jit(solution)/shard_map/ppermute | solution.py:27
  31.5 3.5 %collective-permute-done.7 = bf16[4,32,256]{2,1,0:T(8,128)(2,1)S(1)} collective-permute-done((bf16[4,32,256]{2,1,0:T(8,128)(2,1)S(1)}, bf16[4,32,256]{2,1,0:T(8,128)(2,1)S(1)}, u32[]{:S(2)}, u32[]{:S(2)}) %collective-permute-start.7) | collective-permute-done | bytes 65568 | tf_op jit(solution)/shard_map/ppermute | solution.py:27
  35.1 0.8 %collective-permute-done.10.refs_2_ = bf16[256,1024]{1,0:T(8,128)(2,1)S(1)} collective-permute-done((bf16[256,1024]{1,0:T(8,128)(2,1)S(1)}, bf16[256,1024]{1,0:T(8,128)(2,1)S(1)}, u32[]{:S(2)}, u32[]{:S(2)}) %collective-permute-start.10) | collective-permute-done | bytes 524320 | tf_op jit(solution)/shard_map/ppermute | solution.py:22
  35.9 0.5 collective-permute-start.9
  36.4 1.5 %collective-permute-start.13 = (bf16[16,32,256]{2,1,0:T(8,128)(2,1)S(1)}, bf16[16,32,256]{2,1,0:T(8,128)(2,1)S(1)}, u32[]{:S(2)}, u32[]{:S(2)}) collective-permute-start(bf16[16,32,256]{2,1,0:T(8,128)(2,1)S(1)} %constant_dynamic-update-slice_fusion.3.refs_1_.refs_5_), channel_id=1, source_target_pairs={{0,2},{2,0},{1,3},{3,1},{4,6},{6,4},{5,7},{7,5},{8,10},{10,8},{9,1... | collective-permute-start | bytes 786440 | tf_op jit(solution)/shard_map/ppermute | solution.py:22
  37.9 0.2 collective-permute-done.9.refs_1_
  38.2 4.2 %queries.1.refs_0_ = bf16[384,1024]{1,0:T(8,128)(2,1)S(1)} custom-call(s32[3]{0:T(128)S(1)} %pad_add_fusion.2.meta, bf16[512,1024]{1,0:T(8,128)(2,1)S(1)} %copy-done.1, bf16[512,1024]{1,0:T(8,128)(2,1)S(1)} %collective-permute-done.8.near_ref.refs_1_, bf16[128,1024]{1,0:T(8,128)(2,1)S(1)} %collective-permute-done.refs_0_, ...), custom_call_target="tpu_custom_call" | custom-call | flops 3221225472 | bytes 3145728 | tf_op jit(solution)/shard_map/queries/pallas_call | solution.py:195
  42.4 2.2 %collective-permute-done.13.refs_3_.refs_7_ = bf16[16,32,256]{2,1,0:T(8,128)(2,1)S(1)} collective-permute-done((bf16[16,32,256]{2,1,0:T(8,128)(2,1)S(1)}, bf16[16,32,256]{2,1,0:T(8,128)(2,1)S(1)}, u32[]{:S(2)}, u32[]{:S(2)}) %collective-permute-start.13) | collective-permute-done | bytes 262176 | tf_op jit(solution)/shard_map/ppermute | solution.py:22
  44.6 1.5 %collective-permute-start.18 = (bf16[128,1024]{1,0:T(8,128)(2,1)S(1)}, bf16[128,1024]{1,0:T(8,128)(2,1)S(1)}, u32[]{:S(2)}, u32[]{:S(2)}) collective-permute-start(bf16[128,1024]{1,0:T(8,128)(2,1)S(1)} %get-tuple-element.72), channel_id=1, source_target_pairs={{0,2},{2,0},{1,3},{3,1},{4,6},{6,4},{5,7},{7,5},{8,10},{10,8},{9,1... | collective-permute-start | bytes 786440 | tf_op jit(solution)/shard_map/ppermute | solution.py:22
  46.2 3.3 %chunk.3 = (bf16[2,192,1024]{2,1,0:T(8,128)(2,1)S(1)}, bf16[2,64,1024]{2,1,0:T(8,128)(2,1)S(1)}, bf16[2,64,1024]{2,1,0:T(8,128)(2,1)S(1)}, bf16[2,64,1024]{2,1,0:T(8,128)(2,1)S(1)}) custom-call(s32[3]{0:T(128)S(1)} %pad_add_fusion.2.meta, s32[4,5,16]{2,1,0:T(8,128)S(1)} %constant_dynamic-update-slice_fusion.table, bf16[384,1024]{1,0:T(8,128)(2,1)S(1)} %queries.1.refs_0_, ...), custom_call_target="tpu_custom_call" | custom-call | flops 1811939328 | bytes 393216 | tf_op jit(solution)/shard_map/chunk/pallas_call | solution.py:272
  49.5 0.3 collective-permute-start.15
  49.8 0.3 collective-permute-start.16
  50.1 0.2 collective-permute-start.17
  50.3 3.0 %collective-permute-done.18.refs_2_ = bf16[128,1024]{1,0:T(8,128)(2,1)S(1)} collective-permute-done((bf16[128,1024]{1,0:T(8,128)(2,1)S(1)}, bf16[128,1024]{1,0:T(8,128)(2,1)S(1)}, u32[]{:S(2)}, u32[]{:S(2)}) %collective-permute-start.18) | collective-permute-done | bytes 262176 | tf_op jit(solution)/shard_map/ppermute | solution.py:22
  53.5 1.6 %collective-permute-start.22 = (bf16[192,1024]{1,0:T(8,128)(2,1)S(1)}, bf16[192,1024]{1,0:T(8,128)(2,1)S(1)}, u32[]{:S(2)}, u32[]{:S(2)}) collective-permute-start(bf16[192,1024]{1,0:T(8,128)(2,1)S(1)} %pad_maximum_fusion), channel_id=1, source_target_pairs={{0,2},{2,0},{1,3},{3,1},{4,6},{6,4},{5,7},{7,5},{8,10},{10,8},{9,1... | collective-permute-start | bytes 1179656 | tf_op jit(solution)/shard_map/ppermute | solution.py:22
  55.1 3.3 %chunk.4 = (bf16[2,192,1024]{2,1,0:T(8,128)(2,1)S(1)}, bf16[2,64,1024]{2,1,0:T(8,128)(2,1)S(1)}, bf16[2,64,1024]{2,1,0:T(8,128)(2,1)S(1)}, bf16[2,64,1024]{2,1,0:T(8,128)(2,1)S(1)}) custom-call(s32[3]{0:T(128)S(1)} %pad_add_fusion.2.meta, s32[4,5,16]{2,1,0:T(8,128)S(1)} %constant_dynamic-update-slice_fusion.table, bf16[384,1024]{1,0:T(8,128)(2,1)S(1)} %queries.1.refs_0_, ...), custom_call_target="tpu_custom_call" | custom-call | flops 1811939328 | bytes 393216 | tf_op jit(solution)/shard_map/chunk/pallas_call | solution.py:272
  58.4 0.6 collective-permute-start.19
  59.1 0.4 collective-permute-start.21
  59.6 0.6 collective-permute-done.19
  60.2 0.4 collective-permute-done.20
  60.5 0.4 collective-permute-done.21
  61.1 0.6 collective-permute-start.26
  61.7 2.9 %collective-permute-done.22 = bf16[192,1024]{1,0:T(8,128)(2,1)S(1)} collective-permute-done((bf16[192,1024]{1,0:T(8,128)(2,1)S(1)}, bf16[192,1024]{1,0:T(8,128)(2,1)S(1)}, u32[]{:S(2)}, u32[]{:S(2)}) %collective-permute-start.22) | collective-permute-done | bytes 393248 | tf_op jit(solution)/shard_map/ppermute | solution.py:22
  64.9 4.0 %chunk.5 = (bf16[2,128,1024]{2,1,0:T(8,128)(2,1)S(1)}, bf16[2,64,1024]{2,1,0:T(8,128)(2,1)S(1)}, bf16[2,64,1024]{2,1,0:T(8,128)(2,1)S(1)}) custom-call(s32[3]{0:T(128)S(1)} %pad_add_fusion.2.meta, s32[4,5,16]{2,1,0:T(8,128)S(1)} %constant_dynamic-update-slice_fusion.table, bf16[512,1024]{1,0:T(8,128)(2,1)S(1)} %copy-done.1, ...), custom_call_target="tpu_custom_call" | custom-call | flops 1207959552 | bytes 262144 | tf_op jit(solution)/shard_map/chunk/pallas_call | solution.py:272
  69.0 0.5 collective-permute-start.25
  69.5 1.0 %collective-permute-done.24 = bf16[2,64,1024]{2,1,0:T(8,128)(2,1)S(1)} collective-permute-done((bf16[2,64,1024]{2,1,0:T(8,128)(2,1)S(1)}, bf16[2,64,1024]{2,1,0:T(8,128)(2,1)S(1)}, u32[]{:S(2)}, u32[]{:S(2)}) %collective-permute-start.24) | collective-permute-done | bytes 262176 | tf_op jit(solution)/shard_map/ppermute | solution.py:22
  70.5 0.4 collective-permute-done.25
  71.0 2.5 %collective-permute-start.27 = (bf16[128,1024]{1,0:T(8,128)(2,1)S(1)}, bf16[128,1024]{1,0:T(8,128)(2,1)S(1)}, u32[]{:S(2)}, u32[]{:S(2)}) collective-permute-start(bf16[128,1024]{1,0:T(8,128)(2,1)S(1)} %pad_maximum_fusion.2), channel_id=1, source_target_pairs={{0,2},{2,0},{1,3},{3,1},{4,6},{6,4},{5,7},{7,5},{8,10},{10,8},{9,1... | collective-permute-start | bytes 786440 | tf_op jit(solution)/shard_map/ppermute | solution.py:22
  73.8 6.4 %collective-permute-done.27 = bf16[128,1024]{1,0:T(8,128)(2,1)S(1)} collective-permute-done((bf16[128,1024]{1,0:T(8,128)(2,1)S(1)}, bf16[128,1024]{1,0:T(8,128)(2,1)S(1)}, u32[]{:S(2)}, u32[]{:S(2)}) %collective-permute-start.27) | collective-permute-done | bytes 262176 | tf_op jit(solution)/shard_map/ppermute | solution.py:22
  80.1 0.8 %fusion.8 = bf16[512,1024]{1,0:T(8,128)(2,1)} fusion(bf16[512,1024]{1,0:T(8,128)(2,1)} %copy-done.4, bf16[128,1024]{1,0:T(8,128)(2,1)S(1)} %collective-permute-done.27, bf16[2,128,1024]{2,1,0:T(8,128)(2,1)S(1)} %get-tuple-element.88, bf16[64,1024]{1,0:T(8,128)(2,1)S(1)} %slice_bitcast_fusion.1, bf16[64,1024]{1,0:T(8,128)(2,1)S(1)} %slice_bitcast_fusion.2), kind=kLoop, calls=%fused_computation.14 | loop fusion | flops 1179648 | bytes 1048576 | tf_op jit(solution)/shard_map/dynamic_update_slice | solution.py:406
  (60 shorter events, 1.5 us)
Async XLA Ops:
  0.0 38.2 %copy-start.1 = (bf16[512,1024]{1,0:T(8,128)(2,1)S(1)}, bf16[512,1024]{1,0:T(8,128)(2,1)}, u32[]{:S(2)}) copy-start(bf16[512,1024]{1,0:T(8,128)(2,1)} %refs_0_.1) | copy-start | bytes 3145732
  1.2 9.3 %collective-permute-start = (bf16[128,1024]{1,0:T(8,128)(2,1)S(1)}, bf16[128,1024]{1,0:T(8,128)(2,1)S(1)}, u32[]{:S(2)}, u32[]{:S(2)}) collective-permute-start(bf16[128,1024]{1,0:T(8,128)(2,1)S(1)} %get-tuple-element.98), channel_id=1, source_target_pairs={{0,2},{2,0},{1,3},{3,1},{4,6},{6,4},{5,7},{7,5},{8,10},{10,8},{9,1... | collective-permute-start | bytes 786440 | tf_op jit(solution)/shard_map/ppermute | solution.py:22
  4.2 34.0 %copy-start = (bf16[4096,1024]{1,0:T(8,128)(2,1)S(1)}, bf16[4096,1024]{1,0:T(8,128)(2,1)}, u32[]{:S(2)}) copy-start(bf16[4096,1024]{1,0:T(8,128)(2,1)} %refs_4_.3) | copy-start | bytes 25165828
  4.2 2.3 %copy-start.2 = (bf16[16,128,1024]{2,1,0:T(8,128)(2,1)S(1)}, bf16[16,128,1024]{2,1,0:T(8,128)(2,1)}, u32[]{:S(2)}) copy-start(bf16[16,128,1024]{2,1,0:T(8,128)(2,1)} %x_ref.1) | copy-start | bytes 12582916
  6.6 1.3 %copy-start.3 = (bf16[1024,256]{1,0:T(8,128)(2,1)S(1)}, bf16[1024,256]{1,0:T(8,128)(2,1)}, u32[]{:S(2)}) copy-start(bf16[1024,256]{1,0:T(8,128)(2,1)} %w_ref.1) | copy-start | bytes 1572868
  10.3 35.8 %slice-start = ((s8[8388608]{0:T(1024)(128)(4,1)}), s8[4194304]{0:T(1024)(128)(4,1)S(1)}, s32[]{:S(2)}) async-start(s8[8388608]{0:T(1024)(128)(4,1)} %bitcast.54), calls=%async_computation | async-start | bytes 8388608
  10.5 2.0 %collective-permute-start.1 = (bf16[2,528,256]{2,1,0:T(8,128)(2,1)S(1)}, bf16[2,528,256]{2,1,0:T(8,128)(2,1)S(1)}, u32[]{:S(2)}, u32[]{:S(2)}) collective-permute-start(bf16[2,528,256]{2,1,0:T(8,128)(2,1)S(1)} %get-tuple-element.53), channel_id=1, source_target_pairs={{0,1},{1,0},{2,3},{3,2},{4,5},{5,4},{6,7},{7,6},{8,9},{9,8},{10,11... | collective-permute-start | bytes 1622024 | tf_op jit(solution)/shard_map/ppermute | solution.py:22
  12.6 3.7 %collective-permute-start.2 = (s32[1,5,16]{2,1,0:T(8,128)S(1)}, s32[1,5,16]{2,1,0:T(8,128)S(1)}, u32[]{:S(2)}, u32[]{:S(2)}) collective-permute-start(s32[1,5,16]{2,1,0:T(8,128)S(1)} %fusion.18), channel_id=1, source_target_pairs={{0,4},{4,0},{8,12},{12,8},{1,5},{5,1},{9,13},{13,9},{2,6},{6,2},{1... | collective-permute-start | bytes 968 | tf_op jit(solution)/shard_map/ppermute | solution.py:27
  14.4 8.4 %collective-permute-start.4 = (bf16[528,256]{1,0:T(8,128)(2,1)S(1)}, bf16[528,256]{1,0:T(8,128)(2,1)S(1)}, u32[]{:S(2)}, u32[]{:S(2)}) collective-permute-start(bf16[528,256]{1,0:T(8,128)(2,1)S(1)} %fusion.7), channel_id=1, source_target_pairs={{0,2},{2,0},{1,3},{3,1},{4,6},{6,4},{5,7},{7,5},{8,10},{10,8},{9,1... | collective-permute-start | bytes 811016 | tf_op jit(solution)/shard_map/ppermute | solution.py:22
  16.2 4.5 %collective-permute-start.3 = (s32[2,5,16]{2,1,0:T(8,128)S(1)}, s32[2,5,16]{2,1,0:T(8,128)S(1)}, u32[]{:S(2)}, u32[]{:S(2)}) collective-permute-start(s32[2,5,16]{2,1,0:T(8,128)S(1)} %pad_add_fusion), channel_id=1, source_target_pairs={{0,8},{4,12},{8,0},{12,4},{1,9},{5,13},{9,1},{13,5},{2,10},{6,14},... | collective-permute-start | bytes 1928 | tf_op jit(solution)/shard_map/ppermute | solution.py:27
  22.8 13.0 %collective-permute-start.10 = (bf16[256,1024]{1,0:T(8,128)(2,1)S(1)}, bf16[256,1024]{1,0:T(8,128)(2,1)S(1)}, u32[]{:S(2)}, u32[]{:S(2)}) collective-permute-start(bf16[256,1024]{1,0:T(8,128)(2,1)S(1)} %slice.99), channel_id=1, source_target_pairs={{0,2},{2,0},{1,3},{3,1},{4,6},{6,4},{5,7},{7,5},{8,10},{10,8},{9,1... | collective-permute-start | bytes 1572872 | tf_op jit(solution)/shard_map/ppermute | solution.py:22
  24.3 13.8 %collective-permute-start.8 = (bf16[512,1024]{1,0:T(8,128)(2,1)}, bf16[512,1024]{1,0:T(8,128)(2,1)S(1)}, u32[]{:S(2)}, u32[]{:S(2)}) collective-permute-start(bf16[512,1024]{1,0:T(8,128)(2,1)} %refs_0_.1), channel_id=1, source_target_pairs={{0,1},{1,0},{2,3},{3,2},{4,5},{5,4},{6,7},{7,6},{8,9},{9,8},{10,11... | collective-permute-start | bytes 3145736 | tf_op jit(solution)/shard_map/ppermute | solution.py:22
  25.5 6.0 %collective-permute-start.5 = (bf16[4,32,256]{2,1,0:T(8,128)(2,1)S(1)}, bf16[4,32,256]{2,1,0:T(8,128)(2,1)S(1)}, u32[]{:S(2)}, u32[]{:S(2)}) collective-permute-start(bf16[4,32,256]{2,1,0:T(8,128)(2,1)S(1)} %get-tuple-element.56), channel_id=1, source_target_pairs={{0,4},{4,0},{8,12},{12,8},{1,5},{5,1},{9,13},{13,9},{2,6},{6,2},{1... | collective-permute-start | bytes 196616 | tf_op jit(solution)/shard_map/ppermute | solution.py:27
  26.0 5.5 %collective-permute-start.6 = (bf16[4,32,256]{2,1,0:T(8,128)(2,1)S(1)}, bf16[4,32,256]{2,1,0:T(8,128)(2,1)S(1)}, u32[]{:S(2)}, u32[]{:S(2)}) collective-permute-start(bf16[4,32,256]{2,1,0:T(8,128)(2,1)S(1)} %get-tuple-element.57), channel_id=1, source_target_pairs={{0,8},{4,12},{8,0},{12,4},{1,9},{5,13},{9,1},{13,5},{2,10},{6,14},... | collective-permute-start | bytes 196616 | tf_op jit(solution)/shard_map/ppermute | solution.py:27
  28.6 6.4 %collective-permute-start.7 = (bf16[4,32,256]{2,1,0:T(8,128)(2,1)S(1)}, bf16[4,32,256]{2,1,0:T(8,128)(2,1)S(1)}, u32[]{:S(2)}, u32[]{:S(2)}) collective-permute-start(bf16[4,32,256]{2,1,0:T(8,128)(2,1)S(1)} %get-tuple-element.58), channel_id=1, source_target_pairs={{0,12},{4,8},{8,4},{12,0},{1,13},{5,9},{9,5},{13,1},{2,14},{6,10},... | collective-permute-start | bytes 196616 | tf_op jit(solution)/shard_map/ppermute | solution.py:27
  35.0 11.1 %slice-start.1 = ((s8[8388608]{0:T(1024)(128)(4,1)}), s8[4194304]{0:T(1024)(128)(4,1)S(1)}, s32[]{:S(2)}) async-start(s8[8388608]{0:T(1024)(128)(4,1)} %bitcast.54), calls=%async_computation.1 | async-start | bytes 8388608
  35.9 2.3 %collective-permute-start.11 = (bf16[256,1024]{1,0:T(8,128)(2,1)S(1)}, bf16[256,1024]{1,0:T(8,128)(2,1)S(1)}, u32[]{:S(2)}, u32[]{:S(2)}) collective-permute-start(bf16[256,1024]{1,0:T(8,128)(2,1)S(1)} %collective-permute-done.10.refs_2_), channel_id=1, source_target_pairs={{0,1},{1,0},{2,3},{3,2},{4,5},{5,4},{6,7},{7,6},{8,9},{9,8},{10,11... | collective-permute-start | bytes 1572872 | tf_op jit(solution)/shard_map/ppermute | solution.py:22
  35.9 2.3 %collective-permute-start.9 = (bf16[128,1024]{1,0:T(8,128)(2,1)S(1)}, bf16[128,1024]{1,0:T(8,128)(2,1)S(1)}, u32[]{:S(2)}, u32[]{:S(2)}) collective-permute-start(bf16[128,1024]{1,0:T(8,128)(2,1)S(1)} %collective-permute-done.refs_0_), channel_id=1, source_target_pairs={{0,1},{1,0},{2,3},{3,2},{4,5},{5,4},{6,7},{7,6},{8,9},{9,8},{10,11... | collective-permute-start | bytes 786440 | tf_op jit(solution)/shard_map/ppermute | solution.py:22
  36.4 8.2 %collective-permute-start.13 = (bf16[16,32,256]{2,1,0:T(8,128)(2,1)S(1)}, bf16[16,32,256]{2,1,0:T(8,128)(2,1)S(1)}, u32[]{:S(2)}, u32[]{:S(2)}) collective-permute-start(bf16[16,32,256]{2,1,0:T(8,128)(2,1)S(1)} %constant_dynamic-update-slice_fusion.3.refs_1_.refs_5_), channel_id=1, source_target_pairs={{0,2},{2,0},{1,3},{3,1},{4,6},{6,4},{5,7},{7,5},{8,10},{10,8},{9,1... | collective-permute-start | bytes 786440 | tf_op jit(solution)/shard_map/ppermute | solution.py:22
  37.9 8.2 %collective-permute-start.12 = (bf16[16,32,256]{2,1,0:T(8,128)(2,1)S(1)}, bf16[16,32,256]{2,1,0:T(8,128)(2,1)S(1)}, u32[]{:S(2)}, u32[]{:S(2)}) collective-permute-start(bf16[16,32,256]{2,1,0:T(8,128)(2,1)S(1)} %constant_dynamic-update-slice_fusion.3.refs_1_.refs_5_), channel_id=1, source_target_pairs={{0,1},{1,0},{2,3},{3,2},{4,5},{5,4},{6,7},{7,6},{8,9},{9,8},{10,11... | collective-permute-start | bytes 786440 | tf_op jit(solution)/shard_map/ppermute | solution.py:22
  44.6 1.5 %collective-permute-start.14 = (bf16[16,32,256]{2,1,0:T(8,128)(2,1)S(1)}, bf16[16,32,256]{2,1,0:T(8,128)(2,1)S(1)}, u32[]{:S(2)}, u32[]{:S(2)}) collective-permute-start(bf16[16,32,256]{2,1,0:T(8,128)(2,1)S(1)} %collective-permute-done.13.refs_3_.refs_7_), channel_id=1, source_target_pairs={{0,1},{1,0},{2,3},{3,2},{4,5},{5,4},{6,7},{7,6},{8,9},{9,8},{10,11... | collective-permute-start | bytes 786440 | tf_op jit(solution)/shard_map/ppermute | solution.py:22
  44.6 8.7 %collective-permute-start.18 = (bf16[128,1024]{1,0:T(8,128)(2,1)S(1)}, bf16[128,1024]{1,0:T(8,128)(2,1)S(1)}, u32[]{:S(2)}, u32[]{:S(2)}) collective-permute-start(bf16[128,1024]{1,0:T(8,128)(2,1)S(1)} %get-tuple-element.72), channel_id=1, source_target_pairs={{0,2},{2,0},{1,3},{3,1},{4,6},{6,4},{5,7},{7,5},{8,10},{10,8},{9,1... | collective-permute-start | bytes 786440 | tf_op jit(solution)/shard_map/ppermute | solution.py:22
  49.5 3.8 %collective-permute-start.15 = (bf16[2,64,1024]{2,1,0:T(8,128)(2,1)S(1)}, bf16[2,64,1024]{2,1,0:T(8,128)(2,1)S(1)}, u32[]{:S(2)}, u32[]{:S(2)}) collective-permute-start(bf16[2,64,1024]{2,1,0:T(8,128)(2,1)S(1)} %get-tuple-element.69), channel_id=1, source_target_pairs={{0,1},{1,0},{2,3},{3,2},{4,5},{5,4},{6,7},{7,6},{8,9},{9,8},{10,11... | collective-permute-start | bytes 786440 | tf_op jit(solution)/shard_map/ppermute | solution.py:22
  49.8 3.6 %collective-permute-start.16 = (bf16[2,64,1024]{2,1,0:T(8,128)(2,1)S(1)}, bf16[2,64,1024]{2,1,0:T(8,128)(2,1)S(1)}, u32[]{:S(2)}, u32[]{:S(2)}) collective-permute-start(bf16[2,64,1024]{2,1,0:T(8,128)(2,1)S(1)} %get-tuple-element.70), channel_id=1, source_target_pairs={{0,1},{1,0},{2,3},{3,2},{4,5},{5,4},{6,7},{7,6},{8,9},{9,8},{10,11... | collective-permute-start | bytes 786440 | tf_op jit(solution)/shard_map/ppermute | solution.py:22
  50.1 3.3 %collective-permute-start.17 = (bf16[2,64,1024]{2,1,0:T(8,128)(2,1)S(1)}, bf16[2,64,1024]{2,1,0:T(8,128)(2,1)S(1)}, u32[]{:S(2)}, u32[]{:S(2)}) collective-permute-start(bf16[2,64,1024]{2,1,0:T(8,128)(2,1)S(1)} %get-tuple-element.71), channel_id=1, source_target_pairs={{0,1},{1,0},{2,3},{3,2},{4,5},{5,4},{6,7},{7,6},{8,9},{9,8},{10,11... | collective-permute-start | bytes 786440 | tf_op jit(solution)/shard_map/ppermute | solution.py:22
  53.5 11.0 %collective-permute-start.22 = (bf16[192,1024]{1,0:T(8,128)(2,1)S(1)}, bf16[192,1024]{1,0:T(8,128)(2,1)S(1)}, u32[]{:S(2)}, u32[]{:S(2)}) collective-permute-start(bf16[192,1024]{1,0:T(8,128)(2,1)S(1)} %pad_maximum_fusion), channel_id=1, source_target_pairs={{0,2},{2,0},{1,3},{3,1},{4,6},{6,4},{5,7},{7,5},{8,10},{10,8},{9,1... | collective-permute-start | bytes 1179656 | tf_op jit(solution)/shard_map/ppermute | solution.py:22
  55.1 9.8 %collective-permute-start.23 = (bf16[128,1024]{1,0:T(8,128)(2,1)S(1)}, bf16[128,1024]{1,0:T(8,128)(2,1)S(1)}, u32[]{:S(2)}, u32[]{:S(2)}) collective-permute-start(bf16[128,1024]{1,0:T(8,128)(2,1)S(1)} %collective-permute-done.18.refs_2_), channel_id=1, source_target_pairs={{0,1},{1,0},{2,3},{3,2},{4,5},{5,4},{6,7},{7,6},{8,9},{9,8},{10,11... | collective-permute-start | bytes 786440 | tf_op jit(solution)/shard_map/ppermute | solution.py:22
  58.4 1.7 %collective-permute-start.19 = (bf16[2,64,1024]{2,1,0:T(8,128)(2,1)S(1)}, bf16[2,64,1024]{2,1,0:T(8,128)(2,1)S(1)}, u32[]{:S(2)}, u32[]{:S(2)}) collective-permute-start(bf16[2,64,1024]{2,1,0:T(8,128)(2,1)S(1)} %get-tuple-element.78), channel_id=1, source_target_pairs={{0,1},{1,0},{2,3},{3,2},{4,5},{5,4},{6,7},{7,6},{8,9},{9,8},{10,11... | collective-permute-start | bytes 786440 | tf_op jit(solution)/shard_map/ppermute | solution.py:22
  59.0 1.5 %collective-permute-start.20 = (bf16[2,64,1024]{2,1,0:T(8,128)(2,1)S(1)}, bf16[2,64,1024]{2,1,0:T(8,128)(2,1)S(1)}, u32[]{:S(2)}, u32[]{:S(2)}) collective-permute-start(bf16[2,64,1024]{2,1,0:T(8,128)(2,1)S(1)} %get-tuple-element.79), channel_id=1, source_target_pairs={{0,1},{1,0},{2,3},{3,2},{4,5},{5,4},{6,7},{7,6},{8,9},{9,8},{10,11... | collective-permute-start | bytes 786440 | tf_op jit(solution)/shard_map/ppermute | solution.py:22
  59.1 1.8 %collective-permute-start.21 = (bf16[2,64,1024]{2,1,0:T(8,128)(2,1)S(1)}, bf16[2,64,1024]{2,1,0:T(8,128)(2,1)S(1)}, u32[]{:S(2)}, u32[]{:S(2)}) collective-permute-start(bf16[2,64,1024]{2,1,0:T(8,128)(2,1)S(1)} %get-tuple-element.80), channel_id=1, source_target_pairs={{0,1},{1,0},{2,3},{3,2},{4,5},{5,4},{6,7},{7,6},{8,9},{9,8},{10,11... | collective-permute-start | bytes 786440 | tf_op jit(solution)/shard_map/ppermute | solution.py:22
  61.1 12.4 %collective-permute-start.26 = (bf16[192,1024]{1,0:T(8,128)(2,1)S(1)}, bf16[192,1024]{1,0:T(8,128)(2,1)S(1)}, u32[]{:S(2)}, u32[]{:S(2)}) collective-permute-start(bf16[192,1024]{1,0:T(8,128)(2,1)S(1)} %pad_maximum_fusion.1), channel_id=1, source_target_pairs={{0,2},{2,0},{1,3},{3,1},{4,6},{6,4},{5,7},{7,5},{8,10},{10,8},{9,1... | collective-permute-start | bytes 1179656 | tf_op jit(solution)/shard_map/ppermute | solution.py:22
  68.9 1.6 %collective-permute-start.24 = (bf16[2,64,1024]{2,1,0:T(8,128)(2,1)S(1)}, bf16[2,64,1024]{2,1,0:T(8,128)(2,1)S(1)}, u32[]{:S(2)}, u32[]{:S(2)}) collective-permute-start(bf16[2,64,1024]{2,1,0:T(8,128)(2,1)S(1)} %get-tuple-element.89), channel_id=1, source_target_pairs={{0,1},{1,0},{2,3},{3,2},{4,5},{5,4},{6,7},{7,6},{8,9},{9,8},{10,11... | collective-permute-start | bytes 786440 | tf_op jit(solution)/shard_map/ppermute | solution.py:22
  69.0 1.9 %collective-permute-start.25 = (bf16[2,64,1024]{2,1,0:T(8,128)(2,1)S(1)}, bf16[2,64,1024]{2,1,0:T(8,128)(2,1)S(1)}, u32[]{:S(2)}, u32[]{:S(2)}) collective-permute-start(bf16[2,64,1024]{2,1,0:T(8,128)(2,1)S(1)} %get-tuple-element.90), channel_id=1, source_target_pairs={{0,1},{1,0},{2,3},{3,2},{4,5},{5,4},{6,7},{7,6},{8,9},{9,8},{10,11... | collective-permute-start | bytes 786440 | tf_op jit(solution)/shard_map/ppermute | solution.py:22
  71.0 9.2 %collective-permute-start.27 = (bf16[128,1024]{1,0:T(8,128)(2,1)S(1)}, bf16[128,1024]{1,0:T(8,128)(2,1)S(1)}, u32[]{:S(2)}, u32[]{:S(2)}) collective-permute-start(bf16[128,1024]{1,0:T(8,128)(2,1)S(1)} %pad_maximum_fusion.2), channel_id=1, source_target_pairs={{0,2},{2,0},{1,3},{3,1},{4,6},{6,4},{5,7},{7,5},{8,10},{10,8},{9,1... | collective-permute-start | bytes 786440 | tf_op jit(solution)/shard_map/ppermute | solution.py:22
  73.7 6.4 %copy-start.4 = (bf16[512,1024]{1,0:T(8,128)(2,1)}, bf16[512,1024]{1,0:T(8,128)(2,1)S(1)}, u32[]{:S(2)}) copy-start(bf16[512,1024]{1,0:T(8,128)(2,1)S(1)} %fusion.6) | copy-start | bytes 3145732

commit v8 on v7

--- a/solution.py
+++ b/solution.py
@@ -44,36 +44,37 @@
     return down == lax.broadcasted_iota(jnp.int32, (piece, 128), 1)
 
 
-def encode_kernel(meta, x_ref, w_ref, kept_ref, sent_ref, product, squares, *, pieces, piece, count):
-    step = pl.program_id(0)
+def encode_kernel(meta, x_ref, w_ref, kept_ref, sent_ref, product, squares, *, pieces, piece, block):
     mp, sub, size = meta[1], meta[2], pieces // 2
-    block, tokens, width = x_ref.shape
-    x = x_ref[...].reshape(block * tokens, width)
-    product[...] = jnp.dot(x, w_ref[...], preferred_element_type=f32).astype(bf16).reshape(product.shape)
-    xf = x.astype(f32)
-    square = jnp.sum(xf * xf, axis=1, keepdims=True)
+    count, tokens, width = x_ref.shape
     diagonal = diagonal_of(piece)
-    for a in range(pieces):
-        for n in range(block):
-            low = n * tokens + a * piece
-            column = jnp.broadcast_to(square[low : low + piece], (piece, 128))
-            squares[a, pl.ds(step * block + n, 1), :] = jnp.sum(
-                jnp.where(diagonal, column, 0.0), axis=0, keepdims=True
-            )
-    rows = pl.ds(pl.multiple_of(step * block * piece, block * piece), block * piece)
+
+    @pl.loop(0, count // block)
+    def _(step):
+        x = x_ref[pl.ds(step * block, block)].reshape(block * tokens, width)
+        result = jnp.dot(x, w_ref[...], preferred_element_type=f32).astype(bf16)
+        product[...] = result.reshape(product.shape)
+        xf = x.astype(f32)
+        square = jnp.sum(xf * xf, axis=1, keepdims=True)
+        for a in range(pieces):
+            for n in range(block):
+                low = n * tokens + a * piece
+                column = jnp.broadcast_to(square[low : low + piece], (piece, 128))
+                squares[a, pl.ds(step * block + n, 1), :] = jnp.sum(
+                    jnp.where(diagonal, column, 0.0), axis=0, keepdims=True
+                )
+        rows = pl.ds(pl.multiple_of(step * block * piece, block * piece), block * piece)
+        for ds, out_ref in ((0, kept_ref), (1, sent_ref)):
+            for dm in range(size):
+                a = lax.rem(mp + dm, size) * 2 + lax.rem(sub + ds, 2)
+                taken = product[:, pl.ds(pl.multiple_of(a * piece, piece), piece), :]
+                out_ref[dm, rows, :] = taken.reshape(block * piece, taken.shape[2])
+
     for ds, out_ref in ((0, kept_ref), (1, sent_ref)):
         for dm in range(size):
             a = lax.rem(mp + dm, size) * 2 + lax.rem(sub + ds, 2)
-            taken = product[:, pl.ds(pl.multiple_of(a * piece, piece), piece), :]
-            out_ref[dm, rows, :] = taken.reshape(block * piece, taken.shape[2])
-
-    @pl.when(step == pl.num_programs(0) - 1)
-    def _():
-        for ds, out_ref in ((0, kept_ref), (1, sent_ref)):
-            for dm in range(size):
-                a = lax.rem(mp + dm, size) * 2 + lax.rem(sub + ds, 2)
-                tail = jnp.concatenate([squares[a], jnp.zeros_like(squares[a])], axis=1)
-                out_ref[dm, pl.ds(count * piece, count), :] = tail.astype(bf16)
+            tail = jnp.concatenate([squares[a], jnp.zeros_like(squares[a])], axis=1)
+            out_ref[dm, count * piece : count * piece + count, :] = tail.astype(bf16)
 
 
 def encode(meta, states, weight, pieces):
@@ -83,20 +84,13 @@
     rows = count * piece + count
     block = 4
     return pl.pallas_call(
-        functools.partial(encode_kernel, pieces=pieces, piece=piece, count=count),
-        grid_spec=pltpu.PrefetchScalarGridSpec(
-            num_scalar_prefetch=1,
-            grid=(count // block,),
-            in_specs=[
-                pl.BlockSpec((block, tokens, width), lambda i, m: (i, 0, 0)),
-                pl.BlockSpec((width, out_width), lambda i, m: (0, 0)),
-            ],
-            out_specs=[pl.BlockSpec((pieces // 2, rows, out_width), lambda i, m: (0, 0, 0))] * 2,
-            scratch_shapes=[
-                pltpu.VMEM((block, tokens, out_width), bf16),
-                pltpu.VMEM((pieces, count, 128), f32),
-            ],
-        ),
+        functools.partial(encode_kernel, pieces=pieces, piece=piece, block=block),
+        in_specs=[SMEM, VMEM, VMEM],
+        out_specs=[VMEM] * 2,
+        scratch_shapes=[
+            pltpu.VMEM((block, tokens, out_width), bf16),
+            pltpu.VMEM((pieces, count, 128), f32),
+        ],
         out_shape=[jax.ShapeDtypeStruct((pieces // 2, rows, out_width), bf16)] * 2,
         compiler_params=params(),
         cost_estimate=cost(2 * count * tokens * width * out_width, 2 * count * tokens * width),
@@ -213,10 +207,11 @@
     group = pieces // 2
     piece = kvs[0].shape[1]
     tokens = att.shape[0]
-    if len(sources) == 1:
-        queries = sources[0][low : low + tokens]
-    else:
-        queries = queries_from(meta, sources[:-1], sources[-1], low, gain)
+    ready = min(tokens, sources[0].shape[0] - low)
+    queries = sources[0][low : low + ready]
+    if ready < tokens:
+        late = queries_from(meta, sources[1:-1], sources[-1], low + ready, gain)
+        queries = jnp.concatenate([queries, late], axis=0)
     local = lax.broadcasted_iota(jnp.int32, (piece, size), 0)
     for c in range(pair.shape[0]):
         masks = []
@@ -313,13 +308,10 @@
     span_tokens = token_count // spans_here
     requests = 2 * spans_here
     cap = max(2, (requests + row_count - 1) // row_count)
-    last_spans = spans_here // 4
-    middle_spans = (spans_here - last_spans) // 2
-    chunk_spans = [spans_here - last_spans - middle_spans, middle_spans, last_spans]
-    firsts = [0, chunk_spans[0], spans_here - last_spans]
-    chunks = len(chunk_spans)
+    chunks = 2
+    spans = spans_here // chunks
     first_tokens = token_count // 4
-    last_low = token_count - last_spans * span_tokens
+    last_low = token_count - first_tokens
     gain = 1.0 / (softcap * math.sqrt(size))
     add = lambda *terms: functools.reduce(
         lambda a, b: a + b, [t.astype(f32) for t in terms]
@@ -386,13 +378,13 @@
         outs.append(add(after(kept[c], *earlier)[0], got, *arrived[c]))
 
     for c in range(chunks):
-        sources, low = [queries], firsts[c] * span_tokens
+        sources = [queries]
         if c == chunks - 1:
-            sources = [hidden, near, *with_near(fars_last, *leaving[0]), query_weight]
-        gate = (leaving[c - 1] if c else []) + ([outs[c - 2]] if c > 1 else [])
+            sources += [hidden, near, *with_near(fars_last, *leaving[0]), query_weight]
+        gate = leaving[c - 1] if c else []
         one, *others = run_chunk(
-            after(meta, *gate), table, sources, pairs, output_weight, firsts[c],
-            low, chunk_spans[c], span_tokens, feature_shard, cap, gain,
+            after(meta, *gate), table, sources, pairs, output_weight, c * spans,
+            c * spans * span_tokens, spans, span_tokens, feature_shard, cap, gain,
         )
         kept.append(one)
         received.append([shift(other, "sub", 1) for other in others])
@@ -403,7 +395,7 @@
     total(chunks - 1)
     mixed = jnp.zeros((token_count, feature_shard), bf16)
     for c, out in enumerate(outs):
-        mixed = lax.dynamic_update_slice(after(mixed, meta), out, (firsts[c] * span_tokens, 0))
+        mixed = lax.dynamic_update_slice(after(mixed, meta), out, (c * spans * span_tokens, 0))
     return mixed
 
 

time: 81.1 us -> 80.4 us (level)
  waiting for transfers between devices: 27.6 us -> 33.2 us
  starting transfers between devices: 25.8 us -> 20.7 us
  Pallas kernels: 18.4 us -> 17 us
    ppermute x23 -> x22, waiting for transfers between devices: 20.4 us -> 26.3 us  [shift(): lax.ppermute(value, axis, [(i, (i + by) % size) for i in range(size)])]
    ppermute x23 -> x22, starting transfers between devices: 16.7 us -> 11.3 us  [shift(): lax.ppermute(value, axis, [(i, (i + by) % size) for i in range(size)])]
    pallas_call x3 -> x2, Pallas kernels: 10.6 us -> 9.25 us  [run_chunk(): pl.pallas_call(functools.partial(chunk_kernel, first=first, low=low, span...]
    unnamed x19 -> x17, local copies, waits for them, and re-layouts: 3.69 us -> 3.68 us
  transfers between devices with their start and end apart: 28 -> 27, of which waited for: 17 -> 18; matrix products, arithmetic and copies ran while one was open for 4% -> 4% of each run, Pallas kernels for 23% -> 21%
where the time goes in v8:
time: 80.4 us; the launch traced here: 80.3 us
  waiting for transfers between devices  33.2 us (41%)
  starting transfers between devices  20.7 us (26%)
  Pallas kernels  17 us (21%)
  local copies, waits for them, and re-layouts  6.27 us (8%)
  other arithmetic  2.93 us (4%)
    ppermute x22, waiting for transfers between devices, shift(): lax.ppermute(value, axis, [(i, (i + by) % size) for i in range(size)])  26.3 us
    ppermute x22, starting transfers between devices, shift(): lax.ppermute(value, axis, [(i, (i + by) % size) for i in range(size)])  11.3 us
    ppermute x5, starting transfers between devices, swap(): return lax.ppermute(value, axis, [(i, i ^ by) for i in range(size)])  9.37 us
    pallas_call x2, Pallas kernels, run_chunk(): pl.pallas_call(functools.partial(chunk_kernel, first=first, low=low, span...  9.25 us
    ppermute x5, waiting for transfers between devices, swap(): return lax.ppermute(value, axis, [(i, i ^ by) for i in range(size)])  6.85 us
    pallas_call x1, Pallas kernels, project_queries(): pl.pallas_call(functools.partial(query_kernel, lows=tuple(lows), gain=gai...  4.18 us
    unnamed x17, local copies, waits for them, and re-layouts  3.68 us
    pallas_call x1, Pallas kernels, encode(): pl.pallas_call(functools.partial(encode_kernel, pieces=pieces, piece=piec...  2.42 us
  transfers between devices with their start and end apart: 27, of which 18 were waited for; matrix products, arithmetic and copies ran while one was open for 4% of the time, Pallas kernels for 21%

profile of v8, /device:TPU:0, one launch (start us, length us, event | category | flops | bytes accessed | tf_op | source)
XLA Modules:
  0.0 80.3 jit_solution(17951538795990580388)
XLA Ops:
  0.0 1.2 %fusion.17 = (bf16[128,1024]{1,0:T(8,128)(2,1)S(1)}, bf16[128,1024]{1,0:T(8,128)(2,1)S(1)}) fusion(bf16[512,1024]{1,0:T(8,128)(2,1)} %refs_1_.1), kind=kLoop, calls=%fused_computation.49 | loop fusion | bytes 1048576 | tf_op jit(solution)/shard_map/slice | solution.py:362
  1.2 3.0 %collective-permute-start = (bf16[128,1024]{1,0:T(8,128)(2,1)S(1)}, bf16[128,1024]{1,0:T(8,128)(2,1)S(1)}, u32[]{:S(2)}, u32[]{:S(2)}) collective-permute-start(bf16[128,1024]{1,0:T(8,128)(2,1)S(1)} %get-tuple-element.96), channel_id=1, source_target_pairs={{0,2},{2,0},{1,3},{3,1},{4,6},{6,4},{5,7},{7,5},{8,10},{10,8},{9,1... | collective-permute-start | bytes 786440 | tf_op jit(solution)/shard_map/ppermute | solution.py:22
  4.2 2.3 %copy-done.3 = bf16[16,128,1024]{2,1,0:T(8,128)(2,1)S(1)} copy-done((bf16[16,128,1024]{2,1,0:T(8,128)(2,1)S(1)}, bf16[16,128,1024]{2,1,0:T(8,128)(2,1)}, u32[]{:S(2)}) %copy-start.3) | copy-done | bytes 4194328
  6.6 1.3 %copy-done.4 = bf16[1024,256]{1,0:T(8,128)(2,1)S(1)} copy-done((bf16[1024,256]{1,0:T(8,128)(2,1)S(1)}, bf16[1024,256]{1,0:T(8,128)(2,1)}, u32[]{:S(2)}) %copy-start.4) | copy-done | bytes 524312
  7.9 2.4 %encode.1 = (bf16[2,528,256]{2,1,0:T(8,128)(2,1)S(1)}, bf16[2,528,256]{2,1,0:T(8,128)(2,1)S(1)}) custom-call(s32[3]{0:T(128)S(1)} %pad_add_fusion.2.meta, bf16[16,128,1024]{2,1,0:T(8,128)(2,1)S(1)} %copy-done.3, bf16[1024,256]{1,0:T(8,128)(2,1)S(1)} %copy-done.4), custom_call_target="tpu_custom_call" | custom-call | flops 1073741824 | bytes 4194304 | tf_op jit(solution)/shard_map/encode/pallas_call | solution.py:86
  10.5 1.2 %slice.96 = bf16[256,1024]{1,0:T(8,128)(2,1)S(1)} slice(bf16[512,1024]{1,0:T(8,128)(2,1)} %refs_1_.1), slice={[128:384], [0:1024]} | slice | bytes 1048576 | tf_op jit(solution)/shard_map/slice | solution.py:348
  11.7 1.0 %fusion.16 = s32[1,5,16]{2,1,0:T(8,128)S(1)} fusion(s32[2,8]{1,0:T(2,128)} %bitcast.50, s32[2,8]{1,0:T(2,128)} %bitcast.51, s32[1,16]{1,0:T(1,128)} %bitcast.52), kind=kLoop, calls=%fused_computation.47 | loop fusion | flops 160 | bytes 512 | tf_op jit(solution)/shard_map/broadcast_in_dim | solution.py:335
  12.8 2.0 %collective-permute-start.2 = (s32[1,5,16]{2,1,0:T(8,128)S(1)}, s32[1,5,16]{2,1,0:T(8,128)S(1)}, u32[]{:S(2)}, u32[]{:S(2)}) collective-permute-start(s32[1,5,16]{2,1,0:T(8,128)S(1)} %fusion.16), channel_id=1, source_target_pairs={{0,4},{4,0},{8,12},{12,8},{1,5},{5,1},{9,13},{13,9},{2,6},{6,2},{1... | collective-permute-start | bytes 968 | tf_op jit(solution)/shard_map/ppermute | solution.py:27
  14.8 1.5 %collective-permute-start.4 = (bf16[528,256]{1,0:T(8,128)(2,1)S(1)}, bf16[528,256]{1,0:T(8,128)(2,1)S(1)}, u32[]{:S(2)}, u32[]{:S(2)}) collective-permute-start(bf16[528,256]{1,0:T(8,128)(2,1)S(1)} %fusion.6), channel_id=1, source_target_pairs={{0,2},{2,0},{1,3},{3,1},{4,6},{6,4},{5,7},{7,5},{8,10},{10,8},{9,1... | collective-permute-start | bytes 811016 | tf_op jit(solution)/shard_map/ppermute | solution.py:22
  16.5 2.9 %collective-permute-start.3 = (s32[2,5,16]{2,1,0:T(8,128)S(1)}, s32[2,5,16]{2,1,0:T(8,128)S(1)}, u32[]{:S(2)}, u32[]{:S(2)}) collective-permute-start(s32[2,5,16]{2,1,0:T(8,128)S(1)} %pad_add_fusion), channel_id=1, source_target_pairs={{0,8},{4,12},{8,0},{12,4},{1,9},{5,13},{9,1},{13,5},{2,10},{6,14},... | collective-permute-start | bytes 1928 | tf_op jit(solution)/shard_map/ppermute | solution.py:27
  19.4 1.6 %collective-permute-done.3 = s32[2,5,16]{2,1,0:T(8,128)S(1)} collective-permute-done((s32[2,5,16]{2,1,0:T(8,128)S(1)}, s32[2,5,16]{2,1,0:T(8,128)S(1)}, u32[]{:S(2)}, u32[]{:S(2)}) %collective-permute-start.3) | collective-permute-done | bytes 672 | tf_op jit(solution)/shard_map/ppermute | solution.py:27
  21.0 2.4 %collective-permute-done.4.refs_0_ = bf16[528,256]{1,0:T(8,128)(2,1)S(1)} collective-permute-done((bf16[528,256]{1,0:T(8,128)(2,1)S(1)}, bf16[528,256]{1,0:T(8,128)(2,1)S(1)}, u32[]{:S(2)}, u32[]{:S(2)}) %collective-permute-start.4) | collective-permute-done | bytes 270368 | tf_op jit(solution)/shard_map/ppermute | solution.py:22
  23.4 1.0 %collective-permute-start.10 = (bf16[256,1024]{1,0:T(8,128)(2,1)S(1)}, bf16[256,1024]{1,0:T(8,128)(2,1)S(1)}, u32[]{:S(2)}, u32[]{:S(2)}) collective-permute-start(bf16[256,1024]{1,0:T(8,128)(2,1)S(1)} %slice.96), channel_id=1, source_target_pairs={{0,2},{2,0},{1,3},{3,1},{4,6},{6,4},{5,7},{7,5},{8,10},{10,8},{9,1... | collective-permute-start | bytes 1572872 | tf_op jit(solution)/shard_map/ppermute | solution.py:22
  24.4 1.2 %route.1 = (bf16[4,32,256]{2,1,0:T(8,128)(2,1)S(1)}, bf16[4,32,256]{2,1,0:T(8,128)(2,1)S(1)}, bf16[4,32,256]{2,1,0:T(8,128)(2,1)S(1)}, bf16[4,32,256]{2,1,0:T(8,128)(2,1)S(1)}) custom-call(s32[3]{0:T(128)S(1)} %pad_add_fusion.2.meta, s32[4,5,16]{2,1,0:T(8,128)S(1)} %constant_dynamic-update-slice_fusion.table, ...), custom_call_target="tpu_custom_call" | custom-call | flops 1081344 | bytes 811008 | tf_op jit(solution)/shard_map/route/pallas_call | solution.py:134
  25.6 0.4 collective-permute-start.5
  26.0 2.7 %collective-permute-start.6 = (bf16[4,32,256]{2,1,0:T(8,128)(2,1)S(1)}, bf16[4,32,256]{2,1,0:T(8,128)(2,1)S(1)}, u32[]{:S(2)}, u32[]{:S(2)}) collective-permute-start(bf16[4,32,256]{2,1,0:T(8,128)(2,1)S(1)} %get-tuple-element.53), channel_id=1, source_target_pairs={{0,8},{4,12},{8,0},{12,4},{1,9},{5,13},{9,1},{13,5},{2,10},{6,14},... | collective-permute-start | bytes 196616 | tf_op jit(solution)/shard_map/ppermute | solution.py:27
  28.7 1.4 %collective-permute-start.7 = (bf16[4,32,256]{2,1,0:T(8,128)(2,1)S(1)}, bf16[4,32,256]{2,1,0:T(8,128)(2,1)S(1)}, u32[]{:S(2)}, u32[]{:S(2)}) collective-permute-start(bf16[4,32,256]{2,1,0:T(8,128)(2,1)S(1)} %get-tuple-element.54), channel_id=1, source_target_pairs={{0,12},{4,8},{8,4},{12,0},{1,13},{5,9},{9,5},{13,1},{2,14},{6,10},... | collective-permute-start | bytes 196616 | tf_op jit(solution)/shard_map/ppermute | solution.py:27
  30.0 1.5 %collective-permute-done.5 = bf16[4,32,256]{2,1,0:T(8,128)(2,1)S(1)} collective-permute-done((bf16[4,32,256]{2,1,0:T(8,128)(2,1)S(1)}, bf16[4,32,256]{2,1,0:T(8,128)(2,1)S(1)}, u32[]{:S(2)}, u32[]{:S(2)}) %collective-permute-start.5) | collective-permute-done | bytes 65568 | tf_op jit(solution)/shard_map/ppermute | solution.py:27
  31.6 3.5 %collective-permute-done.7 = bf16[4,32,256]{2,1,0:T(8,128)(2,1)S(1)} collective-permute-done((bf16[4,32,256]{2,1,0:T(8,128)(2,1)S(1)}, bf16[4,32,256]{2,1,0:T(8,128)(2,1)S(1)}, u32[]{:S(2)}, u32[]{:S(2)}) %collective-permute-start.7) | collective-permute-done | bytes 65568 | tf_op jit(solution)/shard_map/ppermute | solution.py:27
  35.1 1.5 %collective-permute-done.10.refs_2_ = bf16[256,1024]{1,0:T(8,128)(2,1)S(1)} collective-permute-done((bf16[256,1024]{1,0:T(8,128)(2,1)S(1)}, bf16[256,1024]{1,0:T(8,128)(2,1)S(1)}, u32[]{:S(2)}, u32[]{:S(2)}) %collective-permute-start.10) | collective-permute-done | bytes 524320 | tf_op jit(solution)/shard_map/ppermute | solution.py:22
  36.6 0.5 collective-permute-start.9
  37.2 0.5 collective-permute-start.13
  37.6 1.3 %collective-permute-done.9.refs_1_ = bf16[128,1024]{1,0:T(8,128)(2,1)S(1)} collective-permute-done((bf16[128,1024]{1,0:T(8,128)(2,1)S(1)}, bf16[128,1024]{1,0:T(8,128)(2,1)S(1)}, u32[]{:S(2)}, u32[]{:S(2)}) %collective-permute-start.9) | collective-permute-done | bytes 262176 | tf_op jit(solution)/shard_map/ppermute | solution.py:22
  39.0 4.2 %queries.1.refs_0_ = bf16[384,1024]{1,0:T(8,128)(2,1)S(1)} custom-call(s32[3]{0:T(128)S(1)} %pad_add_fusion.2.meta, bf16[512,1024]{1,0:T(8,128)(2,1)S(1)} %copy-done.2, bf16[512,1024]{1,0:T(8,128)(2,1)S(1)} %collective-permute-done.8.near_ref.refs_2_, bf16[128,1024]{1,0:T(8,128)(2,1)S(1)} %collective-permute-done.refs_0_, ...), custom_call_target="tpu_custom_call" | custom-call | flops 3221225472 | bytes 3145728 | tf_op jit(solution)/shard_map/queries/pallas_call | solution.py:189
  43.1 2.2 %collective-permute-done.13.refs_3_.refs_8_ = bf16[16,32,256]{2,1,0:T(8,128)(2,1)S(1)} collective-permute-done((bf16[16,32,256]{2,1,0:T(8,128)(2,1)S(1)}, bf16[16,32,256]{2,1,0:T(8,128)(2,1)S(1)}, u32[]{:S(2)}, u32[]{:S(2)}) %collective-permute-start.13) | collective-permute-done | bytes 262176 | tf_op jit(solution)/shard_map/ppermute | solution.py:22
  45.4 0.5 collective-permute-start.19
  45.8 1.1 %collective-permute-done.14.refs_4_.refs_9_ = bf16[16,32,256]{2,1,0:T(8,128)(2,1)S(1)} collective-permute-done((bf16[16,32,256]{2,1,0:T(8,128)(2,1)S(1)}, bf16[16,32,256]{2,1,0:T(8,128)(2,1)S(1)}, u32[]{:S(2)}, u32[]{:S(2)}) %collective-permute-start.14) | collective-permute-done | bytes 262176 | tf_op jit(solution)/shard_map/ppermute | solution.py:22
  46.9 4.0 %chunk.2 = (bf16[2,256,1024]{2,1,0:T(8,128)(2,1)S(1)}, bf16[2,64,1024]{2,1,0:T(8,128)(2,1)S(1)}, bf16[2,64,1024]{2,1,0:T(8,128)(2,1)S(1)}, bf16[2,64,1024]{2,1,0:T(8,128)(2,1)S(1)}, bf16[2,64,1024]{2,1,0:T(8,128)(2,1)S(1)}) custom-call(s32[3]{0:T(128)S(1)} %pad_add_fusion.2.meta, s32[4,5,16]{2,1,0:T(8,128)S(1)} %constant_dynamic-update-slice_fusion.table, ...), custom_call_target="tpu_custom_call" | custom-call | flops 2415919104 | bytes 524288 | tf_op jit(solution)/shard_map/chunk/pallas_call | solution.py:267
  51.0 0.2 collective-permute-start.15
  51.2 0.4 collective-permute-start.16
  51.7 0.4 collective-permute-start.18
  52.0 2.1 %collective-permute-done.19.refs_3_ = bf16[128,1024]{1,0:T(8,128)(2,1)S(1)} collective-permute-done((bf16[128,1024]{1,0:T(8,128)(2,1)S(1)}, bf16[128,1024]{1,0:T(8,128)(2,1)S(1)}, u32[]{:S(2)}, u32[]{:S(2)}) %collective-permute-start.19) | collective-permute-done | bytes 262176 | tf_op jit(solution)/shard_map/ppermute | solution.py:22
  54.1 0.2 fusion.7
  54.4 0.5 collective-permute-start.25
  54.9 1.5 %collective-permute-done.20.refs_4_ = bf16[128,1024]{1,0:T(8,128)(2,1)S(1)} collective-permute-done((bf16[128,1024]{1,0:T(8,128)(2,1)S(1)}, bf16[128,1024]{1,0:T(8,128)(2,1)S(1)}, u32[]{:S(2)}, u32[]{:S(2)}) %collective-permute-start.20) | collective-permute-done | bytes 262176 | tf_op jit(solution)/shard_map/ppermute | solution.py:22
  56.4 5.2 %chunk.3 = (bf16[2,256,1024]{2,1,0:T(8,128)(2,1)S(1)}, bf16[2,64,1024]{2,1,0:T(8,128)(2,1)S(1)}, bf16[2,64,1024]{2,1,0:T(8,128)(2,1)S(1)}, bf16[2,64,1024]{2,1,0:T(8,128)(2,1)S(1)}, bf16[2,64,1024]{2,1,0:T(8,128)(2,1)S(1)}) custom-call(s32[3]{0:T(128)S(1)} %pad_add_fusion.2.meta, s32[4,5,16]{2,1,0:T(8,128)S(1)} %constant_dynamic-update-slice_fusion.table, ...), custom_call_target="tpu_custom_call" | custom-call | flops 2415919104 | bytes 524288 | tf_op jit(solution)/shard_map/chunk/pallas_call | solution.py:267
  61.6 0.2 collective-permute-start.21
  61.9 0.4 collective-permute-start.22
  62.4 0.4 collective-permute-start.24
  62.8 0.5 collective-permute-done.21
  63.3 0.4 collective-permute-done.22
  63.6 0.4 collective-permute-done.23
  64.0 0.4 collective-permute-done.24
  64.6 1.6 %collective-permute-start.26 = (bf16[256,1024]{1,0:T(8,128)(2,1)S(1)}, bf16[256,1024]{1,0:T(8,128)(2,1)S(1)}, u32[]{:S(2)}, u32[]{:S(2)}) collective-permute-start(bf16[256,1024]{1,0:T(8,128)(2,1)S(1)} %pad_maximum_fusion.1), channel_id=1, source_target_pairs={{0,2},{2,0},{1,3},{3,1},{4,6},{6,4},{5,7},{7,5},{8,10},{10,8},{9,1... | collective-permute-start | bytes 1572872 | tf_op jit(solution)/shard_map/ppermute | solution.py:22
  66.3 2.2 %collective-permute-done.25 = bf16[256,1024]{1,0:T(8,128)(2,1)S(1)} collective-permute-done((bf16[256,1024]{1,0:T(8,128)(2,1)S(1)}, bf16[256,1024]{1,0:T(8,128)(2,1)S(1)}, u32[]{:S(2)}, u32[]{:S(2)}) %collective-permute-start.25) | collective-permute-done | bytes 524320 | tf_op jit(solution)/shard_map/ppermute | solution.py:22
  68.6 0.3 fusion.4
  68.9 10.3 %collective-permute-done.26 = bf16[256,1024]{1,0:T(8,128)(2,1)S(1)} collective-permute-done((bf16[256,1024]{1,0:T(8,128)(2,1)S(1)}, bf16[256,1024]{1,0:T(8,128)(2,1)S(1)}, u32[]{:S(2)}, u32[]{:S(2)}) %collective-permute-start.26) | collective-permute-done | bytes 524320 | tf_op jit(solution)/shard_map/ppermute | solution.py:22
  79.2 1.1 %fusion.5 = bf16[512,1024]{1,0:T(8,128)(2,1)} fusion(bf16[512,1024]{1,0:T(8,128)(2,1)} %copy-done.5, bf16[256,1024]{1,0:T(8,128)(2,1)S(1)} %collective-permute-done.26, bf16[2,256,1024]{2,1,0:T(8,128)(2,1)S(1)} %get-tuple-element.76, bf16[64,1024]{1,0:T(8,128)(2,1)S(1)} %slice_bitcast_fusion.1, bf16[64,1024]{1,0:T(8,128)(2,1)S(1)} %slice_bitcast_fusion.2, ...), kind=kLoop, calls=%fused_computation.8 | loop fusion | flops 3407872 | bytes 2097152 | tf_op jit(solution)/shard_map/dynamic_update_slice | solution.py:398
  (51 shorter events, 1.3 us)
Async XLA Ops:
  0.0 38.9 %copy-start.2 = (bf16[512,1024]{1,0:T(8,128)(2,1)S(1)}, bf16[512,1024]{1,0:T(8,128)(2,1)}, u32[]{:S(2)}) copy-start(bf16[512,1024]{1,0:T(8,128)(2,1)} %refs_1_.1) | copy-start | bytes 3145732
  1.2 9.3 %collective-permute-start = (bf16[128,1024]{1,0:T(8,128)(2,1)S(1)}, bf16[128,1024]{1,0:T(8,128)(2,1)S(1)}, u32[]{:S(2)}, u32[]{:S(2)}) collective-permute-start(bf16[128,1024]{1,0:T(8,128)(2,1)S(1)} %get-tuple-element.96), channel_id=1, source_target_pairs={{0,2},{2,0},{1,3},{3,1},{4,6},{6,4},{5,7},{7,5},{8,10},{10,8},{9,1... | collective-permute-start | bytes 786440 | tf_op jit(solution)/shard_map/ppermute | solution.py:22
  4.2 34.8 %copy-start = (bf16[4096,1024]{1,0:T(8,128)(2,1)S(1)}, bf16[4096,1024]{1,0:T(8,128)(2,1)}, u32[]{:S(2)}) copy-start(bf16[4096,1024]{1,0:T(8,128)(2,1)} %refs_5_.3) | copy-start | bytes 25165828
  4.2 2.3 %copy-start.3 = (bf16[16,128,1024]{2,1,0:T(8,128)(2,1)S(1)}, bf16[16,128,1024]{2,1,0:T(8,128)(2,1)}, u32[]{:S(2)}) copy-start(bf16[16,128,1024]{2,1,0:T(8,128)(2,1)} %x_ref.1) | copy-start | bytes 12582916
  6.6 1.3 %copy-start.4 = (bf16[1024,256]{1,0:T(8,128)(2,1)S(1)}, bf16[1024,256]{1,0:T(8,128)(2,1)}, u32[]{:S(2)}) copy-start(bf16[1024,256]{1,0:T(8,128)(2,1)} %w_ref.1) | copy-start | bytes 1572868
  10.3 36.6 %copy-start.1 = (bf16[1024,4096]{1,0:T(8,128)(2,1)S(1)}, bf16[1024,4096]{1,0:T(8,128)(2,1)}, u32[]{:S(2)}) copy-start(bf16[1024,4096]{1,0:T(8,128)(2,1)} %refs_10_.1) | copy-start | bytes 25165828
  10.5 2.2 %collective-permute-start.1 = (bf16[2,528,256]{2,1,0:T(8,128)(2,1)S(1)}, bf16[2,528,256]{2,1,0:T(8,128)(2,1)S(1)}, u32[]{:S(2)}, u32[]{:S(2)}) collective-permute-start(bf16[2,528,256]{2,1,0:T(8,128)(2,1)S(1)} %get-tuple-element.49), channel_id=1, source_target_pairs={{0,1},{1,0},{2,3},{3,2},{4,5},{5,4},{6,7},{7,6},{8,9},{9,8},{10,11... | collective-permute-start | bytes 1622024 | tf_op jit(solution)/shard_map/ppermute | solution.py:22
  12.8 3.7 %collective-permute-start.2 = (s32[1,5,16]{2,1,0:T(8,128)S(1)}, s32[1,5,16]{2,1,0:T(8,128)S(1)}, u32[]{:S(2)}, u32[]{:S(2)}) collective-permute-start(s32[1,5,16]{2,1,0:T(8,128)S(1)} %fusion.16), channel_id=1, source_target_pairs={{0,4},{4,0},{8,12},{12,8},{1,5},{5,1},{9,13},{13,9},{2,6},{6,2},{1... | collective-permute-start | bytes 968 | tf_op jit(solution)/shard_map/ppermute | solution.py:27
  14.8 8.6 %collective-permute-start.4 = (bf16[528,256]{1,0:T(8,128)(2,1)S(1)}, bf16[528,256]{1,0:T(8,128)(2,1)S(1)}, u32[]{:S(2)}, u32[]{:S(2)}) collective-permute-start(bf16[528,256]{1,0:T(8,128)(2,1)S(1)} %fusion.6), channel_id=1, source_target_pairs={{0,2},{2,0},{1,3},{3,1},{4,6},{6,4},{5,7},{7,5},{8,10},{10,8},{9,1... | collective-permute-start | bytes 811016 | tf_op jit(solution)/shard_map/ppermute | solution.py:22
  16.5 4.6 %collective-permute-start.3 = (s32[2,5,16]{2,1,0:T(8,128)S(1)}, s32[2,5,16]{2,1,0:T(8,128)S(1)}, u32[]{:S(2)}, u32[]{:S(2)}) collective-permute-start(s32[2,5,16]{2,1,0:T(8,128)S(1)} %pad_add_fusion), channel_id=1, source_target_pairs={{0,8},{4,12},{8,0},{12,4},{1,9},{5,13},{9,1},{13,5},{2,10},{6,14},... | collective-permute-start | bytes 1928 | tf_op jit(solution)/shard_map/ppermute | solution.py:27
  23.4 13.2 %collective-permute-start.10 = (bf16[256,1024]{1,0:T(8,128)(2,1)S(1)}, bf16[256,1024]{1,0:T(8,128)(2,1)S(1)}, u32[]{:S(2)}, u32[]{:S(2)}) collective-permute-start(bf16[256,1024]{1,0:T(8,128)(2,1)S(1)} %slice.96), channel_id=1, source_target_pairs={{0,2},{2,0},{1,3},{3,1},{4,6},{6,4},{5,7},{7,5},{8,10},{10,8},{9,1... | collective-permute-start | bytes 1572872 | tf_op jit(solution)/shard_map/ppermute | solution.py:22
  24.4 14.5 %collective-permute-start.8 = (bf16[512,1024]{1,0:T(8,128)(2,1)}, bf16[512,1024]{1,0:T(8,128)(2,1)S(1)}, u32[]{:S(2)}, u32[]{:S(2)}) collective-permute-start(bf16[512,1024]{1,0:T(8,128)(2,1)} %refs_1_.1), channel_id=1, source_target_pairs={{0,1},{1,0},{2,3},{3,2},{4,5},{5,4},{6,7},{7,6},{8,9},{9,8},{10,11... | collective-permute-start | bytes 3145736 | tf_op jit(solution)/shard_map/ppermute | solution.py:22
  25.6 6.0 %collective-permute-start.5 = (bf16[4,32,256]{2,1,0:T(8,128)(2,1)S(1)}, bf16[4,32,256]{2,1,0:T(8,128)(2,1)S(1)}, u32[]{:S(2)}, u32[]{:S(2)}) collective-permute-start(bf16[4,32,256]{2,1,0:T(8,128)(2,1)S(1)} %get-tuple-element.52), channel_id=1, source_target_pairs={{0,4},{4,0},{8,12},{12,8},{1,5},{5,1},{9,13},{13,9},{2,6},{6,2},{1... | collective-permute-start | bytes 196616 | tf_op jit(solution)/shard_map/ppermute | solution.py:27
  26.0 5.5 %collective-permute-start.6 = (bf16[4,32,256]{2,1,0:T(8,128)(2,1)S(1)}, bf16[4,32,256]{2,1,0:T(8,128)(2,1)S(1)}, u32[]{:S(2)}, u32[]{:S(2)}) collective-permute-start(bf16[4,32,256]{2,1,0:T(8,128)(2,1)S(1)} %get-tuple-element.53), channel_id=1, source_target_pairs={{0,8},{4,12},{8,0},{12,4},{1,9},{5,13},{9,1},{13,5},{2,10},{6,14},... | collective-permute-start | bytes 196616 | tf_op jit(solution)/shard_map/ppermute | solution.py:27
  28.7 6.4 %collective-permute-start.7 = (bf16[4,32,256]{2,1,0:T(8,128)(2,1)S(1)}, bf16[4,32,256]{2,1,0:T(8,128)(2,1)S(1)}, u32[]{:S(2)}, u32[]{:S(2)}) collective-permute-start(bf16[4,32,256]{2,1,0:T(8,128)(2,1)S(1)} %get-tuple-element.54), channel_id=1, source_target_pairs={{0,12},{4,8},{8,4},{12,0},{1,13},{5,9},{9,5},{13,1},{2,14},{6,10},... | collective-permute-start | bytes 196616 | tf_op jit(solution)/shard_map/ppermute | solution.py:27
  36.6 2.3 %collective-permute-start.11 = (bf16[256,1024]{1,0:T(8,128)(2,1)S(1)}, bf16[256,1024]{1,0:T(8,128)(2,1)S(1)}, u32[]{:S(2)}, u32[]{:S(2)}) collective-permute-start(bf16[256,1024]{1,0:T(8,128)(2,1)S(1)} %collective-permute-done.10.refs_2_), channel_id=1, source_target_pairs={{0,1},{1,0},{2,3},{3,2},{4,5},{5,4},{6,7},{7,6},{8,9},{9,8},{10,11... | collective-permute-start | bytes 1572872 | tf_op jit(solution)/shard_map/ppermute | solution.py:22
  36.6 2.3 %collective-permute-start.9 = (bf16[128,1024]{1,0:T(8,128)(2,1)S(1)}, bf16[128,1024]{1,0:T(8,128)(2,1)S(1)}, u32[]{:S(2)}, u32[]{:S(2)}) collective-permute-start(bf16[128,1024]{1,0:T(8,128)(2,1)S(1)} %collective-permute-done.refs_0_), channel_id=1, source_target_pairs={{0,1},{1,0},{2,3},{3,2},{4,5},{5,4},{6,7},{7,6},{8,9},{9,8},{10,11... | collective-permute-start | bytes 786440 | tf_op jit(solution)/shard_map/ppermute | solution.py:22
  37.2 8.2 %collective-permute-start.13 = (bf16[16,32,256]{2,1,0:T(8,128)(2,1)S(1)}, bf16[16,32,256]{2,1,0:T(8,128)(2,1)S(1)}, u32[]{:S(2)}, u32[]{:S(2)}) collective-permute-start(bf16[16,32,256]{2,1,0:T(8,128)(2,1)S(1)} %constant_dynamic-update-slice_fusion.3.refs_1_.refs_6_), channel_id=1, source_target_pairs={{0,2},{2,0},{1,3},{3,1},{4,6},{6,4},{5,7},{7,5},{8,10},{10,8},{9,1... | collective-permute-start | bytes 786440 | tf_op jit(solution)/shard_map/ppermute | solution.py:22
  37.6 8.2 %collective-permute-start.12 = (bf16[16,32,256]{2,1,0:T(8,128)(2,1)S(1)}, bf16[16,32,256]{2,1,0:T(8,128)(2,1)S(1)}, u32[]{:S(2)}, u32[]{:S(2)}) collective-permute-start(bf16[16,32,256]{2,1,0:T(8,128)(2,1)S(1)} %constant_dynamic-update-slice_fusion.3.refs_1_.refs_6_), channel_id=1, source_target_pairs={{0,1},{1,0},{2,3},{3,2},{4,5},{5,4},{6,7},{7,6},{8,9},{9,8},{10,11... | collective-permute-start | bytes 786440 | tf_op jit(solution)/shard_map/ppermute | solution.py:22
  45.4 1.5 %collective-permute-start.14 = (bf16[16,32,256]{2,1,0:T(8,128)(2,1)S(1)}, bf16[16,32,256]{2,1,0:T(8,128)(2,1)S(1)}, u32[]{:S(2)}, u32[]{:S(2)}) collective-permute-start(bf16[16,32,256]{2,1,0:T(8,128)(2,1)S(1)} %collective-permute-done.13.refs_3_.refs_8_), channel_id=1, source_target_pairs={{0,1},{1,0},{2,3},{3,2},{4,5},{5,4},{6,7},{7,6},{8,9},{9,8},{10,11... | collective-permute-start | bytes 786440 | tf_op jit(solution)/shard_map/ppermute | solution.py:22
  45.4 8.7 %collective-permute-start.19 = (bf16[128,1024]{1,0:T(8,128)(2,1)S(1)}, bf16[128,1024]{1,0:T(8,128)(2,1)S(1)}, u32[]{:S(2)}, u32[]{:S(2)}) collective-permute-start(bf16[128,1024]{1,0:T(8,128)(2,1)S(1)} %get-tuple-element.69), channel_id=1, source_target_pairs={{0,2},{2,0},{1,3},{3,1},{4,6},{6,4},{5,7},{7,5},{8,10},{10,8},{9,1... | collective-permute-start | bytes 786440 | tf_op jit(solution)/shard_map/ppermute | solution.py:22
  51.0 3.1 %collective-permute-start.15 = (bf16[2,64,1024]{2,1,0:T(8,128)(2,1)S(1)}, bf16[2,64,1024]{2,1,0:T(8,128)(2,1)S(1)}, u32[]{:S(2)}, u32[]{:S(2)}) collective-permute-start(bf16[2,64,1024]{2,1,0:T(8,128)(2,1)S(1)} %get-tuple-element.65), channel_id=1, source_target_pairs={{0,1},{1,0},{2,3},{3,2},{4,5},{5,4},{6,7},{7,6},{8,9},{9,8},{10,11... | collective-permute-start | bytes 786440 | tf_op jit(solution)/shard_map/ppermute | solution.py:22
  51.2 2.9 %collective-permute-start.16 = (bf16[2,64,1024]{2,1,0:T(8,128)(2,1)S(1)}, bf16[2,64,1024]{2,1,0:T(8,128)(2,1)S(1)}, u32[]{:S(2)}, u32[]{:S(2)}) collective-permute-start(bf16[2,64,1024]{2,1,0:T(8,128)(2,1)S(1)} %get-tuple-element.66), channel_id=1, source_target_pairs={{0,1},{1,0},{2,3},{3,2},{4,5},{5,4},{6,7},{7,6},{8,9},{9,8},{10,11... | collective-permute-start | bytes 786440 | tf_op jit(solution)/shard_map/ppermute | solution.py:22
  51.5 2.6 %collective-permute-start.17 = (bf16[2,64,1024]{2,1,0:T(8,128)(2,1)S(1)}, bf16[2,64,1024]{2,1,0:T(8,128)(2,1)S(1)}, u32[]{:S(2)}, u32[]{:S(2)}) collective-permute-start(bf16[2,64,1024]{2,1,0:T(8,128)(2,1)S(1)} %get-tuple-element.67), channel_id=1, source_target_pairs={{0,1},{1,0},{2,3},{3,2},{4,5},{5,4},{6,7},{7,6},{8,9},{9,8},{10,11... | collective-permute-start | bytes 786440 | tf_op jit(solution)/shard_map/ppermute | solution.py:22
  51.7 2.4 %collective-permute-start.18 = (bf16[2,64,1024]{2,1,0:T(8,128)(2,1)S(1)}, bf16[2,64,1024]{2,1,0:T(8,128)(2,1)S(1)}, u32[]{:S(2)}, u32[]{:S(2)}) collective-permute-start(bf16[2,64,1024]{2,1,0:T(8,128)(2,1)S(1)} %get-tuple-element.68), channel_id=1, source_target_pairs={{0,1},{1,0},{2,3},{3,2},{4,5},{5,4},{6,7},{7,6},{8,9},{9,8},{10,11... | collective-permute-start | bytes 786440 | tf_op jit(solution)/shard_map/ppermute | solution.py:22
  54.4 14.1 %collective-permute-start.25 = (bf16[256,1024]{1,0:T(8,128)(2,1)S(1)}, bf16[256,1024]{1,0:T(8,128)(2,1)S(1)}, u32[]{:S(2)}, u32[]{:S(2)}) collective-permute-start(bf16[256,1024]{1,0:T(8,128)(2,1)S(1)} %pad_maximum_fusion), channel_id=1, source_target_pairs={{0,2},{2,0},{1,3},{3,1},{4,6},{6,4},{5,7},{7,5},{8,10},{10,8},{9,1... | collective-permute-start | bytes 1572872 | tf_op jit(solution)/shard_map/ppermute | solution.py:22
  54.9 1.5 %collective-permute-start.20 = (bf16[128,1024]{1,0:T(8,128)(2,1)S(1)}, bf16[128,1024]{1,0:T(8,128)(2,1)S(1)}, u32[]{:S(2)}, u32[]{:S(2)}) collective-permute-start(bf16[128,1024]{1,0:T(8,128)(2,1)S(1)} %collective-permute-done.19.refs_3_), channel_id=1, source_target_pairs={{0,1},{1,0},{2,3},{3,2},{4,5},{5,4},{6,7},{7,6},{8,9},{9,8},{10,11... | collective-permute-start | bytes 786440 | tf_op jit(solution)/shard_map/ppermute | solution.py:22
  61.6 1.6 %collective-permute-start.21 = (bf16[2,64,1024]{2,1,0:T(8,128)(2,1)S(1)}, bf16[2,64,1024]{2,1,0:T(8,128)(2,1)S(1)}, u32[]{:S(2)}, u32[]{:S(2)}) collective-permute-start(bf16[2,64,1024]{2,1,0:T(8,128)(2,1)S(1)} %get-tuple-element.77), channel_id=1, source_target_pairs={{0,1},{1,0},{2,3},{3,2},{4,5},{5,4},{6,7},{7,6},{8,9},{9,8},{10,11... | collective-permute-start | bytes 786440 | tf_op jit(solution)/shard_map/ppermute | solution.py:22
  61.9 1.8 %collective-permute-start.22 = (bf16[2,64,1024]{2,1,0:T(8,128)(2,1)S(1)}, bf16[2,64,1024]{2,1,0:T(8,128)(2,1)S(1)}, u32[]{:S(2)}, u32[]{:S(2)}) collective-permute-start(bf16[2,64,1024]{2,1,0:T(8,128)(2,1)S(1)} %get-tuple-element.78), channel_id=1, source_target_pairs={{0,1},{1,0},{2,3},{3,2},{4,5},{5,4},{6,7},{7,6},{8,9},{9,8},{10,11... | collective-permute-start | bytes 786440 | tf_op jit(solution)/shard_map/ppermute | solution.py:22
  62.2 1.8 %collective-permute-start.23 = (bf16[2,64,1024]{2,1,0:T(8,128)(2,1)S(1)}, bf16[2,64,1024]{2,1,0:T(8,128)(2,1)S(1)}, u32[]{:S(2)}, u32[]{:S(2)}) collective-permute-start(bf16[2,64,1024]{2,1,0:T(8,128)(2,1)S(1)} %get-tuple-element.79), channel_id=1, source_target_pairs={{0,1},{1,0},{2,3},{3,2},{4,5},{5,4},{6,7},{7,6},{8,9},{9,8},{10,11... | collective-permute-start | bytes 786440 | tf_op jit(solution)/shard_map/ppermute | solution.py:22
  62.4 2.0 %collective-permute-start.24 = (bf16[2,64,1024]{2,1,0:T(8,128)(2,1)S(1)}, bf16[2,64,1024]{2,1,0:T(8,128)(2,1)S(1)}, u32[]{:S(2)}, u32[]{:S(2)}) collective-permute-start(bf16[2,64,1024]{2,1,0:T(8,128)(2,1)S(1)} %get-tuple-element.80), channel_id=1, source_target_pairs={{0,1},{1,0},{2,3},{3,2},{4,5},{5,4},{6,7},{7,6},{8,9},{9,8},{10,11... | collective-permute-start | bytes 786440 | tf_op jit(solution)/shard_map/ppermute | solution.py:22
  64.6 14.6 %collective-permute-start.26 = (bf16[256,1024]{1,0:T(8,128)(2,1)S(1)}, bf16[256,1024]{1,0:T(8,128)(2,1)S(1)}, u32[]{:S(2)}, u32[]{:S(2)}) collective-permute-start(bf16[256,1024]{1,0:T(8,128)(2,1)S(1)} %pad_maximum_fusion.1), channel_id=1, source_target_pairs={{0,2},{2,0},{1,3},{3,1},{4,6},{6,4},{5,7},{7,5},{8,10},{10,8},{9,1... | collective-permute-start | bytes 1572872 | tf_op jit(solution)/shard_map/ppermute | solution.py:22
  68.9 10.3 %copy-start.5 = (bf16[512,1024]{1,0:T(8,128)(2,1)}, bf16[512,1024]{1,0:T(8,128)(2,1)S(1)}, u32[]{:S(2)}) copy-start(bf16[512,1024]{1,0:T(8,128)(2,1)S(1)} %fusion.4) | copy-start | bytes 3145732

commit v9 on v8

--- a/solution.py
+++ b/solution.py
@@ -311,7 +311,7 @@
     chunks = 2
     spans = spans_here // chunks
     first_tokens = token_count // 4
-    last_low = token_count - first_tokens
+    last_low = token_count - token_count * 10 // 32
     gain = 1.0 / (softcap * math.sqrt(size))
     add = lambda *terms: functools.reduce(
         lambda a, b: a + b, [t.astype(f32) for t in terms]

time: 80.4 us -> 80.2 us (level)
  waiting for transfers between devices: 33.2 us -> 30.6 us
  starting transfers between devices: 20.7 us -> 22 us
  local copies, waits for them, and re-layouts: 6.27 us -> 7.3 us
    ppermute x22, waiting for transfers between devices: 26.3 us -> 23.9 us  [shift(): lax.ppermute(value, axis, [(i, (i + by) % size) for i in range(size)])]
    ppermute x22, starting transfers between devices: 11.3 us -> 12.9 us  [shift(): lax.ppermute(value, axis, [(i, (i + by) % size) for i in range(size)])]
    unnamed x17 -> x21, local copies, waits for them, and re-layouts: 3.68 us -> 4.91 us
    slice x1, local copies, waits for them, and re-layouts: 1.15 us -> 0.02 us  [shards(): fars_last = cross(after(hidden[last_low:], encoded))]
    slice x0 -> x1, local copies, waits for them, and re-layouts: none -> 0.97 us  [shards(): fars_first = cross(hidden[:first_tokens])]
  transfers between devices with their start and end apart: 27 -> 27, of which waited for: 18 -> 17; matrix products, arithmetic and copies ran while one was open for 4% -> 4% of each run, Pallas kernels for 21% -> 21%
where the time goes in v9:
time: 80.2 us; the launch traced here: 80 us
  waiting for transfers between devices  30.6 us (38%)
  starting transfers between devices  22 us (27%)
  Pallas kernels  16.9 us (21%)
  local copies, waits for them, and re-layouts  7.3 us (9%)
  other arithmetic  2.83 us (4%)
    ppermute x22, waiting for transfers between devices, shift(): lax.ppermute(value, axis, [(i, (i + by) % size) for i in range(size)])  23.9 us
    ppermute x22, starting transfers between devices, shift(): lax.ppermute(value, axis, [(i, (i + by) % size) for i in range(size)])  12.9 us
    pallas_call x2, Pallas kernels, run_chunk(): pl.pallas_call(functools.partial(chunk_kernel, first=first, low=low, span...  9.5 us
    ppermute x5, starting transfers between devices, swap(): return lax.ppermute(value, axis, [(i, i ^ by) for i in range(size)])  9.18 us
    ppermute x5, waiting for transfers between devices, swap(): return lax.ppermute(value, axis, [(i, i ^ by) for i in range(size)])  6.7 us
    unnamed x21, local copies, waits for them, and re-layouts  4.91 us
    pallas_call x1, Pallas kernels, project_queries(): pl.pallas_call(functools.partial(query_kernel, lows=tuple(lows), gain=gai...  3.86 us
    pallas_call x1, Pallas kernels, encode(): pl.pallas_call(functools.partial(encode_kernel, pieces=pieces, piece=piec...  2.42 us
  transfers between devices with their start and end apart: 27, of which 17 were waited for; matrix products, arithmetic and copies ran while one was open for 4% of the time, Pallas kernels for 21%

profile of v9, /device:TPU:0, one launch (start us, length us, event | category | flops | bytes accessed | tf_op | source)
XLA Modules:
  0.0 80.0 jit_solution(13868718835510764793)
XLA Ops:
  0.0 1.0 %slice.94 = bf16[128,1024]{1,0:T(8,128)(2,1)S(1)} slice(bf16[512,1024]{1,0:T(8,128)(2,1)} %refs_1_.1), slice={[0:128], [0:1024]} | slice | bytes 524288 | tf_op jit(solution)/shard_map/slice | solution.py:331
  1.0 3.0 %collective-permute-start = (bf16[128,1024]{1,0:T(8,128)(2,1)S(1)}, bf16[128,1024]{1,0:T(8,128)(2,1)S(1)}, u32[]{:S(2)}, u32[]{:S(2)}) collective-permute-start(bf16[128,1024]{1,0:T(8,128)(2,1)S(1)} %slice.94), channel_id=1, source_target_pairs={{0,2},{2,0},{1,3},{3,1},{4,6},{6,4},{5,7},{7,5},{8,10},{10,8},{9,1... | collective-permute-start | bytes 786440 | tf_op jit(solution)/shard_map/ppermute | solution.py:22
  4.1 2.3 %copy-done.3 = bf16[16,128,1024]{2,1,0:T(8,128)(2,1)S(1)} copy-done((bf16[16,128,1024]{2,1,0:T(8,128)(2,1)S(1)}, bf16[16,128,1024]{2,1,0:T(8,128)(2,1)}, u32[]{:S(2)}) %copy-start.3) | copy-done | bytes 4194328
  6.4 1.3 %copy-done.4 = bf16[1024,256]{1,0:T(8,128)(2,1)S(1)} copy-done((bf16[1024,256]{1,0:T(8,128)(2,1)S(1)}, bf16[1024,256]{1,0:T(8,128)(2,1)}, u32[]{:S(2)}) %copy-start.4) | copy-done | bytes 524312
  7.7 2.4 %encode.1 = (bf16[2,528,256]{2,1,0:T(8,128)(2,1)S(1)}, bf16[2,528,256]{2,1,0:T(8,128)(2,1)S(1)}) custom-call(s32[3]{0:T(128)S(1)} %pad_add_fusion.2.meta, bf16[16,128,1024]{2,1,0:T(8,128)(2,1)S(1)} %copy-done.3, bf16[1024,256]{1,0:T(8,128)(2,1)S(1)} %copy-done.4), custom_call_target="tpu_custom_call" | custom-call | flops 1073741824 | bytes 4194304 | tf_op jit(solution)/shard_map/encode/pallas_call | solution.py:86
  10.3 1.2 %slice.96 = bf16[224,1024]{1,0:T(8,128)(2,1)S(1)} slice(bf16[512,1024]{1,0:T(8,128)(2,1)} %refs_1_.1), slice={[128:352], [0:1024]} | slice | bytes 917504 | tf_op jit(solution)/shard_map/slice | solution.py:348
  11.5 0.9 %fusion.16 = s32[1,5,16]{2,1,0:T(8,128)S(1)} fusion(s32[2,8]{1,0:T(2,128)} %bitcast.52, s32[2,8]{1,0:T(2,128)} %bitcast.53, s32[1,16]{1,0:T(1,128)} %bitcast.54), kind=kLoop, calls=%fused_computation.47 | loop fusion | flops 160 | bytes 512 | tf_op jit(solution)/shard_map/broadcast_in_dim | solution.py:335
  12.5 1.9 %collective-permute-start.2 = (s32[1,5,16]{2,1,0:T(8,128)S(1)}, s32[1,5,16]{2,1,0:T(8,128)S(1)}, u32[]{:S(2)}, u32[]{:S(2)}) collective-permute-start(s32[1,5,16]{2,1,0:T(8,128)S(1)} %fusion.16), channel_id=1, source_target_pairs={{0,4},{4,0},{8,12},{12,8},{1,5},{5,1},{9,13},{13,9},{2,6},{6,2},{1... | collective-permute-start | bytes 968 | tf_op jit(solution)/shard_map/ppermute | solution.py:27
  14.4 1.5 %collective-permute-start.4 = (bf16[528,256]{1,0:T(8,128)(2,1)S(1)}, bf16[528,256]{1,0:T(8,128)(2,1)S(1)}, u32[]{:S(2)}, u32[]{:S(2)}) collective-permute-start(bf16[528,256]{1,0:T(8,128)(2,1)S(1)} %fusion.6), channel_id=1, source_target_pairs={{0,2},{2,0},{1,3},{3,1},{4,6},{6,4},{5,7},{7,5},{8,10},{10,8},{9,1... | collective-permute-start | bytes 811016 | tf_op jit(solution)/shard_map/ppermute | solution.py:22
  15.9 0.3 collective-permute-done.2
  16.1 2.8 %collective-permute-start.3 = (s32[2,5,16]{2,1,0:T(8,128)S(1)}, s32[2,5,16]{2,1,0:T(8,128)S(1)}, u32[]{:S(2)}, u32[]{:S(2)}) collective-permute-start(s32[2,5,16]{2,1,0:T(8,128)S(1)} %pad_add_fusion), channel_id=1, source_target_pairs={{0,8},{4,12},{8,0},{12,4},{1,9},{5,13},{9,1},{13,5},{2,10},{6,14},... | collective-permute-start | bytes 1928 | tf_op jit(solution)/shard_map/ppermute | solution.py:27
  19.0 1.7 %collective-permute-done.3 = s32[2,5,16]{2,1,0:T(8,128)S(1)} collective-permute-done((s32[2,5,16]{2,1,0:T(8,128)S(1)}, s32[2,5,16]{2,1,0:T(8,128)S(1)}, u32[]{:S(2)}, u32[]{:S(2)}) %collective-permute-start.3) | collective-permute-done | bytes 672 | tf_op jit(solution)/shard_map/ppermute | solution.py:27
  20.7 1.9 %collective-permute-done.4.refs_0_ = bf16[528,256]{1,0:T(8,128)(2,1)S(1)} collective-permute-done((bf16[528,256]{1,0:T(8,128)(2,1)S(1)}, bf16[528,256]{1,0:T(8,128)(2,1)S(1)}, u32[]{:S(2)}, u32[]{:S(2)}) %collective-permute-start.4) | collective-permute-done | bytes 270368 | tf_op jit(solution)/shard_map/ppermute | solution.py:22
  22.6 1.5 %collective-permute-start.10 = (bf16[224,1024]{1,0:T(8,128)(2,1)S(1)}, bf16[224,1024]{1,0:T(8,128)(2,1)S(1)}, u32[]{:S(2)}, u32[]{:S(2)}) collective-permute-start(bf16[224,1024]{1,0:T(8,128)(2,1)S(1)} %slice.96), channel_id=1, source_target_pairs={{0,2},{2,0},{1,3},{3,1},{4,6},{6,4},{5,7},{7,5},{8,10},{10,8},{9,1... | collective-permute-start | bytes 1376264 | tf_op jit(solution)/shard_map/ppermute | solution.py:22
  24.1 1.2 %route.1 = (bf16[4,32,256]{2,1,0:T(8,128)(2,1)S(1)}, bf16[4,32,256]{2,1,0:T(8,128)(2,1)S(1)}, bf16[4,32,256]{2,1,0:T(8,128)(2,1)S(1)}, bf16[4,32,256]{2,1,0:T(8,128)(2,1)S(1)}) custom-call(s32[3]{0:T(128)S(1)} %pad_add_fusion.2.meta, s32[4,5,16]{2,1,0:T(8,128)S(1)} %constant_dynamic-update-slice_fusion.table, ...), custom_call_target="tpu_custom_call" | custom-call | flops 1081344 | bytes 811008 | tf_op jit(solution)/shard_map/route/pallas_call | solution.py:134
  25.3 0.5 collective-permute-start.5
  25.8 2.6 %collective-permute-start.6 = (bf16[4,32,256]{2,1,0:T(8,128)(2,1)S(1)}, bf16[4,32,256]{2,1,0:T(8,128)(2,1)S(1)}, u32[]{:S(2)}, u32[]{:S(2)}) collective-permute-start(bf16[4,32,256]{2,1,0:T(8,128)(2,1)S(1)} %get-tuple-element.53), channel_id=1, source_target_pairs={{0,8},{4,12},{8,0},{12,4},{1,9},{5,13},{9,1},{13,5},{2,10},{6,14},... | collective-permute-start | bytes 196616 | tf_op jit(solution)/shard_map/ppermute | solution.py:27
  28.4 1.3 %collective-permute-start.7 = (bf16[4,32,256]{2,1,0:T(8,128)(2,1)S(1)}, bf16[4,32,256]{2,1,0:T(8,128)(2,1)S(1)}, u32[]{:S(2)}, u32[]{:S(2)}) collective-permute-start(bf16[4,32,256]{2,1,0:T(8,128)(2,1)S(1)} %get-tuple-element.54), channel_id=1, source_target_pairs={{0,12},{4,8},{8,4},{12,0},{1,13},{5,9},{9,5},{13,1},{2,14},{6,10},... | collective-permute-start | bytes 196616 | tf_op jit(solution)/shard_map/ppermute | solution.py:27
  29.8 2.4 %collective-permute-done.6 = bf16[4,32,256]{2,1,0:T(8,128)(2,1)S(1)} collective-permute-done((bf16[4,32,256]{2,1,0:T(8,128)(2,1)S(1)}, bf16[4,32,256]{2,1,0:T(8,128)(2,1)S(1)}, u32[]{:S(2)}, u32[]{:S(2)}) %collective-permute-start.6) | collective-permute-done | bytes 65568 | tf_op jit(solution)/shard_map/ppermute | solution.py:27
  32.2 2.3 %collective-permute-done.7 = bf16[4,32,256]{2,1,0:T(8,128)(2,1)S(1)} collective-permute-done((bf16[4,32,256]{2,1,0:T(8,128)(2,1)S(1)}, bf16[4,32,256]{2,1,0:T(8,128)(2,1)S(1)}, u32[]{:S(2)}, u32[]{:S(2)}) %collective-permute-start.7) | collective-permute-done | bytes 65568 | tf_op jit(solution)/shard_map/ppermute | solution.py:27
  34.6 0.5 collective-permute-start.9
  35.1 1.0 %collective-permute-start.13 = (bf16[16,32,256]{2,1,0:T(8,128)(2,1)S(1)}, bf16[16,32,256]{2,1,0:T(8,128)(2,1)S(1)}, u32[]{:S(2)}, u32[]{:S(2)}) collective-permute-start(bf16[16,32,256]{2,1,0:T(8,128)(2,1)S(1)} %constant_dynamic-update-slice_fusion.3.refs_1_.refs_6_), channel_id=1, source_target_pairs={{0,2},{2,0},{1,3},{3,1},{4,6},{6,4},{5,7},{7,5},{8,10},{10,8},{9,1... | collective-permute-start | bytes 786440 | tf_op jit(solution)/shard_map/ppermute | solution.py:22
  36.1 0.7 collective-permute-done.9.refs_1_
  36.8 1.2 %copy-done.1 = bf16[512,1024]{1,0:T(8,128)(2,1)S(1)} copy-done((bf16[512,1024]{1,0:T(8,128)(2,1)S(1)}, bf16[512,1024]{1,0:T(8,128)(2,1)}, u32[]{:S(2)}) %copy-start.1) | copy-done | bytes 1048600
  38.0 3.9 %queries.1.refs_0_ = bf16[352,1024]{1,0:T(8,128)(2,1)S(1)} custom-call(s32[3]{0:T(128)S(1)} %pad_add_fusion.2.meta, bf16[512,1024]{1,0:T(8,128)(2,1)S(1)} %copy-done.1, bf16[512,1024]{1,0:T(8,128)(2,1)S(1)} %collective-permute-done.8.near_ref.refs_2_, bf16[128,1024]{1,0:T(8,128)(2,1)S(1)} %collective-permute-done.refs_0_, ...), custom_call_target="tpu_custom_call" | custom-call | flops 2952790016 | bytes 2883584 | tf_op jit(solution)/shard_map/queries/pallas_call | solution.py:189
  41.9 1.5 %collective-permute-done.13.refs_3_.refs_8_ = bf16[16,32,256]{2,1,0:T(8,128)(2,1)S(1)} collective-permute-done((bf16[16,32,256]{2,1,0:T(8,128)(2,1)S(1)}, bf16[16,32,256]{2,1,0:T(8,128)(2,1)S(1)}, u32[]{:S(2)}, u32[]{:S(2)}) %collective-permute-start.13) | collective-permute-done | bytes 262176 | tf_op jit(solution)/shard_map/ppermute | solution.py:22
  43.4 1.0 %collective-permute-start.19 = (bf16[160,1024]{1,0:T(8,128)(2,1)S(1)}, bf16[160,1024]{1,0:T(8,128)(2,1)S(1)}, u32[]{:S(2)}, u32[]{:S(2)}) collective-permute-start(bf16[160,1024]{1,0:T(8,128)(2,1)S(1)} %slice.98), channel_id=1, source_target_pairs={{0,2},{2,0},{1,3},{3,1},{4,6},{6,4},{5,7},{7,5},{8,10},{10,8},{9,1... | collective-permute-start | bytes 983048 | tf_op jit(solution)/shard_map/ppermute | solution.py:22
  44.4 0.5 collective-permute-done.14.refs_4_.refs_9_
  44.9 4.0 %chunk.2 = (bf16[2,256,1024]{2,1,0:T(8,128)(2,1)S(1)}, bf16[2,64,1024]{2,1,0:T(8,128)(2,1)S(1)}, bf16[2,64,1024]{2,1,0:T(8,128)(2,1)S(1)}, bf16[2,64,1024]{2,1,0:T(8,128)(2,1)S(1)}, bf16[2,64,1024]{2,1,0:T(8,128)(2,1)S(1)}) custom-call(s32[3]{0:T(128)S(1)} %pad_add_fusion.2.meta, s32[4,5,16]{2,1,0:T(8,128)S(1)} %constant_dynamic-update-slice_fusion.table, ...), custom_call_target="tpu_custom_call" | custom-call | flops 2415919104 | bytes 524288 | tf_op jit(solution)/shard_map/chunk/pallas_call | solution.py:267
  49.0 0.2 collective-permute-start.15
  49.2 0.4 collective-permute-start.16
  49.7 0.4 collective-permute-start.18
  50.0 3.5 %collective-permute-done.19.refs_3_ = bf16[160,1024]{1,0:T(8,128)(2,1)S(1)} collective-permute-done((bf16[160,1024]{1,0:T(8,128)(2,1)S(1)}, bf16[160,1024]{1,0:T(8,128)(2,1)S(1)}, u32[]{:S(2)}, u32[]{:S(2)}) %collective-permute-start.19) | collective-permute-done | bytes 327712 | tf_op jit(solution)/shard_map/ppermute | solution.py:22
  53.9 1.0 %collective-permute-start.25 = (bf16[256,1024]{1,0:T(8,128)(2,1)S(1)}, bf16[256,1024]{1,0:T(8,128)(2,1)S(1)}, u32[]{:S(2)}, u32[]{:S(2)}) collective-permute-start(bf16[256,1024]{1,0:T(8,128)(2,1)S(1)} %pad_maximum_fusion), channel_id=1, source_target_pairs={{0,2},{2,0},{1,3},{3,1},{4,6},{6,4},{5,7},{7,5},{8,10},{10,8},{9,1... | collective-permute-start | bytes 1572872 | tf_op jit(solution)/shard_map/ppermute | solution.py:22
  54.9 1.6 %collective-permute-done.20.refs_4_ = bf16[160,1024]{1,0:T(8,128)(2,1)S(1)} collective-permute-done((bf16[160,1024]{1,0:T(8,128)(2,1)S(1)}, bf16[160,1024]{1,0:T(8,128)(2,1)S(1)}, u32[]{:S(2)}, u32[]{:S(2)}) %collective-permute-start.20) | collective-permute-done | bytes 327712 | tf_op jit(solution)/shard_map/ppermute | solution.py:22
  56.5 5.5 %chunk.3 = (bf16[2,256,1024]{2,1,0:T(8,128)(2,1)S(1)}, bf16[2,64,1024]{2,1,0:T(8,128)(2,1)S(1)}, bf16[2,64,1024]{2,1,0:T(8,128)(2,1)S(1)}, bf16[2,64,1024]{2,1,0:T(8,128)(2,1)S(1)}, bf16[2,64,1024]{2,1,0:T(8,128)(2,1)S(1)}) custom-call(s32[3]{0:T(128)S(1)} %pad_add_fusion.2.meta, s32[4,5,16]{2,1,0:T(8,128)S(1)} %constant_dynamic-update-slice_fusion.table, ...), custom_call_target="tpu_custom_call" | custom-call | flops 2415919104 | bytes 524288 | tf_op jit(solution)/shard_map/chunk/pallas_call | solution.py:267
  61.9 0.2 collective-permute-start.21
  62.1 0.4 collective-permute-start.22
  62.7 0.4 collective-permute-start.24
  63.1 0.5 collective-permute-done.21
  63.5 0.4 collective-permute-done.22
  63.9 0.4 collective-permute-done.23
  64.3 0.4 collective-permute-done.24
  64.9 1.2 %collective-permute-start.26 = (bf16[256,1024]{1,0:T(8,128)(2,1)S(1)}, bf16[256,1024]{1,0:T(8,128)(2,1)S(1)}, u32[]{:S(2)}, u32[]{:S(2)}) collective-permute-start(bf16[256,1024]{1,0:T(8,128)(2,1)S(1)} %pad_maximum_fusion.1), channel_id=1, source_target_pairs={{0,2},{2,0},{1,3},{3,1},{4,6},{6,4},{5,7},{7,5},{8,10},{10,8},{9,1... | collective-permute-start | bytes 1572872 | tf_op jit(solution)/shard_map/ppermute | solution.py:22
  66.1 1.4 %collective-permute-done.25 = bf16[256,1024]{1,0:T(8,128)(2,1)S(1)} collective-permute-done((bf16[256,1024]{1,0:T(8,128)(2,1)S(1)}, bf16[256,1024]{1,0:T(8,128)(2,1)S(1)}, u32[]{:S(2)}, u32[]{:S(2)}) %collective-permute-start.25) | collective-permute-done | bytes 524320 | tf_op jit(solution)/shard_map/ppermute | solution.py:22
  67.6 0.3 fusion.4
  68.0 11.0 %collective-permute-done.26 = bf16[256,1024]{1,0:T(8,128)(2,1)S(1)} collective-permute-done((bf16[256,1024]{1,0:T(8,128)(2,1)S(1)}, bf16[256,1024]{1,0:T(8,128)(2,1)S(1)}, u32[]{:S(2)}, u32[]{:S(2)}) %collective-permute-start.26) | collective-permute-done | bytes 524320 | tf_op jit(solution)/shard_map/ppermute | solution.py:22
  78.9 1.1 %fusion.5 = bf16[512,1024]{1,0:T(8,128)(2,1)} fusion(bf16[512,1024]{1,0:T(8,128)(2,1)} %copy-done.5, bf16[256,1024]{1,0:T(8,128)(2,1)S(1)} %collective-permute-done.26, bf16[2,256,1024]{2,1,0:T(8,128)(2,1)S(1)} %get-tuple-element.76, bf16[64,1024]{1,0:T(8,128)(2,1)S(1)} %slice_bitcast_fusion.1, bf16[64,1024]{1,0:T(8,128)(2,1)S(1)} %slice_bitcast_fusion.2, ...), kind=kLoop, calls=%fused_computation.8 | loop fusion | flops 3407872 | bytes 2097152 | tf_op jit(solution)/shard_map/dynamic_update_slice | solution.py:398
  (57 shorter events, 1.4 us)
Async XLA Ops:
  1.0 9.3 %collective-permute-start = (bf16[128,1024]{1,0:T(8,128)(2,1)S(1)}, bf16[128,1024]{1,0:T(8,128)(2,1)S(1)}, u32[]{:S(2)}, u32[]{:S(2)}) collective-permute-start(bf16[128,1024]{1,0:T(8,128)(2,1)S(1)} %slice.94), channel_id=1, source_target_pairs={{0,2},{2,0},{1,3},{3,1},{4,6},{6,4},{5,7},{7,5},{8,10},{10,8},{9,1... | collective-permute-start | bytes 786440 | tf_op jit(solution)/shard_map/ppermute | solution.py:22
  4.0 32.8 %copy-start = (bf16[4096,1024]{1,0:T(8,128)(2,1)S(1)}, bf16[4096,1024]{1,0:T(8,128)(2,1)}, u32[]{:S(2)}) copy-start(bf16[4096,1024]{1,0:T(8,128)(2,1)} %refs_5_.3) | copy-start | bytes 25165828
  4.1 2.3 %copy-start.3 = (bf16[16,128,1024]{2,1,0:T(8,128)(2,1)S(1)}, bf16[16,128,1024]{2,1,0:T(8,128)(2,1)}, u32[]{:S(2)}) copy-start(bf16[16,128,1024]{2,1,0:T(8,128)(2,1)} %x_ref.1) | copy-start | bytes 12582916
  6.4 1.3 %copy-start.4 = (bf16[1024,256]{1,0:T(8,128)(2,1)S(1)}, bf16[1024,256]{1,0:T(8,128)(2,1)}, u32[]{:S(2)}) copy-start(bf16[1024,256]{1,0:T(8,128)(2,1)} %w_ref.1) | copy-start | bytes 1572868
  10.3 34.6 %slice-start = ((s8[8388608]{0:T(1024)(128)(4,1)}), s8[4194304]{0:T(1024)(128)(4,1)S(1)}, s32[]{:S(2)}) async-start(s8[8388608]{0:T(1024)(128)(4,1)} %bitcast.50), calls=%async_computation | async-start | bytes 8388608
  10.3 2.1 %collective-permute-start.1 = (bf16[2,528,256]{2,1,0:T(8,128)(2,1)S(1)}, bf16[2,528,256]{2,1,0:T(8,128)(2,1)S(1)}, u32[]{:S(2)}, u32[]{:S(2)}) collective-permute-start(bf16[2,528,256]{2,1,0:T(8,128)(2,1)S(1)} %get-tuple-element.49), channel_id=1, source_target_pairs={{0,1},{1,0},{2,3},{3,2},{4,5},{5,4},{6,7},{7,6},{8,9},{9,8},{10,11... | collective-permute-start | bytes 1622024 | tf_op jit(solution)/shard_map/ppermute | solution.py:22
  12.5 3.7 %collective-permute-start.2 = (s32[1,5,16]{2,1,0:T(8,128)S(1)}, s32[1,5,16]{2,1,0:T(8,128)S(1)}, u32[]{:S(2)}, u32[]{:S(2)}) collective-permute-start(s32[1,5,16]{2,1,0:T(8,128)S(1)} %fusion.16), channel_id=1, source_target_pairs={{0,4},{4,0},{8,12},{12,8},{1,5},{5,1},{9,13},{13,9},{2,6},{6,2},{1... | collective-permute-start | bytes 968 | tf_op jit(solution)/shard_map/ppermute | solution.py:27
  14.4 8.3 %collective-permute-start.4 = (bf16[528,256]{1,0:T(8,128)(2,1)S(1)}, bf16[528,256]{1,0:T(8,128)(2,1)S(1)}, u32[]{:S(2)}, u32[]{:S(2)}) collective-permute-start(bf16[528,256]{1,0:T(8,128)(2,1)S(1)} %fusion.6), channel_id=1, source_target_pairs={{0,2},{2,0},{1,3},{3,1},{4,6},{6,4},{5,7},{7,5},{8,10},{10,8},{9,1... | collective-permute-start | bytes 811016 | tf_op jit(solution)/shard_map/ppermute | solution.py:22
  15.8 20.9 %collective-permute-start.8 = (bf16[512,1024]{1,0:T(8,128)(2,1)}, bf16[512,1024]{1,0:T(8,128)(2,1)S(1)}, u32[]{:S(2)}, u32[]{:S(2)}) collective-permute-start(bf16[512,1024]{1,0:T(8,128)(2,1)} %refs_1_.1), channel_id=1, source_target_pairs={{0,1},{1,0},{2,3},{3,2},{4,5},{5,4},{6,7},{7,6},{8,9},{9,8},{10,11... | collective-permute-start | bytes 3145736 | tf_op jit(solution)/shard_map/ppermute | solution.py:22
  16.1 4.5 %collective-permute-start.3 = (s32[2,5,16]{2,1,0:T(8,128)S(1)}, s32[2,5,16]{2,1,0:T(8,128)S(1)}, u32[]{:S(2)}, u32[]{:S(2)}) collective-permute-start(s32[2,5,16]{2,1,0:T(8,128)S(1)} %pad_add_fusion), channel_id=1, source_target_pairs={{0,8},{4,12},{8,0},{12,4},{1,9},{5,13},{9,1},{13,5},{2,10},{6,14},... | collective-permute-start | bytes 1928 | tf_op jit(solution)/shard_map/ppermute | solution.py:27
  22.6 11.9 %collective-permute-start.10 = (bf16[224,1024]{1,0:T(8,128)(2,1)S(1)}, bf16[224,1024]{1,0:T(8,128)(2,1)S(1)}, u32[]{:S(2)}, u32[]{:S(2)}) collective-permute-start(bf16[224,1024]{1,0:T(8,128)(2,1)S(1)} %slice.96), channel_id=1, source_target_pairs={{0,2},{2,0},{1,3},{3,1},{4,6},{6,4},{5,7},{7,5},{8,10},{10,8},{9,1... | collective-permute-start | bytes 1376264 | tf_op jit(solution)/shard_map/ppermute | solution.py:22
  25.3 4.5 %collective-permute-start.5 = (bf16[4,32,256]{2,1,0:T(8,128)(2,1)S(1)}, bf16[4,32,256]{2,1,0:T(8,128)(2,1)S(1)}, u32[]{:S(2)}, u32[]{:S(2)}) collective-permute-start(bf16[4,32,256]{2,1,0:T(8,128)(2,1)S(1)} %get-tuple-element.52), channel_id=1, source_target_pairs={{0,4},{4,0},{8,12},{12,8},{1,5},{5,1},{9,13},{13,9},{2,6},{6,2},{1... | collective-permute-start | bytes 196616 | tf_op jit(solution)/shard_map/ppermute | solution.py:27
  25.8 6.4 %collective-permute-start.6 = (bf16[4,32,256]{2,1,0:T(8,128)(2,1)S(1)}, bf16[4,32,256]{2,1,0:T(8,128)(2,1)S(1)}, u32[]{:S(2)}, u32[]{:S(2)}) collective-permute-start(bf16[4,32,256]{2,1,0:T(8,128)(2,1)S(1)} %get-tuple-element.53), channel_id=1, source_target_pairs={{0,8},{4,12},{8,0},{12,4},{1,9},{5,13},{9,1},{13,5},{2,10},{6,14},... | collective-permute-start | bytes 196616 | tf_op jit(solution)/shard_map/ppermute | solution.py:27
  28.4 6.1 %collective-permute-start.7 = (bf16[4,32,256]{2,1,0:T(8,128)(2,1)S(1)}, bf16[4,32,256]{2,1,0:T(8,128)(2,1)S(1)}, u32[]{:S(2)}, u32[]{:S(2)}) collective-permute-start(bf16[4,32,256]{2,1,0:T(8,128)(2,1)S(1)} %get-tuple-element.54), channel_id=1, source_target_pairs={{0,12},{4,8},{8,4},{12,0},{1,13},{5,9},{9,5},{13,1},{2,14},{6,10},... | collective-permute-start | bytes 196616 | tf_op jit(solution)/shard_map/ppermute | solution.py:27
  34.5 10.4 %slice-start.1 = ((s8[8388608]{0:T(1024)(128)(4,1)}), s8[4194304]{0:T(1024)(128)(4,1)S(1)}, s32[]{:S(2)}) async-start(s8[8388608]{0:T(1024)(128)(4,1)} %bitcast.50), calls=%async_computation.1 | async-start | bytes 8388608
  34.5 2.3 %collective-permute-start.11 = (bf16[224,1024]{1,0:T(8,128)(2,1)S(1)}, bf16[224,1024]{1,0:T(8,128)(2,1)S(1)}, u32[]{:S(2)}, u32[]{:S(2)}) collective-permute-start(bf16[224,1024]{1,0:T(8,128)(2,1)S(1)} %collective-permute-done.10.refs_2_), channel_id=1, source_target_pairs={{0,1},{1,0},{2,3},{3,2},{4,5},{5,4},{6,7},{7,6},{8,9},{9,8},{10,11... | collective-permute-start | bytes 1376264 | tf_op jit(solution)/shard_map/ppermute | solution.py:22
  34.6 2.2 %collective-permute-start.9 = (bf16[128,1024]{1,0:T(8,128)(2,1)S(1)}, bf16[128,1024]{1,0:T(8,128)(2,1)S(1)}, u32[]{:S(2)}, u32[]{:S(2)}) collective-permute-start(bf16[128,1024]{1,0:T(8,128)(2,1)S(1)} %collective-permute-done.refs_0_), channel_id=1, source_target_pairs={{0,1},{1,0},{2,3},{3,2},{4,5},{5,4},{6,7},{7,6},{8,9},{9,8},{10,11... | collective-permute-start | bytes 786440 | tf_op jit(solution)/shard_map/ppermute | solution.py:22
  35.1 8.3 %collective-permute-start.13 = (bf16[16,32,256]{2,1,0:T(8,128)(2,1)S(1)}, bf16[16,32,256]{2,1,0:T(8,128)(2,1)S(1)}, u32[]{:S(2)}, u32[]{:S(2)}) collective-permute-start(bf16[16,32,256]{2,1,0:T(8,128)(2,1)S(1)} %constant_dynamic-update-slice_fusion.3.refs_1_.refs_6_), channel_id=1, source_target_pairs={{0,2},{2,0},{1,3},{3,1},{4,6},{6,4},{5,7},{7,5},{8,10},{10,8},{9,1... | collective-permute-start | bytes 786440 | tf_op jit(solution)/shard_map/ppermute | solution.py:22
  36.1 8.3 %collective-permute-start.12 = (bf16[16,32,256]{2,1,0:T(8,128)(2,1)S(1)}, bf16[16,32,256]{2,1,0:T(8,128)(2,1)S(1)}, u32[]{:S(2)}, u32[]{:S(2)}) collective-permute-start(bf16[16,32,256]{2,1,0:T(8,128)(2,1)S(1)} %constant_dynamic-update-slice_fusion.3.refs_1_.refs_6_), channel_id=1, source_target_pairs={{0,1},{1,0},{2,3},{3,2},{4,5},{5,4},{6,7},{7,6},{8,9},{9,8},{10,11... | collective-permute-start | bytes 786440 | tf_op jit(solution)/shard_map/ppermute | solution.py:22
  36.8 1.2 %copy-start.1 = (bf16[512,1024]{1,0:T(8,128)(2,1)S(1)}, bf16[512,1024]{1,0:T(8,128)(2,1)}, u32[]{:S(2)}) copy-start(bf16[512,1024]{1,0:T(8,128)(2,1)} %refs_1_.1) | copy-start | bytes 3145732
  41.9 14.6 %copy-start.2 = (bf16[512,1024]{1,0:T(8,128)(2,1)S(1)}, bf16[512,1024]{1,0:T(8,128)(2,1)}, u32[]{:S(2)}) copy-start(bf16[512,1024]{1,0:T(8,128)(2,1)} %refs_1_.1) | copy-start | bytes 3145732
  43.4 1.5 %collective-permute-start.14 = (bf16[16,32,256]{2,1,0:T(8,128)(2,1)S(1)}, bf16[16,32,256]{2,1,0:T(8,128)(2,1)S(1)}, u32[]{:S(2)}, u32[]{:S(2)}) collective-permute-start(bf16[16,32,256]{2,1,0:T(8,128)(2,1)S(1)} %collective-permute-done.13.refs_3_.refs_8_), channel_id=1, source_target_pairs={{0,1},{1,0},{2,3},{3,2},{4,5},{5,4},{6,7},{7,6},{8,9},{9,8},{10,11... | collective-permute-start | bytes 786440 | tf_op jit(solution)/shard_map/ppermute | solution.py:22
  43.4 10.2 %collective-permute-start.19 = (bf16[160,1024]{1,0:T(8,128)(2,1)S(1)}, bf16[160,1024]{1,0:T(8,128)(2,1)S(1)}, u32[]{:S(2)}, u32[]{:S(2)}) collective-permute-start(bf16[160,1024]{1,0:T(8,128)(2,1)S(1)} %slice.98), channel_id=1, source_target_pairs={{0,2},{2,0},{1,3},{3,1},{4,6},{6,4},{5,7},{7,5},{8,10},{10,8},{9,1... | collective-permute-start | bytes 983048 | tf_op jit(solution)/shard_map/ppermute | solution.py:22
  49.0 4.6 %collective-permute-start.15 = (bf16[2,64,1024]{2,1,0:T(8,128)(2,1)S(1)}, bf16[2,64,1024]{2,1,0:T(8,128)(2,1)S(1)}, u32[]{:S(2)}, u32[]{:S(2)}) collective-permute-start(bf16[2,64,1024]{2,1,0:T(8,128)(2,1)S(1)} %get-tuple-element.65), channel_id=1, source_target_pairs={{0,1},{1,0},{2,3},{3,2},{4,5},{5,4},{6,7},{7,6},{8,9},{9,8},{10,11... | collective-permute-start | bytes 786440 | tf_op jit(solution)/shard_map/ppermute | solution.py:22
  49.2 4.4 %collective-permute-start.16 = (bf16[2,64,1024]{2,1,0:T(8,128)(2,1)S(1)}, bf16[2,64,1024]{2,1,0:T(8,128)(2,1)S(1)}, u32[]{:S(2)}, u32[]{:S(2)}) collective-permute-start(bf16[2,64,1024]{2,1,0:T(8,128)(2,1)S(1)} %get-tuple-element.66), channel_id=1, source_target_pairs={{0,1},{1,0},{2,3},{3,2},{4,5},{5,4},{6,7},{7,6},{8,9},{9,8},{10,11... | collective-permute-start | bytes 786440 | tf_op jit(solution)/shard_map/ppermute | solution.py:22
  49.5 4.1 %collective-permute-start.17 = (bf16[2,64,1024]{2,1,0:T(8,128)(2,1)S(1)}, bf16[2,64,1024]{2,1,0:T(8,128)(2,1)S(1)}, u32[]{:S(2)}, u32[]{:S(2)}) collective-permute-start(bf16[2,64,1024]{2,1,0:T(8,128)(2,1)S(1)} %get-tuple-element.67), channel_id=1, source_target_pairs={{0,1},{1,0},{2,3},{3,2},{4,5},{5,4},{6,7},{7,6},{8,9},{9,8},{10,11... | collective-permute-start | bytes 786440 | tf_op jit(solution)/shard_map/ppermute | solution.py:22
  49.7 3.9 %collective-permute-start.18 = (bf16[2,64,1024]{2,1,0:T(8,128)(2,1)S(1)}, bf16[2,64,1024]{2,1,0:T(8,128)(2,1)S(1)}, u32[]{:S(2)}, u32[]{:S(2)}) collective-permute-start(bf16[2,64,1024]{2,1,0:T(8,128)(2,1)S(1)} %get-tuple-element.68), channel_id=1, source_target_pairs={{0,1},{1,0},{2,3},{3,2},{4,5},{5,4},{6,7},{7,6},{8,9},{9,8},{10,11... | collective-permute-start | bytes 786440 | tf_op jit(solution)/shard_map/ppermute | solution.py:22
  53.9 13.6 %collective-permute-start.25 = (bf16[256,1024]{1,0:T(8,128)(2,1)S(1)}, bf16[256,1024]{1,0:T(8,128)(2,1)S(1)}, u32[]{:S(2)}, u32[]{:S(2)}) collective-permute-start(bf16[256,1024]{1,0:T(8,128)(2,1)S(1)} %pad_maximum_fusion), channel_id=1, source_target_pairs={{0,2},{2,0},{1,3},{3,1},{4,6},{6,4},{5,7},{7,5},{8,10},{10,8},{9,1... | collective-permute-start | bytes 1572872 | tf_op jit(solution)/shard_map/ppermute | solution.py:22
  54.8 1.6 %collective-permute-start.20 = (bf16[160,1024]{1,0:T(8,128)(2,1)S(1)}, bf16[160,1024]{1,0:T(8,128)(2,1)S(1)}, u32[]{:S(2)}, u32[]{:S(2)}) collective-permute-start(bf16[160,1024]{1,0:T(8,128)(2,1)S(1)} %collective-permute-done.19.refs_3_), channel_id=1, source_target_pairs={{0,1},{1,0},{2,3},{3,2},{4,5},{5,4},{6,7},{7,6},{8,9},{9,8},{10,11... | collective-permute-start | bytes 983048 | tf_op jit(solution)/shard_map/ppermute | solution.py:22
  61.9 1.6 %collective-permute-start.21 = (bf16[2,64,1024]{2,1,0:T(8,128)(2,1)S(1)}, bf16[2,64,1024]{2,1,0:T(8,128)(2,1)S(1)}, u32[]{:S(2)}, u32[]{:S(2)}) collective-permute-start(bf16[2,64,1024]{2,1,0:T(8,128)(2,1)S(1)} %get-tuple-element.77), channel_id=1, source_target_pairs={{0,1},{1,0},{2,3},{3,2},{4,5},{5,4},{6,7},{7,6},{8,9},{9,8},{10,11... | collective-permute-start | bytes 786440 | tf_op jit(solution)/shard_map/ppermute | solution.py:22
  62.1 1.8 %collective-permute-start.22 = (bf16[2,64,1024]{2,1,0:T(8,128)(2,1)S(1)}, bf16[2,64,1024]{2,1,0:T(8,128)(2,1)S(1)}, u32[]{:S(2)}, u32[]{:S(2)}) collective-permute-start(bf16[2,64,1024]{2,1,0:T(8,128)(2,1)S(1)} %get-tuple-element.78), channel_id=1, source_target_pairs={{0,1},{1,0},{2,3},{3,2},{4,5},{5,4},{6,7},{7,6},{8,9},{9,8},{10,11... | collective-permute-start | bytes 786440 | tf_op jit(solution)/shard_map/ppermute | solution.py:22
  62.5 1.8 %collective-permute-start.23 = (bf16[2,64,1024]{2,1,0:T(8,128)(2,1)S(1)}, bf16[2,64,1024]{2,1,0:T(8,128)(2,1)S(1)}, u32[]{:S(2)}, u32[]{:S(2)}) collective-permute-start(bf16[2,64,1024]{2,1,0:T(8,128)(2,1)S(1)} %get-tuple-element.79), channel_id=1, source_target_pairs={{0,1},{1,0},{2,3},{3,2},{4,5},{5,4},{6,7},{7,6},{8,9},{9,8},{10,11... | collective-permute-start | bytes 786440 | tf_op jit(solution)/shard_map/ppermute | solution.py:22
  62.7 2.0 %collective-permute-start.24 = (bf16[2,64,1024]{2,1,0:T(8,128)(2,1)S(1)}, bf16[2,64,1024]{2,1,0:T(8,128)(2,1)S(1)}, u32[]{:S(2)}, u32[]{:S(2)}) collective-permute-start(bf16[2,64,1024]{2,1,0:T(8,128)(2,1)S(1)} %get-tuple-element.80), channel_id=1, source_target_pairs={{0,1},{1,0},{2,3},{3,2},{4,5},{5,4},{6,7},{7,6},{8,9},{9,8},{10,11... | collective-permute-start | bytes 786440 | tf_op jit(solution)/shard_map/ppermute | solution.py:22
  64.9 14.0 %collective-permute-start.26 = (bf16[256,1024]{1,0:T(8,128)(2,1)S(1)}, bf16[256,1024]{1,0:T(8,128)(2,1)S(1)}, u32[]{:S(2)}, u32[]{:S(2)}) collective-permute-start(bf16[256,1024]{1,0:T(8,128)(2,1)S(1)} %pad_maximum_fusion.1), channel_id=1, source_target_pairs={{0,2},{2,0},{1,3},{3,1},{4,6},{6,4},{5,7},{7,5},{8,10},{10,8},{9,1... | collective-permute-start | bytes 1572872 | tf_op jit(solution)/shard_map/ppermute | solution.py:22
  67.9 11.1 %copy-start.5 = (bf16[512,1024]{1,0:T(8,128)(2,1)}, bf16[512,1024]{1,0:T(8,128)(2,1)S(1)}, u32[]{:S(2)}) copy-start(bf16[512,1024]{1,0:T(8,128)(2,1)S(1)} %fusion.4) | copy-start | bytes 3145732

commit v10 on v9

--- a/solution.py
+++ b/solution.py
@@ -350,7 +350,7 @@
     routed = route(meta, table, kept, received, crossed, cap, features, count, requests)
     encoded = jnp.concatenate(
         [routed[0]]
-        + list(lax.optimization_barrier([swap(routed[d], "rows", d) for d in range(1, row_count)])),
+        + list(lax.optimization_barrier([swap(routed[d], "rows", d) for d in range(row_count - 1, 0, -1)]))[::-1],
         axis=0,
     )
     pairs = [encoded, shift(encoded, "sub", 1)]

time: 80.2 us -> 80.2 us (level)
  starting transfers between devices: 22 us -> 23.1 us
  waiting for transfers between devices: 30.6 us -> 29.6 us
    ppermute x22, starting transfers between devices: 12.9 us -> 13.9 us  [shift(): lax.ppermute(value, axis, [(i, (i + by) % size) for i in range(size)])]
where the time goes in v10:
time: 80.2 us; the launch traced here: 80 us
  waiting for transfers between devices  29.6 us (37%)
  starting transfers between devices  23.1 us (29%)
  Pallas kernels  16.9 us (21%)
  local copies, waits for them, and re-layouts  7.31 us (9%)
  other arithmetic  2.83 us (4%)
    ppermute x22, waiting for transfers between devices, shift(): lax.ppermute(value, axis, [(i, (i + by) % size) for i in range(size)])  23.6 us
    ppermute x22, starting transfers between devices, shift(): lax.ppermute(value, axis, [(i, (i + by) % size) for i in range(size)])  13.9 us
    pallas_call x2, Pallas kernels, run_chunk(): pl.pallas_call(functools.partial(chunk_kernel, first=first, low=low, span...  9.51 us
    ppermute x5, starting transfers between devices, swap(): return lax.ppermute(value, axis, [(i, i ^ by) for i in range(size)])  9.18 us
    ppermute x5, waiting for transfers between devices, swap(): return lax.ppermute(value, axis, [(i, i ^ by) for i in range(size)])  5.95 us
    unnamed x21, local copies, waits for them, and re-layouts  4.91 us
    pallas_call x1, Pallas kernels, project_queries(): pl.pallas_call(functools.partial(query_kernel, lows=tuple(lows), gain=gai...  3.86 us
    pallas_call x1, Pallas kernels, encode(): pl.pallas_call(functools.partial(encode_kernel, pieces=pieces, piece=piec...  2.42 us
  transfers between devices with their start and end apart: 27, of which 17 were waited for; matrix products, arithmetic and copies ran while one was open for 4% of the time, Pallas kernels for 21%

profile of v10, /device:TPU:0, one launch (start us, length us, event | category | flops | bytes accessed | tf_op | source)
XLA Modules:
  0.0 80.0 jit_solution(14689148152320063799)
XLA Ops:
  0.0 1.0 %slice.94 = bf16[128,1024]{1,0:T(8,128)(2,1)S(1)} slice(bf16[512,1024]{1,0:T(8,128)(2,1)} %refs_1_.1), slice={[0:128], [0:1024]} | slice | bytes 524288 | tf_op jit(solution)/shard_map/slice | solution.py:331
  1.0 3.0 %collective-permute-start = (bf16[128,1024]{1,0:T(8,128)(2,1)S(1)}, bf16[128,1024]{1,0:T(8,128)(2,1)S(1)}, u32[]{:S(2)}, u32[]{:S(2)}) collective-permute-start(bf16[128,1024]{1,0:T(8,128)(2,1)S(1)} %slice.94), channel_id=1, source_target_pairs={{0,2},{2,0},{1,3},{3,1},{4,6},{6,4},{5,7},{7,5},{8,10},{10,8},{9,1... | collective-permute-start | bytes 786440 | tf_op jit(solution)/shard_map/ppermute | solution.py:22
  4.1 2.3 %copy-done.3 = bf16[16,128,1024]{2,1,0:T(8,128)(2,1)S(1)} copy-done((bf16[16,128,1024]{2,1,0:T(8,128)(2,1)S(1)}, bf16[16,128,1024]{2,1,0:T(8,128)(2,1)}, u32[]{:S(2)}) %copy-start.3) | copy-done | bytes 4194328
  6.4 1.3 %copy-done.4 = bf16[1024,256]{1,0:T(8,128)(2,1)S(1)} copy-done((bf16[1024,256]{1,0:T(8,128)(2,1)S(1)}, bf16[1024,256]{1,0:T(8,128)(2,1)}, u32[]{:S(2)}) %copy-start.4) | copy-done | bytes 524312
  7.7 2.4 %encode.1 = (bf16[2,528,256]{2,1,0:T(8,128)(2,1)S(1)}, bf16[2,528,256]{2,1,0:T(8,128)(2,1)S(1)}) custom-call(s32[3]{0:T(128)S(1)} %pad_add_fusion.2.meta, bf16[16,128,1024]{2,1,0:T(8,128)(2,1)S(1)} %copy-done.3, bf16[1024,256]{1,0:T(8,128)(2,1)S(1)} %copy-done.4), custom_call_target="tpu_custom_call" | custom-call | flops 1073741824 | bytes 4194304 | tf_op jit(solution)/shard_map/encode/pallas_call | solution.py:86
  10.3 1.2 %slice.96 = bf16[224,1024]{1,0:T(8,128)(2,1)S(1)} slice(bf16[512,1024]{1,0:T(8,128)(2,1)} %refs_1_.1), slice={[128:352], [0:1024]} | slice | bytes 917504 | tf_op jit(solution)/shard_map/slice | solution.py:348
  11.5 0.9 %fusion.16 = s32[1,5,16]{2,1,0:T(8,128)S(1)} fusion(s32[2,8]{1,0:T(2,128)} %bitcast.52, s32[2,8]{1,0:T(2,128)} %bitcast.53, s32[1,16]{1,0:T(1,128)} %bitcast.54), kind=kLoop, calls=%fused_computation.47 | loop fusion | flops 160 | bytes 512 | tf_op jit(solution)/shard_map/broadcast_in_dim | solution.py:335
  12.5 1.9 %collective-permute-start.2 = (s32[1,5,16]{2,1,0:T(8,128)S(1)}, s32[1,5,16]{2,1,0:T(8,128)S(1)}, u32[]{:S(2)}, u32[]{:S(2)}) collective-permute-start(s32[1,5,16]{2,1,0:T(8,128)S(1)} %fusion.16), channel_id=1, source_target_pairs={{0,4},{4,0},{8,12},{12,8},{1,5},{5,1},{9,13},{13,9},{2,6},{6,2},{1... | collective-permute-start | bytes 968 | tf_op jit(solution)/shard_map/ppermute | solution.py:27
  14.4 1.5 %collective-permute-start.4 = (bf16[528,256]{1,0:T(8,128)(2,1)S(1)}, bf16[528,256]{1,0:T(8,128)(2,1)S(1)}, u32[]{:S(2)}, u32[]{:S(2)}) collective-permute-start(bf16[528,256]{1,0:T(8,128)(2,1)S(1)} %fusion.6), channel_id=1, source_target_pairs={{0,2},{2,0},{1,3},{3,1},{4,6},{6,4},{5,7},{7,5},{8,10},{10,8},{9,1... | collective-permute-start | bytes 811016 | tf_op jit(solution)/shard_map/ppermute | solution.py:22
  15.9 0.3 collective-permute-done.2
  16.1 2.8 %collective-permute-start.3 = (s32[2,5,16]{2,1,0:T(8,128)S(1)}, s32[2,5,16]{2,1,0:T(8,128)S(1)}, u32[]{:S(2)}, u32[]{:S(2)}) collective-permute-start(s32[2,5,16]{2,1,0:T(8,128)S(1)} %pad_add_fusion), channel_id=1, source_target_pairs={{0,8},{4,12},{8,0},{12,4},{1,9},{5,13},{9,1},{13,5},{2,10},{6,14},... | collective-permute-start | bytes 1928 | tf_op jit(solution)/shard_map/ppermute | solution.py:27
  19.0 1.7 %collective-permute-done.3 = s32[2,5,16]{2,1,0:T(8,128)S(1)} collective-permute-done((s32[2,5,16]{2,1,0:T(8,128)S(1)}, s32[2,5,16]{2,1,0:T(8,128)S(1)}, u32[]{:S(2)}, u32[]{:S(2)}) %collective-permute-start.3) | collective-permute-done | bytes 672 | tf_op jit(solution)/shard_map/ppermute | solution.py:27
  20.7 1.9 %collective-permute-done.4.refs_0_ = bf16[528,256]{1,0:T(8,128)(2,1)S(1)} collective-permute-done((bf16[528,256]{1,0:T(8,128)(2,1)S(1)}, bf16[528,256]{1,0:T(8,128)(2,1)S(1)}, u32[]{:S(2)}, u32[]{:S(2)}) %collective-permute-start.4) | collective-permute-done | bytes 270368 | tf_op jit(solution)/shard_map/ppermute | solution.py:22
  22.6 1.5 %collective-permute-start.10 = (bf16[224,1024]{1,0:T(8,128)(2,1)S(1)}, bf16[224,1024]{1,0:T(8,128)(2,1)S(1)}, u32[]{:S(2)}, u32[]{:S(2)}) collective-permute-start(bf16[224,1024]{1,0:T(8,128)(2,1)S(1)} %slice.96), channel_id=1, source_target_pairs={{0,2},{2,0},{1,3},{3,1},{4,6},{6,4},{5,7},{7,5},{8,10},{10,8},{9,1... | collective-permute-start | bytes 1376264 | tf_op jit(solution)/shard_map/ppermute | solution.py:22
  24.1 1.2 %route.1 = (bf16[4,32,256]{2,1,0:T(8,128)(2,1)S(1)}, bf16[4,32,256]{2,1,0:T(8,128)(2,1)S(1)}, bf16[4,32,256]{2,1,0:T(8,128)(2,1)S(1)}, bf16[4,32,256]{2,1,0:T(8,128)(2,1)S(1)}) custom-call(s32[3]{0:T(128)S(1)} %pad_add_fusion.2.meta, s32[4,5,16]{2,1,0:T(8,128)S(1)} %constant_dynamic-update-slice_fusion.table, ...), custom_call_target="tpu_custom_call" | custom-call | flops 1081344 | bytes 811008 | tf_op jit(solution)/shard_map/route/pallas_call | solution.py:134
  25.3 2.5 %collective-permute-start.5 = (bf16[4,32,256]{2,1,0:T(8,128)(2,1)S(1)}, bf16[4,32,256]{2,1,0:T(8,128)(2,1)S(1)}, u32[]{:S(2)}, u32[]{:S(2)}) collective-permute-start(bf16[4,32,256]{2,1,0:T(8,128)(2,1)S(1)} %get-tuple-element.52), channel_id=1, source_target_pairs={{0,12},{4,8},{8,4},{12,0},{1,13},{5,9},{9,5},{13,1},{2,14},{6,10},... | collective-permute-start | bytes 196616 | tf_op jit(solution)/shard_map/ppermute | solution.py:27
  27.8 0.2 collective-permute-start.6
  28.0 1.7 %collective-permute-start.7 = (bf16[4,32,256]{2,1,0:T(8,128)(2,1)S(1)}, bf16[4,32,256]{2,1,0:T(8,128)(2,1)S(1)}, u32[]{:S(2)}, u32[]{:S(2)}) collective-permute-start(bf16[4,32,256]{2,1,0:T(8,128)(2,1)S(1)} %get-tuple-element.54), channel_id=1, source_target_pairs={{0,4},{4,0},{8,12},{12,8},{1,5},{5,1},{9,13},{13,9},{2,6},{6,2},{1... | collective-permute-start | bytes 196616 | tf_op jit(solution)/shard_map/ppermute | solution.py:27
  29.8 2.2 %collective-permute-done.5 = bf16[4,32,256]{2,1,0:T(8,128)(2,1)S(1)} collective-permute-done((bf16[4,32,256]{2,1,0:T(8,128)(2,1)S(1)}, bf16[4,32,256]{2,1,0:T(8,128)(2,1)S(1)}, u32[]{:S(2)}, u32[]{:S(2)}) %collective-permute-start.5) | collective-permute-done | bytes 65568 | tf_op jit(solution)/shard_map/ppermute | solution.py:27
  31.9 1.8 %collective-permute-done.6 = bf16[4,32,256]{2,1,0:T(8,128)(2,1)S(1)} collective-permute-done((bf16[4,32,256]{2,1,0:T(8,128)(2,1)S(1)}, bf16[4,32,256]{2,1,0:T(8,128)(2,1)S(1)}, u32[]{:S(2)}, u32[]{:S(2)}) %collective-permute-start.6) | collective-permute-done | bytes 65568 | tf_op jit(solution)/shard_map/ppermute | solution.py:27
  33.8 0.3 collective-permute-done.10.refs_2_
  34.1 0.5 collective-permute-start.9
  34.6 1.5 %collective-permute-start.13 = (bf16[16,32,256]{2,1,0:T(8,128)(2,1)S(1)}, bf16[16,32,256]{2,1,0:T(8,128)(2,1)S(1)}, u32[]{:S(2)}, u32[]{:S(2)}) collective-permute-start(bf16[16,32,256]{2,1,0:T(8,128)(2,1)S(1)} %constant_dynamic-update-slice_fusion.3.refs_1_.refs_6_), channel_id=1, source_target_pairs={{0,2},{2,0},{1,3},{3,1},{4,6},{6,4},{5,7},{7,5},{8,10},{10,8},{9,1... | collective-permute-start | bytes 786440 | tf_op jit(solution)/shard_map/ppermute | solution.py:22
  36.3 1.2 %copy-done.1 = bf16[512,1024]{1,0:T(8,128)(2,1)S(1)} copy-done((bf16[512,1024]{1,0:T(8,128)(2,1)S(1)}, bf16[512,1024]{1,0:T(8,128)(2,1)}, u32[]{:S(2)}) %copy-start.1) | copy-done | bytes 1048600
  37.5 3.9 %queries.1.refs_0_ = bf16[352,1024]{1,0:T(8,128)(2,1)S(1)} custom-call(s32[3]{0:T(128)S(1)} %pad_add_fusion.2.meta, bf16[512,1024]{1,0:T(8,128)(2,1)S(1)} %copy-done.1, bf16[512,1024]{1,0:T(8,128)(2,1)S(1)} %collective-permute-done.8.near_ref.refs_2_, bf16[128,1024]{1,0:T(8,128)(2,1)S(1)} %collective-permute-done.refs_0_, ...), custom_call_target="tpu_custom_call" | custom-call | flops 2952790016 | bytes 2883584 | tf_op jit(solution)/shard_map/queries/pallas_call | solution.py:189
  41.4 1.4 %collective-permute-done.13.refs_3_.refs_8_ = bf16[16,32,256]{2,1,0:T(8,128)(2,1)S(1)} collective-permute-done((bf16[16,32,256]{2,1,0:T(8,128)(2,1)S(1)}, bf16[16,32,256]{2,1,0:T(8,128)(2,1)S(1)}, u32[]{:S(2)}, u32[]{:S(2)}) %collective-permute-start.13) | collective-permute-done | bytes 262176 | tf_op jit(solution)/shard_map/ppermute | solution.py:22
  42.8 1.6 %collective-permute-start.19 = (bf16[160,1024]{1,0:T(8,128)(2,1)S(1)}, bf16[160,1024]{1,0:T(8,128)(2,1)S(1)}, u32[]{:S(2)}, u32[]{:S(2)}) collective-permute-start(bf16[160,1024]{1,0:T(8,128)(2,1)S(1)} %slice.98), channel_id=1, source_target_pairs={{0,2},{2,0},{1,3},{3,1},{4,6},{6,4},{5,7},{7,5},{8,10},{10,8},{9,1... | collective-permute-start | bytes 983048 | tf_op jit(solution)/shard_map/ppermute | solution.py:22
  44.4 4.0 %chunk.2 = (bf16[2,256,1024]{2,1,0:T(8,128)(2,1)S(1)}, bf16[2,64,1024]{2,1,0:T(8,128)(2,1)S(1)}, bf16[2,64,1024]{2,1,0:T(8,128)(2,1)S(1)}, bf16[2,64,1024]{2,1,0:T(8,128)(2,1)S(1)}, bf16[2,64,1024]{2,1,0:T(8,128)(2,1)S(1)}) custom-call(s32[3]{0:T(128)S(1)} %pad_add_fusion.2.meta, s32[4,5,16]{2,1,0:T(8,128)S(1)} %constant_dynamic-update-slice_fusion.table, ...), custom_call_target="tpu_custom_call" | custom-call | flops 2415919104 | bytes 524288 | tf_op jit(solution)/shard_map/chunk/pallas_call | solution.py:267
  48.5 0.3 collective-permute-start.15
  48.8 0.3 collective-permute-start.16
  49.0 0.2 collective-permute-start.17
  49.3 0.3 collective-permute-start.18
  49.6 3.5 %collective-permute-done.19.refs_3_ = bf16[160,1024]{1,0:T(8,128)(2,1)S(1)} collective-permute-done((bf16[160,1024]{1,0:T(8,128)(2,1)S(1)}, bf16[160,1024]{1,0:T(8,128)(2,1)S(1)}, u32[]{:S(2)}, u32[]{:S(2)}) %collective-permute-start.19) | collective-permute-done | bytes 327712 | tf_op jit(solution)/shard_map/ppermute | solution.py:22
  53.3 1.6 %collective-permute-start.25 = (bf16[256,1024]{1,0:T(8,128)(2,1)S(1)}, bf16[256,1024]{1,0:T(8,128)(2,1)S(1)}, u32[]{:S(2)}, u32[]{:S(2)}) collective-permute-start(bf16[256,1024]{1,0:T(8,128)(2,1)S(1)} %pad_maximum_fusion), channel_id=1, source_target_pairs={{0,2},{2,0},{1,3},{3,1},{4,6},{6,4},{5,7},{7,5},{8,10},{10,8},{9,1... | collective-permute-start | bytes 1572872 | tf_op jit(solution)/shard_map/ppermute | solution.py:22
  54.9 1.6 %collective-permute-done.20.refs_4_ = bf16[160,1024]{1,0:T(8,128)(2,1)S(1)} collective-permute-done((bf16[160,1024]{1,0:T(8,128)(2,1)S(1)}, bf16[160,1024]{1,0:T(8,128)(2,1)S(1)}, u32[]{:S(2)}, u32[]{:S(2)}) %collective-permute-start.20) | collective-permute-done | bytes 327712 | tf_op jit(solution)/shard_map/ppermute | solution.py:22
  56.5 5.5 %chunk.3 = (bf16[2,256,1024]{2,1,0:T(8,128)(2,1)S(1)}, bf16[2,64,1024]{2,1,0:T(8,128)(2,1)S(1)}, bf16[2,64,1024]{2,1,0:T(8,128)(2,1)S(1)}, bf16[2,64,1024]{2,1,0:T(8,128)(2,1)S(1)}, bf16[2,64,1024]{2,1,0:T(8,128)(2,1)S(1)}) custom-call(s32[3]{0:T(128)S(1)} %pad_add_fusion.2.meta, s32[4,5,16]{2,1,0:T(8,128)S(1)} %constant_dynamic-update-slice_fusion.table, ...), custom_call_target="tpu_custom_call" | custom-call | flops 2415919104 | bytes 524288 | tf_op jit(solution)/shard_map/chunk/pallas_call | solution.py:267
  61.9 0.2 collective-permute-start.21
  62.1 0.4 collective-permute-start.22
  62.7 0.4 collective-permute-start.24
  63.1 0.5 collective-permute-done.21
  63.5 0.4 collective-permute-done.22
  63.9 0.4 collective-permute-done.23
  64.3 0.4 collective-permute-done.24
  64.9 0.6 collective-permute-start.26
  65.5 1.4 %collective-permute-done.25 = bf16[256,1024]{1,0:T(8,128)(2,1)S(1)} collective-permute-done((bf16[256,1024]{1,0:T(8,128)(2,1)S(1)}, bf16[256,1024]{1,0:T(8,128)(2,1)S(1)}, u32[]{:S(2)}, u32[]{:S(2)}) %collective-permute-start.25) | collective-permute-done | bytes 524320 | tf_op jit(solution)/shard_map/ppermute | solution.py:22
  67.0 0.3 fusion.4
  67.4 11.6 %collective-permute-done.26 = bf16[256,1024]{1,0:T(8,128)(2,1)S(1)} collective-permute-done((bf16[256,1024]{1,0:T(8,128)(2,1)S(1)}, bf16[256,1024]{1,0:T(8,128)(2,1)S(1)}, u32[]{:S(2)}, u32[]{:S(2)}) %collective-permute-start.26) | collective-permute-done | bytes 524320 | tf_op jit(solution)/shard_map/ppermute | solution.py:22
  78.9 1.1 %fusion.5 = bf16[512,1024]{1,0:T(8,128)(2,1)} fusion(bf16[512,1024]{1,0:T(8,128)(2,1)} %copy-done.5, bf16[256,1024]{1,0:T(8,128)(2,1)S(1)} %collective-permute-done.26, bf16[2,256,1024]{2,1,0:T(8,128)(2,1)S(1)} %get-tuple-element.76, bf16[64,1024]{1,0:T(8,128)(2,1)S(1)} %slice_bitcast_fusion.1, bf16[64,1024]{1,0:T(8,128)(2,1)S(1)} %slice_bitcast_fusion.2, ...), kind=kLoop, calls=%fused_computation.8 | loop fusion | flops 3407872 | bytes 2097152 | tf_op jit(solution)/shard_map/dynamic_update_slice | solution.py:398
  (57 shorter events, 1.4 us)
Async XLA Ops:
  1.0 9.3 %collective-permute-start = (bf16[128,1024]{1,0:T(8,128)(2,1)S(1)}, bf16[128,1024]{1,0:T(8,128)(2,1)S(1)}, u32[]{:S(2)}, u32[]{:S(2)}) collective-permute-start(bf16[128,1024]{1,0:T(8,128)(2,1)S(1)} %slice.94), channel_id=1, source_target_pairs={{0,2},{2,0},{1,3},{3,1},{4,6},{6,4},{5,7},{7,5},{8,10},{10,8},{9,1... | collective-permute-start | bytes 786440 | tf_op jit(solution)/shard_map/ppermute | solution.py:22
  4.0 32.3 %copy-start = (bf16[4096,1024]{1,0:T(8,128)(2,1)S(1)}, bf16[4096,1024]{1,0:T(8,128)(2,1)}, u32[]{:S(2)}) copy-start(bf16[4096,1024]{1,0:T(8,128)(2,1)} %refs_5_.3) | copy-start | bytes 25165828
  4.1 2.3 %copy-start.3 = (bf16[16,128,1024]{2,1,0:T(8,128)(2,1)S(1)}, bf16[16,128,1024]{2,1,0:T(8,128)(2,1)}, u32[]{:S(2)}) copy-start(bf16[16,128,1024]{2,1,0:T(8,128)(2,1)} %x_ref.1) | copy-start | bytes 12582916
  6.4 1.3 %copy-start.4 = (bf16[1024,256]{1,0:T(8,128)(2,1)S(1)}, bf16[1024,256]{1,0:T(8,128)(2,1)}, u32[]{:S(2)}) copy-start(bf16[1024,256]{1,0:T(8,128)(2,1)} %w_ref.1) | copy-start | bytes 1572868
  10.3 34.1 %slice-start = ((s8[8388608]{0:T(1024)(128)(4,1)}), s8[4194304]{0:T(1024)(128)(4,1)S(1)}, s32[]{:S(2)}) async-start(s8[8388608]{0:T(1024)(128)(4,1)} %bitcast.50), calls=%async_computation | async-start | bytes 8388608
  10.3 2.1 %collective-permute-start.1 = (bf16[2,528,256]{2,1,0:T(8,128)(2,1)S(1)}, bf16[2,528,256]{2,1,0:T(8,128)(2,1)S(1)}, u32[]{:S(2)}, u32[]{:S(2)}) collective-permute-start(bf16[2,528,256]{2,1,0:T(8,128)(2,1)S(1)} %get-tuple-element.49), channel_id=1, source_target_pairs={{0,1},{1,0},{2,3},{3,2},{4,5},{5,4},{6,7},{7,6},{8,9},{9,8},{10,11... | collective-permute-start | bytes 1622024 | tf_op jit(solution)/shard_map/ppermute | solution.py:22
  12.5 3.7 %collective-permute-start.2 = (s32[1,5,16]{2,1,0:T(8,128)S(1)}, s32[1,5,16]{2,1,0:T(8,128)S(1)}, u32[]{:S(2)}, u32[]{:S(2)}) collective-permute-start(s32[1,5,16]{2,1,0:T(8,128)S(1)} %fusion.16), channel_id=1, source_target_pairs={{0,4},{4,0},{8,12},{12,8},{1,5},{5,1},{9,13},{13,9},{2,6},{6,2},{1... | collective-permute-start | bytes 968 | tf_op jit(solution)/shard_map/ppermute | solution.py:27
  14.4 8.3 %collective-permute-start.4 = (bf16[528,256]{1,0:T(8,128)(2,1)S(1)}, bf16[528,256]{1,0:T(8,128)(2,1)S(1)}, u32[]{:S(2)}, u32[]{:S(2)}) collective-permute-start(bf16[528,256]{1,0:T(8,128)(2,1)S(1)} %fusion.6), channel_id=1, source_target_pairs={{0,2},{2,0},{1,3},{3,1},{4,6},{6,4},{5,7},{7,5},{8,10},{10,8},{9,1... | collective-permute-start | bytes 811016 | tf_op jit(solution)/shard_map/ppermute | solution.py:22
  15.8 20.4 %collective-permute-start.8 = (bf16[512,1024]{1,0:T(8,128)(2,1)}, bf16[512,1024]{1,0:T(8,128)(2,1)S(1)}, u32[]{:S(2)}, u32[]{:S(2)}) collective-permute-start(bf16[512,1024]{1,0:T(8,128)(2,1)} %refs_1_.1), channel_id=1, source_target_pairs={{0,1},{1,0},{2,3},{3,2},{4,5},{5,4},{6,7},{7,6},{8,9},{9,8},{10,11... | collective-permute-start | bytes 3145736 | tf_op jit(solution)/shard_map/ppermute | solution.py:22
  16.1 4.5 %collective-permute-start.3 = (s32[2,5,16]{2,1,0:T(8,128)S(1)}, s32[2,5,16]{2,1,0:T(8,128)S(1)}, u32[]{:S(2)}, u32[]{:S(2)}) collective-permute-start(s32[2,5,16]{2,1,0:T(8,128)S(1)} %pad_add_fusion), channel_id=1, source_target_pairs={{0,8},{4,12},{8,0},{12,4},{1,9},{5,13},{9,1},{13,5},{2,10},{6,14},... | collective-permute-start | bytes 1928 | tf_op jit(solution)/shard_map/ppermute | solution.py:27
  22.6 11.4 %collective-permute-start.10 = (bf16[224,1024]{1,0:T(8,128)(2,1)S(1)}, bf16[224,1024]{1,0:T(8,128)(2,1)S(1)}, u32[]{:S(2)}, u32[]{:S(2)}) collective-permute-start(bf16[224,1024]{1,0:T(8,128)(2,1)S(1)} %slice.96), channel_id=1, source_target_pairs={{0,2},{2,0},{1,3},{3,1},{4,6},{6,4},{5,7},{7,5},{8,10},{10,8},{9,1... | collective-permute-start | bytes 1376264 | tf_op jit(solution)/shard_map/ppermute | solution.py:22
  25.3 6.6 %collective-permute-start.5 = (bf16[4,32,256]{2,1,0:T(8,128)(2,1)S(1)}, bf16[4,32,256]{2,1,0:T(8,128)(2,1)S(1)}, u32[]{:S(2)}, u32[]{:S(2)}) collective-permute-start(bf16[4,32,256]{2,1,0:T(8,128)(2,1)S(1)} %get-tuple-element.52), channel_id=1, source_target_pairs={{0,12},{4,8},{8,4},{12,0},{1,13},{5,9},{9,5},{13,1},{2,14},{6,10},... | collective-permute-start | bytes 196616 | tf_op jit(solution)/shard_map/ppermute | solution.py:27
  27.8 5.9 %collective-permute-start.6 = (bf16[4,32,256]{2,1,0:T(8,128)(2,1)S(1)}, bf16[4,32,256]{2,1,0:T(8,128)(2,1)S(1)}, u32[]{:S(2)}, u32[]{:S(2)}) collective-permute-start(bf16[4,32,256]{2,1,0:T(8,128)(2,1)S(1)} %get-tuple-element.53), channel_id=1, source_target_pairs={{0,8},{4,12},{8,0},{12,4},{1,9},{5,13},{9,1},{13,5},{2,10},{6,14},... | collective-permute-start | bytes 196616 | tf_op jit(solution)/shard_map/ppermute | solution.py:27
  28.0 5.7 %collective-permute-start.7 = (bf16[4,32,256]{2,1,0:T(8,128)(2,1)S(1)}, bf16[4,32,256]{2,1,0:T(8,128)(2,1)S(1)}, u32[]{:S(2)}, u32[]{:S(2)}) collective-permute-start(bf16[4,32,256]{2,1,0:T(8,128)(2,1)S(1)} %get-tuple-element.54), channel_id=1, source_target_pairs={{0,4},{4,0},{8,12},{12,8},{1,5},{5,1},{9,13},{13,9},{2,6},{6,2},{1... | collective-permute-start | bytes 196616 | tf_op jit(solution)/shard_map/ppermute | solution.py:27
  33.7 10.7 %slice-start.1 = ((s8[8388608]{0:T(1024)(128)(4,1)}), s8[4194304]{0:T(1024)(128)(4,1)S(1)}, s32[]{:S(2)}) async-start(s8[8388608]{0:T(1024)(128)(4,1)} %bitcast.50), calls=%async_computation.1 | async-start | bytes 8388608
  34.1 2.2 %collective-permute-start.11 = (bf16[224,1024]{1,0:T(8,128)(2,1)S(1)}, bf16[224,1024]{1,0:T(8,128)(2,1)S(1)}, u32[]{:S(2)}, u32[]{:S(2)}) collective-permute-start(bf16[224,1024]{1,0:T(8,128)(2,1)S(1)} %collective-permute-done.10.refs_2_), channel_id=1, source_target_pairs={{0,1},{1,0},{2,3},{3,2},{4,5},{5,4},{6,7},{7,6},{8,9},{9,8},{10,11... | collective-permute-start | bytes 1376264 | tf_op jit(solution)/shard_map/ppermute | solution.py:22
  34.1 2.2 %collective-permute-start.9 = (bf16[128,1024]{1,0:T(8,128)(2,1)S(1)}, bf16[128,1024]{1,0:T(8,128)(2,1)S(1)}, u32[]{:S(2)}, u32[]{:S(2)}) collective-permute-start(bf16[128,1024]{1,0:T(8,128)(2,1)S(1)} %collective-permute-done.refs_0_), channel_id=1, source_target_pairs={{0,1},{1,0},{2,3},{3,2},{4,5},{5,4},{6,7},{7,6},{8,9},{9,8},{10,11... | collective-permute-start | bytes 786440 | tf_op jit(solution)/shard_map/ppermute | solution.py:22
  34.6 8.2 %collective-permute-start.13 = (bf16[16,32,256]{2,1,0:T(8,128)(2,1)S(1)}, bf16[16,32,256]{2,1,0:T(8,128)(2,1)S(1)}, u32[]{:S(2)}, u32[]{:S(2)}) collective-permute-start(bf16[16,32,256]{2,1,0:T(8,128)(2,1)S(1)} %constant_dynamic-update-slice_fusion.3.refs_1_.refs_6_), channel_id=1, source_target_pairs={{0,2},{2,0},{1,3},{3,1},{4,6},{6,4},{5,7},{7,5},{8,10},{10,8},{9,1... | collective-permute-start | bytes 786440 | tf_op jit(solution)/shard_map/ppermute | solution.py:22
  36.1 8.3 %collective-permute-start.12 = (bf16[16,32,256]{2,1,0:T(8,128)(2,1)S(1)}, bf16[16,32,256]{2,1,0:T(8,128)(2,1)S(1)}, u32[]{:S(2)}, u32[]{:S(2)}) collective-permute-start(bf16[16,32,256]{2,1,0:T(8,128)(2,1)S(1)} %constant_dynamic-update-slice_fusion.3.refs_1_.refs_6_), channel_id=1, source_target_pairs={{0,1},{1,0},{2,3},{3,2},{4,5},{5,4},{6,7},{7,6},{8,9},{9,8},{10,11... | collective-permute-start | bytes 786440 | tf_op jit(solution)/shard_map/ppermute | solution.py:22
  36.3 1.2 %copy-start.1 = (bf16[512,1024]{1,0:T(8,128)(2,1)S(1)}, bf16[512,1024]{1,0:T(8,128)(2,1)}, u32[]{:S(2)}) copy-start(bf16[512,1024]{1,0:T(8,128)(2,1)} %refs_1_.1) | copy-start | bytes 3145732
  41.4 15.1 %copy-start.2 = (bf16[512,1024]{1,0:T(8,128)(2,1)S(1)}, bf16[512,1024]{1,0:T(8,128)(2,1)}, u32[]{:S(2)}) copy-start(bf16[512,1024]{1,0:T(8,128)(2,1)} %refs_1_.1) | copy-start | bytes 3145732
  42.8 1.6 %collective-permute-start.14 = (bf16[16,32,256]{2,1,0:T(8,128)(2,1)S(1)}, bf16[16,32,256]{2,1,0:T(8,128)(2,1)S(1)}, u32[]{:S(2)}, u32[]{:S(2)}) collective-permute-start(bf16[16,32,256]{2,1,0:T(8,128)(2,1)S(1)} %collective-permute-done.13.refs_3_.refs_8_), channel_id=1, source_target_pairs={{0,1},{1,0},{2,3},{3,2},{4,5},{5,4},{6,7},{7,6},{8,9},{9,8},{10,11... | collective-permute-start | bytes 786440 | tf_op jit(solution)/shard_map/ppermute | solution.py:22
  42.8 10.2 %collective-permute-start.19 = (bf16[160,1024]{1,0:T(8,128)(2,1)S(1)}, bf16[160,1024]{1,0:T(8,128)(2,1)S(1)}, u32[]{:S(2)}, u32[]{:S(2)}) collective-permute-start(bf16[160,1024]{1,0:T(8,128)(2,1)S(1)} %slice.98), channel_id=1, source_target_pairs={{0,2},{2,0},{1,3},{3,1},{4,6},{6,4},{5,7},{7,5},{8,10},{10,8},{9,1... | collective-permute-start | bytes 983048 | tf_op jit(solution)/shard_map/ppermute | solution.py:22
  48.5 4.6 %collective-permute-start.15 = (bf16[2,64,1024]{2,1,0:T(8,128)(2,1)S(1)}, bf16[2,64,1024]{2,1,0:T(8,128)(2,1)S(1)}, u32[]{:S(2)}, u32[]{:S(2)}) collective-permute-start(bf16[2,64,1024]{2,1,0:T(8,128)(2,1)S(1)} %get-tuple-element.65), channel_id=1, source_target_pairs={{0,1},{1,0},{2,3},{3,2},{4,5},{5,4},{6,7},{7,6},{8,9},{9,8},{10,11... | collective-permute-start | bytes 786440 | tf_op jit(solution)/shard_map/ppermute | solution.py:22
  48.8 4.3 %collective-permute-start.16 = (bf16[2,64,1024]{2,1,0:T(8,128)(2,1)S(1)}, bf16[2,64,1024]{2,1,0:T(8,128)(2,1)S(1)}, u32[]{:S(2)}, u32[]{:S(2)}) collective-permute-start(bf16[2,64,1024]{2,1,0:T(8,128)(2,1)S(1)} %get-tuple-element.66), channel_id=1, source_target_pairs={{0,1},{1,0},{2,3},{3,2},{4,5},{5,4},{6,7},{7,6},{8,9},{9,8},{10,11... | collective-permute-start | bytes 786440 | tf_op jit(solution)/shard_map/ppermute | solution.py:22
  49.0 4.0 %collective-permute-start.17 = (bf16[2,64,1024]{2,1,0:T(8,128)(2,1)S(1)}, bf16[2,64,1024]{2,1,0:T(8,128)(2,1)S(1)}, u32[]{:S(2)}, u32[]{:S(2)}) collective-permute-start(bf16[2,64,1024]{2,1,0:T(8,128)(2,1)S(1)} %get-tuple-element.67), channel_id=1, source_target_pairs={{0,1},{1,0},{2,3},{3,2},{4,5},{5,4},{6,7},{7,6},{8,9},{9,8},{10,11... | collective-permute-start | bytes 786440 | tf_op jit(solution)/shard_map/ppermute | solution.py:22
  49.3 3.8 %collective-permute-start.18 = (bf16[2,64,1024]{2,1,0:T(8,128)(2,1)S(1)}, bf16[2,64,1024]{2,1,0:T(8,128)(2,1)S(1)}, u32[]{:S(2)}, u32[]{:S(2)}) collective-permute-start(bf16[2,64,1024]{2,1,0:T(8,128)(2,1)S(1)} %get-tuple-element.68), channel_id=1, source_target_pairs={{0,1},{1,0},{2,3},{3,2},{4,5},{5,4},{6,7},{7,6},{8,9},{9,8},{10,11... | collective-permute-start | bytes 786440 | tf_op jit(solution)/shard_map/ppermute | solution.py:22
  53.3 13.6 %collective-permute-start.25 = (bf16[256,1024]{1,0:T(8,128)(2,1)S(1)}, bf16[256,1024]{1,0:T(8,128)(2,1)S(1)}, u32[]{:S(2)}, u32[]{:S(2)}) collective-permute-start(bf16[256,1024]{1,0:T(8,128)(2,1)S(1)} %pad_maximum_fusion), channel_id=1, source_target_pairs={{0,2},{2,0},{1,3},{3,1},{4,6},{6,4},{5,7},{7,5},{8,10},{10,8},{9,1... | collective-permute-start | bytes 1572872 | tf_op jit(solution)/shard_map/ppermute | solution.py:22
  54.8 1.6 %collective-permute-start.20 = (bf16[160,1024]{1,0:T(8,128)(2,1)S(1)}, bf16[160,1024]{1,0:T(8,128)(2,1)S(1)}, u32[]{:S(2)}, u32[]{:S(2)}) collective-permute-start(bf16[160,1024]{1,0:T(8,128)(2,1)S(1)} %collective-permute-done.19.refs_3_), channel_id=1, source_target_pairs={{0,1},{1,0},{2,3},{3,2},{4,5},{5,4},{6,7},{7,6},{8,9},{9,8},{10,11... | collective-permute-start | bytes 983048 | tf_op jit(solution)/shard_map/ppermute | solution.py:22
  61.9 1.6 %collective-permute-start.21 = (bf16[2,64,1024]{2,1,0:T(8,128)(2,1)S(1)}, bf16[2,64,1024]{2,1,0:T(8,128)(2,1)S(1)}, u32[]{:S(2)}, u32[]{:S(2)}) collective-permute-start(bf16[2,64,1024]{2,1,0:T(8,128)(2,1)S(1)} %get-tuple-element.77), channel_id=1, source_target_pairs={{0,1},{1,0},{2,3},{3,2},{4,5},{5,4},{6,7},{7,6},{8,9},{9,8},{10,11... | collective-permute-start | bytes 786440 | tf_op jit(solution)/shard_map/ppermute | solution.py:22
  62.1 1.8 %collective-permute-start.22 = (bf16[2,64,1024]{2,1,0:T(8,128)(2,1)S(1)}, bf16[2,64,1024]{2,1,0:T(8,128)(2,1)S(1)}, u32[]{:S(2)}, u32[]{:S(2)}) collective-permute-start(bf16[2,64,1024]{2,1,0:T(8,128)(2,1)S(1)} %get-tuple-element.78), channel_id=1, source_target_pairs={{0,1},{1,0},{2,3},{3,2},{4,5},{5,4},{6,7},{7,6},{8,9},{9,8},{10,11... | collective-permute-start | bytes 786440 | tf_op jit(solution)/shard_map/ppermute | solution.py:22
  62.5 1.8 %collective-permute-start.23 = (bf16[2,64,1024]{2,1,0:T(8,128)(2,1)S(1)}, bf16[2,64,1024]{2,1,0:T(8,128)(2,1)S(1)}, u32[]{:S(2)}, u32[]{:S(2)}) collective-permute-start(bf16[2,64,1024]{2,1,0:T(8,128)(2,1)S(1)} %get-tuple-element.79), channel_id=1, source_target_pairs={{0,1},{1,0},{2,3},{3,2},{4,5},{5,4},{6,7},{7,6},{8,9},{9,8},{10,11... | collective-permute-start | bytes 786440 | tf_op jit(solution)/shard_map/ppermute | solution.py:22
  62.7 2.0 %collective-permute-start.24 = (bf16[2,64,1024]{2,1,0:T(8,128)(2,1)S(1)}, bf16[2,64,1024]{2,1,0:T(8,128)(2,1)S(1)}, u32[]{:S(2)}, u32[]{:S(2)}) collective-permute-start(bf16[2,64,1024]{2,1,0:T(8,128)(2,1)S(1)} %get-tuple-element.80), channel_id=1, source_target_pairs={{0,1},{1,0},{2,3},{3,2},{4,5},{5,4},{6,7},{7,6},{8,9},{9,8},{10,11... | collective-permute-start | bytes 786440 | tf_op jit(solution)/shard_map/ppermute | solution.py:22
  64.9 14.0 %collective-permute-start.26 = (bf16[256,1024]{1,0:T(8,128)(2,1)S(1)}, bf16[256,1024]{1,0:T(8,128)(2,1)S(1)}, u32[]{:S(2)}, u32[]{:S(2)}) collective-permute-start(bf16[256,1024]{1,0:T(8,128)(2,1)S(1)} %pad_maximum_fusion.1), channel_id=1, source_target_pairs={{0,2},{2,0},{1,3},{3,1},{4,6},{6,4},{5,7},{7,5},{8,10},{10,8},{9,1... | collective-permute-start | bytes 1572872 | tf_op jit(solution)/shard_map/ppermute | solution.py:22
  67.3 11.6 %copy-start.5 = (bf16[512,1024]{1,0:T(8,128)(2,1)}, bf16[512,1024]{1,0:T(8,128)(2,1)S(1)}, u32[]{:S(2)}) copy-start(bf16[512,1024]{1,0:T(8,128)(2,1)S(1)} %fusion.4) | copy-start | bytes 3145732

commit v11 on v10

--- a/solution.py
+++ b/solution.py
@@ -311,7 +311,7 @@
     chunks = 2
     spans = spans_here // chunks
     first_tokens = token_count // 4
-    last_low = token_count - token_count * 10 // 32
+    last_low = token_count - token_count * 9 // 32
     gain = 1.0 / (softcap * math.sqrt(size))
     add = lambda *terms: functools.reduce(
         lambda a, b: a + b, [t.astype(f32) for t in terms]

time: 80.2 us -> 80 us (level)
  no operation moved by 1% of the time
where the time goes in v11:
time: 80 us; the launch traced here: 79.8 us
  waiting for transfers between devices  29.4 us (37%)
  starting transfers between devices  23.1 us (29%)
  Pallas kernels  17 us (21%)
  local copies, waits for them, and re-layouts  7.32 us (9%)
  other arithmetic  2.82 us (4%)
    ppermute x22, waiting for transfers between devices, shift(): lax.ppermute(value, axis, [(i, (i + by) % size) for i in range(size)])  23.5 us
    ppermute x22, starting transfers between devices, shift(): lax.ppermute(value, axis, [(i, (i + by) % size) for i in range(size)])  13.9 us
    pallas_call x2, Pallas kernels, run_chunk(): pl.pallas_call(functools.partial(chunk_kernel, first=first, low=low, span...  9.38 us
    ppermute x5, starting transfers between devices, swap(): return lax.ppermute(value, axis, [(i, i ^ by) for i in range(size)])  9.18 us
    ppermute x5, waiting for transfers between devices, swap(): return lax.ppermute(value, axis, [(i, i ^ by) for i in range(size)])  5.95 us
    unnamed x21, local copies, waits for them, and re-layouts  4.91 us
    pallas_call x1, Pallas kernels, project_queries(): pl.pallas_call(functools.partial(query_kernel, lows=tuple(lows), gain=gai...  4.01 us
    pallas_call x1, Pallas kernels, encode(): pl.pallas_call(functools.partial(encode_kernel, pieces=pieces, piece=piec...  2.42 us
  transfers between devices with their start and end apart: 27, of which 17 were waited for; matrix products, arithmetic and copies ran while one was open for 4% of the time, Pallas kernels for 21%

profile of v11, /device:TPU:0, one launch (start us, length us, event | category | flops | bytes accessed | tf_op | source)
XLA Modules:
  0.0 79.8 jit_solution(18249752448422033308)
XLA Ops:
  0.0 1.0 %slice.94 = bf16[128,1024]{1,0:T(8,128)(2,1)S(1)} slice(bf16[512,1024]{1,0:T(8,128)(2,1)} %refs_1_.1), slice={[0:128], [0:1024]} | slice | bytes 524288 | tf_op jit(solution)/shard_map/slice | solution.py:331
  1.0 3.0 %collective-permute-start = (bf16[128,1024]{1,0:T(8,128)(2,1)S(1)}, bf16[128,1024]{1,0:T(8,128)(2,1)S(1)}, u32[]{:S(2)}, u32[]{:S(2)}) collective-permute-start(bf16[128,1024]{1,0:T(8,128)(2,1)S(1)} %slice.94), channel_id=1, source_target_pairs={{0,2},{2,0},{1,3},{3,1},{4,6},{6,4},{5,7},{7,5},{8,10},{10,8},{9,1... | collective-permute-start | bytes 786440 | tf_op jit(solution)/shard_map/ppermute | solution.py:22
  4.1 2.3 %copy-done.3 = bf16[16,128,1024]{2,1,0:T(8,128)(2,1)S(1)} copy-done((bf16[16,128,1024]{2,1,0:T(8,128)(2,1)S(1)}, bf16[16,128,1024]{2,1,0:T(8,128)(2,1)}, u32[]{:S(2)}) %copy-start.3) | copy-done | bytes 4194328
  6.4 1.3 %copy-done.4 = bf16[1024,256]{1,0:T(8,128)(2,1)S(1)} copy-done((bf16[1024,256]{1,0:T(8,128)(2,1)S(1)}, bf16[1024,256]{1,0:T(8,128)(2,1)}, u32[]{:S(2)}) %copy-start.4) | copy-done | bytes 524312
  7.7 2.4 %encode.1 = (bf16[2,528,256]{2,1,0:T(8,128)(2,1)S(1)}, bf16[2,528,256]{2,1,0:T(8,128)(2,1)S(1)}) custom-call(s32[3]{0:T(128)S(1)} %pad_add_fusion.2.meta, bf16[16,128,1024]{2,1,0:T(8,128)(2,1)S(1)} %copy-done.3, bf16[1024,256]{1,0:T(8,128)(2,1)S(1)} %copy-done.4), custom_call_target="tpu_custom_call" | custom-call | flops 1073741824 | bytes 4194304 | tf_op jit(solution)/shard_map/encode/pallas_call | solution.py:86
  10.3 1.2 %slice.96 = bf16[240,1024]{1,0:T(8,128)(2,1)S(1)} slice(bf16[512,1024]{1,0:T(8,128)(2,1)} %refs_1_.1), slice={[128:368], [0:1024]} | slice | bytes 983040 | tf_op jit(solution)/shard_map/slice | solution.py:348
  11.5 0.9 %fusion.16 = s32[1,5,16]{2,1,0:T(8,128)S(1)} fusion(s32[2,8]{1,0:T(2,128)} %bitcast.52, s32[2,8]{1,0:T(2,128)} %bitcast.53, s32[1,16]{1,0:T(1,128)} %bitcast.54), kind=kLoop, calls=%fused_computation.47 | loop fusion | flops 160 | bytes 512 | tf_op jit(solution)/shard_map/broadcast_in_dim | solution.py:335
  12.5 1.9 %collective-permute-start.2 = (s32[1,5,16]{2,1,0:T(8,128)S(1)}, s32[1,5,16]{2,1,0:T(8,128)S(1)}, u32[]{:S(2)}, u32[]{:S(2)}) collective-permute-start(s32[1,5,16]{2,1,0:T(8,128)S(1)} %fusion.16), channel_id=1, source_target_pairs={{0,4},{4,0},{8,12},{12,8},{1,5},{5,1},{9,13},{13,9},{2,6},{6,2},{1... | collective-permute-start | bytes 968 | tf_op jit(solution)/shard_map/ppermute | solution.py:27
  14.4 1.5 %collective-permute-start.4 = (bf16[528,256]{1,0:T(8,128)(2,1)S(1)}, bf16[528,256]{1,0:T(8,128)(2,1)S(1)}, u32[]{:S(2)}, u32[]{:S(2)}) collective-permute-start(bf16[528,256]{1,0:T(8,128)(2,1)S(1)} %fusion.6), channel_id=1, source_target_pairs={{0,2},{2,0},{1,3},{3,1},{4,6},{6,4},{5,7},{7,5},{8,10},{10,8},{9,1... | collective-permute-start | bytes 811016 | tf_op jit(solution)/shard_map/ppermute | solution.py:22
  15.9 0.3 collective-permute-done.2
  16.2 2.8 %collective-permute-start.3 = (s32[2,5,16]{2,1,0:T(8,128)S(1)}, s32[2,5,16]{2,1,0:T(8,128)S(1)}, u32[]{:S(2)}, u32[]{:S(2)}) collective-permute-start(s32[2,5,16]{2,1,0:T(8,128)S(1)} %pad_add_fusion), channel_id=1, source_target_pairs={{0,8},{4,12},{8,0},{12,4},{1,9},{5,13},{9,1},{13,5},{2,10},{6,14},... | collective-permute-start | bytes 1928 | tf_op jit(solution)/shard_map/ppermute | solution.py:27
  19.0 1.7 %collective-permute-done.3 = s32[2,5,16]{2,1,0:T(8,128)S(1)} collective-permute-done((s32[2,5,16]{2,1,0:T(8,128)S(1)}, s32[2,5,16]{2,1,0:T(8,128)S(1)}, u32[]{:S(2)}, u32[]{:S(2)}) %collective-permute-start.3) | collective-permute-done | bytes 672 | tf_op jit(solution)/shard_map/ppermute | solution.py:27
  20.7 1.9 %collective-permute-done.4.refs_0_ = bf16[528,256]{1,0:T(8,128)(2,1)S(1)} collective-permute-done((bf16[528,256]{1,0:T(8,128)(2,1)S(1)}, bf16[528,256]{1,0:T(8,128)(2,1)S(1)}, u32[]{:S(2)}, u32[]{:S(2)}) %collective-permute-start.4) | collective-permute-done | bytes 270368 | tf_op jit(solution)/shard_map/ppermute | solution.py:22
  22.6 1.5 %collective-permute-start.10 = (bf16[240,1024]{1,0:T(8,128)(2,1)S(1)}, bf16[240,1024]{1,0:T(8,128)(2,1)S(1)}, u32[]{:S(2)}, u32[]{:S(2)}) collective-permute-start(bf16[240,1024]{1,0:T(8,128)(2,1)S(1)} %slice.96), channel_id=1, source_target_pairs={{0,2},{2,0},{1,3},{3,1},{4,6},{6,4},{5,7},{7,5},{8,10},{10,8},{9,1... | collective-permute-start | bytes 1474568 | tf_op jit(solution)/shard_map/ppermute | solution.py:22
  24.1 1.2 %route.1 = (bf16[4,32,256]{2,1,0:T(8,128)(2,1)S(1)}, bf16[4,32,256]{2,1,0:T(8,128)(2,1)S(1)}, bf16[4,32,256]{2,1,0:T(8,128)(2,1)S(1)}, bf16[4,32,256]{2,1,0:T(8,128)(2,1)S(1)}) custom-call(s32[3]{0:T(128)S(1)} %pad_add_fusion.2.meta, s32[4,5,16]{2,1,0:T(8,128)S(1)} %constant_dynamic-update-slice_fusion.table, ...), custom_call_target="tpu_custom_call" | custom-call | flops 1081344 | bytes 811008 | tf_op jit(solution)/shard_map/route/pallas_call | solution.py:134
  25.3 2.5 %collective-permute-start.5 = (bf16[4,32,256]{2,1,0:T(8,128)(2,1)S(1)}, bf16[4,32,256]{2,1,0:T(8,128)(2,1)S(1)}, u32[]{:S(2)}, u32[]{:S(2)}) collective-permute-start(bf16[4,32,256]{2,1,0:T(8,128)(2,1)S(1)} %get-tuple-element.52), channel_id=1, source_target_pairs={{0,12},{4,8},{8,4},{12,0},{1,13},{5,9},{9,5},{13,1},{2,14},{6,10},... | collective-permute-start | bytes 196616 | tf_op jit(solution)/shard_map/ppermute | solution.py:27
  28.0 1.7 %collective-permute-start.7 = (bf16[4,32,256]{2,1,0:T(8,128)(2,1)S(1)}, bf16[4,32,256]{2,1,0:T(8,128)(2,1)S(1)}, u32[]{:S(2)}, u32[]{:S(2)}) collective-permute-start(bf16[4,32,256]{2,1,0:T(8,128)(2,1)S(1)} %get-tuple-element.54), channel_id=1, source_target_pairs={{0,4},{4,0},{8,12},{12,8},{1,5},{5,1},{9,13},{13,9},{2,6},{6,2},{1... | collective-permute-start | bytes 196616 | tf_op jit(solution)/shard_map/ppermute | solution.py:27
  29.8 2.1 %collective-permute-done.5 = bf16[4,32,256]{2,1,0:T(8,128)(2,1)S(1)} collective-permute-done((bf16[4,32,256]{2,1,0:T(8,128)(2,1)S(1)}, bf16[4,32,256]{2,1,0:T(8,128)(2,1)S(1)}, u32[]{:S(2)}, u32[]{:S(2)}) %collective-permute-start.5) | collective-permute-done | bytes 65568 | tf_op jit(solution)/shard_map/ppermute | solution.py:27
  31.9 1.8 %collective-permute-done.6 = bf16[4,32,256]{2,1,0:T(8,128)(2,1)S(1)} collective-permute-done((bf16[4,32,256]{2,1,0:T(8,128)(2,1)S(1)}, bf16[4,32,256]{2,1,0:T(8,128)(2,1)S(1)}, u32[]{:S(2)}, u32[]{:S(2)}) %collective-permute-start.6) | collective-permute-done | bytes 65568 | tf_op jit(solution)/shard_map/ppermute | solution.py:27
  33.8 1.0 %collective-permute-done.10.refs_2_ = bf16[240,1024]{1,0:T(8,128)(2,1)S(1)} collective-permute-done((bf16[240,1024]{1,0:T(8,128)(2,1)S(1)}, bf16[240,1024]{1,0:T(8,128)(2,1)S(1)}, u32[]{:S(2)}, u32[]{:S(2)}) %collective-permute-start.10) | collective-permute-done | bytes 491552 | tf_op jit(solution)/shard_map/ppermute | solution.py:22
  34.8 0.5 collective-permute-start.9
  35.3 1.5 %collective-permute-start.13 = (bf16[16,32,256]{2,1,0:T(8,128)(2,1)S(1)}, bf16[16,32,256]{2,1,0:T(8,128)(2,1)S(1)}, u32[]{:S(2)}, u32[]{:S(2)}) collective-permute-start(bf16[16,32,256]{2,1,0:T(8,128)(2,1)S(1)} %constant_dynamic-update-slice_fusion.3.refs_1_.refs_6_), channel_id=1, source_target_pairs={{0,2},{2,0},{1,3},{3,1},{4,6},{6,4},{5,7},{7,5},{8,10},{10,8},{9,1... | collective-permute-start | bytes 786440 | tf_op jit(solution)/shard_map/ppermute | solution.py:22
  36.8 0.2 collective-permute-done.9.refs_1_
  37.1 1.2 %copy-done.1 = bf16[512,1024]{1,0:T(8,128)(2,1)S(1)} copy-done((bf16[512,1024]{1,0:T(8,128)(2,1)S(1)}, bf16[512,1024]{1,0:T(8,128)(2,1)}, u32[]{:S(2)}) %copy-start.1) | copy-done | bytes 1048600
  38.3 4.0 %queries.1.refs_0_ = bf16[368,1024]{1,0:T(8,128)(2,1)S(1)} custom-call(s32[3]{0:T(128)S(1)} %pad_add_fusion.2.meta, bf16[512,1024]{1,0:T(8,128)(2,1)S(1)} %copy-done.1, bf16[512,1024]{1,0:T(8,128)(2,1)S(1)} %collective-permute-done.8.near_ref.refs_2_, bf16[128,1024]{1,0:T(8,128)(2,1)S(1)} %collective-permute-done.refs_0_, ...), custom_call_target="tpu_custom_call" | custom-call | flops 3087007744 | bytes 3014656 | tf_op jit(solution)/shard_map/queries/pallas_call | solution.py:189
  42.3 1.2 %collective-permute-done.13.refs_3_.refs_8_ = bf16[16,32,256]{2,1,0:T(8,128)(2,1)S(1)} collective-permute-done((bf16[16,32,256]{2,1,0:T(8,128)(2,1)S(1)}, bf16[16,32,256]{2,1,0:T(8,128)(2,1)S(1)}, u32[]{:S(2)}, u32[]{:S(2)}) %collective-permute-start.13) | collective-permute-done | bytes 262176 | tf_op jit(solution)/shard_map/ppermute | solution.py:22
  43.5 1.6 %collective-permute-start.19 = (bf16[144,1024]{1,0:T(8,128)(2,1)S(1)}, bf16[144,1024]{1,0:T(8,128)(2,1)S(1)}, u32[]{:S(2)}, u32[]{:S(2)}) collective-permute-start(bf16[144,1024]{1,0:T(8,128)(2,1)S(1)} %slice.98), channel_id=1, source_target_pairs={{0,2},{2,0},{1,3},{3,1},{4,6},{6,4},{5,7},{7,5},{8,10},{10,8},{9,1... | collective-permute-start | bytes 884744 | tf_op jit(solution)/shard_map/ppermute | solution.py:22
  45.1 4.0 %chunk.2 = (bf16[2,256,1024]{2,1,0:T(8,128)(2,1)S(1)}, bf16[2,64,1024]{2,1,0:T(8,128)(2,1)S(1)}, bf16[2,64,1024]{2,1,0:T(8,128)(2,1)S(1)}, bf16[2,64,1024]{2,1,0:T(8,128)(2,1)S(1)}, bf16[2,64,1024]{2,1,0:T(8,128)(2,1)S(1)}) custom-call(s32[3]{0:T(128)S(1)} %pad_add_fusion.2.meta, s32[4,5,16]{2,1,0:T(8,128)S(1)} %constant_dynamic-update-slice_fusion.table, ...), custom_call_target="tpu_custom_call" | custom-call | flops 2415919104 | bytes 524288 | tf_op jit(solution)/shard_map/chunk/pallas_call | solution.py:267
  49.2 0.3 collective-permute-start.15
  49.5 0.3 collective-permute-start.16
  49.8 0.2 collective-permute-start.17
  50.0 0.3 collective-permute-start.18
  50.3 2.8 %collective-permute-done.19.refs_3_ = bf16[144,1024]{1,0:T(8,128)(2,1)S(1)} collective-permute-done((bf16[144,1024]{1,0:T(8,128)(2,1)S(1)}, bf16[144,1024]{1,0:T(8,128)(2,1)S(1)}, u32[]{:S(2)}, u32[]{:S(2)}) %collective-permute-start.19) | collective-permute-done | bytes 294944 | tf_op jit(solution)/shard_map/ppermute | solution.py:22
  53.3 1.6 %collective-permute-start.25 = (bf16[256,1024]{1,0:T(8,128)(2,1)S(1)}, bf16[256,1024]{1,0:T(8,128)(2,1)S(1)}, u32[]{:S(2)}, u32[]{:S(2)}) collective-permute-start(bf16[256,1024]{1,0:T(8,128)(2,1)S(1)} %pad_maximum_fusion), channel_id=1, source_target_pairs={{0,2},{2,0},{1,3},{3,1},{4,6},{6,4},{5,7},{7,5},{8,10},{10,8},{9,1... | collective-permute-start | bytes 1572872 | tf_op jit(solution)/shard_map/ppermute | solution.py:22
  54.9 1.5 %collective-permute-done.20.refs_4_ = bf16[144,1024]{1,0:T(8,128)(2,1)S(1)} collective-permute-done((bf16[144,1024]{1,0:T(8,128)(2,1)S(1)}, bf16[144,1024]{1,0:T(8,128)(2,1)S(1)}, u32[]{:S(2)}, u32[]{:S(2)}) %collective-permute-start.20) | collective-permute-done | bytes 294944 | tf_op jit(solution)/shard_map/ppermute | solution.py:22
  56.4 5.3 %chunk.3 = (bf16[2,256,1024]{2,1,0:T(8,128)(2,1)S(1)}, bf16[2,64,1024]{2,1,0:T(8,128)(2,1)S(1)}, bf16[2,64,1024]{2,1,0:T(8,128)(2,1)S(1)}, bf16[2,64,1024]{2,1,0:T(8,128)(2,1)S(1)}, bf16[2,64,1024]{2,1,0:T(8,128)(2,1)S(1)}) custom-call(s32[3]{0:T(128)S(1)} %pad_add_fusion.2.meta, s32[4,5,16]{2,1,0:T(8,128)S(1)} %constant_dynamic-update-slice_fusion.table, ...), custom_call_target="tpu_custom_call" | custom-call | flops 2415919104 | bytes 524288 | tf_op jit(solution)/shard_map/chunk/pallas_call | solution.py:267
  61.8 0.2 collective-permute-start.21
  62.0 0.4 collective-permute-start.22
  62.5 0.4 collective-permute-start.24
  62.9 0.5 collective-permute-done.21
  63.4 0.4 collective-permute-done.22
  63.8 0.4 collective-permute-done.23
  64.1 0.4 collective-permute-done.24
  64.7 0.6 collective-permute-start.26
  65.4 1.6 %collective-permute-done.25 = bf16[256,1024]{1,0:T(8,128)(2,1)S(1)} collective-permute-done((bf16[256,1024]{1,0:T(8,128)(2,1)S(1)}, bf16[256,1024]{1,0:T(8,128)(2,1)S(1)}, u32[]{:S(2)}, u32[]{:S(2)}) %collective-permute-start.25) | collective-permute-done | bytes 524320 | tf_op jit(solution)/shard_map/ppermute | solution.py:22
  67.0 0.3 fusion.4
  67.4 11.4 %collective-permute-done.26 = bf16[256,1024]{1,0:T(8,128)(2,1)S(1)} collective-permute-done((bf16[256,1024]{1,0:T(8,128)(2,1)S(1)}, bf16[256,1024]{1,0:T(8,128)(2,1)S(1)}, u32[]{:S(2)}, u32[]{:S(2)}) %collective-permute-start.26) | collective-permute-done | bytes 524320 | tf_op jit(solution)/shard_map/ppermute | solution.py:22
  78.8 1.1 %fusion.5 = bf16[512,1024]{1,0:T(8,128)(2,1)} fusion(bf16[512,1024]{1,0:T(8,128)(2,1)} %copy-done.5, bf16[256,1024]{1,0:T(8,128)(2,1)S(1)} %collective-permute-done.26, bf16[2,256,1024]{2,1,0:T(8,128)(2,1)S(1)} %get-tuple-element.76, bf16[64,1024]{1,0:T(8,128)(2,1)S(1)} %slice_bitcast_fusion.1, bf16[64,1024]{1,0:T(8,128)(2,1)S(1)} %slice_bitcast_fusion.2, ...), kind=kLoop, calls=%fused_computation.8 | loop fusion | flops 3407872 | bytes 2097152 | tf_op jit(solution)/shard_map/dynamic_update_slice | solution.py:398
  (57 shorter events, 1.4 us)
Async XLA Ops:
  1.0 9.3 %collective-permute-start = (bf16[128,1024]{1,0:T(8,128)(2,1)S(1)}, bf16[128,1024]{1,0:T(8,128)(2,1)S(1)}, u32[]{:S(2)}, u32[]{:S(2)}) collective-permute-start(bf16[128,1024]{1,0:T(8,128)(2,1)S(1)} %slice.94), channel_id=1, source_target_pairs={{0,2},{2,0},{1,3},{3,1},{4,6},{6,4},{5,7},{7,5},{8,10},{10,8},{9,1... | collective-permute-start | bytes 786440 | tf_op jit(solution)/shard_map/ppermute | solution.py:22
  4.0 33.1 %copy-start = (bf16[4096,1024]{1,0:T(8,128)(2,1)S(1)}, bf16[4096,1024]{1,0:T(8,128)(2,1)}, u32[]{:S(2)}) copy-start(bf16[4096,1024]{1,0:T(8,128)(2,1)} %refs_5_.3) | copy-start | bytes 25165828
  4.1 2.3 %copy-start.3 = (bf16[16,128,1024]{2,1,0:T(8,128)(2,1)S(1)}, bf16[16,128,1024]{2,1,0:T(8,128)(2,1)}, u32[]{:S(2)}) copy-start(bf16[16,128,1024]{2,1,0:T(8,128)(2,1)} %x_ref.1) | copy-start | bytes 12582916
  6.4 1.3 %copy-start.4 = (bf16[1024,256]{1,0:T(8,128)(2,1)S(1)}, bf16[1024,256]{1,0:T(8,128)(2,1)}, u32[]{:S(2)}) copy-start(bf16[1024,256]{1,0:T(8,128)(2,1)} %w_ref.1) | copy-start | bytes 1572868
  10.3 34.8 %slice-start = ((s8[8388608]{0:T(1024)(128)(4,1)}), s8[4194304]{0:T(1024)(128)(4,1)S(1)}, s32[]{:S(2)}) async-start(s8[8388608]{0:T(1024)(128)(4,1)} %bitcast.50), calls=%async_computation | async-start | bytes 8388608
  10.3 2.1 %collective-permute-start.1 = (bf16[2,528,256]{2,1,0:T(8,128)(2,1)S(1)}, bf16[2,528,256]{2,1,0:T(8,128)(2,1)S(1)}, u32[]{:S(2)}, u32[]{:S(2)}) collective-permute-start(bf16[2,528,256]{2,1,0:T(8,128)(2,1)S(1)} %get-tuple-element.49), channel_id=1, source_target_pairs={{0,1},{1,0},{2,3},{3,2},{4,5},{5,4},{6,7},{7,6},{8,9},{9,8},{10,11... | collective-permute-start | bytes 1622024 | tf_op jit(solution)/shard_map/ppermute | solution.py:22
  12.5 3.7 %collective-permute-start.2 = (s32[1,5,16]{2,1,0:T(8,128)S(1)}, s32[1,5,16]{2,1,0:T(8,128)S(1)}, u32[]{:S(2)}, u32[]{:S(2)}) collective-permute-start(s32[1,5,16]{2,1,0:T(8,128)S(1)} %fusion.16), channel_id=1, source_target_pairs={{0,4},{4,0},{8,12},{12,8},{1,5},{5,1},{9,13},{13,9},{2,6},{6,2},{1... | collective-permute-start | bytes 968 | tf_op jit(solution)/shard_map/ppermute | solution.py:27
  14.4 8.3 %collective-permute-start.4 = (bf16[528,256]{1,0:T(8,128)(2,1)S(1)}, bf16[528,256]{1,0:T(8,128)(2,1)S(1)}, u32[]{:S(2)}, u32[]{:S(2)}) collective-permute-start(bf16[528,256]{1,0:T(8,128)(2,1)S(1)} %fusion.6), channel_id=1, source_target_pairs={{0,2},{2,0},{1,3},{3,1},{4,6},{6,4},{5,7},{7,5},{8,10},{10,8},{9,1... | collective-permute-start | bytes 811016 | tf_op jit(solution)/shard_map/ppermute | solution.py:22
  15.9 21.2 %collective-permute-start.8 = (bf16[512,1024]{1,0:T(8,128)(2,1)}, bf16[512,1024]{1,0:T(8,128)(2,1)S(1)}, u32[]{:S(2)}, u32[]{:S(2)}) collective-permute-start(bf16[512,1024]{1,0:T(8,128)(2,1)} %refs_1_.1), channel_id=1, source_target_pairs={{0,1},{1,0},{2,3},{3,2},{4,5},{5,4},{6,7},{7,6},{8,9},{9,8},{10,11... | collective-permute-start | bytes 3145736 | tf_op jit(solution)/shard_map/ppermute | solution.py:22
  16.2 4.5 %collective-permute-start.3 = (s32[2,5,16]{2,1,0:T(8,128)S(1)}, s32[2,5,16]{2,1,0:T(8,128)S(1)}, u32[]{:S(2)}, u32[]{:S(2)}) collective-permute-start(s32[2,5,16]{2,1,0:T(8,128)S(1)} %pad_add_fusion), channel_id=1, source_target_pairs={{0,8},{4,12},{8,0},{12,4},{1,9},{5,13},{9,1},{13,5},{2,10},{6,14},... | collective-permute-start | bytes 1928 | tf_op jit(solution)/shard_map/ppermute | solution.py:27
  22.6 12.2 %collective-permute-start.10 = (bf16[240,1024]{1,0:T(8,128)(2,1)S(1)}, bf16[240,1024]{1,0:T(8,128)(2,1)S(1)}, u32[]{:S(2)}, u32[]{:S(2)}) collective-permute-start(bf16[240,1024]{1,0:T(8,128)(2,1)S(1)} %slice.96), channel_id=1, source_target_pairs={{0,2},{2,0},{1,3},{3,1},{4,6},{6,4},{5,7},{7,5},{8,10},{10,8},{9,1... | collective-permute-start | bytes 1474568 | tf_op jit(solution)/shard_map/ppermute | solution.py:22
  25.3 6.6 %collective-permute-start.5 = (bf16[4,32,256]{2,1,0:T(8,128)(2,1)S(1)}, bf16[4,32,256]{2,1,0:T(8,128)(2,1)S(1)}, u32[]{:S(2)}, u32[]{:S(2)}) collective-permute-start(bf16[4,32,256]{2,1,0:T(8,128)(2,1)S(1)} %get-tuple-element.52), channel_id=1, source_target_pairs={{0,12},{4,8},{8,4},{12,0},{1,13},{5,9},{9,5},{13,1},{2,14},{6,10},... | collective-permute-start | bytes 196616 | tf_op jit(solution)/shard_map/ppermute | solution.py:27
  27.8 5.9 %collective-permute-start.6 = (bf16[4,32,256]{2,1,0:T(8,128)(2,1)S(1)}, bf16[4,32,256]{2,1,0:T(8,128)(2,1)S(1)}, u32[]{:S(2)}, u32[]{:S(2)}) collective-permute-start(bf16[4,32,256]{2,1,0:T(8,128)(2,1)S(1)} %get-tuple-element.53), channel_id=1, source_target_pairs={{0,8},{4,12},{8,0},{12,4},{1,9},{5,13},{9,1},{13,5},{2,10},{6,14},... | collective-permute-start | bytes 196616 | tf_op jit(solution)/shard_map/ppermute | solution.py:27
  28.0 5.7 %collective-permute-start.7 = (bf16[4,32,256]{2,1,0:T(8,128)(2,1)S(1)}, bf16[4,32,256]{2,1,0:T(8,128)(2,1)S(1)}, u32[]{:S(2)}, u32[]{:S(2)}) collective-permute-start(bf16[4,32,256]{2,1,0:T(8,128)(2,1)S(1)} %get-tuple-element.54), channel_id=1, source_target_pairs={{0,4},{4,0},{8,12},{12,8},{1,5},{5,1},{9,13},{13,9},{2,6},{6,2},{1... | collective-permute-start | bytes 196616 | tf_op jit(solution)/shard_map/ppermute | solution.py:27
  33.8 11.4 %slice-start.1 = ((s8[8388608]{0:T(1024)(128)(4,1)}), s8[4194304]{0:T(1024)(128)(4,1)S(1)}, s32[]{:S(2)}) async-start(s8[8388608]{0:T(1024)(128)(4,1)} %bitcast.50), calls=%async_computation.1 | async-start | bytes 8388608
  34.8 2.2 %collective-permute-start.11 = (bf16[240,1024]{1,0:T(8,128)(2,1)S(1)}, bf16[240,1024]{1,0:T(8,128)(2,1)S(1)}, u32[]{:S(2)}, u32[]{:S(2)}) collective-permute-start(bf16[240,1024]{1,0:T(8,128)(2,1)S(1)} %collective-permute-done.10.refs_2_), channel_id=1, source_target_pairs={{0,1},{1,0},{2,3},{3,2},{4,5},{5,4},{6,7},{7,6},{8,9},{9,8},{10,11... | collective-permute-start | bytes 1474568 | tf_op jit(solution)/shard_map/ppermute | solution.py:22
  34.8 2.2 %collective-permute-start.9 = (bf16[128,1024]{1,0:T(8,128)(2,1)S(1)}, bf16[128,1024]{1,0:T(8,128)(2,1)S(1)}, u32[]{:S(2)}, u32[]{:S(2)}) collective-permute-start(bf16[128,1024]{1,0:T(8,128)(2,1)S(1)} %collective-permute-done.refs_0_), channel_id=1, source_target_pairs={{0,1},{1,0},{2,3},{3,2},{4,5},{5,4},{6,7},{7,6},{8,9},{9,8},{10,11... | collective-permute-start | bytes 786440 | tf_op jit(solution)/shard_map/ppermute | solution.py:22
  35.3 8.2 %collective-permute-start.13 = (bf16[16,32,256]{2,1,0:T(8,128)(2,1)S(1)}, bf16[16,32,256]{2,1,0:T(8,128)(2,1)S(1)}, u32[]{:S(2)}, u32[]{:S(2)}) collective-permute-start(bf16[16,32,256]{2,1,0:T(8,128)(2,1)S(1)} %constant_dynamic-update-slice_fusion.3.refs_1_.refs_6_), channel_id=1, source_target_pairs={{0,2},{2,0},{1,3},{3,1},{4,6},{6,4},{5,7},{7,5},{8,10},{10,8},{9,1... | collective-permute-start | bytes 786440 | tf_op jit(solution)/shard_map/ppermute | solution.py:22
  36.8 8.3 %collective-permute-start.12 = (bf16[16,32,256]{2,1,0:T(8,128)(2,1)S(1)}, bf16[16,32,256]{2,1,0:T(8,128)(2,1)S(1)}, u32[]{:S(2)}, u32[]{:S(2)}) collective-permute-start(bf16[16,32,256]{2,1,0:T(8,128)(2,1)S(1)} %constant_dynamic-update-slice_fusion.3.refs_1_.refs_6_), channel_id=1, source_target_pairs={{0,1},{1,0},{2,3},{3,2},{4,5},{5,4},{6,7},{7,6},{8,9},{9,8},{10,11... | collective-permute-start | bytes 786440 | tf_op jit(solution)/shard_map/ppermute | solution.py:22
  37.0 1.2 %copy-start.1 = (bf16[512,1024]{1,0:T(8,128)(2,1)S(1)}, bf16[512,1024]{1,0:T(8,128)(2,1)}, u32[]{:S(2)}) copy-start(bf16[512,1024]{1,0:T(8,128)(2,1)} %refs_1_.1) | copy-start | bytes 3145732
  42.3 14.1 %copy-start.2 = (bf16[512,1024]{1,0:T(8,128)(2,1)S(1)}, bf16[512,1024]{1,0:T(8,128)(2,1)}, u32[]{:S(2)}) copy-start(bf16[512,1024]{1,0:T(8,128)(2,1)} %refs_1_.1) | copy-start | bytes 3145732
  43.5 1.6 %collective-permute-start.14 = (bf16[16,32,256]{2,1,0:T(8,128)(2,1)S(1)}, bf16[16,32,256]{2,1,0:T(8,128)(2,1)S(1)}, u32[]{:S(2)}, u32[]{:S(2)}) collective-permute-start(bf16[16,32,256]{2,1,0:T(8,128)(2,1)S(1)} %collective-permute-done.13.refs_3_.refs_8_), channel_id=1, source_target_pairs={{0,1},{1,0},{2,3},{3,2},{4,5},{5,4},{6,7},{7,6},{8,9},{9,8},{10,11... | collective-permute-start | bytes 786440 | tf_op jit(solution)/shard_map/ppermute | solution.py:22
  43.5 9.5 %collective-permute-start.19 = (bf16[144,1024]{1,0:T(8,128)(2,1)S(1)}, bf16[144,1024]{1,0:T(8,128)(2,1)S(1)}, u32[]{:S(2)}, u32[]{:S(2)}) collective-permute-start(bf16[144,1024]{1,0:T(8,128)(2,1)S(1)} %slice.98), channel_id=1, source_target_pairs={{0,2},{2,0},{1,3},{3,1},{4,6},{6,4},{5,7},{7,5},{8,10},{10,8},{9,1... | collective-permute-start | bytes 884744 | tf_op jit(solution)/shard_map/ppermute | solution.py:22
  49.2 3.9 %collective-permute-start.15 = (bf16[2,64,1024]{2,1,0:T(8,128)(2,1)S(1)}, bf16[2,64,1024]{2,1,0:T(8,128)(2,1)S(1)}, u32[]{:S(2)}, u32[]{:S(2)}) collective-permute-start(bf16[2,64,1024]{2,1,0:T(8,128)(2,1)S(1)} %get-tuple-element.65), channel_id=1, source_target_pairs={{0,1},{1,0},{2,3},{3,2},{4,5},{5,4},{6,7},{7,6},{8,9},{9,8},{10,11... | collective-permute-start | bytes 786440 | tf_op jit(solution)/shard_map/ppermute | solution.py:22
  49.5 3.6 %collective-permute-start.16 = (bf16[2,64,1024]{2,1,0:T(8,128)(2,1)S(1)}, bf16[2,64,1024]{2,1,0:T(8,128)(2,1)S(1)}, u32[]{:S(2)}, u32[]{:S(2)}) collective-permute-start(bf16[2,64,1024]{2,1,0:T(8,128)(2,1)S(1)} %get-tuple-element.66), channel_id=1, source_target_pairs={{0,1},{1,0},{2,3},{3,2},{4,5},{5,4},{6,7},{7,6},{8,9},{9,8},{10,11... | collective-permute-start | bytes 786440 | tf_op jit(solution)/shard_map/ppermute | solution.py:22
  49.8 3.3 %collective-permute-start.17 = (bf16[2,64,1024]{2,1,0:T(8,128)(2,1)S(1)}, bf16[2,64,1024]{2,1,0:T(8,128)(2,1)S(1)}, u32[]{:S(2)}, u32[]{:S(2)}) collective-permute-start(bf16[2,64,1024]{2,1,0:T(8,128)(2,1)S(1)} %get-tuple-element.67), channel_id=1, source_target_pairs={{0,1},{1,0},{2,3},{3,2},{4,5},{5,4},{6,7},{7,6},{8,9},{9,8},{10,11... | collective-permute-start | bytes 786440 | tf_op jit(solution)/shard_map/ppermute | solution.py:22
  50.0 3.1 %collective-permute-start.18 = (bf16[2,64,1024]{2,1,0:T(8,128)(2,1)S(1)}, bf16[2,64,1024]{2,1,0:T(8,128)(2,1)S(1)}, u32[]{:S(2)}, u32[]{:S(2)}) collective-permute-start(bf16[2,64,1024]{2,1,0:T(8,128)(2,1)S(1)} %get-tuple-element.68), channel_id=1, source_target_pairs={{0,1},{1,0},{2,3},{3,2},{4,5},{5,4},{6,7},{7,6},{8,9},{9,8},{10,11... | collective-permute-start | bytes 786440 | tf_op jit(solution)/shard_map/ppermute | solution.py:22
  53.3 13.6 %collective-permute-start.25 = (bf16[256,1024]{1,0:T(8,128)(2,1)S(1)}, bf16[256,1024]{1,0:T(8,128)(2,1)S(1)}, u32[]{:S(2)}, u32[]{:S(2)}) collective-permute-start(bf16[256,1024]{1,0:T(8,128)(2,1)S(1)} %pad_maximum_fusion), channel_id=1, source_target_pairs={{0,2},{2,0},{1,3},{3,1},{4,6},{6,4},{5,7},{7,5},{8,10},{10,8},{9,1... | collective-permute-start | bytes 1572872 | tf_op jit(solution)/shard_map/ppermute | solution.py:22
  54.9 1.6 %collective-permute-start.20 = (bf16[144,1024]{1,0:T(8,128)(2,1)S(1)}, bf16[144,1024]{1,0:T(8,128)(2,1)S(1)}, u32[]{:S(2)}, u32[]{:S(2)}) collective-permute-start(bf16[144,1024]{1,0:T(8,128)(2,1)S(1)} %collective-permute-done.19.refs_3_), channel_id=1, source_target_pairs={{0,1},{1,0},{2,3},{3,2},{4,5},{5,4},{6,7},{7,6},{8,9},{9,8},{10,11... | collective-permute-start | bytes 884744 | tf_op jit(solution)/shard_map/ppermute | solution.py:22
  61.8 1.6 %collective-permute-start.21 = (bf16[2,64,1024]{2,1,0:T(8,128)(2,1)S(1)}, bf16[2,64,1024]{2,1,0:T(8,128)(2,1)S(1)}, u32[]{:S(2)}, u32[]{:S(2)}) collective-permute-start(bf16[2,64,1024]{2,1,0:T(8,128)(2,1)S(1)} %get-tuple-element.77), channel_id=1, source_target_pairs={{0,1},{1,0},{2,3},{3,2},{4,5},{5,4},{6,7},{7,6},{8,9},{9,8},{10,11... | collective-permute-start | bytes 786440 | tf_op jit(solution)/shard_map/ppermute | solution.py:22
  62.0 1.8 %collective-permute-start.22 = (bf16[2,64,1024]{2,1,0:T(8,128)(2,1)S(1)}, bf16[2,64,1024]{2,1,0:T(8,128)(2,1)S(1)}, u32[]{:S(2)}, u32[]{:S(2)}) collective-permute-start(bf16[2,64,1024]{2,1,0:T(8,128)(2,1)S(1)} %get-tuple-element.78), channel_id=1, source_target_pairs={{0,1},{1,0},{2,3},{3,2},{4,5},{5,4},{6,7},{7,6},{8,9},{9,8},{10,11... | collective-permute-start | bytes 786440 | tf_op jit(solution)/shard_map/ppermute | solution.py:22
  62.4 1.8 %collective-permute-start.23 = (bf16[2,64,1024]{2,1,0:T(8,128)(2,1)S(1)}, bf16[2,64,1024]{2,1,0:T(8,128)(2,1)S(1)}, u32[]{:S(2)}, u32[]{:S(2)}) collective-permute-start(bf16[2,64,1024]{2,1,0:T(8,128)(2,1)S(1)} %get-tuple-element.79), channel_id=1, source_target_pairs={{0,1},{1,0},{2,3},{3,2},{4,5},{5,4},{6,7},{7,6},{8,9},{9,8},{10,11... | collective-permute-start | bytes 786440 | tf_op jit(solution)/shard_map/ppermute | solution.py:22
  62.5 2.0 %collective-permute-start.24 = (bf16[2,64,1024]{2,1,0:T(8,128)(2,1)S(1)}, bf16[2,64,1024]{2,1,0:T(8,128)(2,1)S(1)}, u32[]{:S(2)}, u32[]{:S(2)}) collective-permute-start(bf16[2,64,1024]{2,1,0:T(8,128)(2,1)S(1)} %get-tuple-element.80), channel_id=1, source_target_pairs={{0,1},{1,0},{2,3},{3,2},{4,5},{5,4},{6,7},{7,6},{8,9},{9,8},{10,11... | collective-permute-start | bytes 786440 | tf_op jit(solution)/shard_map/ppermute | solution.py:22
  64.7 14.0 %collective-permute-start.26 = (bf16[256,1024]{1,0:T(8,128)(2,1)S(1)}, bf16[256,1024]{1,0:T(8,128)(2,1)S(1)}, u32[]{:S(2)}, u32[]{:S(2)}) collective-permute-start(bf16[256,1024]{1,0:T(8,128)(2,1)S(1)} %pad_maximum_fusion.1), channel_id=1, source_target_pairs={{0,2},{2,0},{1,3},{3,1},{4,6},{6,4},{5,7},{7,5},{8,10},{10,8},{9,1... | collective-permute-start | bytes 1572872 | tf_op jit(solution)/shard_map/ppermute | solution.py:22
  67.3 11.5 %copy-start.5 = (bf16[512,1024]{1,0:T(8,128)(2,1)}, bf16[512,1024]{1,0:T(8,128)(2,1)S(1)}, u32[]{:S(2)}) copy-start(bf16[512,1024]{1,0:T(8,128)(2,1)S(1)} %fusion.4) | copy-start | bytes 3145732

commit v12 on v11

--- a/solution.py
+++ b/solution.py
@@ -310,7 +310,7 @@
     cap = max(2, (requests + row_count - 1) // row_count)
     chunks = 2
     spans = spans_here // chunks
-    first_tokens = token_count // 4
+    first_tokens = token_count * 9 // 32
     last_low = token_count - token_count * 9 // 32
     gain = 1.0 / (softcap * math.sqrt(size))
     add = lambda *terms: functools.reduce(
@@ -350,7 +350,7 @@
     routed = route(meta, table, kept, received, crossed, cap, features, count, requests)
     encoded = jnp.concatenate(
         [routed[0]]
-        + list(lax.optimization_barrier([swap(routed[d], "rows", d) for d in range(row_count - 1, 0, -1)]))[::-1],
+        + list(lax.optimization_barrier([swap(routed[d], "rows", d) for d in range(1, row_count)])),
         axis=0,
     )
     pairs = [encoded, shift(encoded, "sub", 1)]

time: 80 us -> 80.3 us (level)
  waiting for transfers between devices: 29.4 us -> 32 us
  starting transfers between devices: 23.1 us -> 21.7 us
    ppermute x5, waiting for transfers between devices: 5.95 us -> 7.28 us  [swap(): return lax.ppermute(value, axis, [(i, i ^ by) for i in range(size)])]
    ppermute x22, waiting for transfers between devices: 23.5 us -> 24.7 us  [shift(): lax.ppermute(value, axis, [(i, (i + by) % size) for i in range(size)])]
    unnamed x21 -> x19, local copies, waits for them, and re-layouts: 4.91 us -> 3.69 us
    slice x1, local copies, waits for them, and re-layouts: 0.02 us -> 1.18 us  [shards(): fars_last = cross(after(hidden[last_low:], encoded))]
    slice x1 -> x0, local copies, waits for them, and re-layouts: 0.97 us -> none  [shards(): fars_first = cross(hidden[:first_tokens])]
    ppermute x22, starting transfers between devices: 13.9 us -> 13.1 us  [shift(): lax.ppermute(value, axis, [(i, (i + by) % size) for i in range(size)])]
where the time goes in v12:
time: 80.3 us; the launch traced here: 80.1 us
  waiting for transfers between devices  32 us (40%)
  starting transfers between devices  21.7 us (27%)
  Pallas kernels  17 us (21%)
  local copies, waits for them, and re-layouts  6.53 us (8%)
  other arithmetic  2.61 us (3%)
    ppermute x22, waiting for transfers between devices, shift(): lax.ppermute(value, axis, [(i, (i + by) % size) for i in range(size)])  24.7 us
    ppermute x22, starting transfers between devices, shift(): lax.ppermute(value, axis, [(i, (i + by) % size) for i in range(size)])  13.1 us
    pallas_call x2, Pallas kernels, run_chunk(): pl.pallas_call(functools.partial(chunk_kernel, first=first, low=low, span...  9.39 us
    ppermute x5, starting transfers between devices, swap(): return lax.ppermute(value, axis, [(i, i ^ by) for i in range(size)])  8.68 us
    ppermute x5, waiting for transfers between devices, swap(): return lax.ppermute(value, axis, [(i, i ^ by) for i in range(size)])  7.28 us
    pallas_call x1, Pallas kernels, project_queries(): pl.pallas_call(functools.partial(query_kernel, lows=tuple(lows), gain=gai...  4.01 us
    unnamed x19, local copies, waits for them, and re-layouts  3.69 us
    pallas_call x1, Pallas kernels, encode(): pl.pallas_call(functools.partial(encode_kernel, pieces=pieces, piece=piec...  2.43 us
  transfers between devices with their start and end apart: 27, of which 17 were waited for; matrix products, arithmetic and copies ran while one was open for 4% of the time, Pallas kernels for 21%

profile of v12, /device:TPU:0, one launch (start us, length us, event | category | flops | bytes accessed | tf_op | source)
XLA Modules:
  0.0 80.1 jit_solution(13021866128776805110)
XLA Ops:
  0.0 1.2 %fusion.17 = (bf16[144,1024]{1,0:T(8,128)(2,1)S(1)}, bf16[144,1024]{1,0:T(8,128)(2,1)S(1)}) fusion(bf16[512,1024]{1,0:T(8,128)(2,1)} %refs_1_.1), kind=kLoop, calls=%fused_computation.49 | loop fusion | bytes 1179648 | tf_op jit(solution)/shard_map/slice | solution.py:362
  1.2 3.0 %collective-permute-start = (bf16[144,1024]{1,0:T(8,128)(2,1)S(1)}, bf16[144,1024]{1,0:T(8,128)(2,1)S(1)}, u32[]{:S(2)}, u32[]{:S(2)}) collective-permute-start(bf16[144,1024]{1,0:T(8,128)(2,1)S(1)} %get-tuple-element.96), channel_id=1, source_target_pairs={{0,2},{2,0},{1,3},{3,1},{4,6},{6,4},{5,7},{7,5},{8,10},{10,8},{9,1... | collective-permute-start | bytes 884744 | tf_op jit(solution)/shard_map/ppermute | solution.py:22
  4.3 2.3 %copy-done.2 = bf16[16,128,1024]{2,1,0:T(8,128)(2,1)S(1)} copy-done((bf16[16,128,1024]{2,1,0:T(8,128)(2,1)S(1)}, bf16[16,128,1024]{2,1,0:T(8,128)(2,1)}, u32[]{:S(2)}) %copy-start.2) | copy-done | bytes 4194328
  6.6 1.3 %copy-done.3 = bf16[1024,256]{1,0:T(8,128)(2,1)S(1)} copy-done((bf16[1024,256]{1,0:T(8,128)(2,1)S(1)}, bf16[1024,256]{1,0:T(8,128)(2,1)}, u32[]{:S(2)}) %copy-start.3) | copy-done | bytes 524312
  7.9 2.4 %encode.1 = (bf16[2,528,256]{2,1,0:T(8,128)(2,1)S(1)}, bf16[2,528,256]{2,1,0:T(8,128)(2,1)S(1)}) custom-call(s32[3]{0:T(128)S(1)} %pad_add_fusion.2.meta, bf16[16,128,1024]{2,1,0:T(8,128)(2,1)S(1)} %copy-done.2, bf16[1024,256]{1,0:T(8,128)(2,1)S(1)} %copy-done.3), custom_call_target="tpu_custom_call" | custom-call | flops 1073741824 | bytes 4194304 | tf_op jit(solution)/shard_map/encode/pallas_call | solution.py:86
  10.4 0.8 %collective-permute-done.refs_0_ = bf16[144,1024]{1,0:T(8,128)(2,1)S(1)} collective-permute-done((bf16[144,1024]{1,0:T(8,128)(2,1)S(1)}, bf16[144,1024]{1,0:T(8,128)(2,1)S(1)}, u32[]{:S(2)}, u32[]{:S(2)}) %collective-permute-start) | collective-permute-done | bytes 294944 | tf_op jit(solution)/shard_map/ppermute | solution.py:22
  11.2 1.5 %slice.96 = bf16[224,1024]{1,0:T(8,128)(2,1)S(1)} slice(bf16[512,1024]{1,0:T(8,128)(2,1)} %refs_1_.1), slice={[144:368], [0:1024]} | slice | bytes 917504 | tf_op jit(solution)/shard_map/slice | solution.py:348
  12.7 0.7 fusion.16
  13.4 1.6 %collective-permute-start.2 = (s32[1,5,16]{2,1,0:T(8,128)S(1)}, s32[1,5,16]{2,1,0:T(8,128)S(1)}, u32[]{:S(2)}, u32[]{:S(2)}) collective-permute-start(s32[1,5,16]{2,1,0:T(8,128)S(1)} %fusion.16), channel_id=1, source_target_pairs={{0,4},{4,0},{8,12},{12,8},{1,5},{5,1},{9,13},{13,9},{2,6},{6,2},{1... | collective-permute-start | bytes 968 | tf_op jit(solution)/shard_map/ppermute | solution.py:27
  15.1 1.5 %collective-permute-start.4 = (bf16[528,256]{1,0:T(8,128)(2,1)S(1)}, bf16[528,256]{1,0:T(8,128)(2,1)S(1)}, u32[]{:S(2)}, u32[]{:S(2)}) collective-permute-start(bf16[528,256]{1,0:T(8,128)(2,1)S(1)} %fusion.6), channel_id=1, source_target_pairs={{0,2},{2,0},{1,3},{3,1},{4,6},{6,4},{5,7},{7,5},{8,10},{10,8},{9,1... | collective-permute-start | bytes 811016 | tf_op jit(solution)/shard_map/ppermute | solution.py:22
  16.6 0.5 collective-permute-done.2
  17.1 2.6 %collective-permute-start.3 = (s32[2,5,16]{2,1,0:T(8,128)S(1)}, s32[2,5,16]{2,1,0:T(8,128)S(1)}, u32[]{:S(2)}, u32[]{:S(2)}) collective-permute-start(s32[2,5,16]{2,1,0:T(8,128)S(1)} %pad_add_fusion), channel_id=1, source_target_pairs={{0,8},{4,12},{8,0},{12,4},{1,9},{5,13},{9,1},{13,5},{2,10},{6,14},... | collective-permute-start | bytes 1928 | tf_op jit(solution)/shard_map/ppermute | solution.py:27
  19.7 2.0 %collective-permute-done.3 = s32[2,5,16]{2,1,0:T(8,128)S(1)} collective-permute-done((s32[2,5,16]{2,1,0:T(8,128)S(1)}, s32[2,5,16]{2,1,0:T(8,128)S(1)}, u32[]{:S(2)}, u32[]{:S(2)}) %collective-permute-start.3) | collective-permute-done | bytes 672 | tf_op jit(solution)/shard_map/ppermute | solution.py:27
  21.7 1.9 %collective-permute-done.4.refs_0_ = bf16[528,256]{1,0:T(8,128)(2,1)S(1)} collective-permute-done((bf16[528,256]{1,0:T(8,128)(2,1)S(1)}, bf16[528,256]{1,0:T(8,128)(2,1)S(1)}, u32[]{:S(2)}, u32[]{:S(2)}) %collective-permute-start.4) | collective-permute-done | bytes 270368 | tf_op jit(solution)/shard_map/ppermute | solution.py:22
  23.5 1.5 %collective-permute-start.10 = (bf16[224,1024]{1,0:T(8,128)(2,1)S(1)}, bf16[224,1024]{1,0:T(8,128)(2,1)S(1)}, u32[]{:S(2)}, u32[]{:S(2)}) collective-permute-start(bf16[224,1024]{1,0:T(8,128)(2,1)S(1)} %slice.96), channel_id=1, source_target_pairs={{0,2},{2,0},{1,3},{3,1},{4,6},{6,4},{5,7},{7,5},{8,10},{10,8},{9,1... | collective-permute-start | bytes 1376264 | tf_op jit(solution)/shard_map/ppermute | solution.py:22
  25.0 1.2 %route.1 = (bf16[4,32,256]{2,1,0:T(8,128)(2,1)S(1)}, bf16[4,32,256]{2,1,0:T(8,128)(2,1)S(1)}, bf16[4,32,256]{2,1,0:T(8,128)(2,1)S(1)}, bf16[4,32,256]{2,1,0:T(8,128)(2,1)S(1)}) custom-call(s32[3]{0:T(128)S(1)} %pad_add_fusion.2.meta, s32[4,5,16]{2,1,0:T(8,128)S(1)} %constant_dynamic-update-slice_fusion.table, ...), custom_call_target="tpu_custom_call" | custom-call | flops 1081344 | bytes 811008 | tf_op jit(solution)/shard_map/route/pallas_call | solution.py:134
  26.2 0.5 collective-permute-start.5
  26.7 2.6 %collective-permute-start.6 = (bf16[4,32,256]{2,1,0:T(8,128)(2,1)S(1)}, bf16[4,32,256]{2,1,0:T(8,128)(2,1)S(1)}, u32[]{:S(2)}, u32[]{:S(2)}) collective-permute-start(bf16[4,32,256]{2,1,0:T(8,128)(2,1)S(1)} %get-tuple-element.53), channel_id=1, source_target_pairs={{0,8},{4,12},{8,0},{12,4},{1,9},{5,13},{9,1},{13,5},{2,10},{6,14},... | collective-permute-start | bytes 196616 | tf_op jit(solution)/shard_map/ppermute | solution.py:27
  29.3 1.3 %collective-permute-start.7 = (bf16[4,32,256]{2,1,0:T(8,128)(2,1)S(1)}, bf16[4,32,256]{2,1,0:T(8,128)(2,1)S(1)}, u32[]{:S(2)}, u32[]{:S(2)}) collective-permute-start(bf16[4,32,256]{2,1,0:T(8,128)(2,1)S(1)} %get-tuple-element.54), channel_id=1, source_target_pairs={{0,12},{4,8},{8,4},{12,0},{1,13},{5,9},{9,5},{13,1},{2,14},{6,10},... | collective-permute-start | bytes 196616 | tf_op jit(solution)/shard_map/ppermute | solution.py:27
  30.7 2.4 %collective-permute-done.6 = bf16[4,32,256]{2,1,0:T(8,128)(2,1)S(1)} collective-permute-done((bf16[4,32,256]{2,1,0:T(8,128)(2,1)S(1)}, bf16[4,32,256]{2,1,0:T(8,128)(2,1)S(1)}, u32[]{:S(2)}, u32[]{:S(2)}) %collective-permute-start.6) | collective-permute-done | bytes 65568 | tf_op jit(solution)/shard_map/ppermute | solution.py:27
  33.1 2.4 %collective-permute-done.7 = bf16[4,32,256]{2,1,0:T(8,128)(2,1)S(1)} collective-permute-done((bf16[4,32,256]{2,1,0:T(8,128)(2,1)S(1)}, bf16[4,32,256]{2,1,0:T(8,128)(2,1)S(1)}, u32[]{:S(2)}, u32[]{:S(2)}) %collective-permute-start.7) | collective-permute-done | bytes 65568 | tf_op jit(solution)/shard_map/ppermute | solution.py:27
  35.6 0.5 collective-permute-start.9
  36.1 1.1 %collective-permute-start.13 = (bf16[16,32,256]{2,1,0:T(8,128)(2,1)S(1)}, bf16[16,32,256]{2,1,0:T(8,128)(2,1)S(1)}, u32[]{:S(2)}, u32[]{:S(2)}) collective-permute-start(bf16[16,32,256]{2,1,0:T(8,128)(2,1)S(1)} %constant_dynamic-update-slice_fusion.3.refs_1_.refs_6_), channel_id=1, source_target_pairs={{0,2},{2,0},{1,3},{3,1},{4,6},{6,4},{5,7},{7,5},{8,10},{10,8},{9,1... | collective-permute-start | bytes 786440 | tf_op jit(solution)/shard_map/ppermute | solution.py:22
  37.2 0.6 collective-permute-done.9.refs_1_
  37.8 4.0 %queries.1.refs_0_ = bf16[368,1024]{1,0:T(8,128)(2,1)S(1)} custom-call(s32[3]{0:T(128)S(1)} %pad_add_fusion.2.meta, bf16[512,1024]{1,0:T(8,128)(2,1)S(1)} %copy-done.1, bf16[512,1024]{1,0:T(8,128)(2,1)S(1)} %collective-permute-done.8.near_ref.refs_2_, bf16[144,1024]{1,0:T(8,128)(2,1)S(1)} %collective-permute-done.refs_0_, ...), custom_call_target="tpu_custom_call" | custom-call | flops 3087007744 | bytes 3014656 | tf_op jit(solution)/shard_map/queries/pallas_call | solution.py:189
  41.9 2.5 %collective-permute-done.13.refs_3_.refs_8_ = bf16[16,32,256]{2,1,0:T(8,128)(2,1)S(1)} collective-permute-done((bf16[16,32,256]{2,1,0:T(8,128)(2,1)S(1)}, bf16[16,32,256]{2,1,0:T(8,128)(2,1)S(1)}, u32[]{:S(2)}, u32[]{:S(2)}) %collective-permute-start.13) | collective-permute-done | bytes 262176 | tf_op jit(solution)/shard_map/ppermute | solution.py:22
  44.4 1.0 %collective-permute-start.19 = (bf16[144,1024]{1,0:T(8,128)(2,1)S(1)}, bf16[144,1024]{1,0:T(8,128)(2,1)S(1)}, u32[]{:S(2)}, u32[]{:S(2)}) collective-permute-start(bf16[144,1024]{1,0:T(8,128)(2,1)S(1)} %get-tuple-element.69), channel_id=1, source_target_pairs={{0,2},{2,0},{1,3},{3,1},{4,6},{6,4},{5,7},{7,5},{8,10},{10,8},{9,1... | collective-permute-start | bytes 884744 | tf_op jit(solution)/shard_map/ppermute | solution.py:22
  45.4 0.5 collective-permute-done.14.refs_4_.refs_9_
  45.9 4.0 %chunk.2 = (bf16[2,256,1024]{2,1,0:T(8,128)(2,1)S(1)}, bf16[2,64,1024]{2,1,0:T(8,128)(2,1)S(1)}, bf16[2,64,1024]{2,1,0:T(8,128)(2,1)S(1)}, bf16[2,64,1024]{2,1,0:T(8,128)(2,1)S(1)}, bf16[2,64,1024]{2,1,0:T(8,128)(2,1)S(1)}) custom-call(s32[3]{0:T(128)S(1)} %pad_add_fusion.2.meta, s32[4,5,16]{2,1,0:T(8,128)S(1)} %constant_dynamic-update-slice_fusion.table, ...), custom_call_target="tpu_custom_call" | custom-call | flops 2415919104 | bytes 524288 | tf_op jit(solution)/shard_map/chunk/pallas_call | solution.py:267
  50.0 0.2 collective-permute-start.15
  50.2 0.4 collective-permute-start.16
  50.7 0.4 collective-permute-start.18
  51.0 2.8 %collective-permute-done.19.refs_3_ = bf16[144,1024]{1,0:T(8,128)(2,1)S(1)} collective-permute-done((bf16[144,1024]{1,0:T(8,128)(2,1)S(1)}, bf16[144,1024]{1,0:T(8,128)(2,1)S(1)}, u32[]{:S(2)}, u32[]{:S(2)}) %collective-permute-start.19) | collective-permute-done | bytes 294944 | tf_op jit(solution)/shard_map/ppermute | solution.py:22
  54.0 1.1 %collective-permute-start.25 = (bf16[256,1024]{1,0:T(8,128)(2,1)S(1)}, bf16[256,1024]{1,0:T(8,128)(2,1)S(1)}, u32[]{:S(2)}, u32[]{:S(2)}) collective-permute-start(bf16[256,1024]{1,0:T(8,128)(2,1)S(1)} %pad_maximum_fusion), channel_id=1, source_target_pairs={{0,2},{2,0},{1,3},{3,1},{4,6},{6,4},{5,7},{7,5},{8,10},{10,8},{9,1... | collective-permute-start | bytes 1572872 | tf_op jit(solution)/shard_map/ppermute | solution.py:22
  55.2 1.5 %collective-permute-done.20.refs_4_ = bf16[144,1024]{1,0:T(8,128)(2,1)S(1)} collective-permute-done((bf16[144,1024]{1,0:T(8,128)(2,1)S(1)}, bf16[144,1024]{1,0:T(8,128)(2,1)S(1)}, u32[]{:S(2)}, u32[]{:S(2)}) %collective-permute-start.20) | collective-permute-done | bytes 294944 | tf_op jit(solution)/shard_map/ppermute | solution.py:22
  56.7 5.4 %chunk.3 = (bf16[2,256,1024]{2,1,0:T(8,128)(2,1)S(1)}, bf16[2,64,1024]{2,1,0:T(8,128)(2,1)S(1)}, bf16[2,64,1024]{2,1,0:T(8,128)(2,1)S(1)}, bf16[2,64,1024]{2,1,0:T(8,128)(2,1)S(1)}, bf16[2,64,1024]{2,1,0:T(8,128)(2,1)S(1)}) custom-call(s32[3]{0:T(128)S(1)} %pad_add_fusion.2.meta, s32[4,5,16]{2,1,0:T(8,128)S(1)} %constant_dynamic-update-slice_fusion.table, ...), custom_call_target="tpu_custom_call" | custom-call | flops 2415919104 | bytes 524288 | tf_op jit(solution)/shard_map/chunk/pallas_call | solution.py:267
  62.1 0.2 collective-permute-start.21
  62.3 0.4 collective-permute-start.22
  62.8 0.4 collective-permute-start.24
  63.2 0.5 collective-permute-done.21
  63.7 0.4 collective-permute-done.22
  64.1 0.4 collective-permute-done.23
  64.4 0.4 collective-permute-done.24
  65.0 1.0 %collective-permute-start.26 = (bf16[256,1024]{1,0:T(8,128)(2,1)S(1)}, bf16[256,1024]{1,0:T(8,128)(2,1)S(1)}, u32[]{:S(2)}, u32[]{:S(2)}) collective-permute-start(bf16[256,1024]{1,0:T(8,128)(2,1)S(1)} %pad_maximum_fusion.1), channel_id=1, source_target_pairs={{0,2},{2,0},{1,3},{3,1},{4,6},{6,4},{5,7},{7,5},{8,10},{10,8},{9,1... | collective-permute-start | bytes 1572872 | tf_op jit(solution)/shard_map/ppermute | solution.py:22
  66.1 1.6 %collective-permute-done.25 = bf16[256,1024]{1,0:T(8,128)(2,1)S(1)} collective-permute-done((bf16[256,1024]{1,0:T(8,128)(2,1)S(1)}, bf16[256,1024]{1,0:T(8,128)(2,1)S(1)}, u32[]{:S(2)}, u32[]{:S(2)}) %collective-permute-start.25) | collective-permute-done | bytes 524320 | tf_op jit(solution)/shard_map/ppermute | solution.py:22
  67.8 0.3 fusion.4
  68.1 10.9 %collective-permute-done.26 = bf16[256,1024]{1,0:T(8,128)(2,1)S(1)} collective-permute-done((bf16[256,1024]{1,0:T(8,128)(2,1)S(1)}, bf16[256,1024]{1,0:T(8,128)(2,1)S(1)}, u32[]{:S(2)}, u32[]{:S(2)}) %collective-permute-start.26) | collective-permute-done | bytes 524320 | tf_op jit(solution)/shard_map/ppermute | solution.py:22
  79.1 1.1 %fusion.5 = bf16[512,1024]{1,0:T(8,128)(2,1)} fusion(bf16[512,1024]{1,0:T(8,128)(2,1)} %copy-done.4, bf16[256,1024]{1,0:T(8,128)(2,1)S(1)} %collective-permute-done.26, bf16[2,256,1024]{2,1,0:T(8,128)(2,1)S(1)} %get-tuple-element.76, bf16[64,1024]{1,0:T(8,128)(2,1)S(1)} %slice_bitcast_fusion.1, bf16[64,1024]{1,0:T(8,128)(2,1)S(1)} %slice_bitcast_fusion.2, ...), kind=kLoop, calls=%fused_computation.8 | loop fusion | flops 3407872 | bytes 2097152 | tf_op jit(solution)/shard_map/dynamic_update_slice | solution.py:398
  (54 shorter events, 1.2 us)
Async XLA Ops:
  0.0 37.8 %copy-start.1 = (bf16[512,1024]{1,0:T(8,128)(2,1)S(1)}, bf16[512,1024]{1,0:T(8,128)(2,1)}, u32[]{:S(2)}) copy-start(bf16[512,1024]{1,0:T(8,128)(2,1)} %refs_1_.1) | copy-start | bytes 3145732
  1.2 10.0 %collective-permute-start = (bf16[144,1024]{1,0:T(8,128)(2,1)S(1)}, bf16[144,1024]{1,0:T(8,128)(2,1)S(1)}, u32[]{:S(2)}, u32[]{:S(2)}) collective-permute-start(bf16[144,1024]{1,0:T(8,128)(2,1)S(1)} %get-tuple-element.96), channel_id=1, source_target_pairs={{0,2},{2,0},{1,3},{3,1},{4,6},{6,4},{5,7},{7,5},{8,10},{10,8},{9,1... | collective-permute-start | bytes 884744 | tf_op jit(solution)/shard_map/ppermute | solution.py:22
  4.2 33.6 %copy-start = (bf16[4096,1024]{1,0:T(8,128)(2,1)S(1)}, bf16[4096,1024]{1,0:T(8,128)(2,1)}, u32[]{:S(2)}) copy-start(bf16[4096,1024]{1,0:T(8,128)(2,1)} %refs_5_.3) | copy-start | bytes 25165828
  4.3 2.3 %copy-start.2 = (bf16[16,128,1024]{2,1,0:T(8,128)(2,1)S(1)}, bf16[16,128,1024]{2,1,0:T(8,128)(2,1)}, u32[]{:S(2)}) copy-start(bf16[16,128,1024]{2,1,0:T(8,128)(2,1)} %x_ref.1) | copy-start | bytes 12582916
  6.6 1.3 %copy-start.3 = (bf16[1024,256]{1,0:T(8,128)(2,1)S(1)}, bf16[1024,256]{1,0:T(8,128)(2,1)}, u32[]{:S(2)}) copy-start(bf16[1024,256]{1,0:T(8,128)(2,1)} %w_ref.1) | copy-start | bytes 1572868
  10.3 35.6 %slice-start = ((s8[8388608]{0:T(1024)(128)(4,1)}), s8[4194304]{0:T(1024)(128)(4,1)S(1)}, s32[]{:S(2)}) async-start(s8[8388608]{0:T(1024)(128)(4,1)} %bitcast.50), calls=%async_computation | async-start | bytes 8388608
  11.2 2.2 %collective-permute-start.1 = (bf16[2,528,256]{2,1,0:T(8,128)(2,1)S(1)}, bf16[2,528,256]{2,1,0:T(8,128)(2,1)S(1)}, u32[]{:S(2)}, u32[]{:S(2)}) collective-permute-start(bf16[2,528,256]{2,1,0:T(8,128)(2,1)S(1)} %get-tuple-element.49), channel_id=1, source_target_pairs={{0,1},{1,0},{2,3},{3,2},{4,5},{5,4},{6,7},{7,6},{8,9},{9,8},{10,11... | collective-permute-start | bytes 1622024 | tf_op jit(solution)/shard_map/ppermute | solution.py:22
  13.4 3.7 %collective-permute-start.2 = (s32[1,5,16]{2,1,0:T(8,128)S(1)}, s32[1,5,16]{2,1,0:T(8,128)S(1)}, u32[]{:S(2)}, u32[]{:S(2)}) collective-permute-start(s32[1,5,16]{2,1,0:T(8,128)S(1)} %fusion.16), channel_id=1, source_target_pairs={{0,4},{4,0},{8,12},{12,8},{1,5},{5,1},{9,13},{13,9},{2,6},{6,2},{1... | collective-permute-start | bytes 968 | tf_op jit(solution)/shard_map/ppermute | solution.py:27
  15.1 8.5 %collective-permute-start.4 = (bf16[528,256]{1,0:T(8,128)(2,1)S(1)}, bf16[528,256]{1,0:T(8,128)(2,1)S(1)}, u32[]{:S(2)}, u32[]{:S(2)}) collective-permute-start(bf16[528,256]{1,0:T(8,128)(2,1)S(1)} %fusion.6), channel_id=1, source_target_pairs={{0,2},{2,0},{1,3},{3,1},{4,6},{6,4},{5,7},{7,5},{8,10},{10,8},{9,1... | collective-permute-start | bytes 811016 | tf_op jit(solution)/shard_map/ppermute | solution.py:22
  16.6 21.2 %collective-permute-start.8 = (bf16[512,1024]{1,0:T(8,128)(2,1)}, bf16[512,1024]{1,0:T(8,128)(2,1)S(1)}, u32[]{:S(2)}, u32[]{:S(2)}) collective-permute-start(bf16[512,1024]{1,0:T(8,128)(2,1)} %refs_1_.1), channel_id=1, source_target_pairs={{0,1},{1,0},{2,3},{3,2},{4,5},{5,4},{6,7},{7,6},{8,9},{9,8},{10,11... | collective-permute-start | bytes 3145736 | tf_op jit(solution)/shard_map/ppermute | solution.py:22
  17.1 4.5 %collective-permute-start.3 = (s32[2,5,16]{2,1,0:T(8,128)S(1)}, s32[2,5,16]{2,1,0:T(8,128)S(1)}, u32[]{:S(2)}, u32[]{:S(2)}) collective-permute-start(s32[2,5,16]{2,1,0:T(8,128)S(1)} %pad_add_fusion), channel_id=1, source_target_pairs={{0,8},{4,12},{8,0},{12,4},{1,9},{5,13},{9,1},{13,5},{2,10},{6,14},... | collective-permute-start | bytes 1928 | tf_op jit(solution)/shard_map/ppermute | solution.py:27
  23.5 12.0 %collective-permute-start.10 = (bf16[224,1024]{1,0:T(8,128)(2,1)S(1)}, bf16[224,1024]{1,0:T(8,128)(2,1)S(1)}, u32[]{:S(2)}, u32[]{:S(2)}) collective-permute-start(bf16[224,1024]{1,0:T(8,128)(2,1)S(1)} %slice.96), channel_id=1, source_target_pairs={{0,2},{2,0},{1,3},{3,1},{4,6},{6,4},{5,7},{7,5},{8,10},{10,8},{9,1... | collective-permute-start | bytes 1376264 | tf_op jit(solution)/shard_map/ppermute | solution.py:22
  26.2 4.5 %collective-permute-start.5 = (bf16[4,32,256]{2,1,0:T(8,128)(2,1)S(1)}, bf16[4,32,256]{2,1,0:T(8,128)(2,1)S(1)}, u32[]{:S(2)}, u32[]{:S(2)}) collective-permute-start(bf16[4,32,256]{2,1,0:T(8,128)(2,1)S(1)} %get-tuple-element.52), channel_id=1, source_target_pairs={{0,4},{4,0},{8,12},{12,8},{1,5},{5,1},{9,13},{13,9},{2,6},{6,2},{1... | collective-permute-start | bytes 196616 | tf_op jit(solution)/shard_map/ppermute | solution.py:27
  26.7 6.3 %collective-permute-start.6 = (bf16[4,32,256]{2,1,0:T(8,128)(2,1)S(1)}, bf16[4,32,256]{2,1,0:T(8,128)(2,1)S(1)}, u32[]{:S(2)}, u32[]{:S(2)}) collective-permute-start(bf16[4,32,256]{2,1,0:T(8,128)(2,1)S(1)} %get-tuple-element.53), channel_id=1, source_target_pairs={{0,8},{4,12},{8,0},{12,4},{1,9},{5,13},{9,1},{13,5},{2,10},{6,14},... | collective-permute-start | bytes 196616 | tf_op jit(solution)/shard_map/ppermute | solution.py:27
  29.3 6.1 %collective-permute-start.7 = (bf16[4,32,256]{2,1,0:T(8,128)(2,1)S(1)}, bf16[4,32,256]{2,1,0:T(8,128)(2,1)S(1)}, u32[]{:S(2)}, u32[]{:S(2)}) collective-permute-start(bf16[4,32,256]{2,1,0:T(8,128)(2,1)S(1)} %get-tuple-element.54), channel_id=1, source_target_pairs={{0,12},{4,8},{8,4},{12,0},{1,13},{5,9},{9,5},{13,1},{2,14},{6,10},... | collective-permute-start | bytes 196616 | tf_op jit(solution)/shard_map/ppermute | solution.py:27
  35.5 10.4 %slice-start.1 = ((s8[8388608]{0:T(1024)(128)(4,1)}), s8[4194304]{0:T(1024)(128)(4,1)S(1)}, s32[]{:S(2)}) async-start(s8[8388608]{0:T(1024)(128)(4,1)} %bitcast.50), calls=%async_computation.1 | async-start | bytes 8388608
  35.5 2.3 %collective-permute-start.11 = (bf16[224,1024]{1,0:T(8,128)(2,1)S(1)}, bf16[224,1024]{1,0:T(8,128)(2,1)S(1)}, u32[]{:S(2)}, u32[]{:S(2)}) collective-permute-start(bf16[224,1024]{1,0:T(8,128)(2,1)S(1)} %collective-permute-done.10.refs_2_), channel_id=1, source_target_pairs={{0,1},{1,0},{2,3},{3,2},{4,5},{5,4},{6,7},{7,6},{8,9},{9,8},{10,11... | collective-permute-start | bytes 1376264 | tf_op jit(solution)/shard_map/ppermute | solution.py:22
  35.6 2.2 %collective-permute-start.9 = (bf16[144,1024]{1,0:T(8,128)(2,1)S(1)}, bf16[144,1024]{1,0:T(8,128)(2,1)S(1)}, u32[]{:S(2)}, u32[]{:S(2)}) collective-permute-start(bf16[144,1024]{1,0:T(8,128)(2,1)S(1)} %collective-permute-done.refs_0_), channel_id=1, source_target_pairs={{0,1},{1,0},{2,3},{3,2},{4,5},{5,4},{6,7},{7,6},{8,9},{9,8},{10,11... | collective-permute-start | bytes 884744 | tf_op jit(solution)/shard_map/ppermute | solution.py:22
  36.1 8.3 %collective-permute-start.13 = (bf16[16,32,256]{2,1,0:T(8,128)(2,1)S(1)}, bf16[16,32,256]{2,1,0:T(8,128)(2,1)S(1)}, u32[]{:S(2)}, u32[]{:S(2)}) collective-permute-start(bf16[16,32,256]{2,1,0:T(8,128)(2,1)S(1)} %constant_dynamic-update-slice_fusion.3.refs_1_.refs_6_), channel_id=1, source_target_pairs={{0,2},{2,0},{1,3},{3,1},{4,6},{6,4},{5,7},{7,5},{8,10},{10,8},{9,1... | collective-permute-start | bytes 786440 | tf_op jit(solution)/shard_map/ppermute | solution.py:22
  37.2 8.2 %collective-permute-start.12 = (bf16[16,32,256]{2,1,0:T(8,128)(2,1)S(1)}, bf16[16,32,256]{2,1,0:T(8,128)(2,1)S(1)}, u32[]{:S(2)}, u32[]{:S(2)}) collective-permute-start(bf16[16,32,256]{2,1,0:T(8,128)(2,1)S(1)} %constant_dynamic-update-slice_fusion.3.refs_1_.refs_6_), channel_id=1, source_target_pairs={{0,1},{1,0},{2,3},{3,2},{4,5},{5,4},{6,7},{7,6},{8,9},{9,8},{10,11... | collective-permute-start | bytes 786440 | tf_op jit(solution)/shard_map/ppermute | solution.py:22
  44.4 1.5 %collective-permute-start.14 = (bf16[16,32,256]{2,1,0:T(8,128)(2,1)S(1)}, bf16[16,32,256]{2,1,0:T(8,128)(2,1)S(1)}, u32[]{:S(2)}, u32[]{:S(2)}) collective-permute-start(bf16[16,32,256]{2,1,0:T(8,128)(2,1)S(1)} %collective-permute-done.13.refs_3_.refs_8_), channel_id=1, source_target_pairs={{0,1},{1,0},{2,3},{3,2},{4,5},{5,4},{6,7},{7,6},{8,9},{9,8},{10,11... | collective-permute-start | bytes 786440 | tf_op jit(solution)/shard_map/ppermute | solution.py:22
  44.4 9.4 %collective-permute-start.19 = (bf16[144,1024]{1,0:T(8,128)(2,1)S(1)}, bf16[144,1024]{1,0:T(8,128)(2,1)S(1)}, u32[]{:S(2)}, u32[]{:S(2)}) collective-permute-start(bf16[144,1024]{1,0:T(8,128)(2,1)S(1)} %get-tuple-element.69), channel_id=1, source_target_pairs={{0,2},{2,0},{1,3},{3,1},{4,6},{6,4},{5,7},{7,5},{8,10},{10,8},{9,1... | collective-permute-start | bytes 884744 | tf_op jit(solution)/shard_map/ppermute | solution.py:22
  50.0 3.8 %collective-permute-start.15 = (bf16[2,64,1024]{2,1,0:T(8,128)(2,1)S(1)}, bf16[2,64,1024]{2,1,0:T(8,128)(2,1)S(1)}, u32[]{:S(2)}, u32[]{:S(2)}) collective-permute-start(bf16[2,64,1024]{2,1,0:T(8,128)(2,1)S(1)} %get-tuple-element.65), channel_id=1, source_target_pairs={{0,1},{1,0},{2,3},{3,2},{4,5},{5,4},{6,7},{7,6},{8,9},{9,8},{10,11... | collective-permute-start | bytes 786440 | tf_op jit(solution)/shard_map/ppermute | solution.py:22
  50.2 3.6 %collective-permute-start.16 = (bf16[2,64,1024]{2,1,0:T(8,128)(2,1)S(1)}, bf16[2,64,1024]{2,1,0:T(8,128)(2,1)S(1)}, u32[]{:S(2)}, u32[]{:S(2)}) collective-permute-start(bf16[2,64,1024]{2,1,0:T(8,128)(2,1)S(1)} %get-tuple-element.66), channel_id=1, source_target_pairs={{0,1},{1,0},{2,3},{3,2},{4,5},{5,4},{6,7},{7,6},{8,9},{9,8},{10,11... | collective-permute-start | bytes 786440 | tf_op jit(solution)/shard_map/ppermute | solution.py:22
  50.5 3.3 %collective-permute-start.17 = (bf16[2,64,1024]{2,1,0:T(8,128)(2,1)S(1)}, bf16[2,64,1024]{2,1,0:T(8,128)(2,1)S(1)}, u32[]{:S(2)}, u32[]{:S(2)}) collective-permute-start(bf16[2,64,1024]{2,1,0:T(8,128)(2,1)S(1)} %get-tuple-element.67), channel_id=1, source_target_pairs={{0,1},{1,0},{2,3},{3,2},{4,5},{5,4},{6,7},{7,6},{8,9},{9,8},{10,11... | collective-permute-start | bytes 786440 | tf_op jit(solution)/shard_map/ppermute | solution.py:22
  50.7 3.1 %collective-permute-start.18 = (bf16[2,64,1024]{2,1,0:T(8,128)(2,1)S(1)}, bf16[2,64,1024]{2,1,0:T(8,128)(2,1)S(1)}, u32[]{:S(2)}, u32[]{:S(2)}) collective-permute-start(bf16[2,64,1024]{2,1,0:T(8,128)(2,1)S(1)} %get-tuple-element.68), channel_id=1, source_target_pairs={{0,1},{1,0},{2,3},{3,2},{4,5},{5,4},{6,7},{7,6},{8,9},{9,8},{10,11... | collective-permute-start | bytes 786440 | tf_op jit(solution)/shard_map/ppermute | solution.py:22
  54.0 13.6 %collective-permute-start.25 = (bf16[256,1024]{1,0:T(8,128)(2,1)S(1)}, bf16[256,1024]{1,0:T(8,128)(2,1)S(1)}, u32[]{:S(2)}, u32[]{:S(2)}) collective-permute-start(bf16[256,1024]{1,0:T(8,128)(2,1)S(1)} %pad_maximum_fusion), channel_id=1, source_target_pairs={{0,2},{2,0},{1,3},{3,1},{4,6},{6,4},{5,7},{7,5},{8,10},{10,8},{9,1... | collective-permute-start | bytes 1572872 | tf_op jit(solution)/shard_map/ppermute | solution.py:22
  55.2 1.6 %collective-permute-start.20 = (bf16[144,1024]{1,0:T(8,128)(2,1)S(1)}, bf16[144,1024]{1,0:T(8,128)(2,1)S(1)}, u32[]{:S(2)}, u32[]{:S(2)}) collective-permute-start(bf16[144,1024]{1,0:T(8,128)(2,1)S(1)} %collective-permute-done.19.refs_3_), channel_id=1, source_target_pairs={{0,1},{1,0},{2,3},{3,2},{4,5},{5,4},{6,7},{7,6},{8,9},{9,8},{10,11... | collective-permute-start | bytes 884744 | tf_op jit(solution)/shard_map/ppermute | solution.py:22
  62.1 1.6 %collective-permute-start.21 = (bf16[2,64,1024]{2,1,0:T(8,128)(2,1)S(1)}, bf16[2,64,1024]{2,1,0:T(8,128)(2,1)S(1)}, u32[]{:S(2)}, u32[]{:S(2)}) collective-permute-start(bf16[2,64,1024]{2,1,0:T(8,128)(2,1)S(1)} %get-tuple-element.77), channel_id=1, source_target_pairs={{0,1},{1,0},{2,3},{3,2},{4,5},{5,4},{6,7},{7,6},{8,9},{9,8},{10,11... | collective-permute-start | bytes 786440 | tf_op jit(solution)/shard_map/ppermute | solution.py:22
  62.3 1.8 %collective-permute-start.22 = (bf16[2,64,1024]{2,1,0:T(8,128)(2,1)S(1)}, bf16[2,64,1024]{2,1,0:T(8,128)(2,1)S(1)}, u32[]{:S(2)}, u32[]{:S(2)}) collective-permute-start(bf16[2,64,1024]{2,1,0:T(8,128)(2,1)S(1)} %get-tuple-element.78), channel_id=1, source_target_pairs={{0,1},{1,0},{2,3},{3,2},{4,5},{5,4},{6,7},{7,6},{8,9},{9,8},{10,11... | collective-permute-start | bytes 786440 | tf_op jit(solution)/shard_map/ppermute | solution.py:22
  62.7 1.8 %collective-permute-start.23 = (bf16[2,64,1024]{2,1,0:T(8,128)(2,1)S(1)}, bf16[2,64,1024]{2,1,0:T(8,128)(2,1)S(1)}, u32[]{:S(2)}, u32[]{:S(2)}) collective-permute-start(bf16[2,64,1024]{2,1,0:T(8,128)(2,1)S(1)} %get-tuple-element.79), channel_id=1, source_target_pairs={{0,1},{1,0},{2,3},{3,2},{4,5},{5,4},{6,7},{7,6},{8,9},{9,8},{10,11... | collective-permute-start | bytes 786440 | tf_op jit(solution)/shard_map/ppermute | solution.py:22
  62.8 2.0 %collective-permute-start.24 = (bf16[2,64,1024]{2,1,0:T(8,128)(2,1)S(1)}, bf16[2,64,1024]{2,1,0:T(8,128)(2,1)S(1)}, u32[]{:S(2)}, u32[]{:S(2)}) collective-permute-start(bf16[2,64,1024]{2,1,0:T(8,128)(2,1)S(1)} %get-tuple-element.80), channel_id=1, source_target_pairs={{0,1},{1,0},{2,3},{3,2},{4,5},{5,4},{6,7},{7,6},{8,9},{9,8},{10,11... | collective-permute-start | bytes 786440 | tf_op jit(solution)/shard_map/ppermute | solution.py:22
  65.0 14.0 %collective-permute-start.26 = (bf16[256,1024]{1,0:T(8,128)(2,1)S(1)}, bf16[256,1024]{1,0:T(8,128)(2,1)S(1)}, u32[]{:S(2)}, u32[]{:S(2)}) collective-permute-start(bf16[256,1024]{1,0:T(8,128)(2,1)S(1)} %pad_maximum_fusion.1), channel_id=1, source_target_pairs={{0,2},{2,0},{1,3},{3,1},{4,6},{6,4},{5,7},{7,5},{8,10},{10,8},{9,1... | collective-permute-start | bytes 1572872 | tf_op jit(solution)/shard_map/ppermute | solution.py:22
  68.1 11.0 %copy-start.4 = (bf16[512,1024]{1,0:T(8,128)(2,1)}, bf16[512,1024]{1,0:T(8,128)(2,1)S(1)}, u32[]{:S(2)}) copy-start(bf16[512,1024]{1,0:T(8,128)(2,1)S(1)} %fusion.4) | copy-start | bytes 3145732
